TPU v7x, 32 devices: a whole 2x2x4 slice. The times are simulated.
32 devices in a mesh: rep: 2 (over y), ep: 4 (over x, core), ad: 4 (over z).
Axes of the slice: x: 2, y: 2, z: 4, core: 2. Of those that a mesh axis runs over, the one named last changes fastest.
Arguments:
- tokens: bfloat16 [1024, 3072], P(('rep', 'ep')), parts along dimension 0, may hold values from -6 to 6
- chosen_experts: int32 [1024, 2], P(('rep', 'ep')), parts along dimension 0, may hold values from 0 to 7, all different within a row; in each aligned block of 128 rows (0 to 127, 128 to 255, ...) at most 48 rows name the same one
- router_gate_logits: float32 [1024, 2], P(('rep', 'ep')), parts along dimension 0, may hold values from -6 to 6
- token_tenant: int32 [1024], P(('rep', 'ep')), parts along dimension 0, may hold values from 0 to 15
- adapter_of_tenant: int32 [32], P('rep'), parts along dimension 0, may hold values from 0 to 63
- adapter_pool_slot: int32 [64], replicated, may hold values from 0 to 63, each once
- gate_weight: bfloat16 [16, 3072, 4096], P('ep', None, 'ad'), may hold values from -0.109375 to 0.109375
- up_weight: bfloat16 [16, 3072, 4096], P('ep', None, 'ad'), may hold values from -0.109375 to 0.109375
- down_weight: bfloat16 [16, 4096, 3072], P('ep', 'ad'), may hold values from -0.0625 to 0.0625
- adapter_input_factors: bfloat16 [64, 16, 16, 4096], P(None, 'ep', None, 'ad'), may hold values from -0.0625 to 0.0625
- adapter_output_factors: bfloat16 [64, 8, 16, 3072], P('ep', None, None, 'ad'), may hold values from -1.5 to 1.5
Outputs:
- mixed: bfloat16 [1024, 3072], P(('rep', 'ep'), 'ad'), parts along dimension 0
There are 2 independent parts, one for each index of `rep`. A program takes and returns all parts, laid end to end along the dimension named above; an argument that names none is the same for every part. Nothing has to cross between parts.
Inputs may be any that keep to these rules, and one draw needn't show every extreme that they name: `chosen_experts`: each row names 2 different experts. Among the 128 rows of one index of ep no expert is named by more than 48 rows, a bound that some block reaches of them. `adapter_pool_slot`: A permutation: every adapter has its own slot.
All inputs are finite; a program needn't handle non-finite values.
Results may differ from a plain program's by a relative error of at most 0.012.
Values may be sent and summed in bfloat16 or wider, within the bound.
No kernel may reach another device: no remote copies, remote signals or barrier semaphores. Data moves between devices by JAX's collectives and lax.ppermute only.
A program may use at most 256 MiB of HBM per device.

v0:
```python
import jax
import jax.numpy as jnp
from jax import lax
from jax.sharding import PartitionSpec as P

EXPERT_COUNT = 8
TOP = 2
ADAPTER_RANK = 16
TENANTS = 16
CAP = 48


def slot_targets(chosen_experts):
    route_onehot = (
        chosen_experts[:, :, None] == jnp.arange(EXPERT_COUNT, dtype=jnp.int32)[None, None, :]
    ).astype(jnp.int32)
    flat_hits = route_onehot.reshape(-1, EXPERT_COUNT)
    earlier = jnp.cumsum(flat_hits, axis=0) - flat_hits
    position = jnp.sum(earlier * flat_hits, axis=1).reshape(chosen_experts.shape)
    return (chosen_experts * CAP + position, route_onehot)


def per_device(
    tokens,
    chosen_experts,
    router_gate_logits,
    token_tenant,
    adapter_of_tenant,
    adapter_pool_slot,
    gate_weight,
    up_weight,
    down_weight,
    adapter_input_factors,
    adapter_output_factors,
):
    row_count = tokens.shape[0]
    feature_count = tokens.shape[1]
    local_halves = gate_weight.shape[0]
    slot_count = EXPERT_COUNT * CAP
    target, route_onehot = slot_targets(chosen_experts)
    slot_index = jnp.arange(slot_count, dtype=jnp.int32)
    picked = jnp.any(target[None, :, :] == slot_index[:, None, None], axis=2)
    packed = jnp.dot(
        picked.astype(jnp.bfloat16), tokens, preferred_element_type=jnp.float32
    ).astype(jnp.bfloat16)
    packed_tenant = jnp.max(jnp.where(picked, token_tenant[None, :], -1), axis=1)
    doubled = jnp.broadcast_to(
        packed.reshape(EXPERT_COUNT, 1, CAP, feature_count), (EXPERT_COUNT, 2, CAP, feature_count)
    ).reshape(2 * EXPERT_COUNT, CAP, feature_count)
    doubled_tenant = jnp.broadcast_to(
        packed_tenant.reshape(EXPERT_COUNT, 1, CAP), (EXPERT_COUNT, 2, CAP)
    ).reshape(2 * EXPERT_COUNT, CAP)
    arrived, arrived_tenant = (
        lax.all_to_all(doubled, "ep", split_axis=0, concat_axis=1, tiled=True),
        lax.all_to_all(doubled_tenant, "ep", split_axis=0, concat_axis=1, tiled=True),
    )
    slot_of_tenant = adapter_pool_slot[adapter_of_tenant]
    tenant_index = jnp.arange(TENANTS, dtype=jnp.int32)
    partial_list = []
    lowrank_list = []
    for half_index in range(local_halves):
        block_rows = arrived[half_index]
        gate_value = jnp.dot(
            block_rows, gate_weight[half_index], preferred_element_type=jnp.float32
        )
        up_value = jnp.dot(block_rows, up_weight[half_index], preferred_element_type=jnp.float32)
        hidden_units = (jax.nn.silu(gate_value) * up_value).astype(jnp.bfloat16)
        partial_list.append(
            jnp.dot(hidden_units, down_weight[half_index], preferred_element_type=jnp.float32)
        )
        adapter_factors = adapter_input_factors[slot_of_tenant, half_index]
        down_projected = jnp.einsum(
            "uk,xvk->uxv", hidden_units, adapter_factors, preferred_element_type=jnp.float32
        )
        member = (arrived_tenant[half_index][:, None] == tenant_index[None, :]).astype(jnp.float32)
        lowrank_list.append(jnp.sum(down_projected * member[:, :, None], axis=1))
    partials = jnp.stack(partial_list)
    lowrank = jnp.stack(lowrank_list)
    summed = lax.psum_scatter(partials.astype(jnp.bfloat16), "ad", scatter_dimension=2, tiled=True)
    lowrank_total = lax.psum(lowrank.astype(jnp.bfloat16), "ad").astype(jnp.float32)
    returned, returned_low = (
        lax.all_to_all(summed, "ep", split_axis=1, concat_axis=0, tiled=True),
        lax.all_to_all(
            lowrank_total.astype(jnp.bfloat16), "ep", split_axis=1, concat_axis=0, tiled=True
        ).astype(lowrank_total.dtype),
    )
    span_width = returned.shape[2]
    pair_sum = (
        returned.astype(jnp.float32)
        .reshape(EXPERT_COUNT, 2, CAP, span_width)
        .sum(axis=1)
        .reshape(slot_count, span_width)
    )
    low_sum = (
        returned_low.reshape(EXPERT_COUNT, 2, CAP, ADAPTER_RANK)
        .sum(axis=1)
        .reshape(slot_count, ADAPTER_RANK)
    )
    pool_slot_rows = lax.all_gather(adapter_output_factors, "ep", axis=0, tiled=True)
    chosen = pool_slot_rows[slot_of_tenant]
    chosen_blocks = chosen.reshape(TENANTS * EXPERT_COUNT, ADAPTER_RANK, span_width)
    weights = jax.nn.sigmoid(router_gate_logits - router_gate_logits[:, ::-1])
    mixed_rows = jnp.zeros((row_count, span_width), jnp.float32)
    for pick_index in range(TOP):
        slot_at = target[:, pick_index]
        base_rows = pair_sum[slot_at]
        low_rows = low_sum[slot_at]
        block_id = token_tenant * EXPERT_COUNT + chosen_experts[:, pick_index]
        factor_rows = chosen_blocks[block_id].astype(jnp.float32)
        adapter = jnp.sum(low_rows[:, :, None] * factor_rows, axis=1)
        mixed_rows = mixed_rows + weights[:, pick_index, None] * (base_rows + adapter)
    return mixed_rows.astype(jnp.bfloat16)


def solution(mesh):
    placed = (
        P(("rep", "ep"), None),
        P(("rep", "ep"), None),
        P(("rep", "ep"), None),
        P(("rep", "ep")),
        P("rep"),
        P(),
        P("ep", None, "ad"),
        P("ep", None, "ad"),
        P("ep", "ad", None),
        P(None, "ep", None, "ad"),
        P("ep", None, None, "ad"),
    )
    return jax.shard_map(
        per_device, mesh=mesh, in_specs=placed, out_specs=P(("rep", "ep"), "ad"), check_vma=False
    )
```

profile of v0, /device:TPU:0, one launch (start us, length us, event | category | flops | bytes accessed | tf_op | source)
XLA Modules:
  0.0 255.4 jit_solution(8504975418224400489)
XLA Ops:
  7.4 0.9 copy.55
  8.5 0.6 reduce-window.6
  9.7 0.7 multiply_add_fusion
  10.4 0.8 convolution_convert_fusion
  11.2 0.6 broadcast_in_dim.27
  11.8 57.8 %all_to_all.49 = bf16[16,48,3072]{2,1,0:T(8,128)(2,1)S(1)} all-to-all(bf16[16,48,3072]{2,1,0:T(8,128)(2,1)S(1)} %bitcast.196), channel_id=1, replica_groups=mesh['rep'=2,'ep'=4,'ad'=4] {'ep'}, dimensions={0} | all-to-all | bytes 9437184 | tf_op jit(solution)/shard_map/all_to_all | solution.py:54
  70.0 4.2 %fusion.4 = f32[192,1024]{1,0:T(8,128)S(1)} fusion(bf16[192,3072]{1,0:T(8,128)(2,1)S(1)} %bitcast.208, bf16[4,3072,1024]{2,1,0:T(8,128)(2,1)} %param.17), kind=kOutput, calls=%fused_computation.16 | convolution fusion | flops 1207959552 | bytes 8257536 | tf_op jit(solution)/shard_map/dot_general | solution.py:63
  74.3 4.2 %fusion.22 = f32[192,1024]{1,0:T(8,128)S(1)} fusion(bf16[192,3072]{1,0:T(8,128)(2,1)S(1)} %bitcast.206, bf16[4,3072,1024]{2,1,0:T(8,128)(2,1)} %param.17), kind=kOutput, calls=%fused_computation.34 | convolution fusion | flops 1207959552 | bytes 8257536 | tf_op jit(solution)/shard_map/dot_general | solution.py:63
  78.5 4.4 %fusion.72 = bf16[192,1024]{1,0:T(8,128)(2,1)S(1)} fusion(bf16[192,3072]{1,0:T(8,128)(2,1)S(1)} %bitcast.209, bf16[4,3072,1024]{2,1,0:T(8,128)(2,1)} %param.18, f32[192,1024]{1,0:T(8,128)S(1)} %fusion.4), kind=kOutput, calls=%fused_computation.65 | convolution fusion | flops 1209139200 | bytes 8650752 | tf_op jit(solution)/shard_map/dot_general | solution.py:66
  82.9 4.4 %fusion.81 = bf16[192,1024]{1,0:T(8,128)(2,1)S(1)} fusion(bf16[192,3072]{1,0:T(8,128)(2,1)S(1)} %bitcast.207, bf16[4,3072,1024]{2,1,0:T(8,128)(2,1)} %param.18, f32[192,1024]{1,0:T(8,128)S(1)} %fusion.22), kind=kOutput, calls=%fused_computation.68 | convolution fusion | flops 1209139200 | bytes 8650752 | tf_op jit(solution)/shard_map/dot_general | solution.py:66
  87.4 4.3 %fusion.48 = bf16[1,192,3072]{2,1,0:T(8,128)(2,1)S(1)} fusion(bf16[192,1024]{1,0:T(8,128)(2,1)S(1)} %fusion.72, bf16[4,1024,3072]{2,1,0:T(8,128)(2,1)} %param.19), kind=kOutput, calls=%fused_computation.56 | convolution fusion | flops 1208549376 | bytes 7864320 | tf_op jit(solution)/shard_map/dot_general | solution.py:69
  91.7 4.3 %fusion.57 = bf16[1,192,3072]{2,1,0:T(8,128)(2,1)S(1)} fusion(bf16[192,1024]{1,0:T(8,128)(2,1)S(1)} %fusion.81, bf16[4,1024,3072]{2,1,0:T(8,128)(2,1)} %param.19), kind=kOutput, calls=%fused_computation.59 | convolution fusion | flops 1208549376 | bytes 7864320 | tf_op jit(solution)/shard_map/dot_general | solution.py:69
  96.2 1.4 fusion.10
  97.6 4.3 %fusion.75 = bf16[192,1024]{1,0:T(8,128)(2,1)S(1)} fusion(bf16[192,3072]{1,0:T(8,128)(2,1)S(1)} %bitcast.205, bf16[4,3072,1024]{2,1,0:T(8,128)(2,1)} %param.18, f32[192,1024]{1,0:T(8,128)S(1)} %fusion.10), kind=kOutput, calls=%fused_computation.66 | convolution fusion | flops 1209139200 | bytes 8650752 | tf_op jit(solution)/shard_map/dot_general | solution.py:66
  101.8 4.2 %fusion.51 = bf16[1,192,3072]{2,1,0:T(8,128)(2,1)S(1)} fusion(bf16[192,1024]{1,0:T(8,128)(2,1)S(1)} %fusion.75, bf16[4,1024,3072]{2,1,0:T(8,128)(2,1)} %param.19), kind=kOutput, calls=%fused_computation.57 | convolution fusion | flops 1208549376 | bytes 7864320 | tf_op jit(solution)/shard_map/dot_general | solution.py:69
  106.0 1.6 fusion.16
  107.7 4.3 %fusion.78 = bf16[192,1024]{1,0:T(8,128)(2,1)S(1)} fusion(bf16[192,3072]{1,0:T(8,128)(2,1)S(1)} %bitcast.203, bf16[4,3072,1024]{2,1,0:T(8,128)(2,1)} %param.18, f32[192,1024]{1,0:T(8,128)S(1)} %fusion.16), kind=kOutput, calls=%fused_computation.67 | convolution fusion | flops 1209139200 | bytes 8650752 | tf_op jit(solution)/shard_map/dot_general | solution.py:66
  111.9 4.3 %fusion.54 = bf16[1,192,3072]{2,1,0:T(8,128)(2,1)S(1)} fusion(bf16[192,1024]{1,0:T(8,128)(2,1)S(1)} %fusion.78, bf16[4,1024,3072]{2,1,0:T(8,128)(2,1)} %param.19), kind=kOutput, calls=%fused_computation.58 | convolution fusion | flops 1208549376 | bytes 7864320 | tf_op jit(solution)/shard_map/dot_general | solution.py:69
  116.3 2.5 pad_maximum_fusion
  118.8 0.5 all-gather.2.cloned.1.call-update
  119.6 0.7 reshape.315
  120.3 3.2 %all-to-all-start.2 = ((s32[4,1,192]{2,1,0:T(1,128)}), s32[4,1,192]{2,1,0:T(1,128)S(1)}, u32[]{:S(2)}, u32[]{:S(2)}) async-start(s32[4,1,192]{2,1,0:T(1,128)} %reshape.315), calls=%async_computation.3 | async-start | bytes 8192 | tf_op jit(solution)/shard_map/all_to_all | solution.py:55
  123.6 0.7 gather_fusion.1
  124.3 5.6 %gather_fusion.2 = bf16[16,16,1024]{2,1,0:T(8,128)(2,1)S(1)} fusion(bf16[64,4,16,1024]{3,2,1,0:T(8,128)(2,1)} %param.20, s32[16]{0:T(128)S(1)} %get-tuple-element.19), kind=kCustom, calls=%fused_computation.2 | custom fusion | bytes 1048704 | tf_op jit(solution)/shard_map/gather | solution.py:71
  129.9 5.4 %gather_fusion.3 = bf16[16,16,1024]{2,1,0:T(8,128)(2,1)S(1)} fusion(bf16[64,4,16,1024]{3,2,1,0:T(8,128)(2,1)} %param.20, s32[16]{0:T(128)S(1)} %get-tuple-element.20), kind=kCustom, calls=%fused_computation.3 | custom fusion | bytes 1048704 | tf_op jit(solution)/shard_map/gather | solution.py:71
  135.3 4.4 %gather_fusion.4 = bf16[16,16,1024]{2,1,0:T(8,128)(2,1)S(1)} fusion(bf16[64,4,16,1024]{3,2,1,0:T(8,128)(2,1)} %param.20, s32[16]{0:T(128)S(1)} %get-tuple-element.21), kind=kCustom, calls=%fused_computation.4 | custom fusion | bytes 1048704 | tf_op jit(solution)/shard_map/gather | solution.py:71
  139.7 4.1 %gather_fusion.5 = bf16[16,16,1024]{2,1,0:T(8,128)(2,1)S(1)} fusion(bf16[64,4,16,1024]{3,2,1,0:T(8,128)(2,1)} %param.20, s32[16]{0:T(128)S(1)} %get-tuple-element.22), kind=kCustom, calls=%fused_computation.5 | custom fusion | bytes 1048704 | tf_op jit(solution)/shard_map/gather | solution.py:71
  143.8 0.5 broadcast.321
  144.3 0.7 reduce.18
  146.8 21.2 %psum.7 = bf16[4,192,16]{1,2,0:T(8,128)(2,1)S(1)} all-reduce(bf16[4,192,16]{1,2,0:T(8,128)(2,1)S(1)} %pad_maximum_fusion.1), channel_id=1, replica_groups=mesh['rep'=2,'ep'=4,'ad'=4] {'ad'}, use_global_device_ids=true, to_apply=%region_11.12 | all-reduce | flops 12288 | bytes 49152 | tf_op jit(solution)/shard_map/psum | solution.py:80
  168.2 0.8 reshape.317
  169.0 3.3 %all-to-all-start.3 = ((bf16[4,2,1536]{2,1,0:T(2,128)(2,1)}), bf16[4,2,1536]{2,1,0:T(2,128)(2,1)S(1)}, u32[]{:S(2)}, u32[]{:S(2)}) async-start(bf16[4,2,1536]{2,1,0:T(2,128)(2,1)} %reshape.317), calls=%async_computation.4 | async-start | bytes 49152 | tf_op jit(solution)/shard_map/all_to_all | solution.py:83
  172.3 0.6 pad_clamp_fusion
  172.9 32.7 %reduce-scatter.2.cloned.1.call-done = bf16[4,192,768]{2,1,0:T(8,128)(2,1)} async-done(((bf16[4,192,3072]{2,1,0:T(8,128)(2,1)}), bf16[4,192,768]{2,1,0:T(8,128)(2,1)}) %reduce-scatter.2.cloned.1.call-update) | async-done | bytes 1179664 | tf_op jit(solution)/shard_map/reduce_scatter | solution.py:79
  205.6 3.3 %copy.58 = bf16[4,192,768]{2,0,1:T(4,128)(2,1)} copy(bf16[4,192,768]{2,1,0:T(8,128)(2,1)} %reduce-scatter.2.cloned.1.call-done) | data formatting | bytes 2359296 | tf_op jit(solution)/shard_map/reduce_scatter | solution.py:79
  208.8 3.7 %all-to-all-start.1 = ((bf16[4,192,768]{2,0,1:T(4,128)(2,1)}), bf16[4,192,768]{2,0,1:T(4,128)(2,1)S(1)}, u32[]{:S(2)}, u32[]{:S(2)}) async-start(bf16[4,192,768]{2,0,1:T(4,128)(2,1)} %copy.58), calls=%async_computation.2 | async-start | bytes 2359296 | tf_op jit(solution)/shard_map/all_to_all | solution.py:82
  212.7 0.6 slice_bitcast_fusion.1
  213.9 1.2 gather_fusion.10
  215.1 1.2 gather_fusion.6
  216.4 11.9 %all-to-all-done.1 = bf16[4,192,768]{2,0,1:T(4,128)(2,1)S(1)} async-done(((bf16[4,192,768]{2,0,1:T(4,128)(2,1)}), bf16[4,192,768]{2,0,1:T(4,128)(2,1)S(1)}, u32[]{:S(2)}, u32[]{:S(2)}) %all-to-all-start.1) | async-done | bytes 1179680 | tf_op jit(solution)/shard_map/all_to_all | solution.py:82
  229.0 0.8 gather_fusion.9
  229.8 1.6 gather_fusion
  231.4 5.3 %gather_fusion.7 = bf16[16,8,16,768]{3,2,1,0:T(8,128)(2,1)S(1)} fusion(bf16[64,8,16,768]{3,2,1,0:T(8,128)(2,1)} %all-gather.2.cloned.1.call-done, s32[1024]{0:T(1024)S(1)} %pad_clamp_fusion.3), kind=kCustom, calls=%fused_computation.7 | custom fusion | bytes 6291520 | tf_op jit(solution)/shard_map/gather | solution.py:100
  236.8 2.5 gather_fusion.11
  239.3 2.4 gather_fusion.8
  241.8 3.7 %multiply_reduce_fusion = f32[128,768]{1,0:T(8,128)S(1)} fusion(bf16[128,16,768]{2,1,0:T(8,128)(2,1)} %gather_fusion.11, f32[128,16]{1,0:T(8,128)} %gather_fusion.10), kind=kLoop, calls=%fused_computation.36 | loop fusion | flops 4620288 | bytes 3547136 | tf_op jit(solution)/shard_map/reduce_sum | solution.py:110
  245.5 1.6 multiply_reduce_fusion.1
  247.1 0.8 add_convert_fusion
  (96 shorter events, 5.2 us)
Async XLA Ops:
  7.4 3.1 %copy-start = (bf16[128,3072]{1,0:T(8,128)(2,1)S(1)}, bf16[128,3072]{1,0:T(8,128)(2,1)}, u32[]{:S(2)}) copy-start(bf16[128,3072]{1,0:T(8,128)(2,1)} %param.11) | copy-start | bytes 2359300
  7.4 198.2 %reduce-scatter.2.cloned.1.call-start = ((), (), s32[]{:S(2)}) async-start(), calls=%async_computation.5 | async-start | bytes 5898240 | tf_op jit(solution)/shard_map/reduce_scatter | solution.py:79
  78.5 17.6 %slice-start = ((s8[25165824]{0:T(1024)(128)(4,1)}), s8[4194304]{0:T(1024)(128)(4,1)S(1)}, s32[]{:S(2)}) async-start(s8[25165824]{0:T(1024)(128)(4,1)} %bitcast.220), calls=%async_computation.7 | async-start | bytes 8388608
  78.5 17.6 %slice-start.1 = ((s8[25165824]{0:T(1024)(128)(4,1)}), s8[4194304]{0:T(1024)(128)(4,1)S(1)}, s32[]{:S(2)}) async-start(s8[25165824]{0:T(1024)(128)(4,1)} %bitcast.220), calls=%async_computation.8 | async-start | bytes 8388608
  82.9 13.2 %slice-start.2 = ((s8[25165824]{0:T(1024)(128)(4,1)}), s8[4194304]{0:T(1024)(128)(4,1)S(1)}, s32[]{:S(2)}) async-start(s8[25165824]{0:T(1024)(128)(4,1)} %bitcast.220), calls=%async_computation.9 | async-start | bytes 8388608
  82.9 13.2 %slice-start.3 = ((s8[25165824]{0:T(1024)(128)(4,1)}), s8[4194304]{0:T(1024)(128)(4,1)S(1)}, s32[]{:S(2)}) async-start(s8[25165824]{0:T(1024)(128)(4,1)} %bitcast.220), calls=%async_computation.10 | async-start | bytes 8388608
  87.4 8.8 %slice-start.4 = ((s8[25165824]{0:T(1024)(128)(4,1)}), s8[4194304]{0:T(1024)(128)(4,1)S(1)}, s32[]{:S(2)}) async-start(s8[25165824]{0:T(1024)(128)(4,1)} %bitcast.220), calls=%async_computation.11 | async-start | bytes 8388608
  91.7 4.4 %slice-start.5 = ((s8[25165824]{0:T(1024)(128)(4,1)}), s8[4194304]{0:T(1024)(128)(4,1)S(1)}, s32[]{:S(2)}) async-start(s8[25165824]{0:T(1024)(128)(4,1)} %bitcast.220), calls=%async_computation.12 | async-start | bytes 8388608
  111.9 4.3 %copy-start.12 = (bf16[192,1024]{1,0:T(8,128)(2,1)}, bf16[192,1024]{1,0:T(8,128)(2,1)S(1)}, u32[]{:S(2)}) copy-start(bf16[192,1024]{1,0:T(8,128)(2,1)S(1)} %fusion.78) | copy-start | bytes 1179652
  118.7 0.7 copy-start.8
  118.7 4.8 %copy-start.11 = (s32[16]{0:T(128)S(1)}, s32[16]{0:T(128)}, u32[]{:S(2)}) copy-start(s32[16]{0:T(128)} %param.15) | copy-start | bytes 196
  118.7 4.9 %copy-start.2 = (s32[64]{0:T(128)S(1)}, s32[64]{0:T(128)}, u32[]{:S(2)}) copy-start(s32[64]{0:T(128)} %param.16) | copy-start | bytes 772
  118.7 5.5 %copy-start.6 = (s32[128,2]{0,1:T(2,128)S(1)}, s32[128,2]{0,1:T(2,128)}, u32[]{:S(2)}) copy-start(s32[128,2]{0,1:T(2,128)} %param.12) | copy-start | bytes 3076
  118.8 112.7 %all-gather.2.cloned.1.call-start = ((), (), s32[]{:S(2)}) async-start(), calls=%async_computation.6 | async-start | bytes 15728640 | tf_op jit(solution)/shard_map/all_gather | solution.py:99
  120.3 23.4 %all-to-all-start.2 = ((s32[4,1,192]{2,1,0:T(1,128)}), s32[4,1,192]{2,1,0:T(1,128)S(1)}, u32[]{:S(2)}, u32[]{:S(2)}) async-start(s32[4,1,192]{2,1,0:T(1,128)} %reshape.315), calls=%async_computation.3 | async-start | bytes 8192 | tf_op jit(solution)/shard_map/all_to_all | solution.py:55
  145.4 1.1 copy-start.13
  145.4 27.4 %copy-start.7 = (f32[128,2]{0,1:T(2,128)S(1)}, f32[128,2]{0,1:T(2,128)}, u32[]{:S(2)}) copy-start(f32[128,2]{0,1:T(2,128)} %param.13) | copy-start | bytes 3076
  169.0 39.8 %all-to-all-start.3 = ((bf16[4,2,1536]{2,1,0:T(2,128)(2,1)}), bf16[4,2,1536]{2,1,0:T(2,128)(2,1)S(1)}, u32[]{:S(2)}, u32[]{:S(2)}) async-start(bf16[4,2,1536]{2,1,0:T(2,128)(2,1)} %reshape.317), calls=%async_computation.4 | async-start | bytes 49152 | tf_op jit(solution)/shard_map/all_to_all | solution.py:83
  208.8 19.4 %all-to-all-start.1 = ((bf16[4,192,768]{2,0,1:T(4,128)(2,1)}), bf16[4,192,768]{2,0,1:T(4,128)(2,1)S(1)}, u32[]{:S(2)}, u32[]{:S(2)}) async-start(bf16[4,192,768]{2,0,1:T(4,128)(2,1)} %copy.58), calls=%async_computation.2 | async-start | bytes 2359296 | tf_op jit(solution)/shard_map/all_to_all | solution.py:82
  241.7 3.7 %copy-start.3 = (bf16[128,16,768]{2,1,0:T(8,128)(2,1)S(1)}, bf16[128,16,768]{2,1,0:T(8,128)(2,1)}, u32[]{:S(2)}) copy-start(bf16[128,16,768]{2,1,0:T(8,128)(2,1)} %gather_fusion.8) | copy-start | bytes 9437188
  241.7 3.7 %copy-start.5 = (f32[128,16]{1,0:T(8,128)S(1)}, f32[128,16]{1,0:T(8,128)}, u32[]{:S(2)}) copy-start(f32[128,16]{1,0:T(8,128)} %gather_fusion.6) | copy-start | bytes 24580
  241.7 5.4 %copy-start.4 = (f32[128,768]{1,0:T(8,128)S(1)}, f32[128,768]{1,0:T(8,128)}, u32[]{:S(2)}) copy-start(f32[128,768]{1,0:T(8,128)} %gather_fusion) | copy-start | bytes 1179652
  241.7 5.4 %copy-start.9 = (f32[128]{0:T(128)S(1)}, f32[128]{0:T(128)}, u32[]{:S(2)}) copy-start(f32[128]{0:T(128)} %get-tuple-element.15) | copy-start | bytes 1540
  241.8 5.4 %copy-start.10 = (f32[128]{0:T(128)S(1)}, f32[128]{0:T(128)}, u32[]{:S(2)}) copy-start(f32[128]{0:T(128)} %get-tuple-element.16) | copy-start | bytes 1540
  241.8 6.2 %copy-start.1 = (bf16[128,3072]{1,0:T(8,128)(2,1)S(1)}, bf16[128,3072]{1,0:T(8,128)(2,1)}, u32[]{:S(2)}) copy-start(bf16[128,3072]{1,0:T(8,128)(2,1)} %param.11) | copy-start | bytes 2359300
Sparse Core Ops, SparseCore 0:
  118.9 86.6 reduce-scatter.1
Sparse Core Ops, SparseCore 1:
  120.8 82.5 all-gather.1
where the time goes:
time: 256 us; the launch traced here: 255 us
  blocking collectives  79 us (31%)
  matrix products  48.1 us (19%)
  local copies, waits for them, and re-layouts  45.4 us (18%)
  waiting for transfers between devices  45.1 us (18%)
  between operations  15.5 us (6%)
  other arithmetic  12 us (5%)
  starting transfers between devices  10.3 us (4%)
    all_to_all x1, blocking collectives, per_device(): lax.all_to_all(doubled, 'ep', split_axis=0, concat_axis=1, tiled=True)  57.8 us
    reduce_scatter x1, waiting for transfers between devices, per_device(): lax.psum_scatter(partials.astype(jnp.bfloat16), 'ad', scatter_dimension=2...  32.7 us
    psum x1, blocking collectives, per_device(): lax.psum(lowrank.astype(jnp.bfloat16), 'ad').astype(jnp.float32)  21.2 us
    gather x4, local copies, waits for them, and re-layouts, per_device(): adapter_factors = adapter_input_factors[slot_of_tenant, half_index]  19.4 us
    dot_general x4, matrix products, per_device(): jnp.dot(block_rows, up_weight[half_index], preferred_element_type=jnp.flo...  17.3 us
    dot_general x4, matrix products, per_device(): jnp.dot(hidden_units, down_weight[half_index], preferred_element_type=jnp...  17.2 us
    all_to_all x1, waiting for transfers between devices, per_device(): lax.all_to_all(summed, 'ep', split_axis=1, concat_axis=0, tiled=True)  11.9 us
    dot_general x4, matrix products, per_device(): jnp.dot(block_rows, gate_weight[half_index], preferred_element_type=jnp.f...  11.4 us
  transfers between devices with their start and end apart: 5, of which 2 were waited for; matrix products, arithmetic and copies ran while one was open for 14% of the time, Pallas kernels for 0%

commit v1 on v0

v1 whole, which is shorter than its diff:
```python
import functools

import jax
import jax.numpy as jnp
from jax import lax
from jax.experimental import pallas as pl
from jax.experimental.pallas import tpu as pltpu
from jax.sharding import PartitionSpec as P

EXPERT_COUNT = 8
TOP = 2
RANK = 16
CAP = 48
K_CHUNKS = 2
N_TILE = 512
MIB = 1 << 20

F32 = jnp.float32
BF16 = jnp.bfloat16


def mm(a, b):
    return jnp.dot(a, b, preferred_element_type=F32)


def mm_nt(a, b):
    return lax.dot_general(a, b, (((1,), (1,)), ((), ())), preferred_element_type=F32)


def cost(flops, moved, trans=0):
    return pl.CostEstimate(flops=int(flops), bytes_accessed=int(moved), transcendentals=int(trans))


def params(mib):
    return pltpu.CompilerParams(vmem_limit_bytes=mib * MIB)


def vmem():
    return pl.BlockSpec(memory_space=pltpu.VMEM)


def smem():
    return pl.BlockSpec(memory_space=pltpu.SMEM)


def meta_kernel(n_local, scalar_ref, slots_ref, *refs):
    blocks, (p_ref, pt_ref, cols_ref, rows_ref, tslot_ref) = refs[:-5], refs[-5:]
    info = jnp.concatenate([block[...] for block in blocks], axis=1)
    count = info.shape[1]
    first, second, tenant = info[0:1], info[1:2], info[4:5]
    weight_first = jax.nn.sigmoid(info[2:3] - info[3:4])
    weight_second = jax.nn.sigmoid(info[3:4] - info[2:3])
    slot = jnp.zeros_like(tenant)
    for number in range(slots_ref.shape[0]):
        slot = jnp.where(tenant == number, slots_ref[number].astype(F32), slot)
    members, weights = [], []
    for i in range(n_local):
        expert = (scalar_ref[0] + i).astype(F32)
        hit_first, hit_second = first == expert, second == expert
        members.append(jnp.where(hit_first | hit_second, 1.0, 0.0))
        weights.append(jnp.where(hit_first, weight_first, 0.0) + jnp.where(hit_second, weight_second, 0.0))
    member = jnp.concatenate(members + [jnp.zeros((8 - n_local, count), F32)], axis=0)
    before = (
        lax.broadcasted_iota(jnp.int32, (count, count), 0) < lax.broadcasted_iota(jnp.int32, (count, count), 1)
    ).astype(BF16)
    place = jnp.where(member > 0, mm(member.astype(BF16), before), -1.0)
    table = jnp.concatenate(
        [place[0:n_local]] + weights + [slot] + [jnp.zeros((127 - 2 * n_local, count), F32)], axis=0
    )
    columns = table.T
    cols_ref[...] = columns
    rows_ref[...] = table[0:8]
    row_count = p_ref.shape[1]
    tenant_rows = jnp.broadcast_to(tenant, (8, count)).astype(BF16)
    down = lax.broadcasted_iota(jnp.int32, (row_count, count), 0).astype(F32)
    across = lax.broadcasted_iota(jnp.int32, (count, row_count), 1).astype(F32)
    for i in range(n_local):
        picked = (down == place[i : i + 1]).astype(BF16)
        p_ref[i] = picked
        pt_ref[i] = (across == columns[:, i : i + 1]).astype(BF16)
        tslot_ref[i] = mm_nt(tenant_rows, picked)


def build_meta(blocks, expert_base, slots, n_local, row_count):
    count = sum(block.shape[1] for block in blocks)
    return pl.pallas_call(
        functools.partial(meta_kernel, n_local),
        out_shape=(
            jax.ShapeDtypeStruct((n_local, row_count, count), BF16),
            jax.ShapeDtypeStruct((n_local, count, row_count), BF16),
            jax.ShapeDtypeStruct((count, 128), F32),
            jax.ShapeDtypeStruct((8, count), F32),
            jax.ShapeDtypeStruct((n_local, 8, row_count), F32),
        ),
        in_specs=[smem(), smem()] + [vmem()] * len(blocks),
        out_specs=(vmem(),) * 5,
        compiler_params=params(48),
        cost_estimate=cost(2 * 8 * count * count, 4 * n_local * row_count * count),
        name="routing_tables",
    )(expert_base, slots, *blocks)


def factor_kernel(slots_ref, pool_ref, out_ref, sems):
    copies = []
    for number in range(out_ref.shape[0]):
        copies.append(pltpu.make_async_copy(pool_ref.at[slots_ref[number]], out_ref.at[number], sems.at[number]))
    for copy in copies:
        copy.start()
    for copy in copies:
        copy.wait()


def take_factors(slots, pool):
    tenants = slots.shape[0]
    shape = (tenants,) + pool.shape[1:]
    return pl.pallas_call(
        factor_kernel,
        out_shape=jax.ShapeDtypeStruct(shape, pool.dtype),
        in_specs=[smem(), pl.BlockSpec(memory_space=pl.ANY)],
        out_specs=pl.BlockSpec(memory_space=pl.ANY),
        scratch_shapes=[pltpu.SemaphoreType.DMA((tenants,))],
        cost_estimate=cost(0, 2 * shape[0] * shape[1] * shape[2] * shape[3] * 2),
        name="tenant_factors",
    )(slots, pool)


def expert_kernel(n_blocks, halves_each, is_first, is_last, *refs):
    blocks, refs = refs[:n_blocks], refs[n_blocks:]
    p_ref, gate_ref, up_ref, refs = refs[0], refs[1], refs[2], refs[3:]
    if not is_first:
        gate_in, up_in, refs = refs[0], refs[1], refs[2:]
    half, tile = pl.program_id(0), pl.program_id(1)
    if is_last:
        factor_ref, tslot_ref, rows_ref, hidden_ref, low_ref, packed, low_acc = refs
    else:
        gate_out, up_out, packed = refs

    @pl.when((tile == 0) & (half % halves_each == 0))
    def _():
        whole = jnp.concatenate([block[...] for block in blocks], axis=0)
        packed[...] = mm(p_ref[half // halves_each], whole).astype(BF16)

    rows = packed[...]
    gate = mm(rows, gate_ref[0])
    up = mm(rows, up_ref[0])
    if not is_first:
        gate = gate + gate_in[0]
        up = up + up_in[0]
    if not is_last:
        gate_out[0] = gate
        up_out[0] = up
        return
    hidden = (jax.nn.silu(gate) * up).astype(BF16)
    hidden_ref[0] = hidden
    tenants, rank = factor_ref.shape[0], factor_ref.shape[2]
    factors = factor_ref[:, 0].reshape(tenants * rank, factor_ref.shape[3])
    low = mm_nt(factors, hidden)
    starts = (tile == 0) & (half % halves_each == 0)

    @pl.when(starts)
    def _():
        low_acc[...] = low

    @pl.when(jnp.logical_not(starts))
    def _():
        low_acc[...] += low

    @pl.when((tile == pl.num_programs(1) - 1) & (half % halves_each == halves_each - 1))
    def _():
        for i in range(p_ref.shape[0]):

            @pl.when(half // halves_each == i)
            def _():
                owner = tslot_ref[i][0:1]
                total = jnp.zeros((rank, packed.shape[0]), F32)
                for number in range(tenants):
                    total = total + jnp.where(owner == number, low_acc[number * rank : (number + 1) * rank], 0.0)
                weight = rows_ref[p_ref.shape[0] + i : p_ref.shape[0] + i + 1]
                low_ref[i * rank : (i + 1) * rank] = (mm(total.astype(BF16), p_ref[i]) * weight).astype(BF16)


def expert_part(blocks, part, parts, picked, gate, up, sums, factors, tslot, table_rows):
    local_halves, width, hidden_count = gate.shape
    part_width = width // parts
    n_local, row_count, count = picked.shape
    halves_each = local_halves // n_local
    tile = min(N_TILE, hidden_count)
    is_first, is_last = part == 0, part == parts - 1

    def constant(array):
        return pl.BlockSpec(array.shape, lambda h, n: (0,) * array.ndim)

    weight_spec = pl.BlockSpec((1, part_width, tile), lambda h, n: (h, part, n))
    sum_spec = pl.BlockSpec((1, row_count, tile), lambda h, n: (h, 0, n))
    in_specs = [constant(block) for block in blocks] + [constant(picked), weight_spec, weight_spec]
    operands = list(blocks) + [picked, gate, up]
    aliases = {}
    if not is_first:
        if not is_last:
            aliases = {len(operands): 0, len(operands) + 1: 1}
        in_specs += [sum_spec, sum_spec]
        operands += list(sums)
    scratch = [pltpu.VMEM((row_count, part_width), BF16)]
    if is_last:
        tenants, _, rank, _ = factors.shape
        in_specs += [
            pl.BlockSpec((tenants, 1, rank, tile), lambda h, n: (0, h, 0, n)),
            constant(tslot),
            constant(table_rows),
        ]
        operands += [factors, tslot, table_rows]
        out_shape = (
            jax.ShapeDtypeStruct((local_halves, row_count, hidden_count), BF16),
            jax.ShapeDtypeStruct((n_local * rank, count), BF16),
        )
        out_specs = (sum_spec, pl.BlockSpec((n_local * rank, count), lambda h, n: (0, 0)))
        scratch.append(pltpu.VMEM((tenants * rank, row_count), F32))
    else:
        out_shape = (jax.ShapeDtypeStruct((local_halves, row_count, hidden_count), F32),) * 2
        out_specs = (sum_spec, sum_spec)
    return pl.pallas_call(
        functools.partial(expert_kernel, len(blocks), halves_each, is_first, is_last),
        grid=(local_halves, hidden_count // tile),
        out_shape=out_shape,
        in_specs=in_specs,
        out_specs=out_specs,
        scratch_shapes=scratch,
        input_output_aliases=aliases,
        compiler_params=params(48),
        cost_estimate=cost(
            4 * local_halves * row_count * part_width * hidden_count, 4 * local_halves * part_width * hidden_count
        ),
        name="gate_up_part",
    )(*operands)


def down_kernel(halves_each, raw, target_ref, hidden_ref, weight_ref, pt_ref, cols_ref, *refs):
    half = pl.program_id(0)
    outs, (part_sum, total) = refs[:-2], refs[-2:]
    product = mm(hidden_ref[0], weight_ref[0])
    n_local = pt_ref.shape[0]

    @pl.when(half % halves_each == 0)
    def _():
        part_sum[...] = product

    @pl.when(half % halves_each != 0)
    def _():
        part_sum[...] += product

    for i in range(n_local):

        @pl.when(half == (i + 1) * halves_each - 1)
        def _():
            laid = mm(pt_ref[i], part_sum[...].astype(BF16)) * cols_ref[:, n_local + i : n_local + i + 1]
            if i > 0:
                laid = laid + total[...]
            if i < n_local - 1:
                total[...] = laid
            elif raw:
                outs[0][...] = laid
            else:
                write_pairs(laid, outs)


def write_pairs(total, outs):
    keep, send = outs
    for b in range(total.shape[0] // 128):
        (send if b % 2 else keep)[b // 2 * 128 : b // 2 * 128 + 128] = total[b * 128 : b * 128 + 128].astype(BF16)


def down_part(target, hidden, down, pt, cols, span, raw):
    local_halves, row_count, hidden_count = hidden.shape
    n_local, count, _ = pt.shape
    halves_each = local_halves // n_local
    if raw:
        out_shape = (jax.ShapeDtypeStruct((count, span), F32),)
    else:
        out_shape = (jax.ShapeDtypeStruct((count // 2, span), BF16),) * 2
    return pl.pallas_call(
        functools.partial(down_kernel, halves_each, raw),
        grid_spec=pltpu.PrefetchScalarGridSpec(
            num_scalar_prefetch=1,
            grid=(local_halves,),
            in_specs=[
                pl.BlockSpec((1, row_count, hidden_count), lambda h, t: (h, 0, 0)),
                pl.BlockSpec((1, hidden_count, span), lambda h, t: (h, 0, t[0])),
                pl.BlockSpec(pt.shape, lambda h, t: (0, 0, 0)),
                pl.BlockSpec(cols.shape, lambda h, t: (0, 0)),
            ],
            out_specs=tuple(pl.BlockSpec(s.shape, lambda h, t: (0, 0)) for s in out_shape),
            scratch_shapes=[pltpu.VMEM((row_count, span), F32), pltpu.VMEM((count, span), F32)],
        ),
        out_shape=out_shape,
        compiler_params=params(48),
        cost_estimate=cost(
            2 * local_halves * row_count * hidden_count * span, 2 * local_halves * hidden_count * span
        ),
        name="down_part",
    )(target, hidden, down, pt, cols)


def adapter_kernel(scalar_ref, base_ref, factor_ref, cols_ref, slot_column, *refs):
    lows, (keep, send, wide) = refs[:-3], refs[-3:]
    wide[...] = jnp.zeros_like(wide)
    height = lows[0].shape[0]
    count = base_ref.shape[0]
    blocks = count // 128
    for m in range(len(lows)):
        start = pl.multiple_of(scalar_ref[1 + m], RANK)
        value = lows[m][...].astype(F32)
        value = jnp.concatenate([value[:, (m ^ b) * 128 : (m ^ b) * 128 + 128] for b in range(blocks)], axis=1)
        wide[pl.ds(start, height)] += value
    low = wide[...].T.astype(BF16)
    zero = jnp.zeros_like(low)
    slot = cols_ref[:, slot_column : slot_column + 1]
    depth = EXPERT_COUNT * RANK
    slot_count = factor_ref.shape[0] // depth
    total = base_ref[...]
    for j in range(0, slot_count, 2):
        spread = jnp.concatenate(
            [jnp.where(slot == (scalar_ref[0] + j + i).astype(F32), low, zero) for i in range(2)], axis=1
        )
        total = total + mm(spread, factor_ref[j * depth : (j + 2) * depth])
    write_pairs(total, (keep, send))


def adapter_part(scalars, base, factors, cols, slot_column, lows):
    count, span = base.shape

    def kernel(scalar_ref, base_ref, factor_ref, cols_ref, *refs):
        adapter_kernel(scalar_ref, base_ref, factor_ref, cols_ref, slot_column, *refs)

    return pl.pallas_call(
        kernel,
        out_shape=(jax.ShapeDtypeStruct((count // 2, span), BF16),) * 2,
        in_specs=[smem()] + [vmem()] * (3 + len(lows)),
        out_specs=(vmem(),) * 2,
        scratch_shapes=[pltpu.VMEM((EXPERT_COUNT * RANK, count), F32)],
        compiler_params=params(48),
        cost_estimate=cost(2 * count * factors.shape[0] * span, 2 * factors.shape[0] * span),
        name="adapter_part",
    )(scalars, base, factors, cols, *lows)


def per_device(
    n_ep,
    n_ad,
    tokens,
    chosen_experts,
    router_gate_logits,
    token_tenant,
    adapter_of_tenant,
    adapter_pool_slot,
    gate_weight,
    up_weight,
    down_weight,
    adapter_input_factors,
    adapter_output_factors,
):
    width = tokens.shape[1]
    span = width // n_ad
    local_halves = gate_weight.shape[0]
    n_local = max(1, local_halves // 2)
    row_count = n_ep * CAP
    bits = n_ep.bit_length() - 1
    ep_index, ad_index = lax.axis_index("ep"), lax.axis_index("ad")

    def swap(x, mask):
        return lax.ppermute(x, "ep", [(i, i ^ mask) for i in range(n_ep)])

    def shift(x, step):
        return lax.ppermute(x, "ad", [(i, (i + step) % n_ad) for i in range(n_ad)])

    info = jnp.concatenate(
        [
            chosen_experts.astype(F32).T,
            router_gate_logits.T,
            token_tenant.astype(F32)[None],
            jnp.zeros((3, tokens.shape[0]), F32),
        ],
        axis=0,
    )
    infos = [info] + [swap(info, mask) for mask in range(1, n_ep)]

    parts = K_CHUNKS
    part_width = width // parts
    token_parts = []
    for part in range(parts):
        blocks = {0: tokens[:, part * part_width : (part + 1) * part_width]}
        for bit in reversed(range(bits)):
            for mask in list(blocks):
                blocks[mask | 1 << bit] = swap(blocks[mask], 1 << bit)
        token_parts.append([blocks[mask] for mask in range(n_ep)])

    slots = adapter_pool_slot[adapter_of_tenant]
    expert_base = (ep_index * local_halves // 2).astype(jnp.int32).reshape(1)
    picked, pt, cols, table_rows, tslot = build_meta(infos, expert_base, slots, n_local, row_count)
    factors = take_factors(slots, adapter_input_factors)

    state = None
    for part in range(parts):
        state = expert_part(
            token_parts[part], part, parts, picked, gate_weight, up_weight, state, factors, tslot, table_rows
        )
    hidden, low = state

    arrived = [low] + [shift(low, step) for step in range(1, n_ad)]
    low_total = sum(x.astype(F32) for x in arrived).astype(BF16)
    lows = [low_total] + [swap(low_total, mask) for mask in range(1, n_ep)]

    def combine(keep, send):
        mine = (keep.astype(F32) + swap(send, 1).astype(F32)).astype(BF16)
        for bit in range(1, bits):
            half = mine.shape[0] // 128 // 2
            grouped = mine.reshape(half, 2, 128, mine.shape[1])
            keep = grouped[:, 0].reshape(half * 128, -1)
            send = grouped[:, 1].reshape(half * 128, -1)
            mine = (keep.astype(F32) + swap(send, 1 << bit).astype(F32)).astype(BF16)
        return mine

    results = []
    for step in range(1, n_ad):
        target = ((ad_index + step) % n_ad).astype(jnp.int32).reshape(1)
        keep, send = down_part(target, hidden, down_weight, pt, cols, span, False)
        results.append(shift(combine(keep, send), step))
    (base,) = down_part(ad_index.astype(jnp.int32).reshape(1), hidden, down_weight, pt, cols, span, True)
    slot_count = adapter_output_factors.shape[0]
    scalars = jnp.stack(
        [ep_index * slot_count] + [((ep_index ^ mask) * local_halves // 2) * RANK for mask in range(n_ep)]
    ).astype(jnp.int32)
    flat_factors = adapter_output_factors.reshape(slot_count * EXPERT_COUNT * RANK, span)
    keep, send = adapter_part(scalars, base, flat_factors, cols, 2 * n_local, lows)
    results.append(combine(keep, send))
    return sum(x.astype(F32) for x in results).astype(BF16)


def solution(mesh):
    placed = (
        P(("rep", "ep"), None),
        P(("rep", "ep"), None),
        P(("rep", "ep"), None),
        P(("rep", "ep")),
        P("rep"),
        P(),
        P("ep", None, "ad"),
        P("ep", None, "ad"),
        P("ep", "ad", None),
        P(None, "ep", None, "ad"),
        P("ep", None, None, "ad"),
    )
    return jax.shard_map(
        functools.partial(per_device, mesh.shape["ep"], mesh.shape["ad"]),
        mesh=mesh,
        in_specs=placed,
        out_specs=P(("rep", "ep"), "ad"),
        check_vma=False,
    )
```

time: 256 us -> 179 us (0.70)
  Pallas kernels: 0 us -> 120 us
  blocking collectives: 79 us -> 0 us
  matrix products: 48.1 us -> 0 us
  local copies, waits for them, and re-layouts: 45.4 us -> 4.32 us
  waiting for transfers between devices: 45.1 us -> 28.3 us
  between operations: 15.5 us -> 0.29 us
  starting transfers between devices: 10.3 us -> 21.1 us
  other arithmetic: 12 us -> 4.11 us
    pallas_call x0 -> x9, Pallas kernels: none -> 120 us  [the longest x1 65.6 us: take_factors(): pl.pallas_call(factor_kernel, out_shape=jax.ShapeDtypeStruct(shape, pool....]
    all_to_all x1 -> x0, blocking collectives: 57.8 us -> none  [per_device(): lax.all_to_all(doubled, 'ep', split_axis=0, concat_axis=1, tiled=True)]
    dot_general x17 -> x0, matrix products: 48.1 us -> none  [the longest x4 17.3 us: per_device(): jnp.dot(block_rows, up_weight[half_index], preferred_element_type=jnp.flo...]
    gather x12 -> x1, local copies, waits for them, and re-layouts: 35.2 us -> 1.2 us  [per_device(): slots = adapter_pool_slot[adapter_of_tenant]]
    reduce_scatter x1 -> x0, waiting for transfers between devices: 32.7 us -> none  [per_device(): lax.psum_scatter(partials.astype(jnp.bfloat16), 'ad', scatter_dimension=2...]
    ppermute x0 -> x26, waiting for transfers between devices: none -> 28.3 us  [the longest x20 21.9 us: swap(): return lax.ppermute(x, 'ep', [(i, i ^ mask) for i in range(n_ep)])]
    psum x1 -> x0, blocking collectives: 21.2 us -> none  [per_device(): lax.psum(lowrank.astype(jnp.bfloat16), 'ad').astype(jnp.float32)]
    ppermute x0 -> x26, starting transfers between devices: none -> 21.1 us  [the longest x20 13.9 us: swap(): return lax.ppermute(x, 'ep', [(i, i ^ mask) for i in range(n_ep)])]
  transfers between devices with their start and end apart: 5 -> 26, of which waited for: 2 -> 7; matrix products, arithmetic and copies ran while one was open for 14% -> 3% of each run, Pallas kernels for 0% -> 59%
where the time goes in v1:
time: 179 us; the launch traced here: 178 us
  Pallas kernels  120 us (67%)
  waiting for transfers between devices  28.3 us (16%)
  starting transfers between devices  21.1 us (12%)
  local copies, waits for them, and re-layouts  4.32 us (2%)
  other arithmetic  4.11 us (2%)
    pallas_call x1, Pallas kernels, take_factors(): pl.pallas_call(factor_kernel, out_shape=jax.ShapeDtypeStruct(shape, pool....  65.6 us
    pallas_call x2, Pallas kernels, expert_part(): pl.pallas_call(functools.partial(expert_kernel, len(blocks), halves_each,...  29.6 us
    ppermute x20, waiting for transfers between devices, swap(): return lax.ppermute(x, 'ep', [(i, i ^ mask) for i in range(n_ep)])  21.9 us
    pallas_call x4, Pallas kernels, down_part(): pl.pallas_call(functools.partial(down_kernel, halves_each, raw), grid_spe...  21.4 us
    ppermute x20, starting transfers between devices, swap(): return lax.ppermute(x, 'ep', [(i, i ^ mask) for i in range(n_ep)])  13.9 us
    ppermute x6, starting transfers between devices, shift(): return lax.ppermute(x, 'ad', [(i, (i + step) % n_ad) for i in range(n_ad)])  7.17 us
    ppermute x6, waiting for transfers between devices, shift(): return lax.ppermute(x, 'ad', [(i, (i + step) % n_ad) for i in range(n_ad)])  6.36 us
  transfers between devices with their start and end apart: 26, of which 7 were waited for; matrix products, arithmetic and copies ran while one was open for 3% of the time, Pallas kernels for 59%

profile of v1, /device:TPU:0, one launch (start us, length us, event | category | flops | bytes accessed | tf_op | source)
XLA Modules:
  0.0 178.4 jit_solution(1622794897661681725)
XLA Ops:
  0.0 1.2 fusion.4
  1.2 3.0 %collective-permute-start.7 = (bf16[128,1536]{1,0:T(8,128)(2,1)S(1)}, bf16[128,1536]{1,0:T(8,128)(2,1)S(1)}, u32[]{:S(2)}, u32[]{:S(2)}) collective-permute-start(bf16[128,1536]{1,0:T(8,128)(2,1)S(1)} %get-tuple-element.39.refs_0_), channel_id=1, source_target_pairs={{0,8},{4,12},{8,0},{12,4},{1,9},{5,13},{9,1},{13,5},{2,10},{6,14},... | collective-permute-start | bytes 1179656 | tf_op jit(solution)/shard_map/ppermute | solution.py:370
  4.2 0.2 collective-permute-start.1
  4.4 0.7 convert_bitcast_fusion.1
  5.1 0.7 convert_bitcast_fusion
  5.8 8.4 %collective-permute-done.7.refs_2_ = bf16[128,1536]{1,0:T(8,128)(2,1)S(1)} collective-permute-done((bf16[128,1536]{1,0:T(8,128)(2,1)S(1)}, bf16[128,1536]{1,0:T(8,128)(2,1)S(1)}, u32[]{:S(2)}, u32[]{:S(2)}) %collective-permute-start.7) | collective-permute-done | bytes 393248 | tf_op jit(solution)/shard_map/ppermute | solution.py:370
  14.1 0.7 maximum_maximum_fusion.refs_0_
  14.9 0.5 collective-permute-start.3
  15.4 2.1 %collective-permute-start.4 = (f32[8,128]{1,0:T(8,128)S(1)}, f32[8,128]{1,0:T(8,128)S(1)}, u32[]{:S(2)}, u32[]{:S(2)}) collective-permute-start(f32[8,128]{1,0:T(8,128)S(1)} %maximum_maximum_fusion.refs_0_), channel_id=1, source_target_pairs={{0,8},{4,12},{8,0},{12,4},{1,9},{5,13},{9,1},{13,5},{2,10},{6,14},... | collective-permute-start | bytes 12296 | tf_op jit(solution)/shard_map/ppermute | solution.py:370
  17.4 0.7 compare_select_fusion
  18.1 0.1 collective-permute-start.5
  18.3 1.2 gather_fusion
  19.5 65.6 %tenant_factors.1.refs_9_ = bf16[16,4,16,1024]{3,2,1,0:T(8,128)(2,1)} custom-call(s32[16]{0:T(128)} %gather_fusion, bf16[64,4,16,1024]{3,2,1,0:T(8,128)(2,1)} %pool_ref.1), custom_call_target="tpu_custom_call" | custom-call | bytes 4194304 | tf_op jit(solution)/shard_map/tenant_factors/pallas_call | solution.py:116
  85.2 0.1 collective-permute-start
  85.3 1.1 routing_tables.1
  86.4 0.5 collective-permute-start.2
  86.9 14.5 %gate_up_part.2 = (f32[4,192,1024]{2,1,0:T(8,128)S(1)}, f32[4,192,1024]{2,1,0:T(8,128)}) custom-call(bf16[128,1536]{1,0:T(8,128)(2,1)S(1)} %get-tuple-element.39.refs_0_, bf16[128,1536]{1,0:T(8,128)(2,1)S(1)} %collective-permute-done.6.refs_1_, bf16[128,1536]{1,0:T(8,128)(2,1)S(1)} %collective-permute-done.7.refs_2_, ...), custom_call_target="tpu_custom_call" | custom-call | flops 4831838208 | bytes 25165824 | tf_op jit(solution)/shard_map/gate_up_part/pallas_call | solution.py:221
  101.4 1.7 copy-done.3
  103.1 15.1 %gate_up_part.3 = (bf16[4,192,1024]{2,1,0:T(8,128)(2,1)S(1)}, bf16[32,512]{1,0:T(8,128)(2,1)S(1)}) custom-call(bf16[128,1536]{1,0:T(8,128)(2,1)S(1)} %get-tuple-element.40.refs_0_, bf16[128,1536]{1,0:T(8,128)(2,1)S(1)} %collective-permute-done.refs_1_, bf16[128,1536]{1,0:T(8,128)(2,1)S(1)} %collective-permute-done.1.refs_2_, ...), custom_call_target="tpu_custom_call" | custom-call | flops 4831838208 | bytes 25165824 | tf_op jit(solution)/shard_map/gate_up_part/pallas_call | solution.py:221
  118.2 1.7 collective-permute-start.18
  119.9 2.6 %collective-permute-start.19 = (bf16[32,512]{1,0:T(8,128)(2,1)S(1)}, bf16[32,512]{1,0:T(8,128)(2,1)S(1)}, u32[]{:S(2)}, u32[]{:S(2)}) collective-permute-start(bf16[32,512]{1,0:T(8,128)(2,1)S(1)} %get-tuple-element.36), channel_id=1, source_target_pairs={{0,2},{1,3},{2,0},{3,1},{4,6},{5,7},{6,4},{7,5},{8,10},{9,11},{10,... | collective-permute-start | bytes 98312 | tf_op jit(solution)/shard_map/ppermute | solution.py:373
  122.5 1.3 collective-permute-start.20
  123.9 5.3 %down_part.7.base_ref = f32[512,768]{1,0:T(8,128)S(1)} custom-call(s32[1]{0:T(128)} %bitcast.21.target_ref, bf16[4,192,1024]{2,1,0:T(8,128)(2,1)S(1)} %get-tuple-element.27.hidden_ref, bf16[4,1024,3072]{2,1,0:T(8,128)(2,1)} %weight_ref.7, bf16[2,512,192]{2,1,0:T(8,128)(2,1)S(1)} %get-tuple-element.28.pt_ref, f32[512,128]{1,0:T(8,128)S(1)} %get-tuple-element.29.cols_ref), custom_call_target="tpu_custom_call" | custom-call | flops 1207959552 | bytes 6291456 | tf_op jit(solution)/shard_map/down_part/pallas_call | solution.py:280
  129.2 5.3 %down_part.4 = (bf16[256,768]{1,0:T(8,128)(2,1)S(1)}, bf16[256,768]{1,0:T(8,128)(2,1)S(1)}) custom-call(s32[1]{0:T(128)} %bitcast.target_ref, bf16[4,192,1024]{2,1,0:T(8,128)(2,1)S(1)} %get-tuple-element.27.hidden_ref, bf16[4,1024,3072]{2,1,0:T(8,128)(2,1)} %weight_ref.7, bf16[2,512,192]{2,1,0:T(8,128)(2,1)S(1)} %get-tuple-element.28.pt_ref, ...), custom_call_target="tpu_custom_call" | custom-call | flops 1207959552 | bytes 6291456 | tf_op jit(solution)/shard_map/down_part/pallas_call | solution.py:280
  134.6 5.3 %down_part.5 = (bf16[256,768]{1,0:T(8,128)(2,1)S(1)}, bf16[256,768]{1,0:T(8,128)(2,1)S(1)}) custom-call(s32[1]{0:T(128)} %bitcast.8.target_ref, bf16[4,192,1024]{2,1,0:T(8,128)(2,1)S(1)} %get-tuple-element.27.hidden_ref, bf16[4,1024,3072]{2,1,0:T(8,128)(2,1)} %weight_ref.7, bf16[2,512,192]{2,1,0:T(8,128)(2,1)S(1)} %get-tuple-element.28.pt_ref, ...), custom_call_target="tpu_custom_call" | custom-call | flops 1207959552 | bytes 6291456 | tf_op jit(solution)/shard_map/down_part/pallas_call | solution.py:280
  139.9 0.6 collective-permute-start.12
  140.5 0.1 collective-permute-start.21
  140.6 1.5 collective-permute-start.22
  142.1 0.3 collective-permute-start.23
  142.4 5.4 %down_part.6 = (bf16[256,768]{1,0:T(8,128)(2,1)S(1)}, bf16[256,768]{1,0:T(8,128)(2,1)S(1)}) custom-call(s32[1]{0:T(128)} %bitcast.12.target_ref, bf16[4,192,1024]{2,1,0:T(8,128)(2,1)S(1)} %get-tuple-element.27.hidden_ref, bf16[4,1024,3072]{2,1,0:T(8,128)(2,1)} %weight_ref.7, bf16[2,512,192]{2,1,0:T(8,128)(2,1)S(1)} %get-tuple-element.28.pt_ref, ...), custom_call_target="tpu_custom_call" | custom-call | flops 1207959552 | bytes 6291456 | tf_op jit(solution)/shard_map/down_part/pallas_call | solution.py:280
  147.9 0.4 collective-permute-start.15
  148.3 2.7 %adapter_part.1 = (bf16[256,768]{1,0:T(8,128)(2,1)S(1)}, bf16[256,768]{1,0:T(8,128)(2,1)S(1)}) custom-call(s32[5]{0:T(128)S(1)} %stack.23.scalar_ref, f32[512,768]{1,0:T(8,128)S(1)} %down_part.7.base_ref, bf16[2048,768]{1,0:T(8,128)(2,1)S(1)} %bitcast.48, f32[512,128]{1,0:T(8,128)S(1)} %get-tuple-element.29.cols_ref, ...), custom_call_target="tpu_custom_call" | custom-call | flops 1610612736 | bytes 3145728 | tf_op jit(solution)/shard_map/adapter_part/pallas_call | solution.py:334
  151.0 0.2 collective-permute-start.24
  151.2 0.1 add_convert_fusion.3
  151.4 1.5 collective-permute-start.10
  153.0 0.6 collective-permute-start.13
  153.8 1.5 collective-permute-start.16
  155.4 0.6 collective-permute-start.25
  156.1 3.1 %collective-permute-done.10 = bf16[128,768]{1,0:T(8,128)(2,1)S(1)} collective-permute-done((bf16[128,768]{1,0:T(8,128)(2,1)S(1)}, bf16[128,768]{1,0:T(8,128)(2,1)S(1)}, u32[]{:S(2)}, u32[]{:S(2)}) %collective-permute-start.10) | collective-permute-done | bytes 196640 | tf_op jit(solution)/shard_map/ppermute | solution.py:370
  159.2 0.7 collective-permute-start.11
  159.9 3.4 %collective-permute-done.13 = bf16[128,768]{1,0:T(8,128)(2,1)S(1)} collective-permute-done((bf16[128,768]{1,0:T(8,128)(2,1)S(1)}, bf16[128,768]{1,0:T(8,128)(2,1)S(1)}, u32[]{:S(2)}, u32[]{:S(2)}) %collective-permute-start.13) | collective-permute-done | bytes 196640 | tf_op jit(solution)/shard_map/ppermute | solution.py:370
  163.4 0.3 collective-permute-start.14
  163.7 3.9 %collective-permute-done.16 = bf16[128,768]{1,0:T(8,128)(2,1)S(1)} collective-permute-done((bf16[128,768]{1,0:T(8,128)(2,1)S(1)}, bf16[128,768]{1,0:T(8,128)(2,1)S(1)}, u32[]{:S(2)}, u32[]{:S(2)}) %collective-permute-start.16) | collective-permute-done | bytes 196640 | tf_op jit(solution)/shard_map/ppermute | solution.py:370
  167.6 0.5 collective-permute-start.17
  168.1 3.1 %collective-permute-done.25 = bf16[128,768]{1,0:T(8,128)(2,1)S(1)} collective-permute-done((bf16[128,768]{1,0:T(8,128)(2,1)S(1)}, bf16[128,768]{1,0:T(8,128)(2,1)S(1)}, u32[]{:S(2)}, u32[]{:S(2)}) %collective-permute-start.25) | collective-permute-done | bytes 196640 | tf_op jit(solution)/shard_map/ppermute | solution.py:370
  171.2 4.2 %collective-permute-done.14 = bf16[128,768]{1,0:T(8,128)(2,1)S(1)} collective-permute-done((bf16[128,768]{1,0:T(8,128)(2,1)S(1)}, bf16[128,768]{1,0:T(8,128)(2,1)S(1)}, u32[]{:S(2)}, u32[]{:S(2)}) %collective-permute-start.14) | collective-permute-done | bytes 196640 | tf_op jit(solution)/shard_map/ppermute | solution.py:373
  175.4 2.2 %collective-permute-done.17 = bf16[128,768]{1,0:T(8,128)(2,1)S(1)} collective-permute-done((bf16[128,768]{1,0:T(8,128)(2,1)S(1)}, bf16[128,768]{1,0:T(8,128)(2,1)S(1)}, u32[]{:S(2)}, u32[]{:S(2)}) %collective-permute-start.17) | collective-permute-done | bytes 196640 | tf_op jit(solution)/shard_map/ppermute | solution.py:373
  177.6 0.8 add_convert_fusion.4
  (48 shorter events, 0.8 us)
Async XLA Ops:
  0.0 18.3 %copy-start = (s32[64]{0:T(128)S(1)}, s32[64]{0:T(128)}, u32[]{:S(2)}) copy-start(s32[64]{0:T(128)} %param.16) | copy-start | bytes 772
  1.2 12.9 %collective-permute-start.7 = (bf16[128,1536]{1,0:T(8,128)(2,1)S(1)}, bf16[128,1536]{1,0:T(8,128)(2,1)S(1)}, u32[]{:S(2)}, u32[]{:S(2)}) collective-permute-start(bf16[128,1536]{1,0:T(8,128)(2,1)S(1)} %get-tuple-element.39.refs_0_), channel_id=1, source_target_pairs={{0,8},{4,12},{8,0},{12,4},{1,9},{5,13},{9,1},{13,5},{2,10},{6,14},... | collective-permute-start | bytes 1179656 | tf_op jit(solution)/shard_map/ppermute | solution.py:370
  4.2 82.7 %collective-permute-start.6 = (bf16[128,1536]{1,0:T(8,128)(2,1)S(1)}, bf16[128,1536]{1,0:T(8,128)(2,1)S(1)}, u32[]{:S(2)}, u32[]{:S(2)}) collective-permute-start(bf16[128,1536]{1,0:T(8,128)(2,1)S(1)} %get-tuple-element.39.refs_0_), channel_id=1, source_target_pairs={{0,4},{4,0},{8,12},{12,8},{1,5},{5,1},{9,13},{13,9},{2,6},{6,2},{1... | collective-permute-start | bytes 1179656 | tf_op jit(solution)/shard_map/ppermute | solution.py:370
  4.2 82.2 %collective-permute-start.1 = (bf16[128,1536]{1,0:T(8,128)(2,1)S(1)}, bf16[128,1536]{1,0:T(8,128)(2,1)S(1)}, u32[]{:S(2)}, u32[]{:S(2)}) collective-permute-start(bf16[128,1536]{1,0:T(8,128)(2,1)S(1)} %get-tuple-element.40.refs_0_), channel_id=1, source_target_pairs={{0,8},{4,12},{8,0},{12,4},{1,9},{5,13},{9,1},{13,5},{2,10},{6,14},... | collective-permute-start | bytes 1179656 | tf_op jit(solution)/shard_map/ppermute | solution.py:370
  14.1 72.7 %collective-permute-start.8 = (bf16[128,1536]{1,0:T(8,128)(2,1)S(1)}, bf16[128,1536]{1,0:T(8,128)(2,1)S(1)}, u32[]{:S(2)}, u32[]{:S(2)}) collective-permute-start(bf16[128,1536]{1,0:T(8,128)(2,1)S(1)} %collective-permute-done.7.refs_2_), channel_id=1, source_target_pairs={{0,4},{4,0},{8,12},{12,8},{1,5},{5,1},{9,13},{13,9},{2,6},{6,2},{1... | collective-permute-start | bytes 1179656 | tf_op jit(solution)/shard_map/ppermute | solution.py:370
  14.9 3.2 %collective-permute-start.3 = (f32[8,128]{1,0:T(8,128)S(1)}, f32[8,128]{1,0:T(8,128)S(1)}, u32[]{:S(2)}, u32[]{:S(2)}) collective-permute-start(f32[8,128]{1,0:T(8,128)S(1)} %maximum_maximum_fusion.refs_0_), channel_id=1, source_target_pairs={{0,4},{4,0},{8,12},{12,8},{1,5},{5,1},{9,13},{13,9},{2,6},{6,2},{1... | collective-permute-start | bytes 12296 | tf_op jit(solution)/shard_map/ppermute | solution.py:370
  15.4 69.8 %collective-permute-start.4 = (f32[8,128]{1,0:T(8,128)S(1)}, f32[8,128]{1,0:T(8,128)S(1)}, u32[]{:S(2)}, u32[]{:S(2)}) collective-permute-start(f32[8,128]{1,0:T(8,128)S(1)} %maximum_maximum_fusion.refs_0_), channel_id=1, source_target_pairs={{0,8},{4,12},{8,0},{12,4},{1,9},{5,13},{9,1},{13,5},{2,10},{6,14},... | collective-permute-start | bytes 12296 | tf_op jit(solution)/shard_map/ppermute | solution.py:370
  18.1 67.2 %collective-permute-start.5 = (f32[8,128]{1,0:T(8,128)S(1)}, f32[8,128]{1,0:T(8,128)S(1)}, u32[]{:S(2)}, u32[]{:S(2)}) collective-permute-start(f32[8,128]{1,0:T(8,128)S(1)} %maximum_maximum_fusion.refs_0_), channel_id=1, source_target_pairs={{0,12},{4,8},{8,4},{12,0},{1,13},{5,9},{9,5},{13,1},{2,14},{6,10},... | collective-permute-start | bytes 12296 | tf_op jit(solution)/shard_map/ppermute | solution.py:370
  19.5 65.8 %copy-start.4 = (s32[16]{0:T(128)S(1)}, s32[16]{0:T(128)}, u32[]{:S(2)}) copy-start(s32[16]{0:T(128)} %gather_fusion) | copy-start | bytes 196
  85.2 17.9 %collective-permute-start = (bf16[128,1536]{1,0:T(8,128)(2,1)S(1)}, bf16[128,1536]{1,0:T(8,128)(2,1)S(1)}, u32[]{:S(2)}, u32[]{:S(2)}) collective-permute-start(bf16[128,1536]{1,0:T(8,128)(2,1)S(1)} %get-tuple-element.40.refs_0_), channel_id=1, source_target_pairs={{0,4},{4,0},{8,12},{12,8},{1,5},{5,1},{9,13},{13,9},{2,6},{6,2},{1... | collective-permute-start | bytes 1179656 | tf_op jit(solution)/shard_map/ppermute | solution.py:370
  86.4 16.7 %collective-permute-start.2 = (bf16[128,1536]{1,0:T(8,128)(2,1)S(1)}, bf16[128,1536]{1,0:T(8,128)(2,1)S(1)}, u32[]{:S(2)}, u32[]{:S(2)}) collective-permute-start(bf16[128,1536]{1,0:T(8,128)(2,1)S(1)} %collective-permute-done.1.refs_2_), channel_id=1, source_target_pairs={{0,4},{4,0},{8,12},{12,8},{1,5},{5,1},{9,13},{13,9},{2,6},{6,2},{1... | collective-permute-start | bytes 1179656 | tf_op jit(solution)/shard_map/ppermute | solution.py:370
  86.9 16.2 %copy-start.2 = (bf16[16,4,16,1024]{3,2,1,0:T(8,128)(2,1)S(1)}, bf16[16,4,16,1024]{3,2,1,0:T(8,128)(2,1)}, u32[]{:S(2)}) copy-start(bf16[16,4,16,1024]{3,2,1,0:T(8,128)(2,1)} %tenant_factors.1.refs_9_) | copy-start | bytes 6291460
  101.4 1.7 copy-start.3
  118.2 22.2 %collective-permute-start.18 = (bf16[32,512]{1,0:T(8,128)(2,1)S(1)}, bf16[32,512]{1,0:T(8,128)(2,1)S(1)}, u32[]{:S(2)}, u32[]{:S(2)}) collective-permute-start(bf16[32,512]{1,0:T(8,128)(2,1)S(1)} %get-tuple-element.36), channel_id=1, source_target_pairs={{0,1},{1,2},{2,3},{3,0},{4,5},{5,6},{6,7},{7,4},{8,9},{9,10},{10,1... | collective-permute-start | bytes 98312 | tf_op jit(solution)/shard_map/ppermute | solution.py:373
  119.9 20.5 %collective-permute-start.19 = (bf16[32,512]{1,0:T(8,128)(2,1)S(1)}, bf16[32,512]{1,0:T(8,128)(2,1)S(1)}, u32[]{:S(2)}, u32[]{:S(2)}) collective-permute-start(bf16[32,512]{1,0:T(8,128)(2,1)S(1)} %get-tuple-element.36), channel_id=1, source_target_pairs={{0,2},{1,3},{2,0},{3,1},{4,6},{5,7},{6,4},{7,5},{8,10},{9,11},{10,... | collective-permute-start | bytes 98312 | tf_op jit(solution)/shard_map/ppermute | solution.py:373
  122.5 17.9 %collective-permute-start.20 = (bf16[32,512]{1,0:T(8,128)(2,1)S(1)}, bf16[32,512]{1,0:T(8,128)(2,1)S(1)}, u32[]{:S(2)}, u32[]{:S(2)}) collective-permute-start(bf16[32,512]{1,0:T(8,128)(2,1)S(1)} %get-tuple-element.36), channel_id=1, source_target_pairs={{0,3},{1,0},{2,1},{3,2},{4,7},{5,4},{6,5},{7,6},{8,11},{9,8},{10,9... | collective-permute-start | bytes 98312 | tf_op jit(solution)/shard_map/ppermute | solution.py:373
  134.5 16.8 %collective-permute-start.9 = (bf16[256,768]{1,0:T(8,128)(2,1)S(1)}, bf16[256,768]{1,0:T(8,128)(2,1)S(1)}, u32[]{:S(2)}, u32[]{:S(2)}) collective-permute-start(bf16[256,768]{1,0:T(8,128)(2,1)S(1)} %get-tuple-element.31), channel_id=1, source_target_pairs={{0,4},{4,0},{8,12},{12,8},{1,5},{5,1},{9,13},{13,9},{2,6},{6,2},{1... | collective-permute-start | bytes 1179656 | tf_op jit(solution)/shard_map/ppermute | solution.py:370
  139.9 13.0 %collective-permute-start.12 = (bf16[256,768]{1,0:T(8,128)(2,1)S(1)}, bf16[256,768]{1,0:T(8,128)(2,1)S(1)}, u32[]{:S(2)}, u32[]{:S(2)}) collective-permute-start(bf16[256,768]{1,0:T(8,128)(2,1)S(1)} %get-tuple-element.33), channel_id=1, source_target_pairs={{0,4},{4,0},{8,12},{12,8},{1,5},{5,1},{9,13},{13,9},{2,6},{6,2},{1... | collective-permute-start | bytes 1179656 | tf_op jit(solution)/shard_map/ppermute | solution.py:370
  140.5 7.4 %collective-permute-start.21 = (bf16[32,512]{1,0:T(8,128)(2,1)S(1)}, bf16[32,512]{1,0:T(8,128)(2,1)S(1)}, u32[]{:S(2)}, u32[]{:S(2)}) collective-permute-start(bf16[32,512]{1,0:T(8,128)(2,1)S(1)} %add_convert_fusion.5.refs_0_), channel_id=1, source_target_pairs={{0,4},{4,0},{8,12},{12,8},{1,5},{5,1},{9,13},{13,9},{2,6},{6,2},{1... | collective-permute-start | bytes 98312 | tf_op jit(solution)/shard_map/ppermute | solution.py:370
  140.6 7.7 %collective-permute-start.22 = (bf16[32,512]{1,0:T(8,128)(2,1)S(1)}, bf16[32,512]{1,0:T(8,128)(2,1)S(1)}, u32[]{:S(2)}, u32[]{:S(2)}) collective-permute-start(bf16[32,512]{1,0:T(8,128)(2,1)S(1)} %add_convert_fusion.5.refs_0_), channel_id=1, source_target_pairs={{0,8},{4,12},{8,0},{12,4},{1,9},{5,13},{9,1},{13,5},{2,10},{6,14},... | collective-permute-start | bytes 98312 | tf_op jit(solution)/shard_map/ppermute | solution.py:370
  142.1 6.2 %collective-permute-start.23 = (bf16[32,512]{1,0:T(8,128)(2,1)S(1)}, bf16[32,512]{1,0:T(8,128)(2,1)S(1)}, u32[]{:S(2)}, u32[]{:S(2)}) collective-permute-start(bf16[32,512]{1,0:T(8,128)(2,1)S(1)} %add_convert_fusion.5.refs_0_), channel_id=1, source_target_pairs={{0,12},{4,8},{8,4},{12,0},{1,13},{5,9},{9,5},{13,1},{2,14},{6,10},... | collective-permute-start | bytes 98312 | tf_op jit(solution)/shard_map/ppermute | solution.py:370
  142.4 5.9 %copy-start.5 = (bf16[16,8,16,768]{3,2,1,0:T(8,128)(2,1)S(1)}, bf16[16,8,16,768]{3,2,1,0:T(8,128)(2,1)}, u32[]{:S(2)}) copy-start(bf16[16,8,16,768]{3,2,1,0:T(8,128)(2,1)} %param.21) | copy-start | bytes 9437188
  147.9 5.8 %collective-permute-start.15 = (bf16[256,768]{1,0:T(8,128)(2,1)S(1)}, bf16[256,768]{1,0:T(8,128)(2,1)S(1)}, u32[]{:S(2)}, u32[]{:S(2)}) collective-permute-start(bf16[256,768]{1,0:T(8,128)(2,1)S(1)} %get-tuple-element.35), channel_id=1, source_target_pairs={{0,4},{4,0},{8,12},{12,8},{1,5},{5,1},{9,13},{13,9},{2,6},{6,2},{1... | collective-permute-start | bytes 1179656 | tf_op jit(solution)/shard_map/ppermute | solution.py:370
  151.0 4.3 %collective-permute-start.24 = (bf16[256,768]{1,0:T(8,128)(2,1)S(1)}, bf16[256,768]{1,0:T(8,128)(2,1)S(1)}, u32[]{:S(2)}, u32[]{:S(2)}) collective-permute-start(bf16[256,768]{1,0:T(8,128)(2,1)S(1)} %get-tuple-element.38), channel_id=1, source_target_pairs={{0,4},{4,0},{8,12},{12,8},{1,5},{5,1},{9,13},{13,9},{2,6},{6,2},{1... | collective-permute-start | bytes 1179656 | tf_op jit(solution)/shard_map/ppermute | solution.py:370
  151.4 7.8 %collective-permute-start.10 = (bf16[128,768]{1,0:T(8,128)(2,1)S(1)}, bf16[128,768]{1,0:T(8,128)(2,1)S(1)}, u32[]{:S(2)}, u32[]{:S(2)}) collective-permute-start(bf16[128,768]{1,0:T(8,128)(2,1)S(1)} %slice_bitcast_fusion.6), channel_id=1, source_target_pairs={{0,8},{4,12},{8,0},{12,4},{1,9},{5,13},{9,1},{13,5},{2,10},{6,14},... | collective-permute-start | bytes 589832 | tf_op jit(solution)/shard_map/ppermute | solution.py:370
  153.0 25.4 %copy-start.1 = (s32[64]{0:T(128)S(1)}, s32[64]{0:T(128)}, u32[]{:S(2)}) copy-start(s32[64]{0:T(128)} %param.16) | copy-start | bytes 772
  153.0 10.3 %collective-permute-start.13 = (bf16[128,768]{1,0:T(8,128)(2,1)S(1)}, bf16[128,768]{1,0:T(8,128)(2,1)S(1)}, u32[]{:S(2)}, u32[]{:S(2)}) collective-permute-start(bf16[128,768]{1,0:T(8,128)(2,1)S(1)} %slice_bitcast_fusion.4), channel_id=1, source_target_pairs={{0,8},{4,12},{8,0},{12,4},{1,9},{5,13},{9,1},{13,5},{2,10},{6,14},... | collective-permute-start | bytes 589832 | tf_op jit(solution)/shard_map/ppermute | solution.py:370
  153.8 13.8 %collective-permute-start.16 = (bf16[128,768]{1,0:T(8,128)(2,1)S(1)}, bf16[128,768]{1,0:T(8,128)(2,1)S(1)}, u32[]{:S(2)}, u32[]{:S(2)}) collective-permute-start(bf16[128,768]{1,0:T(8,128)(2,1)S(1)} %slice_bitcast_fusion.2), channel_id=1, source_target_pairs={{0,8},{4,12},{8,0},{12,4},{1,9},{5,13},{9,1},{13,5},{2,10},{6,14},... | collective-permute-start | bytes 589832 | tf_op jit(solution)/shard_map/ppermute | solution.py:370
  155.4 15.8 %collective-permute-start.25 = (bf16[128,768]{1,0:T(8,128)(2,1)S(1)}, bf16[128,768]{1,0:T(8,128)(2,1)S(1)}, u32[]{:S(2)}, u32[]{:S(2)}) collective-permute-start(bf16[128,768]{1,0:T(8,128)(2,1)S(1)} %slice_bitcast_fusion), channel_id=1, source_target_pairs={{0,8},{4,12},{8,0},{12,4},{1,9},{5,13},{9,1},{13,5},{2,10},{6,14},... | collective-permute-start | bytes 589832 | tf_op jit(solution)/shard_map/ppermute | solution.py:370
  159.2 12.0 %collective-permute-start.11 = (bf16[128,768]{1,0:T(8,128)(2,1)S(1)}, bf16[128,768]{1,0:T(8,128)(2,1)S(1)}, u32[]{:S(2)}, u32[]{:S(2)}) collective-permute-start(bf16[128,768]{1,0:T(8,128)(2,1)S(1)} %fusion.3), channel_id=1, source_target_pairs={{0,1},{1,2},{2,3},{3,0},{4,5},{5,6},{6,7},{7,4},{8,9},{9,10},{10,1... | collective-permute-start | bytes 589832 | tf_op jit(solution)/shard_map/ppermute | solution.py:373
  163.4 12.0 %collective-permute-start.14 = (bf16[128,768]{1,0:T(8,128)(2,1)S(1)}, bf16[128,768]{1,0:T(8,128)(2,1)S(1)}, u32[]{:S(2)}, u32[]{:S(2)}) collective-permute-start(bf16[128,768]{1,0:T(8,128)(2,1)S(1)} %fusion.2), channel_id=1, source_target_pairs={{0,2},{1,3},{2,0},{3,1},{4,6},{5,7},{6,4},{7,5},{8,10},{9,11},{10,... | collective-permute-start | bytes 589832 | tf_op jit(solution)/shard_map/ppermute | solution.py:373
  167.6 9.9 %collective-permute-start.17 = (bf16[128,768]{1,0:T(8,128)(2,1)S(1)}, bf16[128,768]{1,0:T(8,128)(2,1)S(1)}, u32[]{:S(2)}, u32[]{:S(2)}) collective-permute-start(bf16[128,768]{1,0:T(8,128)(2,1)S(1)} %fusion.1), channel_id=1, source_target_pairs={{0,3},{1,0},{2,1},{3,2},{4,7},{5,4},{6,5},{7,6},{8,11},{9,8},{10,9... | collective-permute-start | bytes 589832 | tf_op jit(solution)/shard_map/ppermute | solution.py:373

commit v2 on v1

v2 whole, which is shorter than its diff:
```python
import functools

import jax
import jax.numpy as jnp
from jax import lax
from jax.experimental import pallas as pl
from jax.experimental.pallas import tpu as pltpu
from jax.sharding import PartitionSpec as P

EXPERT_COUNT = 8
TOP = 2
RANK = 16
CAP = 48
K_CHUNKS = 3
N_TILE = 512
MIB = 1 << 20

F32 = jnp.float32
BF16 = jnp.bfloat16


def mm(a, b):
    return jnp.dot(a, b, preferred_element_type=F32)


def mm_nt(a, b):
    return lax.dot_general(a, b, (((1,), (1,)), ((), ())), preferred_element_type=F32)


def cost(flops, moved, trans=0):
    return pl.CostEstimate(flops=int(flops), bytes_accessed=int(moved), transcendentals=int(trans))


def params(mib):
    return pltpu.CompilerParams(vmem_limit_bytes=mib * MIB)


def vmem():
    return pl.BlockSpec(memory_space=pltpu.VMEM)


def smem():
    return pl.BlockSpec(memory_space=pltpu.SMEM)


def meta_kernel(n_local, scalar_ref, slots_ref, *refs):
    blocks, (p_ref, pt_ref, cols_ref, rows_ref, tslot_ref) = refs[:-5], refs[-5:]
    info = jnp.concatenate([block[...] for block in blocks], axis=1)
    count = info.shape[1]
    first, second, tenant = info[0:1], info[1:2], info[4:5]
    weight_first = jax.nn.sigmoid(info[2:3] - info[3:4])
    weight_second = jax.nn.sigmoid(info[3:4] - info[2:3])
    slot = jnp.zeros_like(tenant)
    for number in range(slots_ref.shape[0]):
        slot = jnp.where(tenant == number, slots_ref[number].astype(F32), slot)
    members, weights = [], []
    for i in range(n_local):
        expert = (scalar_ref[0] + i).astype(F32)
        hit_first, hit_second = first == expert, second == expert
        members.append(jnp.where(hit_first | hit_second, 1.0, 0.0))
        weights.append(jnp.where(hit_first, weight_first, 0.0) + jnp.where(hit_second, weight_second, 0.0))
    member = jnp.concatenate(members + [jnp.zeros((8 - n_local, count), F32)], axis=0)
    before = (
        lax.broadcasted_iota(jnp.int32, (count, count), 0) < lax.broadcasted_iota(jnp.int32, (count, count), 1)
    ).astype(BF16)
    place = jnp.where(member > 0, mm(member.astype(BF16), before), -1.0)
    table = jnp.concatenate(
        [place[0:n_local]] + weights + [slot] + [jnp.zeros((127 - 2 * n_local, count), F32)], axis=0
    )
    columns = table.T
    cols_ref[...] = columns
    rows_ref[...] = table[0:8]
    row_count = p_ref.shape[1]
    tenant_rows = jnp.broadcast_to(tenant, (8, count)).astype(BF16)
    down = lax.broadcasted_iota(jnp.int32, (row_count, count), 0).astype(F32)
    across = lax.broadcasted_iota(jnp.int32, (count, row_count), 1).astype(F32)
    for i in range(n_local):
        picked = (down == place[i : i + 1]).astype(BF16)
        p_ref[i] = picked
        pt_ref[i] = (across == columns[:, i : i + 1]).astype(BF16)
        tslot_ref[i] = mm_nt(tenant_rows, picked)


def build_meta(blocks, expert_base, slots, n_local, row_count):
    count = sum(block.shape[1] for block in blocks)
    return pl.pallas_call(
        functools.partial(meta_kernel, n_local),
        out_shape=(
            jax.ShapeDtypeStruct((n_local, row_count, count), BF16),
            jax.ShapeDtypeStruct((n_local, count, row_count), BF16),
            jax.ShapeDtypeStruct((count, 128), F32),
            jax.ShapeDtypeStruct((8, count), F32),
            jax.ShapeDtypeStruct((n_local, 8, row_count), F32),
        ),
        in_specs=[smem(), smem()] + [vmem()] * len(blocks),
        out_specs=(vmem(),) * 5,
        compiler_params=params(max(8, 12 * count * count // MIB)),
        cost_estimate=cost(2 * 8 * count * count, 4 * n_local * row_count * count),
        name="routing_tables",
    )(expert_base, slots, *blocks)


def slab(ref, part, half, tile, ring_ref):
    depth, width = ring_ref.shape[1], ring_ref.shape[2]
    return ref.at[half, pl.ds(part * depth, depth), pl.ds(tile * width, width)]


def slab_copy(gate_ref, up_ref, ring_ref, sems, part, half, tile, which):
    tiles = gate_ref.shape[2] // ring_ref.shape[2]
    slot = (half * tiles + tile) * 2 + which
    source = slab((gate_ref, up_ref)[which], part, half, tile, ring_ref)
    return pltpu.make_async_copy(source, ring_ref.at[slot], sems.at[slot])


def prefetch_kernel(gate_ref, up_ref, ring_ref, mark_ref, sems):
    tiles = gate_ref.shape[2] // ring_ref.shape[2]
    copies = [
        slab_copy(gate_ref, up_ref, ring_ref, sems, 0, half, tile, which)
        for half in range(gate_ref.shape[0])
        for tile in range(tiles)
        for which in range(2)
    ]
    for copy in copies:
        copy.start()
    mark_ref[...] = jnp.zeros_like(mark_ref)
    for copy in copies:
        copy.wait()


def prefetch(gate, up, part_width):
    local_halves, _, hidden_count = gate.shape
    tile = min(N_TILE, hidden_count)
    slots = 2 * local_halves * (hidden_count // tile)
    return pl.pallas_call(
        prefetch_kernel,
        out_shape=(
            pltpu.VMEM((slots, part_width, tile), BF16),
            jax.ShapeDtypeStruct((8, 128), F32),
        ),
        in_specs=[pl.BlockSpec(memory_space=pltpu.HBM)] * 2,
        out_specs=(vmem(), vmem()),
        scratch_shapes=[pltpu.SemaphoreType.DMA((slots,))],
        compiler_params=params(4),
        cost_estimate=cost(0, 2 * slots * part_width * tile * 2),
        name="weight_prefetch",
    )(gate, up)


def expert_kernel(n_blocks, part, parts, *refs):
    is_first, is_last = part == 0, part == parts - 1
    blocks, refs = refs[:n_blocks], refs[n_blocks:]
    p_ref, gate_ref, up_ref, ring_ref, refs = refs[1], refs[2], refs[3], refs[4], refs[5:]
    if not is_first:
        gate_in, up_in, refs = refs[0], refs[1], refs[2:]
    if is_last:
        slots_ref, target_ref, pool_ref, tslot_ref, rows_ref, down_ref = refs[:6]
        ring_out, hidden_ref, low_ref, next_ref, packed, sems, factors, factor_sems, down_sems = refs[6:]
    else:
        ring_out, gate_out, up_out, packed, sems = refs
    n_local = p_ref.shape[0]
    local_halves, _, hidden_count = gate_ref.shape
    halves_each = local_halves // n_local
    width = ring_ref.shape[2]
    tiles = hidden_count // width
    last = (local_halves - 1, tiles - 1)

    def refill(number, half, tile, which):
        return slab_copy(gate_ref, up_ref, ring_out, sems, number, half, tile, which)

    if not is_first:
        for which in range(2):
            refill(part, *last, which).start()
    if is_last:
        down_copies = down_fetch(target_ref, down_ref, next_ref, down_sems)
        for copy in down_copies:
            copy.start()
        tenants, rank = slots_ref.shape[0], pool_ref.shape[2]
        factor_copies = [
            pltpu.make_async_copy(
                pool_ref.at[slots_ref[number]], factors.at[:, number * rank : (number + 1) * rank], factor_sems.at[number]
            )
            for number in range(tenants)
        ]
        for copy in factor_copies:
            copy.start()
    whole = jnp.concatenate([block[...] for block in blocks], axis=0)
    for i in range(n_local):
        packed[i] = mm(p_ref[i], whole).astype(BF16)

    def step(half, carry):
        rows = packed[half // halves_each]
        for tile in range(tiles):
            slot = (half * tiles + tile) * 2
            if tile == tiles - 1 and not is_first:

                @pl.when(half == local_halves - 1)
                def _():
                    for which in range(2):
                        refill(part, *last, which).wait()

            span = slice(tile * width, (tile + 1) * width)
            gate = mm(rows, ring_out[slot])
            up = mm(rows, ring_out[slot + 1])
            if not is_first:
                gate = gate + gate_in[half, :, span]
                up = up + up_in[half, :, span]
            if is_last:
                hidden_ref[half, :, span] = (jax.nn.silu(gate) * up).astype(BF16)
                continue
            gate_out[half, :, span] = gate
            up_out[half, :, span] = up
            if tile < tiles - 1:
                for which in range(2):
                    refill(part + 1, half, tile, which).start()
            else:

                @pl.when(half < local_halves - 1)
                def _():
                    for which in range(2):
                        refill(part + 1, half, tile, which).start()

        return carry

    lax.fori_loop(0, local_halves, step, 0)
    if not is_last:
        for half in range(local_halves):
            for tile in range(tiles):
                if (half, tile) != last:
                    for which in range(2):
                        refill(part + 1, half, tile, which).wait()
        return
    for copy in factor_copies:
        copy.wait()
    for i in range(n_local):
        low = mm_nt(factors[i * halves_each], hidden_ref[i * halves_each])
        for half in range(i * halves_each + 1, (i + 1) * halves_each):
            low = low + mm_nt(factors[half], hidden_ref[half])
        owner = tslot_ref[i][0:1]
        total = jnp.zeros((rank, low.shape[1]), F32)
        for number in range(tenants):
            total = total + jnp.where(owner == number, low[number * rank : (number + 1) * rank], 0.0)
        weight = rows_ref[n_local + i : n_local + i + 1]
        low_ref[i * rank : (i + 1) * rank] = (mm(total.astype(BF16), p_ref[i]) * weight).astype(BF16)
    for copy in down_copies:
        copy.wait()


def expert_part(blocks, part, parts, mark, picked, gate, up, ring, sums, slots, target, pool, tslot, table_rows, down, span):
    local_halves, width, hidden_count = gate.shape
    part_width = width // parts
    n_local, row_count, count = picked.shape
    is_first, is_last = part == 0, part == parts - 1
    hbm = pl.BlockSpec(memory_space=pltpu.HBM)
    in_specs = [vmem()] * (len(blocks) + 2) + [hbm, hbm, vmem()]
    operands = list(blocks) + [mark, picked, gate, up, ring]
    aliases = {len(operands) - 1: 0}
    if not is_first:
        if not is_last:
            aliases.update({len(operands): 1, len(operands) + 1: 2})
        in_specs += [vmem(), vmem()]
        operands += [pltpu.with_memory_space_constraint(x, pltpu.VMEM) for x in sums]
    scratch = [pltpu.VMEM((n_local, row_count, part_width), BF16), pltpu.SemaphoreType.DMA((ring.shape[0],))]
    if is_last:
        tenants, rank = slots.shape[0], pool.shape[2]
        in_specs += [smem(), smem(), hbm, vmem(), vmem(), hbm]
        operands += [slots, target, pool, tslot, table_rows, down]
        out_shape = (
            pltpu.VMEM(ring.shape, BF16),
            pltpu.VMEM((local_halves, row_count, hidden_count), BF16),
            jax.ShapeDtypeStruct((n_local * rank, count), BF16),
            pltpu.VMEM((local_halves, hidden_count, span), BF16),
        )
        scratch += [
            pltpu.VMEM((local_halves, tenants * rank, hidden_count), BF16),
            pltpu.SemaphoreType.DMA((tenants,)),
            pltpu.SemaphoreType.DMA((local_halves,)),
        ]
    else:
        out_shape = (pltpu.VMEM(ring.shape, BF16),) + (pltpu.VMEM((local_halves, row_count, hidden_count), F32),) * 2
    return pl.pallas_call(
        functools.partial(expert_kernel, len(blocks), part, parts),
        out_shape=out_shape,
        in_specs=in_specs,
        out_specs=(vmem(),) * len(out_shape),
        scratch_shapes=scratch,
        input_output_aliases=aliases,
        compiler_params=params(max(10, 10 * n_local * row_count * part_width // MIB)),
        cost_estimate=cost(
            4 * local_halves * row_count * part_width * hidden_count, 4 * local_halves * part_width * hidden_count
        ),
        name="gate_up_part",
    )(*operands)


def down_fetch(target_ref, down_ref, next_ref, sems):
    span = next_ref.shape[2]
    start = pl.multiple_of(target_ref[0] * span, span)
    return [
        pltpu.make_async_copy(down_ref.at[half, :, pl.ds(start, span)], next_ref.at[half], sems.at[half])
        for half in range(down_ref.shape[0])
    ]


def down_kernel(is_final, *refs):
    if is_final:
        hidden_ref, weight_ref, pt_ref, cols_ref, base_ref = refs
    else:
        target_ref, hidden_ref, weight_ref, down_ref, pt_ref, cols_ref, keep, send, next_ref, sems = refs
        copies = down_fetch(target_ref, down_ref, next_ref, sems)
        for copy in copies:
            copy.start()
    n_local = pt_ref.shape[0]
    halves_each = hidden_ref.shape[0] // n_local
    total = None
    for i in range(n_local):
        part_sum = mm(hidden_ref[i * halves_each], weight_ref[i * halves_each])
        for half in range(i * halves_each + 1, (i + 1) * halves_each):
            part_sum = part_sum + mm(hidden_ref[half], weight_ref[half])
        laid = mm(pt_ref[i], part_sum.astype(BF16)) * cols_ref[:, n_local + i : n_local + i + 1]
        total = laid if total is None else total + laid
    if is_final:
        base_ref[...] = total
    else:
        write_pairs(total, (keep, send))
        for copy in copies:
            copy.wait()


def down_part(next_target, hidden, weights, down, pt, cols):
    local_halves, row_count, hidden_count = hidden.shape
    count, span = pt.shape[1], weights.shape[2]
    is_final = next_target is None
    weights = pltpu.with_memory_space_constraint(weights, pltpu.VMEM)
    if is_final:
        out_shape = (jax.ShapeDtypeStruct((count, span), F32),)
        in_specs, operands = [vmem()] * 4, (hidden, weights, pt, cols)
        scratch = []
    else:
        out_shape = (jax.ShapeDtypeStruct((count // 2, span), BF16),) * 2 + (pltpu.VMEM(weights.shape, BF16),)
        in_specs = [smem(), vmem(), vmem(), pl.BlockSpec(memory_space=pltpu.HBM), vmem(), vmem()]
        operands = (next_target, hidden, weights, down, pt, cols)
        scratch = [pltpu.SemaphoreType.DMA((local_halves,))]
    return pl.pallas_call(
        functools.partial(down_kernel, is_final),
        out_shape=out_shape,
        in_specs=in_specs,
        out_specs=(vmem(),) * len(out_shape),
        scratch_shapes=scratch,
        compiler_params=params(max(10, 12 * count * span // MIB)),
        cost_estimate=cost(
            2 * local_halves * row_count * hidden_count * span, 2 * local_halves * hidden_count * span
        ),
        name="down_part",
    )(*operands)


def write_pairs(total, outs):
    keep, send = outs
    for b in range(total.shape[0] // 128):
        (send if b % 2 else keep)[b // 2 * 128 : b // 2 * 128 + 128] = total[b * 128 : b * 128 + 128].astype(BF16)


def adapter_kernel(scalar_ref, base_ref, factor_ref, cols_ref, slot_column, *refs):
    lows, (keep, send, wide) = refs[:-3], refs[-3:]
    wide[...] = jnp.zeros_like(wide)
    height = lows[0].shape[0]
    count = base_ref.shape[0]
    blocks = count // 128
    for m in range(len(lows)):
        start = pl.multiple_of(scalar_ref[1 + m], RANK)
        value = lows[m][...].astype(F32)
        value = jnp.concatenate([value[:, (m ^ b) * 128 : (m ^ b) * 128 + 128] for b in range(blocks)], axis=1)
        wide[pl.ds(start, height)] += value
    low = wide[...].T.astype(BF16)
    zero = jnp.zeros_like(low)
    slot = cols_ref[:, slot_column : slot_column + 1]
    depth = EXPERT_COUNT * RANK
    slot_count = factor_ref.shape[0] // depth
    total = base_ref[...]
    for j in range(0, slot_count, 2):
        spread = jnp.concatenate(
            [jnp.where(slot == (scalar_ref[0] + j + i).astype(F32), low, zero) for i in range(2)], axis=1
        )
        total = total + mm(spread, factor_ref[j * depth : (j + 2) * depth])
    write_pairs(total, (keep, send))


def adapter_part(scalars, base, factors, cols, slot_column, lows):
    count, span = base.shape

    def kernel(scalar_ref, base_ref, factor_ref, cols_ref, *refs):
        adapter_kernel(scalar_ref, base_ref, factor_ref, cols_ref, slot_column, *refs)

    return pl.pallas_call(
        kernel,
        out_shape=(jax.ShapeDtypeStruct((count // 2, span), BF16),) * 2,
        in_specs=[smem()] + [vmem()] * (3 + len(lows)),
        out_specs=(vmem(),) * 2,
        scratch_shapes=[pltpu.VMEM((EXPERT_COUNT * RANK, count), F32)],
        compiler_params=params(max(16, 24 * count * span // MIB)),
        cost_estimate=cost(2 * count * factors.shape[0] * span, 2 * factors.shape[0] * span),
        name="adapter_part",
    )(scalars, base, factors, cols, *lows)


def per_device(
    n_ep,
    n_ad,
    tokens,
    chosen_experts,
    router_gate_logits,
    token_tenant,
    adapter_of_tenant,
    adapter_pool_slot,
    gate_weight,
    up_weight,
    down_weight,
    adapter_input_factors,
    adapter_output_factors,
):
    gate_weight, up_weight, down_weight, adapter_input_factors = [
        pltpu.with_memory_space_constraint(x, pltpu.HBM)
        for x in (gate_weight, up_weight, down_weight, adapter_input_factors)
    ]
    width = tokens.shape[1]
    span = width // n_ad
    local_halves = gate_weight.shape[0]
    n_local = max(1, local_halves // 2)
    row_count = n_ep * CAP
    bits = n_ep.bit_length() - 1
    ep_index, ad_index = lax.axis_index("ep"), lax.axis_index("ad")

    def swap(x, mask):
        return lax.ppermute(x, "ep", [(i, i ^ mask) for i in range(n_ep)])

    def shift(x, step):
        return lax.ppermute(x, "ad", [(i, (i + step) % n_ad) for i in range(n_ad)])

    info = jnp.concatenate(
        [
            chosen_experts.astype(F32).T,
            router_gate_logits.T,
            token_tenant.astype(F32)[None],
            jnp.zeros((3, tokens.shape[0]), F32),
        ],
        axis=0,
    )
    infos = [info] + [swap(info, mask) for mask in range(1, n_ep)]

    parts = K_CHUNKS
    part_width = width // parts
    ring, mark = prefetch(gate_weight, up_weight, part_width)
    token_parts = []
    for part in range(parts):
        blocks = {0: tokens[:, part * part_width : (part + 1) * part_width]}
        for bit in reversed(range(bits)):
            for mask in list(blocks):
                blocks[mask | 1 << bit] = swap(blocks[mask], 1 << bit)
            if bit == bits - 1:
                high = 1 << bit
                blocks[high], mark = lax.optimization_barrier((blocks[high], mark))
        token_parts.append([blocks[mask] for mask in range(n_ep)])

    slots = adapter_pool_slot[adapter_of_tenant]
    expert_base = (ep_index * local_halves // 2).astype(jnp.int32).reshape(1)
    picked, pt, cols, table_rows, tslot = build_meta(infos, expert_base, slots, n_local, row_count)

    def target(step):
        return ((ad_index + step) % n_ad).astype(jnp.int32).reshape(1)

    sums = None
    for part in range(parts):
        state = expert_part(
            token_parts[part], part, parts, mark, picked, gate_weight, up_weight, ring, sums,
            slots, target(1), adapter_input_factors, tslot, table_rows, down_weight, span,
        )
        if part < parts - 1:
            ring, sums = state[0], state[1:]
    _, hidden, low, weights = state

    arrived = [low] + [shift(low, step) for step in range(1, n_ad)]
    low_total = sum(x.astype(F32) for x in arrived).astype(BF16)
    lows = [low_total] + [swap(low_total, mask) for mask in range(1, n_ep)]

    def between(keep, send):
        return (keep.astype(F32) + swap(send, 1).astype(F32)).astype(BF16)

    def across(mine):
        for bit in range(1, bits):
            half = mine.shape[0] // 128 // 2
            grouped = mine.reshape(half, 2, 128, mine.shape[1])
            keep = grouped[:, 0].reshape(half * 128, -1)
            send = grouped[:, 1].reshape(half * 128, -1)
            mine = (keep.astype(F32) + swap(send, 1 << bit).astype(F32)).astype(BF16)
        return mine

    results, pending = [], None
    for step in range(1, n_ad):
        following = target(step + 1)
        if pending is not None:
            pending, following = lax.optimization_barrier((pending, following))
            results.append(shift(across(pending), step - 1))
        keep, send, weights = down_part(following, hidden, weights, down_weight, pt, cols)
        pending = between(keep, send)
    results.append(shift(across(pending), n_ad - 1))
    (base,) = down_part(None, hidden, weights, down_weight, pt, cols)
    slot_count = adapter_output_factors.shape[0]
    scalars = jnp.stack(
        [ep_index * slot_count] + [((ep_index ^ mask) * local_halves // 2) * RANK for mask in range(n_ep)]
    ).astype(jnp.int32)
    flat_factors = adapter_output_factors.reshape(slot_count * EXPERT_COUNT * RANK, span)
    keep, send = adapter_part(scalars, base, flat_factors, cols, 2 * n_local, lows)
    results.append(across(between(keep, send)))
    return sum(x.astype(F32) for x in results).astype(BF16)


def solution(mesh):
    placed = (
        P(("rep", "ep"), None),
        P(("rep", "ep"), None),
        P(("rep", "ep"), None),
        P(("rep", "ep")),
        P("rep"),
        P(),
        P("ep", None, "ad"),
        P("ep", None, "ad"),
        P("ep", "ad", None),
        P(None, "ep", None, "ad"),
        P("ep", None, None, "ad"),
    )
    return jax.shard_map(
        functools.partial(per_device, mesh.shape["ep"], mesh.shape["ad"]),
        mesh=mesh,
        in_specs=placed,
        out_specs=P(("rep", "ep"), "ad"),
        check_vma=False,
    )
```

time: 179 us -> 117 us (0.65)
  Pallas kernels: 120 us -> 46.6 us
  local copies, waits for them, and re-layouts: 4.32 us -> 19 us
  waiting for transfers between devices: 28.3 us -> 21.6 us
  starting transfers between devices: 21.1 us -> 25.1 us
    pallas_call x7 -> x8, Pallas kernels: 117 us -> 42.7 us  [the longest x3 20.9 us: expert_part(): pl.pallas_call(functools.partial(expert_kernel, len(blocks), part, parts)...]
    unnamed x12 -> x16, local copies, waits for them, and re-layouts: 1.72 us -> 17 us
    ppermute x20 -> x23, waiting for transfers between devices: 21.9 us -> 14.9 us  [swap(): return lax.ppermute(x, 'ep', [(i, i ^ mask) for i in range(n_ep)])]
    ppermute x6, starting transfers between devices: 7.17 us -> 9.49 us  [shift(): return lax.ppermute(x, 'ad', [(i, (i + step) % n_ad) for i in range(n_ad)])]
    ppermute x20 -> x23, starting transfers between devices: 13.9 us -> 15.6 us  [swap(): return lax.ppermute(x, 'ep', [(i, i ^ mask) for i in range(n_ep)])]
  transfers between devices with their start and end apart: 26 -> 29, of which waited for: 7 -> 5; matrix products, arithmetic and copies ran while one was open for 3% -> 4% of each run, Pallas kernels for 59% -> 29%
where the time goes in v2:
time: 117 us
  Pallas kernels  46.6 us (40%)
  starting transfers between devices  25.1 us (21%)
  waiting for transfers between devices  21.6 us (18%)
  local copies, waits for them, and re-layouts  19 us (16%)
  other arithmetic  4.48 us (4%)
    pallas_call x3, Pallas kernels, expert_part(): pl.pallas_call(functools.partial(expert_kernel, len(blocks), part, parts)...  20.9 us
    unnamed x16, local copies, waits for them, and re-layouts  17 us
    pallas_call x4, Pallas kernels, down_part(): pl.pallas_call(functools.partial(down_kernel, is_final), out_shape=out_sh...  15.9 us
    ppermute x23, starting transfers between devices, swap(): return lax.ppermute(x, 'ep', [(i, i ^ mask) for i in range(n_ep)])  15.6 us
    ppermute x23, waiting for transfers between devices, swap(): return lax.ppermute(x, 'ep', [(i, i ^ mask) for i in range(n_ep)])  14.9 us
    ppermute x6, starting transfers between devices, shift(): return lax.ppermute(x, 'ad', [(i, (i + step) % n_ad) for i in range(n_ad)])  9.49 us
    ppermute x6, waiting for transfers between devices, shift(): return lax.ppermute(x, 'ad', [(i, (i + step) % n_ad) for i in range(n_ad)])  6.69 us
    pallas_call x1, Pallas kernels, prefetch(): pl.pallas_call(prefetch_kernel, out_shape=(pltpu.VMEM((slots, part_width,...  5.93 us
  transfers between devices with their start and end apart: 29, of which 5 were waited for; matrix products, arithmetic and copies ran while one was open for 4% of the time, Pallas kernels for 29%

profile of v2, /device:TPU:0, one launch (start us, length us, event | category | flops | bytes accessed | tf_op | source)
XLA Modules:
  0.0 117.1 jit_solution(9629876845826185771)
XLA Ops:
  0.0 1.2 %fusion.4 = (bf16[128,1024]{1,0:T(8,128)(2,1)S(1)}, bf16[128,1024]{1,0:T(8,128)(2,1)S(1)}, bf16[128,1024]{1,0:T(8,128)(2,1)S(1)}) fusion(bf16[128,3072]{1,0:T(8,128)(2,1)} %param.11), kind=kLoop, calls=%fused_computation.28 | loop fusion | bytes 1572864 | tf_op jit(solution)/shard_map/slice | solution.py:455
  1.2 3.0 %collective-permute-start.3 = (bf16[128,1024]{1,0:T(8,128)(2,1)S(1)}, bf16[128,1024]{1,0:T(8,128)(2,1)S(1)}, u32[]{:S(2)}, u32[]{:S(2)}) collective-permute-start(bf16[128,1024]{1,0:T(8,128)(2,1)S(1)} %get-tuple-element.79.refs_0_), channel_id=1, source_target_pairs={{0,8},{4,12},{8,0},{12,4},{1,9},{5,13},{9,1},{13,5},{2,10},{6,14},... | collective-permute-start | bytes 786440 | tf_op jit(solution)/shard_map/ppermute | solution.py:434
  4.2 0.7 convert_bitcast_fusion
  4.9 0.7 convert_bitcast_fusion.1
  5.6 0.7 maximum_maximum_fusion.refs_0_
  6.4 0.5 collective-permute-start.10
  6.9 1.7 %collective-permute-start.2 = (bf16[128,1024]{1,0:T(8,128)(2,1)S(1)}, bf16[128,1024]{1,0:T(8,128)(2,1)S(1)}, u32[]{:S(2)}, u32[]{:S(2)}) collective-permute-start(bf16[128,1024]{1,0:T(8,128)(2,1)S(1)} %get-tuple-element.81.refs_0_), channel_id=1, source_target_pairs={{0,8},{4,12},{8,0},{12,4},{1,9},{5,13},{9,1},{13,5},{2,10},{6,14},... | collective-permute-start | bytes 786440 | tf_op jit(solution)/shard_map/ppermute | solution.py:434
  8.6 5.9 %weight_prefetch.1 = (bf16[16,1024,512]{2,1,0:T(8,128)(2,1)S(1)}, f32[8,128]{1,0:T(8,128)S(1)}) custom-call(bf16[4,3072,1024]{2,1,0:T(8,128)(2,1)} %refs_6_.5, bf16[4,3072,1024]{2,1,0:T(8,128)(2,1)} %refs_7_.5), custom_call_target="tpu_custom_call" | custom-call | bytes 33554432 | tf_op jit(solution)/shard_map/weight_prefetch/pallas_call | solution.py:134
  14.6 5.7 %copy-done.2 = bf16[16,1024,512]{2,1,0:T(8,128)(2,1)} copy-done((bf16[16,1024,512]{2,1,0:T(8,128)(2,1)}, bf16[16,1024,512]{2,1,0:T(8,128)(2,1)S(1)}, u32[]{:S(2)}) %copy-start.2) | copy-done | bytes 16777240
  20.3 0.3 collective-permute-start.1
  20.6 1.9 %collective-permute-start.7 = (f32[8,128]{1,0:T(8,128)S(1)}, f32[8,128]{1,0:T(8,128)S(1)}, u32[]{:S(2)}, u32[]{:S(2)}) collective-permute-start(f32[8,128]{1,0:T(8,128)S(1)} %maximum_maximum_fusion.refs_0_), channel_id=1, source_target_pairs={{0,12},{4,8},{8,4},{12,0},{1,13},{5,9},{9,5},{13,1},{2,14},{6,10},... | collective-permute-start | bytes 12296 | tf_op jit(solution)/shard_map/ppermute | solution.py:434
  22.5 0.7 gather_fusion
  23.2 4.4 %collective-permute-done.7.refs_3_ = f32[8,128]{1,0:T(8,128)S(1)} collective-permute-done((f32[8,128]{1,0:T(8,128)S(1)}, f32[8,128]{1,0:T(8,128)S(1)}, u32[]{:S(2)}, u32[]{:S(2)}) %collective-permute-start.7) | collective-permute-done | bytes 4128 | tf_op jit(solution)/shard_map/ppermute | solution.py:434
  27.7 1.0 collective-permute-start.8
  28.7 1.1 routing_tables.1
  29.9 0.5 collective-permute-start.9
  30.4 5.8 %copy-done.3 = bf16[16,1024,512]{2,1,0:T(8,128)(2,1)S(1)} copy-done((bf16[16,1024,512]{2,1,0:T(8,128)(2,1)S(1)}, bf16[16,1024,512]{2,1,0:T(8,128)(2,1)}, u32[]{:S(2)}) %copy-start.3) | copy-done | bytes 16777240
  36.2 6.5 %gate_up_part.3 = (bf16[16,1024,512]{2,1,0:T(8,128)(2,1)S(1)}, f32[4,192,1024]{2,1,0:T(8,128)S(1)}, f32[4,192,1024]{2,1,0:T(8,128)S(1)}) custom-call(bf16[128,1024]{1,0:T(8,128)(2,1)S(1)} %get-tuple-element.79.refs_0_, bf16[128,1024]{1,0:T(8,128)(2,1)S(1)} %collective-permute-done.10.refs_1_, ...), custom_call_target="tpu_custom_call", output_to_operand_aliasing={{0}: (8, {})} | custom-call | flops 3221225472 | bytes 16777216 | tf_op jit(solution)/shard_map/gate_up_part/pallas_call | solution.py:280
  42.8 6.6 %gate_up_part.4 = (bf16[16,1024,512]{2,1,0:T(8,128)(2,1)S(1)}, f32[4,192,1024]{2,1,0:T(8,128)S(1)}, f32[4,192,1024]{2,1,0:T(8,128)S(1)}) custom-call(bf16[128,1024]{1,0:T(8,128)(2,1)S(1)} %get-tuple-element.81.refs_0_, bf16[128,1024]{1,0:T(8,128)(2,1)S(1)} %collective-permute-done.8.refs_1_, ...), custom_call_target="tpu_custom_call", output_to_operand_aliasing={{0}: (8, {}), {1}: (9, {}), {2}: (10, {})} | custom-call | flops 3221225472 | bytes 16777216 | tf_op jit(solution)/shard_map/gate_up_part/pallas_call | solution.py:280
  49.4 7.8 %gate_up_part.5 = (bf16[16,1024,512]{2,1,0:T(8,128)(2,1)S(1)}, bf16[4,192,1024]{2,1,0:T(8,128)(2,1)S(1)}, bf16[32,512]{1,0:T(8,128)(2,1)S(1)}, bf16[4,1024,768]{2,1,0:T(8,128)(2,1)S(1)}) custom-call(bf16[128,1024]{1,0:T(8,128)(2,1)S(1)} %get-tuple-element.80.refs_0_, ...), custom_call_target="tpu_custom_call", output_to_operand_aliasing={{0}: (8, {})} | custom-call | flops 3221225472 | bytes 16777216 | tf_op jit(solution)/shard_map/gate_up_part/pallas_call | solution.py:280
  57.2 4.6 %down_part.4 = (bf16[256,768]{1,0:T(8,128)(2,1)S(1)}, bf16[256,768]{1,0:T(8,128)(2,1)S(1)}, bf16[4,1024,768]{2,1,0:T(8,128)(2,1)S(1)}) custom-call(s32[1]{0:T(128)} %bitcast.refs_0_, bf16[4,192,1024]{2,1,0:T(8,128)(2,1)S(1)} %get-tuple-element.59.refs_1_.refs_0_, bf16[4,1024,768]{2,1,0:T(8,128)(2,1)S(1)} %get-tuple-element.60.refs_2_, ...), custom_call_target="tpu_custom_call" | custom-call | flops 1207959552 | bytes 6291456 | tf_op jit(solution)/shard_map/down_part/pallas_call | solution.py:343
  61.8 2.7 %copy-done.4 = bf16[4,1024,768]{2,1,0:T(8,128)(2,1)} copy-done((bf16[4,1024,768]{2,1,0:T(8,128)(2,1)}, bf16[4,1024,768]{2,1,0:T(8,128)(2,1)S(1)}, u32[]{:S(2)}) %copy-start.4) | copy-done | bytes 6291480
  64.5 0.4 collective-permute-start.12
  65.0 1.6 %collective-permute-start.21 = (bf16[32,512]{1,0:T(8,128)(2,1)S(1)}, bf16[32,512]{1,0:T(8,128)(2,1)S(1)}, u32[]{:S(2)}, u32[]{:S(2)}) collective-permute-start(bf16[32,512]{1,0:T(8,128)(2,1)S(1)} %get-tuple-element.76), channel_id=1, source_target_pairs={{0,1},{1,2},{2,3},{3,0},{4,5},{5,6},{6,7},{7,4},{8,9},{9,10},{10,1... | collective-permute-start | bytes 98312 | tf_op jit(solution)/shard_map/ppermute | solution.py:437
  66.6 2.6 %collective-permute-start.22 = (bf16[32,512]{1,0:T(8,128)(2,1)S(1)}, bf16[32,512]{1,0:T(8,128)(2,1)S(1)}, u32[]{:S(2)}, u32[]{:S(2)}) collective-permute-start(bf16[32,512]{1,0:T(8,128)(2,1)S(1)} %get-tuple-element.76), channel_id=1, source_target_pairs={{0,2},{1,3},{2,0},{3,1},{4,6},{5,7},{6,4},{7,5},{8,10},{9,11},{10,... | collective-permute-start | bytes 98312 | tf_op jit(solution)/shard_map/ppermute | solution.py:437
  69.2 1.4 %collective-permute-start.23 = (bf16[32,512]{1,0:T(8,128)(2,1)S(1)}, bf16[32,512]{1,0:T(8,128)(2,1)S(1)}, u32[]{:S(2)}, u32[]{:S(2)}) collective-permute-start(bf16[32,512]{1,0:T(8,128)(2,1)S(1)} %get-tuple-element.76), channel_id=1, source_target_pairs={{0,3},{1,0},{2,1},{3,2},{4,7},{5,4},{6,5},{7,6},{8,11},{9,8},{10,9... | collective-permute-start | bytes 98312 | tf_op jit(solution)/shard_map/ppermute | solution.py:437
  70.5 1.1 add_convert_fusion.3
  71.6 2.8 %copy-done.5 = bf16[4,1024,768]{2,1,0:T(8,128)(2,1)S(1)} copy-done((bf16[4,1024,768]{2,1,0:T(8,128)(2,1)S(1)}, bf16[4,1024,768]{2,1,0:T(8,128)(2,1)}, u32[]{:S(2)}) %copy-start.5) | copy-done | bytes 6291480
  74.4 4.6 %down_part.5 = (bf16[256,768]{1,0:T(8,128)(2,1)S(1)}, bf16[256,768]{1,0:T(8,128)(2,1)S(1)}, bf16[4,1024,768]{2,1,0:T(8,128)(2,1)S(1)}) custom-call(s32[1]{0:T(128)} %bitcast.6.refs_0_, bf16[4,192,1024]{2,1,0:T(8,128)(2,1)S(1)} %get-tuple-element.59.refs_1_.refs_0_, bf16[4,1024,768]{2,1,0:T(8,128)(2,1)S(1)} %copy-done.5, bf16[4,1024,3072]{2,1,0:T(8,128)(2,1)} %refs_3_.5, ...), custom_call_target="tpu_custom_call" | custom-call | flops 1207959552 | bytes 6291456 | tf_op jit(solution)/shard_map/down_part/pallas_call | solution.py:343
  79.1 0.6 collective-permute-start.13
  79.7 0.3 collective-permute-start.24
  80.0 1.5 %collective-permute-start.25 = (bf16[32,512]{1,0:T(8,128)(2,1)S(1)}, bf16[32,512]{1,0:T(8,128)(2,1)S(1)}, u32[]{:S(2)}, u32[]{:S(2)}) collective-permute-start(bf16[32,512]{1,0:T(8,128)(2,1)S(1)} %add_convert_fusion.5.refs_0_), channel_id=1, source_target_pairs={{0,8},{4,12},{8,0},{12,4},{1,9},{5,13},{9,1},{13,5},{2,10},{6,14},... | collective-permute-start | bytes 98312 | tf_op jit(solution)/shard_map/ppermute | solution.py:434
  81.5 0.2 collective-permute-start.26
  81.7 5.2 %collective-permute-done.13 = bf16[128,768]{1,0:T(8,128)(2,1)S(1)} collective-permute-done((bf16[128,768]{1,0:T(8,128)(2,1)S(1)}, bf16[128,768]{1,0:T(8,128)(2,1)S(1)}, u32[]{:S(2)}, u32[]{:S(2)}) %collective-permute-start.13) | collective-permute-done | bytes 196640 | tf_op jit(solution)/shard_map/ppermute | solution.py:434
  87.1 0.6 collective-permute-start.16
  87.7 4.6 %down_part.6 = (bf16[256,768]{1,0:T(8,128)(2,1)S(1)}, bf16[256,768]{1,0:T(8,128)(2,1)S(1)}, bf16[4,1024,768]{2,1,0:T(8,128)(2,1)S(1)}) custom-call(s32[1]{0:T(128)} %bitcast.10.refs_0_, bf16[4,192,1024]{2,1,0:T(8,128)(2,1)S(1)} %get-tuple-element.59.refs_1_.refs_0_, bf16[4,1024,768]{2,1,0:T(8,128)(2,1)S(1)} %get-tuple-element.72.refs_2_, ...), custom_call_target="tpu_custom_call" | custom-call | flops 1207959552 | bytes 6291456 | tf_op jit(solution)/shard_map/down_part/pallas_call | solution.py:343
  92.3 2.2 %down_part.7.base_ref = f32[512,768]{1,0:T(8,128)S(1)} custom-call(bf16[4,192,1024]{2,1,0:T(8,128)(2,1)S(1)} %get-tuple-element.59.refs_1_.refs_0_, bf16[4,1024,768]{2,1,0:T(8,128)(2,1)S(1)} %get-tuple-element.75.refs_1_, bf16[2,512,192]{2,1,0:T(8,128)(2,1)S(1)} %get-tuple-element.61.refs_4_.refs_2_, f32[512,128]{1,0:T(8,128)S(1)} %get-tuple-element.62.refs_5_.refs_3_.cols_ref), custom_call_target="tpu_custom_call" | custom-call | flops 1207959552 | bytes 6291456 | tf_op jit(solution)/shard_map/down_part/pallas_call | solution.py:343
  94.5 0.7 collective-permute-start.14
  95.2 2.8 %adapter_part.1 = (bf16[256,768]{1,0:T(8,128)(2,1)S(1)}, bf16[256,768]{1,0:T(8,128)(2,1)S(1)}) custom-call(s32[5]{0:T(128)S(1)} %stack.23.scalar_ref, f32[512,768]{1,0:T(8,128)S(1)} %down_part.7.base_ref, bf16[2048,768]{1,0:T(8,128)(2,1)S(1)} %bitcast.48, f32[512,128]{1,0:T(8,128)S(1)} %get-tuple-element.62.refs_5_.refs_3_.cols_ref, ...), custom_call_target="tpu_custom_call" | custom-call | flops 1610612736 | bytes 3145728 | tf_op jit(solution)/shard_map/adapter_part/pallas_call | solution.py:394
  98.0 0.3 collective-permute-start.27
  98.3 0.4 collective-permute-start.17
  98.8 1.6 %collective-permute-start.19 = (bf16[128,768]{1,0:T(8,128)(2,1)S(1)}, bf16[128,768]{1,0:T(8,128)(2,1)S(1)}, u32[]{:S(2)}, u32[]{:S(2)}) collective-permute-start(bf16[128,768]{1,0:T(8,128)(2,1)S(1)} %slice_bitcast_fusion.2), channel_id=1, source_target_pairs={{0,8},{4,12},{8,0},{12,4},{1,9},{5,13},{9,1},{13,5},{2,10},{6,14},... | collective-permute-start | bytes 589832 | tf_op jit(solution)/shard_map/ppermute | solution.py:434
  100.6 0.9 collective-permute-start.28
  101.5 5.2 %collective-permute-done.19 = bf16[128,768]{1,0:T(8,128)(2,1)S(1)} collective-permute-done((bf16[128,768]{1,0:T(8,128)(2,1)S(1)}, bf16[128,768]{1,0:T(8,128)(2,1)S(1)}, u32[]{:S(2)}, u32[]{:S(2)}) %collective-permute-start.19) | collective-permute-done | bytes 196640 | tf_op jit(solution)/shard_map/ppermute | solution.py:434
  106.7 2.9 %collective-permute-start.20 = (bf16[128,768]{1,0:T(8,128)(2,1)S(1)}, bf16[128,768]{1,0:T(8,128)(2,1)S(1)}, u32[]{:S(2)}, u32[]{:S(2)}) collective-permute-start(bf16[128,768]{1,0:T(8,128)(2,1)S(1)} %fusion.1), channel_id=1, source_target_pairs={{0,3},{1,0},{2,1},{3,2},{4,7},{5,4},{6,5},{7,6},{8,11},{9,8},{10,9... | collective-permute-start | bytes 589832 | tf_op jit(solution)/shard_map/ppermute | solution.py:437
  109.6 2.6 %collective-permute-done.17 = bf16[128,768]{1,0:T(8,128)(2,1)S(1)} collective-permute-done((bf16[128,768]{1,0:T(8,128)(2,1)S(1)}, bf16[128,768]{1,0:T(8,128)(2,1)S(1)}, u32[]{:S(2)}, u32[]{:S(2)}) %collective-permute-start.17) | collective-permute-done | bytes 196640 | tf_op jit(solution)/shard_map/ppermute | solution.py:437
  112.2 4.1 %collective-permute-done.20 = bf16[128,768]{1,0:T(8,128)(2,1)S(1)} collective-permute-done((bf16[128,768]{1,0:T(8,128)(2,1)S(1)}, bf16[128,768]{1,0:T(8,128)(2,1)S(1)}, u32[]{:S(2)}, u32[]{:S(2)}) %collective-permute-start.20) | collective-permute-done | bytes 196640 | tf_op jit(solution)/shard_map/ppermute | solution.py:437
  116.3 0.8 add_convert_fusion.4
  (59 shorter events, 1.1 us)
Async XLA Ops:
  0.0 22.5 %copy-start = (s32[64]{0:T(128)S(1)}, s32[64]{0:T(128)}, u32[]{:S(2)}) copy-start(s32[64]{0:T(128)} %param.16) | copy-start | bytes 772
  1.2 19.1 %collective-permute-start.3 = (bf16[128,1024]{1,0:T(8,128)(2,1)S(1)}, bf16[128,1024]{1,0:T(8,128)(2,1)S(1)}, u32[]{:S(2)}, u32[]{:S(2)}) collective-permute-start(bf16[128,1024]{1,0:T(8,128)(2,1)S(1)} %get-tuple-element.79.refs_0_), channel_id=1, source_target_pairs={{0,8},{4,12},{8,0},{12,4},{1,9},{5,13},{9,1},{13,5},{2,10},{6,14},... | collective-permute-start | bytes 786440 | tf_op jit(solution)/shard_map/ppermute | solution.py:434
  6.4 14.2 %collective-permute-start.5 = (f32[8,128]{1,0:T(8,128)S(1)}, f32[8,128]{1,0:T(8,128)S(1)}, u32[]{:S(2)}, u32[]{:S(2)}) collective-permute-start(f32[8,128]{1,0:T(8,128)S(1)} %maximum_maximum_fusion.refs_0_), channel_id=1, source_target_pairs={{0,4},{4,0},{8,12},{12,8},{1,5},{5,1},{9,13},{13,9},{2,6},{6,2},{1... | collective-permute-start | bytes 12296 | tf_op jit(solution)/shard_map/ppermute | solution.py:434
  6.4 14.3 %collective-permute-start.6 = (f32[8,128]{1,0:T(8,128)S(1)}, f32[8,128]{1,0:T(8,128)S(1)}, u32[]{:S(2)}, u32[]{:S(2)}) collective-permute-start(f32[8,128]{1,0:T(8,128)S(1)} %maximum_maximum_fusion.refs_0_), channel_id=1, source_target_pairs={{0,8},{4,12},{8,0},{12,4},{1,9},{5,13},{9,1},{13,5},{2,10},{6,14},... | collective-permute-start | bytes 12296 | tf_op jit(solution)/shard_map/ppermute | solution.py:434
  6.4 24.0 %collective-permute-start.10 = (bf16[128,1024]{1,0:T(8,128)(2,1)S(1)}, bf16[128,1024]{1,0:T(8,128)(2,1)S(1)}, u32[]{:S(2)}, u32[]{:S(2)}) collective-permute-start(bf16[128,1024]{1,0:T(8,128)(2,1)S(1)} %get-tuple-element.79.refs_0_), channel_id=1, source_target_pairs={{0,4},{4,0},{8,12},{12,8},{1,5},{5,1},{9,13},{13,9},{2,6},{6,2},{1... | collective-permute-start | bytes 786440 | tf_op jit(solution)/shard_map/ppermute | solution.py:434
  6.9 13.7 %copy-start.7 = (s32[16]{0:T(128)S(1)}, s32[16]{0:T(128)}, u32[]{:S(2)}) copy-start(s32[16]{0:T(128)} %param.15) | copy-start | bytes 196
  6.9 22.9 %collective-permute-start.2 = (bf16[128,1024]{1,0:T(8,128)(2,1)S(1)}, bf16[128,1024]{1,0:T(8,128)(2,1)S(1)}, u32[]{:S(2)}, u32[]{:S(2)}) collective-permute-start(bf16[128,1024]{1,0:T(8,128)(2,1)S(1)} %get-tuple-element.81.refs_0_), channel_id=1, source_target_pairs={{0,8},{4,12},{8,0},{12,4},{1,9},{5,13},{9,1},{13,5},{2,10},{6,14},... | collective-permute-start | bytes 786440 | tf_op jit(solution)/shard_map/ppermute | solution.py:434
  14.5 5.8 %copy-start.2 = (bf16[16,1024,512]{2,1,0:T(8,128)(2,1)}, bf16[16,1024,512]{2,1,0:T(8,128)(2,1)S(1)}, u32[]{:S(2)}) copy-start(bf16[16,1024,512]{2,1,0:T(8,128)(2,1)S(1)} %get-tuple-element.50.refs_8_) | copy-start | bytes 50331652
  20.3 9.5 %collective-permute-start.1 = (bf16[128,1024]{1,0:T(8,128)(2,1)S(1)}, bf16[128,1024]{1,0:T(8,128)(2,1)S(1)}, u32[]{:S(2)}, u32[]{:S(2)}) collective-permute-start(bf16[128,1024]{1,0:T(8,128)(2,1)S(1)} %get-tuple-element.80.refs_0_), channel_id=1, source_target_pairs={{0,8},{4,12},{8,0},{12,4},{1,9},{5,13},{9,1},{13,5},{2,10},{6,14},... | collective-permute-start | bytes 786440 | tf_op jit(solution)/shard_map/ppermute | solution.py:434
  20.6 9.8 %collective-permute-start.11 = (bf16[128,1024]{1,0:T(8,128)(2,1)S(1)}, bf16[128,1024]{1,0:T(8,128)(2,1)S(1)}, u32[]{:S(2)}, u32[]{:S(2)}) collective-permute-start(bf16[128,1024]{1,0:T(8,128)(2,1)S(1)} %collective-permute-done.3.refs_2_), channel_id=1, source_target_pairs={{0,4},{4,0},{8,12},{12,8},{1,5},{5,1},{9,13},{13,9},{2,6},{6,2},{1... | collective-permute-start | bytes 786440 | tf_op jit(solution)/shard_map/ppermute | solution.py:434
  20.6 7.0 %collective-permute-start.7 = (f32[8,128]{1,0:T(8,128)S(1)}, f32[8,128]{1,0:T(8,128)S(1)}, u32[]{:S(2)}, u32[]{:S(2)}) collective-permute-start(f32[8,128]{1,0:T(8,128)S(1)} %maximum_maximum_fusion.refs_0_), channel_id=1, source_target_pairs={{0,12},{4,8},{8,4},{12,0},{1,13},{5,9},{9,5},{13,1},{2,14},{6,10},... | collective-permute-start | bytes 12296 | tf_op jit(solution)/shard_map/ppermute | solution.py:434
  27.7 15.1 %collective-permute-start.8 = (bf16[128,1024]{1,0:T(8,128)(2,1)S(1)}, bf16[128,1024]{1,0:T(8,128)(2,1)S(1)}, u32[]{:S(2)}, u32[]{:S(2)}) collective-permute-start(bf16[128,1024]{1,0:T(8,128)(2,1)S(1)} %get-tuple-element.81.refs_0_), channel_id=1, source_target_pairs={{0,4},{4,0},{8,12},{12,8},{1,5},{5,1},{9,13},{13,9},{2,6},{6,2},{1... | collective-permute-start | bytes 786440 | tf_op jit(solution)/shard_map/ppermute | solution.py:434
  29.8 19.6 %collective-permute-start = (bf16[128,1024]{1,0:T(8,128)(2,1)S(1)}, bf16[128,1024]{1,0:T(8,128)(2,1)S(1)}, u32[]{:S(2)}, u32[]{:S(2)}) collective-permute-start(bf16[128,1024]{1,0:T(8,128)(2,1)S(1)} %get-tuple-element.80.refs_0_), channel_id=1, source_target_pairs={{0,4},{4,0},{8,12},{12,8},{1,5},{5,1},{9,13},{13,9},{2,6},{6,2},{1... | collective-permute-start | bytes 786440 | tf_op jit(solution)/shard_map/ppermute | solution.py:434
  29.9 12.9 %collective-permute-start.9 = (bf16[128,1024]{1,0:T(8,128)(2,1)S(1)}, bf16[128,1024]{1,0:T(8,128)(2,1)S(1)}, u32[]{:S(2)}, u32[]{:S(2)}) collective-permute-start(bf16[128,1024]{1,0:T(8,128)(2,1)S(1)} %collective-permute-done.2.refs_2_), channel_id=1, source_target_pairs={{0,4},{4,0},{8,12},{12,8},{1,5},{5,1},{9,13},{13,9},{2,6},{6,2},{1... | collective-permute-start | bytes 786440 | tf_op jit(solution)/shard_map/ppermute | solution.py:434
  30.3 19.0 %collective-permute-start.4 = (bf16[128,1024]{1,0:T(8,128)(2,1)S(1)}, bf16[128,1024]{1,0:T(8,128)(2,1)S(1)}, u32[]{:S(2)}, u32[]{:S(2)}) collective-permute-start(bf16[128,1024]{1,0:T(8,128)(2,1)S(1)} %collective-permute-done.1.refs_2_), channel_id=1, source_target_pairs={{0,4},{4,0},{8,12},{12,8},{1,5},{5,1},{9,13},{13,9},{2,6},{6,2},{1... | collective-permute-start | bytes 786440 | tf_op jit(solution)/shard_map/ppermute | solution.py:434
  30.4 5.8 %copy-start.3 = (bf16[16,1024,512]{2,1,0:T(8,128)(2,1)S(1)}, bf16[16,1024,512]{2,1,0:T(8,128)(2,1)}, u32[]{:S(2)}) copy-start(bf16[16,1024,512]{2,1,0:T(8,128)(2,1)} %copy-done.2) | copy-start | bytes 50331652
  61.8 2.7 %copy-start.4 = (bf16[4,1024,768]{2,1,0:T(8,128)(2,1)}, bf16[4,1024,768]{2,1,0:T(8,128)(2,1)S(1)}, u32[]{:S(2)}) copy-start(bf16[4,1024,768]{2,1,0:T(8,128)(2,1)S(1)} %get-tuple-element.67.refs_2_) | copy-start | bytes 18874372
  64.5 6.0 %collective-permute-start.12 = (bf16[256,768]{1,0:T(8,128)(2,1)S(1)}, bf16[256,768]{1,0:T(8,128)(2,1)}, u32[]{:S(2)}, u32[]{:S(2)}) collective-permute-start(bf16[256,768]{1,0:T(8,128)(2,1)S(1)} %get-tuple-element.64), channel_id=1, source_target_pairs={{0,4},{4,0},{8,12},{12,8},{1,5},{5,1},{9,13},{13,9},{2,6},{6,2},{1... | collective-permute-start | bytes 1179656 | tf_op jit(solution)/shard_map/ppermute | solution.py:434
  65.0 14.7 %collective-permute-start.21 = (bf16[32,512]{1,0:T(8,128)(2,1)S(1)}, bf16[32,512]{1,0:T(8,128)(2,1)S(1)}, u32[]{:S(2)}, u32[]{:S(2)}) collective-permute-start(bf16[32,512]{1,0:T(8,128)(2,1)S(1)} %get-tuple-element.76), channel_id=1, source_target_pairs={{0,1},{1,2},{2,3},{3,0},{4,5},{5,6},{6,7},{7,4},{8,9},{9,10},{10,1... | collective-permute-start | bytes 98312 | tf_op jit(solution)/shard_map/ppermute | solution.py:437
  66.6 13.1 %collective-permute-start.22 = (bf16[32,512]{1,0:T(8,128)(2,1)S(1)}, bf16[32,512]{1,0:T(8,128)(2,1)S(1)}, u32[]{:S(2)}, u32[]{:S(2)}) collective-permute-start(bf16[32,512]{1,0:T(8,128)(2,1)S(1)} %get-tuple-element.76), channel_id=1, source_target_pairs={{0,2},{1,3},{2,0},{3,1},{4,6},{5,7},{6,4},{7,5},{8,10},{9,11},{10,... | collective-permute-start | bytes 98312 | tf_op jit(solution)/shard_map/ppermute | solution.py:437
  69.2 10.5 %collective-permute-start.23 = (bf16[32,512]{1,0:T(8,128)(2,1)S(1)}, bf16[32,512]{1,0:T(8,128)(2,1)S(1)}, u32[]{:S(2)}, u32[]{:S(2)}) collective-permute-start(bf16[32,512]{1,0:T(8,128)(2,1)S(1)} %get-tuple-element.76), channel_id=1, source_target_pairs={{0,3},{1,0},{2,1},{3,2},{4,7},{5,4},{6,5},{7,6},{8,11},{9,8},{10,9... | collective-permute-start | bytes 98312 | tf_op jit(solution)/shard_map/ppermute | solution.py:437
  71.6 2.8 %copy-start.5 = (bf16[4,1024,768]{2,1,0:T(8,128)(2,1)S(1)}, bf16[4,1024,768]{2,1,0:T(8,128)(2,1)}, u32[]{:S(2)}) copy-start(bf16[4,1024,768]{2,1,0:T(8,128)(2,1)} %copy-done.4) | copy-start | bytes 18874372
  79.0 7.9 %collective-permute-start.15 = (bf16[256,768]{1,0:T(8,128)(2,1)S(1)}, bf16[256,768]{1,0:T(8,128)(2,1)S(1)}, u32[]{:S(2)}, u32[]{:S(2)}) collective-permute-start(bf16[256,768]{1,0:T(8,128)(2,1)S(1)} %get-tuple-element.69), channel_id=1, source_target_pairs={{0,4},{4,0},{8,12},{12,8},{1,5},{5,1},{9,13},{13,9},{2,6},{6,2},{1... | collective-permute-start | bytes 1179656 | tf_op jit(solution)/shard_map/ppermute | solution.py:434
  79.1 7.8 %collective-permute-start.13 = (bf16[128,768]{1,0:T(8,128)(2,1)S(1)}, bf16[128,768]{1,0:T(8,128)(2,1)S(1)}, u32[]{:S(2)}, u32[]{:S(2)}) collective-permute-start(bf16[128,768]{1,0:T(8,128)(2,1)S(1)} %slice_bitcast_fusion.6), channel_id=1, source_target_pairs={{0,8},{4,12},{8,0},{12,4},{1,9},{5,13},{9,1},{13,5},{2,10},{6,14},... | collective-permute-start | bytes 589832 | tf_op jit(solution)/shard_map/ppermute | solution.py:434
  79.7 14.8 %collective-permute-start.24 = (bf16[32,512]{1,0:T(8,128)(2,1)S(1)}, bf16[32,512]{1,0:T(8,128)(2,1)S(1)}, u32[]{:S(2)}, u32[]{:S(2)}) collective-permute-start(bf16[32,512]{1,0:T(8,128)(2,1)S(1)} %add_convert_fusion.5.refs_0_), channel_id=1, source_target_pairs={{0,4},{4,0},{8,12},{12,8},{1,5},{5,1},{9,13},{13,9},{2,6},{6,2},{1... | collective-permute-start | bytes 98312 | tf_op jit(solution)/shard_map/ppermute | solution.py:434
  80.0 15.2 %collective-permute-start.25 = (bf16[32,512]{1,0:T(8,128)(2,1)S(1)}, bf16[32,512]{1,0:T(8,128)(2,1)S(1)}, u32[]{:S(2)}, u32[]{:S(2)}) collective-permute-start(bf16[32,512]{1,0:T(8,128)(2,1)S(1)} %add_convert_fusion.5.refs_0_), channel_id=1, source_target_pairs={{0,8},{4,12},{8,0},{12,4},{1,9},{5,13},{9,1},{13,5},{2,10},{6,14},... | collective-permute-start | bytes 98312 | tf_op jit(solution)/shard_map/ppermute | solution.py:434
  81.5 13.7 %collective-permute-start.26 = (bf16[32,512]{1,0:T(8,128)(2,1)S(1)}, bf16[32,512]{1,0:T(8,128)(2,1)S(1)}, u32[]{:S(2)}, u32[]{:S(2)}) collective-permute-start(bf16[32,512]{1,0:T(8,128)(2,1)S(1)} %add_convert_fusion.5.refs_0_), channel_id=1, source_target_pairs={{0,12},{4,8},{8,4},{12,0},{1,13},{5,9},{9,5},{13,1},{2,14},{6,10},... | collective-permute-start | bytes 98312 | tf_op jit(solution)/shard_map/ppermute | solution.py:434
  87.1 11.2 %collective-permute-start.16 = (bf16[128,768]{1,0:T(8,128)(2,1)S(1)}, bf16[128,768]{1,0:T(8,128)(2,1)S(1)}, u32[]{:S(2)}, u32[]{:S(2)}) collective-permute-start(bf16[128,768]{1,0:T(8,128)(2,1)S(1)} %slice_bitcast_fusion.4), channel_id=1, source_target_pairs={{0,8},{4,12},{8,0},{12,4},{1,9},{5,13},{9,1},{13,5},{2,10},{6,14},... | collective-permute-start | bytes 589832 | tf_op jit(solution)/shard_map/ppermute | solution.py:434
  92.2 3.0 %copy-start.6 = (bf16[16,8,16,768]{3,2,1,0:T(8,128)(2,1)S(1)}, bf16[16,8,16,768]{3,2,1,0:T(8,128)(2,1)}, u32[]{:S(2)}) copy-start(bf16[16,8,16,768]{3,2,1,0:T(8,128)(2,1)} %param.21) | copy-start | bytes 9437188
  92.2 6.5 %collective-permute-start.18 = (bf16[256,768]{1,0:T(8,128)(2,1)S(1)}, bf16[256,768]{1,0:T(8,128)(2,1)S(1)}, u32[]{:S(2)}, u32[]{:S(2)}) collective-permute-start(bf16[256,768]{1,0:T(8,128)(2,1)S(1)} %get-tuple-element.74), channel_id=1, source_target_pairs={{0,4},{4,0},{8,12},{12,8},{1,5},{5,1},{9,13},{13,9},{2,6},{6,2},{1... | collective-permute-start | bytes 1179656 | tf_op jit(solution)/shard_map/ppermute | solution.py:434
  92.3 24.8 %copy-start.1 = (s32[64]{0:T(128)S(1)}, s32[64]{0:T(128)}, u32[]{:S(2)}) copy-start(s32[64]{0:T(128)} %param.16) | copy-start | bytes 772
  94.5 15.1 %collective-permute-start.14 = (bf16[128,768]{1,0:T(8,128)(2,1)S(1)}, bf16[128,768]{1,0:T(8,128)(2,1)S(1)}, u32[]{:S(2)}, u32[]{:S(2)}) collective-permute-start(bf16[128,768]{1,0:T(8,128)(2,1)S(1)} %fusion.3), channel_id=1, source_target_pairs={{0,1},{1,2},{2,3},{3,0},{4,5},{5,6},{6,7},{7,4},{8,9},{9,10},{10,1... | collective-permute-start | bytes 589832 | tf_op jit(solution)/shard_map/ppermute | solution.py:437
  98.0 2.4 %collective-permute-start.27 = (bf16[256,768]{1,0:T(8,128)(2,1)S(1)}, bf16[256,768]{1,0:T(8,128)(2,1)S(1)}, u32[]{:S(2)}, u32[]{:S(2)}) collective-permute-start(bf16[256,768]{1,0:T(8,128)(2,1)S(1)} %get-tuple-element.78), channel_id=1, source_target_pairs={{0,4},{4,0},{8,12},{12,8},{1,5},{5,1},{9,13},{13,9},{2,6},{6,2},{1... | collective-permute-start | bytes 1179656 | tf_op jit(solution)/shard_map/ppermute | solution.py:434
  98.3 13.8 %collective-permute-start.17 = (bf16[128,768]{1,0:T(8,128)(2,1)S(1)}, bf16[128,768]{1,0:T(8,128)(2,1)S(1)}, u32[]{:S(2)}, u32[]{:S(2)}) collective-permute-start(bf16[128,768]{1,0:T(8,128)(2,1)S(1)} %fusion.2), channel_id=1, source_target_pairs={{0,2},{1,3},{2,0},{3,1},{4,6},{5,7},{6,4},{7,5},{8,10},{9,11},{10,... | collective-permute-start | bytes 589832 | tf_op jit(solution)/shard_map/ppermute | solution.py:437
  98.8 7.8 %collective-permute-start.19 = (bf16[128,768]{1,0:T(8,128)(2,1)S(1)}, bf16[128,768]{1,0:T(8,128)(2,1)S(1)}, u32[]{:S(2)}, u32[]{:S(2)}) collective-permute-start(bf16[128,768]{1,0:T(8,128)(2,1)S(1)} %slice_bitcast_fusion.2), channel_id=1, source_target_pairs={{0,8},{4,12},{8,0},{12,4},{1,9},{5,13},{9,1},{13,5},{2,10},{6,14},... | collective-permute-start | bytes 589832 | tf_op jit(solution)/shard_map/ppermute | solution.py:434
  100.6 11.6 %collective-permute-start.28 = (bf16[128,768]{1,0:T(8,128)(2,1)S(1)}, bf16[128,768]{1,0:T(8,128)(2,1)S(1)}, u32[]{:S(2)}, u32[]{:S(2)}) collective-permute-start(bf16[128,768]{1,0:T(8,128)(2,1)S(1)} %slice_bitcast_fusion), channel_id=1, source_target_pairs={{0,8},{4,12},{8,0},{12,4},{1,9},{5,13},{9,1},{13,5},{2,10},{6,14},... | collective-permute-start | bytes 589832 | tf_op jit(solution)/shard_map/ppermute | solution.py:434
  106.7 9.6 %collective-permute-start.20 = (bf16[128,768]{1,0:T(8,128)(2,1)S(1)}, bf16[128,768]{1,0:T(8,128)(2,1)S(1)}, u32[]{:S(2)}, u32[]{:S(2)}) collective-permute-start(bf16[128,768]{1,0:T(8,128)(2,1)S(1)} %fusion.1), channel_id=1, source_target_pairs={{0,3},{1,0},{2,1},{3,2},{4,7},{5,4},{6,5},{7,6},{8,11},{9,8},{10,9... | collective-permute-start | bytes 589832 | tf_op jit(solution)/shard_map/ppermute | solution.py:437

commit v3 on v2

v3 whole, which is shorter than its diff:
```python
import functools

import jax
import jax.numpy as jnp
from jax import lax
from jax.experimental import pallas as pl
from jax.experimental.pallas import tpu as pltpu
from jax.sharding import PartitionSpec as P

EXPERT_COUNT = 8
TOP = 2
RANK = 16
CAP = 48
PIECES = 4
LIMIT = 16
LIMIT_EARLY = 8
N_TILE = 512
MIB = 1 << 20

F32 = jnp.float32
BF16 = jnp.bfloat16


def mm(a, b):
    return jnp.dot(a, b, preferred_element_type=F32)


def mm_nt(a, b):
    return lax.dot_general(a, b, (((1,), (1,)), ((), ())), preferred_element_type=F32)


def cost(flops, moved, trans=0):
    return pl.CostEstimate(flops=int(flops), bytes_accessed=int(moved), transcendentals=int(trans))


def params(mib):
    return pltpu.CompilerParams(vmem_limit_bytes=mib * MIB)


def vmem():
    return pl.BlockSpec(memory_space=pltpu.VMEM)


def smem():
    return pl.BlockSpec(memory_space=pltpu.SMEM)


def fact_columns(chosen_experts, logits, tenant):
    pieces, rest = [], logits
    for _ in range(3):
        piece = lax.reduce_precision(rest, 8, 7)
        pieces.append(piece)
        rest = rest - piece
    facts = jnp.concatenate([chosen_experts.astype(F32), tenant.astype(F32)[:, None]] + pieces, axis=1)
    return jnp.pad(facts, ((0, 0), (0, 128 - facts.shape[1]))).astype(BF16)


def meta_kernel(n_local, local_halves, ids_ref, adapter_ref, pool_slot_ref, *refs):
    blocks, (p_ref, pt_ref, cols_ref, rows_ref, tslot_ref) = refs[:-5], refs[-5:]
    at = blocks[0].shape[1] - 128
    facts = jnp.concatenate([block[:, at:] for block in blocks], axis=0).astype(F32).T
    count = facts.shape[1]
    first, second, tenant = facts[0:1], facts[1:2], facts[2:3]
    logit_first = (facts[3:4] + facts[5:6]) + facts[7:8]
    logit_second = (facts[4:5] + facts[6:7]) + facts[8:9]
    weight_first = jax.nn.sigmoid(logit_first - logit_second)
    weight_second = jax.nn.sigmoid(logit_second - logit_first)
    slot = jnp.zeros_like(tenant)
    for number in range(adapter_ref.shape[0]):
        slot = jnp.where(tenant == number, pool_slot_ref[adapter_ref[number]].astype(F32), slot)
    members, weights = [], []
    for i in range(n_local):
        expert = (ids_ref[0] * local_halves // 2 + i).astype(F32)
        hit_first, hit_second = first == expert, second == expert
        members.append(jnp.where(hit_first | hit_second, 1.0, 0.0))
        weights.append(jnp.where(hit_first, weight_first, 0.0) + jnp.where(hit_second, weight_second, 0.0))
    member = jnp.concatenate(members + [jnp.zeros((8 - n_local, count), F32)], axis=0)
    before = (
        lax.broadcasted_iota(jnp.int32, (count, count), 0) < lax.broadcasted_iota(jnp.int32, (count, count), 1)
    ).astype(BF16)
    place = jnp.where(member > 0, mm(member.astype(BF16), before), -1.0)
    table = jnp.concatenate(
        [place[0:n_local]] + weights + [slot] + [jnp.zeros((127 - 2 * n_local, count), F32)], axis=0
    )
    columns = table.T
    cols_ref[...] = columns
    rows_ref[...] = table[0:8]
    row_count = p_ref.shape[1]
    tenant_rows = jnp.broadcast_to(tenant, (8, count)).astype(BF16)
    down = lax.broadcasted_iota(jnp.int32, (row_count, count), 0).astype(F32)
    across = lax.broadcasted_iota(jnp.int32, (count, row_count), 1).astype(F32)
    for i in range(n_local):
        picked = (down == place[i : i + 1]).astype(BF16)
        p_ref[i] = picked
        pt_ref[i] = (across == columns[:, i : i + 1]).astype(BF16)
        tslot_ref[i] = mm_nt(tenant_rows, picked)


def build_meta(blocks, ids, adapters, pool_slots, n_local, local_halves, row_count):
    count = sum(block.shape[0] for block in blocks)
    return pl.pallas_call(
        functools.partial(meta_kernel, n_local, local_halves),
        out_shape=(
            jax.ShapeDtypeStruct((n_local, row_count, count), BF16),
            jax.ShapeDtypeStruct((n_local, count, row_count), BF16),
            jax.ShapeDtypeStruct((count, 128), F32),
            jax.ShapeDtypeStruct((8, count), F32),
            jax.ShapeDtypeStruct((n_local, 8, row_count), F32),
        ),
        in_specs=[smem()] * 3 + [vmem()] * len(blocks),
        out_specs=(vmem(),) * 5,
        compiler_params=params(max(LIMIT_EARLY, 12 * count * count // MIB)),
        cost_estimate=cost(2 * 8 * count * count, 4 * n_local * row_count * count),
        name="routing_tables",
    )(ids, adapters, pool_slots, *blocks)


def slab_copies(gate_ref, up_ref, into_ref, sems, part, half):
    depth, width = into_ref.shape[1], into_ref.shape[2]
    copies = []
    for number in range(into_ref.shape[0]):
        source = (gate_ref, up_ref)[number % 2].at[half, pl.ds(part * depth, depth), pl.ds(number // 2 * width, width)]
        copies.append(pltpu.make_async_copy(source, into_ref.at[number], sems.at[half, number]))
    return copies


def prefetch_kernel(ids_ref, gate_ref, up_ref, *refs):
    slabs, mark_ref, sems = refs[:-2], refs[-2], refs[-1]
    copies = [copy for half, slab in enumerate(slabs) for copy in slab_copies(gate_ref, up_ref, slab, sems, 0, half)]
    for copy in copies:
        copy.start()
    mark_ref[...] = jnp.zeros_like(mark_ref)
    for copy in copies:
        copy.wait()


def prefetch(ids, gate, up, part_width):
    local_halves, _, hidden_count = gate.shape
    tile = min(N_TILE, hidden_count)
    each = 2 * hidden_count // tile
    return pl.pallas_call(
        prefetch_kernel,
        out_shape=(pltpu.VMEM((each, part_width, tile), BF16),) * local_halves + (jax.ShapeDtypeStruct((8, 128), F32),),
        in_specs=[smem()] + [pl.BlockSpec(memory_space=pltpu.HBM)] * 2,
        out_specs=(vmem(),) * (local_halves + 1),
        scratch_shapes=[pltpu.SemaphoreType.DMA((local_halves, each))],
        compiler_params=params(LIMIT_EARLY),
        cost_estimate=cost(0, 4 * local_halves * part_width * hidden_count * 2),
        name="weight_prefetch",
    )(ids, gate, up)


def pack(blocks, p_ref, packed):
    depth = packed.shape[2]
    whole = jnp.concatenate([block[:, :depth] for block in blocks], axis=0)
    for i in range(p_ref.shape[0]):
        packed[i] = mm(p_ref[i], whole).astype(BF16)


def first_kernel(n_blocks, local_halves, *refs):
    blocks, refs = refs[:n_blocks], refs[n_blocks:]
    _, p_ref, gate_ref, up_ref, refs = refs[0], refs[1], refs[2], refs[3], refs[4:]
    slabs, refs = refs[:local_halves], refs[local_halves:]
    ahead, (gate_out, up_out, packed, sems) = refs[:-4], refs[-4:]
    pack(blocks, p_ref, packed)
    slabs = list(ahead) + list(slabs[len(ahead) :])
    copies = [slab_copies(gate_ref, up_ref, slab, sems, 1, half) for half, slab in enumerate(ahead)]
    halves_each = local_halves // p_ref.shape[0]
    for half in range(local_halves):
        rows = packed[half // halves_each]
        tiles, _, width = slabs[half].shape
        for tile in range(tiles // 2):
            span = slice(tile * width, (tile + 1) * width)
            gate_out[half, :, span] = mm(rows, slabs[half][2 * tile])
            up_out[half, :, span] = mm(rows, slabs[half][2 * tile + 1])
            if half < len(ahead):
                copies[half][2 * tile].start()
                copies[half][2 * tile + 1].start()
    for copy in [copy for half in copies for copy in half]:
        copy.wait()


def first_part(blocks, mark, picked, gate, up, slabs):
    local_halves, _, hidden_count = gate.shape
    n_local, row_count, _ = picked.shape
    each, part_width, _ = slabs[0].shape
    hbm = pl.BlockSpec(memory_space=pltpu.HBM)
    sums = pltpu.VMEM((local_halves, row_count, hidden_count), F32)
    n_ahead = max(1, local_halves // 2)
    return pl.pallas_call(
        functools.partial(first_kernel, len(blocks), local_halves),
        out_shape=(pltpu.VMEM(slabs[0].shape, BF16),) * n_ahead + (sums, sums),
        in_specs=[vmem()] * (len(blocks) + 2) + [hbm, hbm] + [vmem()] * local_halves,
        out_specs=(vmem(),) * (n_ahead + 2),
        scratch_shapes=[
            pltpu.VMEM((n_local, row_count, part_width), BF16),
            pltpu.SemaphoreType.DMA((n_ahead, each)),
        ],
        input_output_aliases={len(blocks) + 4 + half: half for half in range(n_ahead)},
        compiler_params=params(max(LIMIT_EARLY, 10 * n_local * row_count * part_width // MIB)),
        cost_estimate=cost(
            4 * local_halves * row_count * part_width * hidden_count, 2 * local_halves * part_width * hidden_count
        ),
        name="gate_up_first",
    )(*blocks, mark, picked, gate, up, *[pltpu.with_memory_space_constraint(x, pltpu.VMEM) for x in slabs])


def second_kernel(n_blocks, n_ahead, n_ad, *refs):
    blocks, refs = refs[:n_blocks], refs[n_blocks:]
    p_ref, gate_ref, up_ref, refs = refs[0], refs[1], refs[2], refs[3:]
    ahead, gate_in, up_in, refs = refs[:n_ahead], refs[n_ahead], refs[n_ahead + 1], refs[n_ahead + 2 :]
    ids_ref, adapter_ref, pool_slot_ref, pool_ref, tslot_ref, rows_ref, down_ref, refs = *refs[:7], refs[7:]
    hidden_ref, low_ref, next_ref, packed, factors, factor_sems, down_sems, refs = *refs[:7], refs[7:]
    late, sems = refs
    n_local = p_ref.shape[0]
    local_halves, _, hidden_count = gate_ref.shape
    halves_each = local_halves // n_local
    slabs = list(ahead) + [late] * (local_halves - n_ahead)
    copies = {
        half: slab_copies(gate_ref, up_ref, slabs[half], sems, 1, half) for half in range(n_ahead, local_halves)
    }
    tenants, rank = adapter_ref.shape[0], pool_ref.shape[2]
    factor_copies = [
        pltpu.make_async_copy(
            pool_ref.at[pool_slot_ref[adapter_ref[number]]],
            factors.at[:, number * rank : (number + 1) * rank],
            factor_sems.at[number],
        )
        for number in range(tenants)
    ]
    down_copies = down_fetch(n_ad, 1, ids_ref, down_ref, next_ref, down_sems)
    for copy in copies.get(n_ahead, []) + factor_copies + down_copies:
        copy.start()
    pack(blocks, p_ref, packed)
    for half in range(local_halves):
        rows = packed[half // halves_each]
        tiles, _, width = slabs[half].shape
        for tile in range(tiles // 2):
            span = slice(tile * width, (tile + 1) * width)
            values = []
            for number in (2 * tile, 2 * tile + 1):
                if half in copies:
                    copies[half][number].wait()
                values.append(mm(rows, slabs[half][number]))
                if half in copies and half + 1 in copies:
                    copies[half + 1][number].start()
            gate = values[0] + gate_in[half, :, span]
            up = values[1] + up_in[half, :, span]
            hidden_ref[half, :, span] = (jax.nn.silu(gate) * up).astype(BF16)
    for copy in factor_copies:
        copy.wait()
    for i in range(n_local):
        low = mm_nt(factors[i * halves_each], hidden_ref[i * halves_each])
        for half in range(i * halves_each + 1, (i + 1) * halves_each):
            low = low + mm_nt(factors[half], hidden_ref[half])
        owner = tslot_ref[i][0:1]
        total = jnp.zeros((rank, low.shape[1]), F32)
        for number in range(tenants):
            total = total + jnp.where(owner == number, low[number * rank : (number + 1) * rank], 0.0)
        weight = rows_ref[n_local + i : n_local + i + 1]
        low_ref[i * rank : (i + 1) * rank] = (mm(total.astype(BF16), p_ref[i]) * weight).astype(BF16)
    for copy in down_copies:
        copy.wait()


def second_part(blocks, picked, gate, up, ahead, sums, ids, adapters, pool_slots, pool, tslot, table_rows, down, n_ad):
    local_halves, _, hidden_count = gate.shape
    n_local, row_count, count = picked.shape
    each, part_width, tile = ahead[0].shape
    tenants, rank = adapters.shape[0], pool.shape[2]
    span = down.shape[2] // n_ad
    hbm = pl.BlockSpec(memory_space=pltpu.HBM)
    held = [pltpu.with_memory_space_constraint(x, pltpu.VMEM) for x in (*ahead, *sums)]
    late_bytes = 2 * each * part_width * tile
    return pl.pallas_call(
        functools.partial(second_kernel, len(blocks), len(ahead), n_ad),
        out_shape=(
            pltpu.VMEM((local_halves, row_count, hidden_count), BF16),
            jax.ShapeDtypeStruct((n_local * rank, count), BF16),
            pltpu.VMEM((local_halves, hidden_count, span), BF16),
        ),
        in_specs=[vmem()] * (len(blocks) + 1) + [hbm, hbm] + [vmem()] * len(held) + [smem()] * 3 + [hbm, vmem(), vmem(), hbm],
        out_specs=(vmem(),) * 3,
        scratch_shapes=[
            pltpu.VMEM((n_local, row_count, part_width), BF16),
            pltpu.VMEM((local_halves, tenants * rank, hidden_count), BF16),
            pltpu.SemaphoreType.DMA((tenants,)),
            pltpu.SemaphoreType.DMA((local_halves * PIECES,)),
            pltpu.VMEM((each, part_width, tile), BF16),
            pltpu.SemaphoreType.DMA((local_halves, each)),
        ],
        compiler_params=params(
            max(LIMIT_EARLY, 10 * n_local * row_count * part_width // MIB) + late_bytes // MIB + 1
        ),
        cost_estimate=cost(
            4 * local_halves * row_count * part_width * hidden_count, 4 * local_halves * part_width * hidden_count
        ),
        name="gate_up_second",
    )(*blocks, picked, gate, up, *held, ids, adapters, pool_slots, pool, tslot, table_rows, down)


def down_fetch(n_ad, step, ids_ref, down_ref, next_ref, sems):
    span = next_ref.shape[2]
    rows = next_ref.shape[1] // PIECES
    start = pl.multiple_of(lax.rem(ids_ref[1] + step, n_ad) * span, span)
    return [
        pltpu.make_async_copy(
            down_ref.at[half, pl.ds(piece * rows, rows), pl.ds(start, span)],
            next_ref.at[half, pl.ds(piece * rows, rows)],
            sems.at[half * PIECES + piece],
        )
        for half in range(down_ref.shape[0])
        for piece in range(PIECES)
    ]


def weighted_down(hidden_ref, weight_ref, pt_ref, cols_ref):
    n_local = pt_ref.shape[0]
    halves_each = hidden_ref.shape[0] // n_local
    total = None
    for i in range(n_local):
        part_sum = mm(hidden_ref[i * halves_each], weight_ref[i * halves_each])
        for half in range(i * halves_each + 1, (i + 1) * halves_each):
            part_sum = part_sum + mm(hidden_ref[half], weight_ref[half])
        laid = mm(pt_ref[i], part_sum.astype(BF16)) * cols_ref[:, n_local + i : n_local + i + 1]
        total = laid if total is None else total + laid
    return total


def down_kernel(n_ad, step, ids_ref, hidden_ref, weight_ref, down_ref, pt_ref, cols_ref, keep, send, next_ref, sems):
    copies = down_fetch(n_ad, step + 1, ids_ref, down_ref, next_ref, sems)
    for copy in copies:
        copy.start()
    write_pairs(weighted_down(hidden_ref, weight_ref, pt_ref, cols_ref), (keep, send))
    for copy in copies:
        copy.wait()


def down_part(n_ad, step, ids, hidden, weights, down, pt, cols):
    local_halves, row_count, hidden_count = hidden.shape
    count, span = pt.shape[1], weights.shape[2]
    weights = pltpu.with_memory_space_constraint(weights, pltpu.VMEM)
    return pl.pallas_call(
        functools.partial(down_kernel, n_ad, step),
        out_shape=(jax.ShapeDtypeStruct((count // 2, span), BF16),) * 2 + (pltpu.VMEM(weights.shape, BF16),),
        in_specs=[smem(), vmem(), vmem(), pl.BlockSpec(memory_space=pltpu.HBM), vmem(), vmem()],
        out_specs=(vmem(),) * 3,
        scratch_shapes=[pltpu.SemaphoreType.DMA((local_halves * PIECES,))],
        compiler_params=params(max(LIMIT, 12 * count * span // MIB)),
        cost_estimate=cost(
            2 * local_halves * row_count * hidden_count * span, 2 * local_halves * hidden_count * span
        ),
        name="down_part",
    )(ids, hidden, weights, down, pt, cols)


def write_pairs(total, outs):
    keep, send = outs
    for b in range(total.shape[0] // 128):
        (send if b % 2 else keep)[b // 2 * 128 : b // 2 * 128 + 128] = total[b * 128 : b * 128 + 128].astype(BF16)


def final_kernel(local_halves, slot_column, ids_ref, hidden_ref, weight_ref, pt_ref, cols_ref, factor_ref, low_ref, *refs):
    keep, send, wide = refs
    count = pt_ref.shape[1]
    blocks = count // 128
    height = low_ref.shape[0] // blocks
    wide[...] = jnp.zeros_like(wide)
    for m in range(blocks):
        start = pl.multiple_of(((ids_ref[0] ^ m) * local_halves // 2) * RANK, RANK)
        value = low_ref[m * height : (m + 1) * height].astype(F32)
        value = jnp.concatenate([value[:, (m ^ b) * 128 : (m ^ b) * 128 + 128] for b in range(blocks)], axis=1)
        wide[pl.ds(start, height)] += value
    low = wide[...].T.astype(BF16)
    zero = jnp.zeros_like(low)
    slot = cols_ref[:, slot_column : slot_column + 1]
    depth = EXPERT_COUNT * RANK
    slot_count = factor_ref.shape[0] // depth
    total = weighted_down(hidden_ref, weight_ref, pt_ref, cols_ref)
    for j in range(0, slot_count, 2):
        spread = jnp.concatenate(
            [jnp.where(slot == (ids_ref[0] * slot_count + j + i).astype(F32), low, zero) for i in range(2)], axis=1
        )
        total = total + mm(spread, factor_ref[j * depth : (j + 2) * depth])
    write_pairs(total, (keep, send))


def final_part(ids, hidden, weights, pt, cols, slot_column, factors, lows):
    local_halves, row_count, hidden_count = hidden.shape
    count, span = pt.shape[1], weights.shape[2]
    weights = pltpu.with_memory_space_constraint(weights, pltpu.VMEM)
    return pl.pallas_call(
        functools.partial(final_kernel, local_halves, slot_column),
        out_shape=(jax.ShapeDtypeStruct((count // 2, span), BF16),) * 2,
        in_specs=[smem()] + [vmem()] * 6,
        out_specs=(vmem(),) * 2,
        scratch_shapes=[pltpu.VMEM((EXPERT_COUNT * RANK, count), F32)],
        compiler_params=params(max(LIMIT, 24 * count * span // MIB)),
        cost_estimate=cost(
            2 * (count * factors.shape[0] + local_halves * row_count * hidden_count) * span,
            2 * (factors.shape[0] + local_halves * hidden_count) * span,
        ),
        name="down_and_adapters",
    )(ids, hidden, weights, pt, cols, factors, lows)


def per_device(
    n_ep,
    n_ad,
    tokens,
    chosen_experts,
    router_gate_logits,
    token_tenant,
    adapter_of_tenant,
    adapter_pool_slot,
    gate_weight,
    up_weight,
    down_weight,
    adapter_input_factors,
    adapter_output_factors,
):
    gate_weight, up_weight, down_weight, adapter_input_factors = [
        pltpu.with_memory_space_constraint(x, pltpu.HBM)
        for x in (gate_weight, up_weight, down_weight, adapter_input_factors)
    ]
    width = tokens.shape[1]
    span = width // n_ad
    local_halves = gate_weight.shape[0]
    n_local = max(1, local_halves // 2)
    row_count = n_ep * CAP
    bits = n_ep.bit_length() - 1
    ids = jnp.stack([lax.axis_index("ep"), lax.axis_index("ad")]).astype(jnp.int32)

    def swap(x, mask):
        return lax.ppermute(x, "ep", [(i, i ^ mask) for i in range(n_ep)])

    def shift(x, step):
        return lax.ppermute(x, "ad", [(i, (i + step) % n_ad) for i in range(n_ad)])

    parts = 2
    part_width = width // parts
    *slabs, mark = prefetch(ids, gate_weight, up_weight, part_width)
    facts = fact_columns(chosen_experts, router_gate_logits, token_tenant)
    token_parts = []
    for part in range(parts):
        own = tokens[:, part * part_width : (part + 1) * part_width]
        blocks = {0: jnp.concatenate([own, facts], axis=1) if part == 0 else own}
        for bit in reversed(range(bits)):
            for mask in list(blocks):
                blocks[mask | 1 << bit] = swap(blocks[mask], 1 << bit)
            if bit == bits - 1:
                high = 1 << bit
                blocks[high], mark = lax.optimization_barrier((blocks[high], mark))
        token_parts.append([blocks[mask] for mask in range(n_ep)])

    picked, pt, cols, table_rows, tslot = build_meta(
        token_parts[0], ids, adapter_of_tenant, adapter_pool_slot, n_local, local_halves, row_count
    )
    *ahead, gate_sum, up_sum = first_part(token_parts[0], mark, picked, gate_weight, up_weight, slabs)
    hidden, low, weights = second_part(
        token_parts[1], picked, gate_weight, up_weight, ahead, (gate_sum, up_sum), ids, adapter_of_tenant, adapter_pool_slot,
        adapter_input_factors, tslot, table_rows, down_weight, n_ad,
    )

    def low_sum(low):
        for bit in range(n_ad.bit_length() - 1):
            other = lax.ppermute(low, "ad", [(i, i ^ 1 << bit) for i in range(n_ad)])
            low = (low.astype(F32) + other.astype(F32)).astype(BF16)
        for bit in range(bits):
            low = jnp.concatenate([low, swap(low, 1 << bit)], axis=0)
        return low

    def between(keep, send):
        return (keep.astype(F32) + swap(send, 1).astype(F32)).astype(BF16)

    def across(mine):
        for bit in range(1, bits):
            half = mine.shape[0] // 128 // 2
            grouped = mine.reshape(half, 2, 128, mine.shape[1])
            keep = grouped[:, 0].reshape(half * 128, -1)
            send = grouped[:, 1].reshape(half * 128, -1)
            mine = (keep.astype(F32) + swap(send, 1 << bit).astype(F32)).astype(BF16)
        return mine

    slot_count = adapter_output_factors.shape[0]
    flat_factors = adapter_output_factors.reshape(slot_count * EXPERT_COUNT * RANK, span)
    mines, crossed, results = [], [], []
    for step in range(1, n_ad + 1):
        if step > 2:
            mines[step - 3], hidden = lax.optimization_barrier((mines[step - 3], hidden))
            crossed.append(across(mines[step - 3]))
        if step < n_ad:
            keep, send, weights = down_part(n_ad, step, ids, hidden, weights, down_weight, pt, cols)
        else:
            keep, send = final_part(ids, hidden, weights, pt, cols, 2 * n_local, flat_factors, low_sum(low))
        if step > 2:
            crossed[-1], keep = lax.optimization_barrier((crossed[-1], keep))
            results.append(shift(crossed[-1], step - 2))
        mines.append(between(keep, send))
    for step in range(n_ad - 2, n_ad):
        results.append(across(mines[step]))
        if step < n_ad - 1:
            results[-1] = shift(results[-1], step + 1)
    return sum(x.astype(F32) for x in results).astype(BF16)


def solution(mesh):
    placed = (
        P(("rep", "ep"), None),
        P(("rep", "ep"), None),
        P(("rep", "ep"), None),
        P(("rep", "ep")),
        P("rep"),
        P(),
        P("ep", None, "ad"),
        P("ep", None, "ad"),
        P("ep", "ad", None),
        P(None, "ep", None, "ad"),
        P("ep", None, None, "ad"),
    )
    return jax.shard_map(
        functools.partial(per_device, mesh.shape["ep"], mesh.shape["ad"]),
        mesh=mesh,
        in_specs=placed,
        out_specs=P(("rep", "ep"), "ad"),
        check_vma=False,
    )
```

time: 117 us -> 114 us (0.974)
  local copies, waits for them, and re-layouts: 19 us -> 1.49 us
  waiting for transfers between devices: 21.6 us -> 31.9 us
  Pallas kernels: 46.6 us -> 52.7 us
  starting transfers between devices: 25.1 us -> 23.5 us
    unnamed x16 -> x6, local copies, waits for them, and re-layouts: 17 us -> 0.01 us
    ppermute x23 -> x16, waiting for transfers between devices: 14.9 us -> 24.1 us  [swap(): return lax.ppermute(x, 'ep', [(i, i ^ mask) for i in range(n_ep)])]
    pallas_call x10 -> x8, Pallas kernels: 46.6 us -> 52.7 us  [the longest x3 16.8 us: down_part(): pl.pallas_call(functools.partial(down_kernel, n_ad, step), out_shape=(jax...]
    ppermute x0 -> x2, starting transfers between devices: none -> 4.81 us  [low_sum(): other = lax.ppermute(low, 'ad', [(i, i ^ 1 << bit) for i in range(n_ad)])]
    ppermute x0 -> x2, waiting for transfers between devices: none -> 4.05 us  [low_sum(): other = lax.ppermute(low, 'ad', [(i, i ^ 1 << bit) for i in range(n_ad)])]
    ppermute x23 -> x16, starting transfers between devices: 15.6 us -> 12 us  [swap(): return lax.ppermute(x, 'ep', [(i, i ^ mask) for i in range(n_ep)])]
    ppermute x6 -> x3, waiting for transfers between devices: 6.69 us -> 3.7 us  [shift(): return lax.ppermute(x, 'ad', [(i, (i + step) % n_ad) for i in range(n_ad)])]
    ppermute x6 -> x3, starting transfers between devices: 9.49 us -> 6.64 us  [shift(): return lax.ppermute(x, 'ad', [(i, (i + step) % n_ad) for i in range(n_ad)])]
  transfers between devices with their start and end apart: 29 -> 21, of which waited for: 5 -> 10; matrix products, arithmetic and copies ran while one was open for 4% -> 1% of each run, Pallas kernels for 29% -> 25%
where the time goes in v3:
time: 114 us; the launch traced here: 113 us
  Pallas kernels  52.7 us (46%)
  waiting for transfers between devices  31.9 us (28%)
  starting transfers between devices  23.5 us (21%)
  other arithmetic  3.5 us (3%)
  local copies, waits for them, and re-layouts  1.49 us (1%)
    ppermute x16, waiting for transfers between devices, swap(): return lax.ppermute(x, 'ep', [(i, i ^ mask) for i in range(n_ep)])  24.1 us
    pallas_call x3, Pallas kernels, down_part(): pl.pallas_call(functools.partial(down_kernel, n_ad, step), out_shape=(jax...  16.8 us
    pallas_call x1, Pallas kernels, second_part(): pl.pallas_call(functools.partial(second_kernel, len(blocks), len(ahead),...  13.8 us
    ppermute x16, starting transfers between devices, swap(): return lax.ppermute(x, 'ep', [(i, i ^ mask) for i in range(n_ep)])  12 us
    pallas_call x1, Pallas kernels, prefetch(): pl.pallas_call(prefetch_kernel, out_shape=(pltpu.VMEM((each, part_width,...  8.89 us
    pallas_call x1, Pallas kernels, first_part(): pl.pallas_call(functools.partial(first_kernel, len(blocks), local_halves)...  7.55 us
    ppermute x3, starting transfers between devices, shift(): return lax.ppermute(x, 'ad', [(i, (i + step) % n_ad) for i in range(n_ad)])  6.64 us
    ppermute x2, starting transfers between devices, low_sum(): other = lax.ppermute(low, 'ad', [(i, i ^ 1 << bit) for i in range(n_ad)])  4.81 us
  transfers between devices with their start and end apart: 21, of which 10 were waited for; matrix products, arithmetic and copies ran while one was open for 1% of the time, Pallas kernels for 25%

profile of v3, /device:TPU:0, one launch (start us, length us, event | category | flops | bytes accessed | tf_op | source)
XLA Modules:
  0.0 113.3 jit_solution(16060662991802012123)
XLA Ops:
  0.0 0.7 fusion.7
  0.7 0.7 convert_bitcast_fusion
  1.3 0.7 convert_convert_fusion
  2.0 0.1 concatenate.14
  2.2 0.1 copy.18
  2.3 1.2 %fusion.8 = (bf16[128,1536]{1,0:T(8,128)(2,1)S(1)}, bf16[128,1536]{1,0:T(8,128)(2,1)S(1)}) fusion(bf16[128,3072]{1,0:T(8,128)(2,1)} %param.11), kind=kLoop, calls=%fused_computation.37 | loop fusion | bytes 1572864 | tf_op jit(solution)/shard_map/slice | solution.py:446
  3.5 3.0 %collective-permute-start.2 = (bf16[128,1664]{1,0:T(8,128)(2,1)S(1)}, bf16[128,1664]{1,0:T(8,128)(2,1)S(1)}, u32[]{:S(2)}, u32[]{:S(2)}) collective-permute-start(bf16[128,1664]{1,0:T(8,128)(2,1)S(1)} %fusion.1.refs_0_), channel_id=1, source_target_pairs={{0,8},{4,12},{8,0},{12,4},{1,9},{5,13},{9,1},{13,5},{2,10},{6,14},... | collective-permute-start | bytes 1277960 | tf_op jit(solution)/shard_map/ppermute | solution.py:435
  6.5 0.1 pad_add_fusion.ids_ref.refs_11_
  6.6 8.9 %weight_prefetch.1 = (bf16[4,1536,512]{2,1,0:T(8,128)(2,1)S(1)}, bf16[4,1536,512]{2,1,0:T(8,128)(2,1)S(1)}, bf16[4,1536,512]{2,1,0:T(8,128)(2,1)S(1)}, bf16[4,1536,512]{2,1,0:T(8,128)(2,1)S(1)}, f32[8,128]{1,0:T(8,128)S(1)}) custom-call(s32[2]{0:T(128)S(1)} %pad_add_fusion.ids_ref.refs_11_, bf16[4,3072,1024]{2,1,0:T(8,128)(2,1)} %refs_5_.1, ...), custom_call_target="tpu_custom_call" | custom-call | bytes 50331648 | tf_op jit(solution)/shard_map/weight_prefetch/pallas_call | solution.py:141
  15.5 0.8 collective-permute-done.2.refs_2_
  16.3 1.7 %collective-permute-start.1 = (bf16[128,1536]{1,0:T(8,128)(2,1)S(1)}, bf16[128,1536]{1,0:T(8,128)(2,1)S(1)}, u32[]{:S(2)}, u32[]{:S(2)}) collective-permute-start(bf16[128,1536]{1,0:T(8,128)(2,1)S(1)} %get-tuple-element.86.refs_0_), channel_id=1, source_target_pairs={{0,8},{4,12},{8,0},{12,4},{1,9},{5,13},{9,1},{13,5},{2,10},{6,14},... | collective-permute-start | bytes 1179656 | tf_op jit(solution)/shard_map/ppermute | solution.py:435
  18.1 0.2 collective-permute-start
  18.3 9.6 %collective-permute-done.1.refs_2_ = bf16[128,1536]{1,0:T(8,128)(2,1)S(1)} collective-permute-done((bf16[128,1536]{1,0:T(8,128)(2,1)S(1)}, bf16[128,1536]{1,0:T(8,128)(2,1)S(1)}, u32[]{:S(2)}, u32[]{:S(2)}) %collective-permute-start.1) | collective-permute-done | bytes 393248 | tf_op jit(solution)/shard_map/ppermute | solution.py:435
  27.9 1.1 routing_tables.1
  29.0 7.5 %gate_up_first.1 = (bf16[4,1536,512]{2,1,0:T(8,128)(2,1)S(1)}, bf16[4,1536,512]{2,1,0:T(8,128)(2,1)S(1)}, f32[4,192,1024]{2,1,0:T(8,128)S(1)}, f32[4,192,1024]{2,1,0:T(8,128)S(1)}) custom-call(bf16[128,1664]{1,0:T(8,128)(2,1)S(1)} %fusion.1.refs_0_, ...), custom_call_target="tpu_custom_call", output_to_operand_aliasing={{0}: (8, {}), {1}: (9, {})} | custom-call | flops 4831838208 | bytes 12582912 | tf_op jit(solution)/shard_map/gate_up_first/pallas_call | solution.py:190
  36.6 13.8 %gate_up_second.1 = (bf16[4,192,1024]{2,1,0:T(8,128)(2,1)S(1)}, bf16[32,512]{1,0:T(8,128)(2,1)S(1)}, bf16[4,1024,768]{2,1,0:T(8,128)(2,1)S(1)}) custom-call(bf16[128,1536]{1,0:T(8,128)(2,1)S(1)} %get-tuple-element.86.refs_0_, bf16[128,1536]{1,0:T(8,128)(2,1)S(1)} %collective-permute-done.refs_1_, bf16[128,1536]{1,0:T(8,128)(2,1)S(1)} %collective-permute-done.1.refs_2_, ...), custom_call_target="tpu_custom_call" | custom-call | flops 4831838208 | bytes 25165824 | tf_op jit(solution)/shard_map/gate_up_second/pallas_call | solution.py:275
  50.4 1.9 %collective-permute-start.11 = (bf16[32,512]{1,0:T(8,128)(2,1)S(1)}, bf16[32,512]{1,0:T(8,128)(2,1)S(1)}, u32[]{:S(2)}, u32[]{:S(2)}) collective-permute-start(bf16[32,512]{1,0:T(8,128)(2,1)S(1)} %get-tuple-element.78), channel_id=1, source_target_pairs={{0,1},{1,0},{2,3},{3,2},{4,5},{5,4},{6,7},{7,6},{8,9},{9,8},{10,11... | collective-permute-start | bytes 98312 | tf_op jit(solution)/shard_map/ppermute | solution.py:467
  52.3 2.1 %collective-permute-done.11 = bf16[32,512]{1,0:T(8,128)(2,1)S(1)} collective-permute-done((bf16[32,512]{1,0:T(8,128)(2,1)S(1)}, bf16[32,512]{1,0:T(8,128)(2,1)S(1)}, u32[]{:S(2)}, u32[]{:S(2)}) %collective-permute-start.11) | collective-permute-done | bytes 32800 | tf_op jit(solution)/shard_map/ppermute | solution.py:467
  54.4 2.9 %collective-permute-start.12 = (bf16[32,512]{1,0:T(8,128)(2,1)S(1)}, bf16[32,512]{1,0:T(8,128)(2,1)S(1)}, u32[]{:S(2)}, u32[]{:S(2)}) collective-permute-start(bf16[32,512]{1,0:T(8,128)(2,1)S(1)} %add_convert_fusion.6), channel_id=1, source_target_pairs={{0,2},{1,3},{2,0},{3,1},{4,6},{5,7},{6,4},{7,5},{8,10},{9,11},{10,... | collective-permute-start | bytes 98312 | tf_op jit(solution)/shard_map/ppermute | solution.py:467
  57.3 2.0 %collective-permute-done.12 = bf16[32,512]{1,0:T(8,128)(2,1)S(1)} collective-permute-done((bf16[32,512]{1,0:T(8,128)(2,1)S(1)}, bf16[32,512]{1,0:T(8,128)(2,1)S(1)}, u32[]{:S(2)}, u32[]{:S(2)}) %collective-permute-start.12) | collective-permute-done | bytes 32800 | tf_op jit(solution)/shard_map/ppermute | solution.py:467
  59.3 0.1 collective-permute-start.13
  59.3 5.7 %down_part.3 = (bf16[256,768]{1,0:T(8,128)(2,1)S(1)}, bf16[256,768]{1,0:T(8,128)(2,1)S(1)}, bf16[4,1024,768]{2,1,0:T(8,128)(2,1)S(1)}) custom-call(s32[2]{0:T(128)S(1)} %pad_add_fusion.ids_ref.refs_11_, bf16[4,192,1024]{2,1,0:T(8,128)(2,1)S(1)} %get-tuple-element.76.hidden_ref, bf16[4,1024,768]{2,1,0:T(8,128)(2,1)S(1)} %get-tuple-element.62.weight_ref, ...), custom_call_target="tpu_custom_call" | custom-call | flops 1207959552 | bytes 6291456 | tf_op jit(solution)/shard_map/down_part/pallas_call | solution.py:343
  65.1 0.6 collective-permute-start.6
  65.6 1.8 %collective-permute-start.14 = (bf16[64,512]{1,0:T(8,128)(2,1)S(1)}, bf16[64,512]{1,0:T(8,128)(2,1)S(1)}, u32[]{:S(2)}, u32[]{:S(2)}) collective-permute-start(bf16[64,512]{1,0:T(8,128)(2,1)S(1)} %pad_maximum_fusion.1), channel_id=1, source_target_pairs={{0,8},{4,12},{8,0},{12,4},{1,9},{5,13},{9,1},{13,5},{2,10},{6,14},... | collective-permute-start | bytes 196616 | tf_op jit(solution)/shard_map/ppermute | solution.py:435
  67.4 5.5 %down_part.4 = (bf16[256,768]{1,0:T(8,128)(2,1)S(1)}, bf16[256,768]{1,0:T(8,128)(2,1)S(1)}, bf16[4,1024,768]{2,1,0:T(8,128)(2,1)S(1)}) custom-call(s32[2]{0:T(128)S(1)} %pad_add_fusion.ids_ref.refs_11_, bf16[4,192,1024]{2,1,0:T(8,128)(2,1)S(1)} %get-tuple-element.76.hidden_ref, bf16[4,1024,768]{2,1,0:T(8,128)(2,1)S(1)} %get-tuple-element.69.weight_ref, ...), custom_call_target="tpu_custom_call" | custom-call | flops 1207959552 | bytes 6291456 | tf_op jit(solution)/shard_map/down_part/pallas_call | solution.py:343
  73.0 0.1 collective-permute-start.9
  73.1 0.1 add_convert_fusion.3
  73.2 1.6 %collective-permute-done.9 = bf16[256,768]{1,0:T(8,128)(2,1)S(1)} collective-permute-done((bf16[256,768]{1,0:T(8,128)(2,1)S(1)}, bf16[256,768]{1,0:T(8,128)(2,1)S(1)}, u32[]{:S(2)}, u32[]{:S(2)}) %collective-permute-start.9) | collective-permute-done | bytes 393248 | tf_op jit(solution)/shard_map/ppermute | solution.py:435
  74.8 0.1 add_convert_fusion.2
  74.9 0.0 copy-start
  74.9 5.5 %down_part.5 = (bf16[256,768]{1,0:T(8,128)(2,1)S(1)}, bf16[256,768]{1,0:T(8,128)(2,1)S(1)}, bf16[4,1024,768]{2,1,0:T(8,128)(2,1)S(1)}) custom-call(s32[2]{0:T(128)S(1)} %pad_add_fusion.ids_ref.refs_11_, bf16[4,192,1024]{2,1,0:T(8,128)(2,1)S(1)} %get-tuple-element.76.hidden_ref, bf16[4,1024,768]{2,1,0:T(8,128)(2,1)S(1)} %get-tuple-element.70.weight_ref, ...), custom_call_target="tpu_custom_call" | custom-call | flops 1207959552 | bytes 6291456 | tf_op jit(solution)/shard_map/down_part/pallas_call | solution.py:343
  80.4 4.6 %down_and_adapters.1 = (bf16[256,768]{1,0:T(8,128)(2,1)S(1)}, bf16[256,768]{1,0:T(8,128)(2,1)S(1)}) custom-call(s32[2]{0:T(128)S(1)} %pad_add_fusion.ids_ref.refs_11_, bf16[4,192,1024]{2,1,0:T(8,128)(2,1)S(1)} %get-tuple-element.76.hidden_ref, bf16[4,1024,768]{2,1,0:T(8,128)(2,1)S(1)} %get-tuple-element.77.weight_ref, ...), custom_call_target="tpu_custom_call" | custom-call | flops 2818572288 | bytes 9437184 | tf_op jit(solution)/shard_map/down_and_adapters/pallas_call | solution.py:392
  85.0 0.2 collective-permute-start.19
  85.3 0.4 collective-permute-start.10
  85.7 1.8 %collective-permute-start.7 = (bf16[128,768]{1,0:T(8,128)(2,1)S(1)}, bf16[128,768]{1,0:T(8,128)(2,1)S(1)}, u32[]{:S(2)}, u32[]{:S(2)}) collective-permute-start(bf16[128,768]{1,0:T(8,128)(2,1)S(1)} %slice_bitcast_fusion.6), channel_id=1, source_target_pairs={{0,8},{4,12},{8,0},{12,4},{1,9},{5,13},{9,1},{13,5},{2,10},{6,14},... | collective-permute-start | bytes 589832 | tf_op jit(solution)/shard_map/ppermute | solution.py:435
  87.5 5.6 %collective-permute-done.10 = bf16[128,768]{1,0:T(8,128)(2,1)S(1)} collective-permute-done((bf16[128,768]{1,0:T(8,128)(2,1)S(1)}, bf16[128,768]{1,0:T(8,128)(2,1)S(1)}, u32[]{:S(2)}, u32[]{:S(2)}) %collective-permute-start.10) | collective-permute-done | bytes 196640 | tf_op jit(solution)/shard_map/ppermute | solution.py:435
  93.1 2.7 %collective-permute-start.15 = (bf16[128,768]{1,0:T(8,128)(2,1)S(1)}, bf16[128,768]{1,0:T(8,128)(2,1)S(1)}, u32[]{:S(2)}, u32[]{:S(2)}) collective-permute-start(bf16[128,768]{1,0:T(8,128)(2,1)S(1)} %fusion.4), channel_id=1, source_target_pairs={{0,2},{1,3},{2,0},{3,1},{4,6},{5,7},{6,4},{7,5},{8,10},{9,11},{10,... | collective-permute-start | bytes 589832 | tf_op jit(solution)/shard_map/ppermute | solution.py:438
  95.8 0.9 collective-permute-done.7
  96.8 1.6 %collective-permute-start.8 = (bf16[128,768]{1,0:T(8,128)(2,1)S(1)}, bf16[128,768]{1,0:T(8,128)(2,1)S(1)}, u32[]{:S(2)}, u32[]{:S(2)}) collective-permute-start(bf16[128,768]{1,0:T(8,128)(2,1)S(1)} %fusion.5), channel_id=1, source_target_pairs={{0,1},{1,2},{2,3},{3,0},{4,5},{5,6},{6,7},{7,4},{8,9},{9,10},{10,1... | collective-permute-start | bytes 589832 | tf_op jit(solution)/shard_map/ppermute | solution.py:438
  98.4 0.1 add_convert_fusion.1
  98.5 0.6 collective-permute-start.17
  99.1 0.1 add_convert_fusion
  99.2 1.6 %collective-permute-start.20 = (bf16[128,768]{1,0:T(8,128)(2,1)S(1)}, bf16[128,768]{1,0:T(8,128)(2,1)S(1)}, u32[]{:S(2)}, u32[]{:S(2)}) collective-permute-start(bf16[128,768]{1,0:T(8,128)(2,1)S(1)} %slice_bitcast_fusion), channel_id=1, source_target_pairs={{0,8},{4,12},{8,0},{12,4},{1,9},{5,13},{9,1},{13,5},{2,10},{6,14},... | collective-permute-start | bytes 589832 | tf_op jit(solution)/shard_map/ppermute | solution.py:435
  100.8 5.6 %collective-permute-done.17 = bf16[128,768]{1,0:T(8,128)(2,1)S(1)} collective-permute-done((bf16[128,768]{1,0:T(8,128)(2,1)S(1)}, bf16[128,768]{1,0:T(8,128)(2,1)S(1)}, u32[]{:S(2)}, u32[]{:S(2)}) %collective-permute-start.17) | collective-permute-done | bytes 196640 | tf_op jit(solution)/shard_map/ppermute | solution.py:435
  106.4 2.4 %collective-permute-start.18 = (bf16[128,768]{1,0:T(8,128)(2,1)S(1)}, bf16[128,768]{1,0:T(8,128)(2,1)S(1)}, u32[]{:S(2)}, u32[]{:S(2)}) collective-permute-start(bf16[128,768]{1,0:T(8,128)(2,1)S(1)} %fusion.3), channel_id=1, source_target_pairs={{0,3},{1,0},{2,1},{3,2},{4,7},{5,4},{6,5},{7,6},{8,11},{9,8},{10,9... | collective-permute-start | bytes 589832 | tf_op jit(solution)/shard_map/ppermute | solution.py:438
  108.8 0.9 collective-permute-done.15
  109.7 2.8 %collective-permute-done.18 = bf16[128,768]{1,0:T(8,128)(2,1)S(1)} collective-permute-done((bf16[128,768]{1,0:T(8,128)(2,1)S(1)}, bf16[128,768]{1,0:T(8,128)(2,1)S(1)}, u32[]{:S(2)}, u32[]{:S(2)}) %collective-permute-start.18) | collective-permute-done | bytes 196640 | tf_op jit(solution)/shard_map/ppermute | solution.py:438
  112.5 0.8 add_convert_fusion.4
  (32 shorter events, 0.3 us)
Async XLA Ops:
  3.5 12.8 %collective-permute-start.2 = (bf16[128,1664]{1,0:T(8,128)(2,1)S(1)}, bf16[128,1664]{1,0:T(8,128)(2,1)S(1)}, u32[]{:S(2)}, u32[]{:S(2)}) collective-permute-start(bf16[128,1664]{1,0:T(8,128)(2,1)S(1)} %fusion.1.refs_0_), channel_id=1, source_target_pairs={{0,8},{4,12},{8,0},{12,4},{1,9},{5,13},{9,1},{13,5},{2,10},{6,14},... | collective-permute-start | bytes 1277960 | tf_op jit(solution)/shard_map/ppermute | solution.py:435
  6.5 21.4 %collective-permute-start.4 = (bf16[128,1664]{1,0:T(8,128)(2,1)S(1)}, bf16[128,1664]{1,0:T(8,128)(2,1)S(1)}, u32[]{:S(2)}, u32[]{:S(2)}) collective-permute-start(bf16[128,1664]{1,0:T(8,128)(2,1)S(1)} %fusion.1.refs_0_), channel_id=1, source_target_pairs={{0,4},{4,0},{8,12},{12,8},{1,5},{5,1},{9,13},{13,9},{2,6},{6,2},{1... | collective-permute-start | bytes 1277960 | tf_op jit(solution)/shard_map/ppermute | solution.py:435
  6.6 21.3 %copy-start.1 = (s32[16]{0:T(128)S(1)}, s32[16]{0:T(128)}, u32[]{:S(2)}) copy-start(s32[16]{0:T(128)} %refs_12_.1) | copy-start | bytes 196
  6.6 21.3 %copy-start.2 = (s32[64]{0:T(128)S(1)}, s32[64]{0:T(128)}, u32[]{:S(2)}) copy-start(s32[64]{0:T(128)} %refs_13_.1) | copy-start | bytes 772
  16.3 11.5 %collective-permute-start.5 = (bf16[128,1664]{1,0:T(8,128)(2,1)S(1)}, bf16[128,1664]{1,0:T(8,128)(2,1)S(1)}, u32[]{:S(2)}, u32[]{:S(2)}) collective-permute-start(bf16[128,1664]{1,0:T(8,128)(2,1)S(1)} %collective-permute-done.2.refs_2_), channel_id=1, source_target_pairs={{0,4},{4,0},{8,12},{12,8},{1,5},{5,1},{9,13},{13,9},{2,6},{6,2},{1... | collective-permute-start | bytes 1277960 | tf_op jit(solution)/shard_map/ppermute | solution.py:435
  16.3 11.5 %collective-permute-start.1 = (bf16[128,1536]{1,0:T(8,128)(2,1)S(1)}, bf16[128,1536]{1,0:T(8,128)(2,1)S(1)}, u32[]{:S(2)}, u32[]{:S(2)}) collective-permute-start(bf16[128,1536]{1,0:T(8,128)(2,1)S(1)} %get-tuple-element.86.refs_0_), channel_id=1, source_target_pairs={{0,8},{4,12},{8,0},{12,4},{1,9},{5,13},{9,1},{13,5},{2,10},{6,14},... | collective-permute-start | bytes 1179656 | tf_op jit(solution)/shard_map/ppermute | solution.py:435
  18.1 18.5 %collective-permute-start = (bf16[128,1536]{1,0:T(8,128)(2,1)S(1)}, bf16[128,1536]{1,0:T(8,128)(2,1)S(1)}, u32[]{:S(2)}, u32[]{:S(2)}) collective-permute-start(bf16[128,1536]{1,0:T(8,128)(2,1)S(1)} %get-tuple-element.86.refs_0_), channel_id=1, source_target_pairs={{0,4},{4,0},{8,12},{12,8},{1,5},{5,1},{9,13},{13,9},{2,6},{6,2},{1... | collective-permute-start | bytes 1179656 | tf_op jit(solution)/shard_map/ppermute | solution.py:435
  27.8 8.7 %collective-permute-start.3 = (bf16[128,1536]{1,0:T(8,128)(2,1)S(1)}, bf16[128,1536]{1,0:T(8,128)(2,1)S(1)}, u32[]{:S(2)}, u32[]{:S(2)}) collective-permute-start(bf16[128,1536]{1,0:T(8,128)(2,1)S(1)} %collective-permute-done.1.refs_2_), channel_id=1, source_target_pairs={{0,4},{4,0},{8,12},{12,8},{1,5},{5,1},{9,13},{13,9},{2,6},{6,2},{1... | collective-permute-start | bytes 1179656 | tf_op jit(solution)/shard_map/ppermute | solution.py:435
  50.4 4.0 %collective-permute-start.11 = (bf16[32,512]{1,0:T(8,128)(2,1)S(1)}, bf16[32,512]{1,0:T(8,128)(2,1)S(1)}, u32[]{:S(2)}, u32[]{:S(2)}) collective-permute-start(bf16[32,512]{1,0:T(8,128)(2,1)S(1)} %get-tuple-element.78), channel_id=1, source_target_pairs={{0,1},{1,0},{2,3},{3,2},{4,5},{5,4},{6,7},{7,6},{8,9},{9,8},{10,11... | collective-permute-start | bytes 98312 | tf_op jit(solution)/shard_map/ppermute | solution.py:467
  54.4 4.9 %collective-permute-start.12 = (bf16[32,512]{1,0:T(8,128)(2,1)S(1)}, bf16[32,512]{1,0:T(8,128)(2,1)S(1)}, u32[]{:S(2)}, u32[]{:S(2)}) collective-permute-start(bf16[32,512]{1,0:T(8,128)(2,1)S(1)} %add_convert_fusion.6), channel_id=1, source_target_pairs={{0,2},{1,3},{2,0},{3,1},{4,6},{5,7},{6,4},{7,5},{8,10},{9,11},{10,... | collective-permute-start | bytes 98312 | tf_op jit(solution)/shard_map/ppermute | solution.py:467
  59.3 6.4 %collective-permute-start.13 = (bf16[32,512]{1,0:T(8,128)(2,1)S(1)}, bf16[32,512]{1,0:T(8,128)(2,1)S(1)}, u32[]{:S(2)}, u32[]{:S(2)}) collective-permute-start(bf16[32,512]{1,0:T(8,128)(2,1)S(1)} %add_convert_fusion.5), channel_id=1, source_target_pairs={{0,4},{4,0},{8,12},{12,8},{1,5},{5,1},{9,13},{13,9},{2,6},{6,2},{1... | collective-permute-start | bytes 98312 | tf_op jit(solution)/shard_map/ppermute | solution.py:435
  65.1 8.0 %collective-permute-start.6 = (bf16[256,768]{1,0:T(8,128)(2,1)S(1)}, bf16[256,768]{1,0:T(8,128)(2,1)S(1)}, u32[]{:S(2)}, u32[]{:S(2)}) collective-permute-start(bf16[256,768]{1,0:T(8,128)(2,1)S(1)} %get-tuple-element.66), channel_id=1, source_target_pairs={{0,4},{4,0},{8,12},{12,8},{1,5},{5,1},{9,13},{13,9},{2,6},{6,2},{1... | collective-permute-start | bytes 1179656 | tf_op jit(solution)/shard_map/ppermute | solution.py:435
  65.6 7.4 %collective-permute-start.14 = (bf16[64,512]{1,0:T(8,128)(2,1)S(1)}, bf16[64,512]{1,0:T(8,128)(2,1)S(1)}, u32[]{:S(2)}, u32[]{:S(2)}) collective-permute-start(bf16[64,512]{1,0:T(8,128)(2,1)S(1)} %pad_maximum_fusion.1), channel_id=1, source_target_pairs={{0,8},{4,12},{8,0},{12,4},{1,9},{5,13},{9,1},{13,5},{2,10},{6,14},... | collective-permute-start | bytes 196616 | tf_op jit(solution)/shard_map/ppermute | solution.py:435
  73.0 1.8 %collective-permute-start.9 = (bf16[256,768]{1,0:T(8,128)(2,1)S(1)}, bf16[256,768]{1,0:T(8,128)(2,1)S(1)}, u32[]{:S(2)}, u32[]{:S(2)}) collective-permute-start(bf16[256,768]{1,0:T(8,128)(2,1)S(1)} %get-tuple-element.74), channel_id=1, source_target_pairs={{0,4},{4,0},{8,12},{12,8},{1,5},{5,1},{9,13},{13,9},{2,6},{6,2},{1... | collective-permute-start | bytes 1179656 | tf_op jit(solution)/shard_map/ppermute | solution.py:435
  74.9 5.5 %copy-start = (bf16[16,8,16,768]{3,2,1,0:T(8,128)(2,1)S(1)}, bf16[16,8,16,768]{3,2,1,0:T(8,128)(2,1)}, u32[]{:S(2)}) copy-start(bf16[16,8,16,768]{3,2,1,0:T(8,128)(2,1)} %param.21) | copy-start | bytes 9437188
  85.0 14.0 %collective-permute-start.19 = (bf16[256,768]{1,0:T(8,128)(2,1)S(1)}, bf16[256,768]{1,0:T(8,128)(2,1)S(1)}, u32[]{:S(2)}, u32[]{:S(2)}) collective-permute-start(bf16[256,768]{1,0:T(8,128)(2,1)S(1)} %get-tuple-element.84), channel_id=1, source_target_pairs={{0,4},{4,0},{8,12},{12,8},{1,5},{5,1},{9,13},{13,9},{2,6},{6,2},{1... | collective-permute-start | bytes 1179656 | tf_op jit(solution)/shard_map/ppermute | solution.py:435
  85.3 7.8 %collective-permute-start.10 = (bf16[128,768]{1,0:T(8,128)(2,1)S(1)}, bf16[128,768]{1,0:T(8,128)(2,1)S(1)}, u32[]{:S(2)}, u32[]{:S(2)}) collective-permute-start(bf16[128,768]{1,0:T(8,128)(2,1)S(1)} %slice_bitcast_fusion.4), channel_id=1, source_target_pairs={{0,8},{4,12},{8,0},{12,4},{1,9},{5,13},{9,1},{13,5},{2,10},{6,14},... | collective-permute-start | bytes 589832 | tf_op jit(solution)/shard_map/ppermute | solution.py:435
  85.7 11.1 %collective-permute-start.7 = (bf16[128,768]{1,0:T(8,128)(2,1)S(1)}, bf16[128,768]{1,0:T(8,128)(2,1)S(1)}, u32[]{:S(2)}, u32[]{:S(2)}) collective-permute-start(bf16[128,768]{1,0:T(8,128)(2,1)S(1)} %slice_bitcast_fusion.6), channel_id=1, source_target_pairs={{0,8},{4,12},{8,0},{12,4},{1,9},{5,13},{9,1},{13,5},{2,10},{6,14},... | collective-permute-start | bytes 589832 | tf_op jit(solution)/shard_map/ppermute | solution.py:435
  87.5 10.9 %collective-permute-start.16 = (bf16[256,768]{1,0:T(8,128)(2,1)S(1)}, bf16[256,768]{1,0:T(8,128)(2,1)S(1)}, u32[]{:S(2)}, u32[]{:S(2)}) collective-permute-start(bf16[256,768]{1,0:T(8,128)(2,1)S(1)} %get-tuple-element.82), channel_id=1, source_target_pairs={{0,4},{4,0},{8,12},{12,8},{1,5},{5,1},{9,13},{13,9},{2,6},{6,2},{1... | collective-permute-start | bytes 1179656 | tf_op jit(solution)/shard_map/ppermute | solution.py:435
  93.1 16.6 %collective-permute-start.15 = (bf16[128,768]{1,0:T(8,128)(2,1)S(1)}, bf16[128,768]{1,0:T(8,128)(2,1)S(1)}, u32[]{:S(2)}, u32[]{:S(2)}) collective-permute-start(bf16[128,768]{1,0:T(8,128)(2,1)S(1)} %fusion.4), channel_id=1, source_target_pairs={{0,2},{1,3},{2,0},{3,1},{4,6},{5,7},{6,4},{7,5},{8,10},{9,11},{10,... | collective-permute-start | bytes 589832 | tf_op jit(solution)/shard_map/ppermute | solution.py:438
  96.8 12.9 %collective-permute-start.8 = (bf16[128,768]{1,0:T(8,128)(2,1)S(1)}, bf16[128,768]{1,0:T(8,128)(2,1)S(1)}, u32[]{:S(2)}, u32[]{:S(2)}) collective-permute-start(bf16[128,768]{1,0:T(8,128)(2,1)S(1)} %fusion.5), channel_id=1, source_target_pairs={{0,1},{1,2},{2,3},{3,0},{4,5},{5,6},{6,7},{7,4},{8,9},{9,10},{10,1... | collective-permute-start | bytes 589832 | tf_op jit(solution)/shard_map/ppermute | solution.py:438
  98.5 7.9 %collective-permute-start.17 = (bf16[128,768]{1,0:T(8,128)(2,1)S(1)}, bf16[128,768]{1,0:T(8,128)(2,1)S(1)}, u32[]{:S(2)}, u32[]{:S(2)}) collective-permute-start(bf16[128,768]{1,0:T(8,128)(2,1)S(1)} %slice_bitcast_fusion.2), channel_id=1, source_target_pairs={{0,8},{4,12},{8,0},{12,4},{1,9},{5,13},{9,1},{13,5},{2,10},{6,14},... | collective-permute-start | bytes 589832 | tf_op jit(solution)/shard_map/ppermute | solution.py:435
  99.2 10.5 %collective-permute-start.20 = (bf16[128,768]{1,0:T(8,128)(2,1)S(1)}, bf16[128,768]{1,0:T(8,128)(2,1)S(1)}, u32[]{:S(2)}, u32[]{:S(2)}) collective-permute-start(bf16[128,768]{1,0:T(8,128)(2,1)S(1)} %slice_bitcast_fusion), channel_id=1, source_target_pairs={{0,8},{4,12},{8,0},{12,4},{1,9},{5,13},{9,1},{13,5},{2,10},{6,14},... | collective-permute-start | bytes 589832 | tf_op jit(solution)/shard_map/ppermute | solution.py:435
  106.4 6.1 %collective-permute-start.18 = (bf16[128,768]{1,0:T(8,128)(2,1)S(1)}, bf16[128,768]{1,0:T(8,128)(2,1)S(1)}, u32[]{:S(2)}, u32[]{:S(2)}) collective-permute-start(bf16[128,768]{1,0:T(8,128)(2,1)S(1)} %fusion.3), channel_id=1, source_target_pairs={{0,3},{1,0},{2,1},{3,2},{4,7},{5,4},{6,5},{7,6},{8,11},{9,8},{10,9... | collective-permute-start | bytes 589832 | tf_op jit(solution)/shard_map/ppermute | solution.py:438

commit v4 on v0

v4 whole, which is shorter than its diff:
```python
import functools
import math

import jax
import jax.numpy as jnp
from jax import lax
from jax.experimental import pallas as pl
from jax.experimental.pallas import tpu as pltpu
from jax.sharding import PartitionSpec as P

EXPERT_COUNT = 8
TOP = 2
RANK = 16
CAP = 48
LIMIT = 16
LIMIT_EARLY = 24
N_TILE = 512
HELD_EACH = 2
HELD_ARRAYS = 4
RING = 4
MIB = 1 << 20

F32 = jnp.float32
BF16 = jnp.bfloat16


def mm(a, b):
    return jnp.dot(a, b, preferred_element_type=F32)


def mm_nt(a, b):
    return lax.dot_general(a, b, (((1,), (1,)), ((), ())), preferred_element_type=F32)


SMALL = pl.CostEstimate(flops=1, bytes_accessed=1, transcendentals=0)


def params(mib):
    return pltpu.CompilerParams(vmem_limit_bytes=mib * MIB)


def vmem():
    return pl.BlockSpec(memory_space=pltpu.VMEM)


def smem():
    return pl.BlockSpec(memory_space=pltpu.SMEM)


def facts_kernel(tokens_ref, chosen_ref, logits_ref, tenant_ref, out_ref, sem):
    rows, width = tokens_ref.shape
    copy = pltpu.make_async_copy(tokens_ref, out_ref.at[:, pl.ds(0, width)], sem)
    copy.start()
    diagonal = lax.broadcasted_iota(jnp.int32, (rows, rows), 0) == lax.broadcasted_iota(jnp.int32, (rows, rows), 1)
    tenant = jnp.sum(jnp.where(diagonal, tenant_ref[...].astype(F32), 0.0), axis=1, keepdims=True)
    chosen = chosen_ref[...].astype(F32)
    columns, rest = [chosen[:, 0:1], chosen[:, 1:2], tenant], logits_ref[...]
    for _ in range(3):
        piece = rest.astype(BF16).astype(F32)
        columns += [piece[:, 0:1], piece[:, 1:2]]
        rest = rest - piece
    lane = lax.broadcasted_iota(jnp.int32, (rows, 128), 1)
    facts = jnp.zeros((rows, 128), F32)
    for number, column in enumerate(columns):
        facts = jnp.where(lane == number, column, facts)
    out_ref[:, width:] = facts.astype(BF16)
    copy.wait()


def with_facts(tokens, chosen_experts, logits, tenant):
    rows, width = tokens.shape
    return pl.pallas_call(
        facts_kernel,
        out_shape=jax.ShapeDtypeStruct((rows, width + 128), BF16),
        in_specs=[pl.BlockSpec(memory_space=pltpu.HBM)] + [vmem()] * 3,
        out_specs=vmem(),
        scratch_shapes=[pltpu.SemaphoreType.DMA],
        cost_estimate=SMALL,
        compiler_params=params(LIMIT_EARLY),
        name="tokens_with_facts",
    )(pltpu.with_memory_space_constraint(tokens, pltpu.HBM), chosen_experts, logits, tenant.reshape(1, rows))


def meta_kernel(n_local, local_halves, ids_ref, adapter_ref, pool_slot_ref, *refs):
    blocks, (p_ref, pt_ref, cols_ref, rows_ref, tslot_ref) = refs[:-5], refs[-5:]
    at = blocks[0].shape[1] - 128
    facts = jnp.concatenate([block[:, at:] for block in blocks], axis=0).astype(F32).T
    count = facts.shape[1]
    first, second, tenant = facts[0:1], facts[1:2], facts[2:3]
    logit_first = (facts[3:4] + facts[5:6]) + facts[7:8]
    logit_second = (facts[4:5] + facts[6:7]) + facts[8:9]
    weight_first = jax.nn.sigmoid(logit_first - logit_second)
    weight_second = jax.nn.sigmoid(logit_second - logit_first)
    slot = jnp.zeros_like(tenant)
    for number in range(adapter_ref.shape[0]):
        slot = jnp.where(tenant == number, pool_slot_ref[adapter_ref[number]].astype(F32), slot)
    members, weights = [], []
    for i in range(n_local):
        expert = (ids_ref[0] * local_halves // 2 + i).astype(F32)
        hit_first, hit_second = first == expert, second == expert
        members.append(jnp.where(hit_first | hit_second, 1.0, 0.0))
        weights.append(jnp.where(hit_first, weight_first, 0.0) + jnp.where(hit_second, weight_second, 0.0))
    member = jnp.concatenate(members + [jnp.zeros((8 - n_local, count), F32)], axis=0)
    before = (
        lax.broadcasted_iota(jnp.int32, (count, count), 0) < lax.broadcasted_iota(jnp.int32, (count, count), 1)
    ).astype(BF16)
    place = jnp.where(member > 0, mm(member.astype(BF16), before), -1.0)
    table = jnp.concatenate(
        [place[0:n_local]] + weights + [slot] + [jnp.zeros((127 - 2 * n_local, count), F32)], axis=0
    )
    columns = table.T
    cols_ref[...] = columns
    rows_ref[...] = table[0:8]
    row_count = p_ref.shape[1]
    tenant_rows = jnp.broadcast_to(tenant, (8, count)).astype(BF16)
    down = lax.broadcasted_iota(jnp.int32, (row_count, count), 0).astype(F32)
    across = lax.broadcasted_iota(jnp.int32, (count, row_count), 1).astype(F32)
    for i in range(n_local):
        picked = (down == place[i : i + 1]).astype(BF16)
        p_ref[i] = picked
        pt_ref[i] = (across == columns[:, i : i + 1]).astype(BF16)
        tslot_ref[i] = mm_nt(tenant_rows, picked)


def build_meta(blocks, ids, adapters, pool_slots, n_local, local_halves, row_count):
    count = sum(block.shape[0] for block in blocks)
    return pl.pallas_call(
        functools.partial(meta_kernel, n_local, local_halves),
        out_shape=(
            jax.ShapeDtypeStruct((n_local, row_count, count), BF16),
            jax.ShapeDtypeStruct((n_local, count, row_count), BF16),
            jax.ShapeDtypeStruct((count, 128), F32),
            jax.ShapeDtypeStruct((8, count), F32),
            jax.ShapeDtypeStruct((n_local, 8, row_count), F32),
        ),
        in_specs=[smem()] * 3 + [vmem()] * len(blocks),
        out_specs=(vmem(),) * 5,
        cost_estimate=SMALL,
        compiler_params=params(min(38, LIMIT_EARLY * count // 512)),
        name="routing_tables",
    )(ids, adapters, pool_slots, *blocks)


class Slabs:
    def __init__(self, gate_ref, up_ref, down_ref, resident, ring, sems):
        self.sources, self.down, self.resident, self.ring, self.sems = (gate_ref, up_ref), down_ref, resident, ring, sems
        self.halves, self.depth, self.hidden = gate_ref.shape
        self.width = resident[0].shape[2]
        self.each = resident[0].shape[0]
        self.first = len(resident) * self.each
        self.capacity = 1 if ring is None else ring.shape[0]
        self.tiles = self.hidden // self.width
        self.early = 2 * self.halves * self.tiles
        self.held = self.depth // self.hidden
        self.columns = down_ref.shape[2] // self.width
        self.count = self.early + -(-self.columns * self.halves // self.held)

    def place(self, number):
        if number < self.first:
            return self.resident[number // self.each].at[number % self.each]
        return self.ring.at[(number - self.first) % self.capacity]

    def copies(self, number):
        place = self.place(number)
        slot = number if number < self.first else (number - self.first) % self.capacity
        if number < self.early:
            half, tile, which = number // (2 * self.tiles), number // 2 % self.tiles, number % 2
            source = self.sources[which].at[half, :, pl.ds(tile * self.width, self.width)]
            return [pltpu.make_async_copy(source, place, self.sems.at[slot, 0])]
        made = []
        for i in range(self.held):
            piece = (number - self.early) * self.held + i
            if piece < self.columns * self.halves:
                source = self.down.at[piece % self.halves, :, pl.ds(piece // self.halves * self.width, self.width)]
                into = place.at[pl.ds(i * self.hidden, self.hidden)]
                made.append(pltpu.make_async_copy(source, into, self.sems.at[slot, i]))
        return made

    def start(self, number):
        for copy in self.copies(number):
            copy.start()

    def wait(self, number):
        for copy in self.copies(number):
            copy.wait()

    def down_piece(self, column, half):
        piece = column * self.halves + half
        return self.early + piece // self.held, piece % self.held


def resident_shapes(gate, down):
    local_halves, width, hidden_count = gate.shape
    tile = min(N_TILE, hidden_count)
    pieces = local_halves * down.shape[2] // tile
    count = 2 * local_halves * hidden_count // tile + -(-pieces * hidden_count // width)
    each = min(HELD_EACH, count)
    return [(each, width, tile)] * min(HELD_ARRAYS, count // each)


def ring_size(gate, down, resident):
    pieces = gate.shape[0] * down.shape[2] // resident[0].shape[2]
    count = 2 * gate.shape[0] * gate.shape[2] // resident[0].shape[2] + -(-pieces * gate.shape[2] // gate.shape[1])
    return max(1, min(RING, count - len(resident) * resident[0].shape[0]))


def semaphores(gate, slots):
    return pltpu.SemaphoreType.DMA((slots, max(1, gate.shape[1] // gate.shape[2])))


def prefetch_kernel(ids_ref, gate_ref, up_ref, down_ref, *refs):
    resident, mark_ref, sems = refs[:-2], refs[-2], refs[-1]
    slabs = Slabs(gate_ref, up_ref, down_ref, resident, None, sems)
    for number in range(slabs.first):
        slabs.start(number)
    mark_ref[...] = jnp.zeros_like(mark_ref)
    for number in range(slabs.first):
        slabs.wait(number)


def prefetch(ids, gate, up, down, count):
    shapes = resident_shapes(gate, down)
    return pl.pallas_call(
        prefetch_kernel,
        out_shape=(*[pltpu.VMEM(shape, BF16) for shape in shapes], jax.ShapeDtypeStruct((8, 128), F32)),
        in_specs=[smem()] + [pl.BlockSpec(memory_space=pltpu.HBM)] * 3,
        out_specs=(vmem(),) * (len(shapes) + 1),
        scratch_shapes=[semaphores(gate, len(shapes) * shapes[0][0])],
        cost_estimate=SMALL,
        compiler_params=params(min(38, LIMIT_EARLY * count // 512)),
        name="weight_prefetch",
    )(ids, gate, up, down)


def expert_kernel(n_blocks, n_resident, n_ad, order, *refs):
    blocks, refs = refs[:n_blocks], refs[n_blocks:]
    ids_ref, adapter_ref, pool_slot_ref, p_ref, pt_ref, cols_ref, tslot_ref, rows_ref = refs[1:9]
    gate_ref, up_ref, down_ref, pool_ref = refs[9:13]
    resident, refs = refs[13 : 13 + n_resident], refs[13 + n_resident :]
    keep, send, base, packed, hidden, factors, factor_sems, ring, sems = refs
    slabs = Slabs(gate_ref, up_ref, down_ref, resident, ring, sems)
    n_local = p_ref.shape[0]
    local_halves, depth, _ = gate_ref.shape
    halves_each = local_halves // n_local
    tenants, rank = adapter_ref.shape[0], pool_ref.shape[2]
    factor_copies = [
        pltpu.make_async_copy(
            pool_ref.at[pool_slot_ref[adapter_ref[number]]],
            factors.at[:, number * rank : (number + 1) * rank],
            factor_sems.at[number],
        )
        for number in range(tenants)
    ]
    for copy in factor_copies:
        copy.start()
    for number in range(slabs.first, min(slabs.count, slabs.first + slabs.capacity)):
        slabs.start(number)

    def ready(number):
        if number >= slabs.first:
            slabs.wait(number)

    def used(number):
        if slabs.first <= number < slabs.count - slabs.capacity:
            slabs.start(number + slabs.capacity)

    whole = jnp.concatenate([block[:, :depth] for block in blocks], axis=0)
    for i in range(n_local):
        packed[i] = mm(p_ref[i], whole).astype(BF16)
    for half in range(local_halves):
        rows = packed[half // halves_each]
        for tile in range(slabs.tiles):
            values = []
            for which in range(2):
                number = (half * slabs.tiles + tile) * 2 + which
                ready(number)
                values.append(mm(rows, slabs.place(number)[...]))
                used(number)
            span = slice(tile * slabs.width, (tile + 1) * slabs.width)
            hidden[half, :, span] = (jax.nn.silu(values[0]) * values[1]).astype(BF16)
    span = base.shape[1]
    at = span * len(order)
    for copy in factor_copies:
        copy.wait()
    for out in (keep, send):
        out[:, at:] = jnp.zeros((out.shape[0], 256), BF16)
    for i in range(n_local):
        low = mm_nt(factors[i * halves_each], hidden[i * halves_each])
        for half in range(i * halves_each + 1, (i + 1) * halves_each):
            low = low + mm_nt(factors[half], hidden[half])
        owner = tslot_ref[i][0:1]
        total = jnp.zeros((rank, low.shape[1]), F32)
        for number in range(tenants):
            total = total + jnp.where(owner == number, low[number * rank : (number + 1) * rank], 0.0)
        weight = rows_ref[n_local + i : n_local + i + 1]
        value = (mm(total.astype(BF16), p_ref[i]) * weight).astype(BF16)
        row = pl.multiple_of((ids_ref[0] * local_halves // 2 + i) * rank, rank)
        for place, out in enumerate((keep, send)):
            for b in range(value.shape[1] // 128):
                lane = at + (b % 2 ^ place) * 128
                out[pl.ds(b // 2 * 128 + row, rank), lane : lane + 128] = value[:, b * 128 : b * 128 + 128]
    part = math.gcd(span, slabs.width)
    for column in range(slabs.columns):
        total = None
        for i in range(n_local):
            part_sum = None
            for half in range(i * halves_each, (i + 1) * halves_each):
                number, piece = slabs.down_piece(column, half)
                if piece == 0:
                    ready(number)
                value = mm(hidden[half], slabs.place(number)[piece * slabs.hidden : (piece + 1) * slabs.hidden])
                if piece == slabs.held - 1:
                    used(number)
                part_sum = value if part_sum is None else part_sum + value
            laid = mm(pt_ref[i], part_sum.astype(BF16)) * cols_ref[:, n_local + i : n_local + i + 1]
            total = laid if total is None else total + laid
        for first in range(0, slabs.width, part):
            feature = column * slabs.width + first
            owner, inside = feature // span, feature % span
            step = lax.rem(owner - ids_ref[1] + n_ad, n_ad)
            position = sum(jnp.where(step == s, position, 0) for position, s in enumerate(order))
            value = total[:, first : first + part]

            @pl.when(step == 0)
            def _():
                base[:, inside : inside + part] = value

            @pl.when(step != 0)
            def _():
                write_pairs(value, (keep, send), pl.multiple_of(position * span + inside, 128))


def expert_part(
    blocks, mark, ids, adapters, pool_slots, picked, pt, cols, tslot, table_rows, gate, up, down, pool, resident, n_ad, order
):
    local_halves, width, hidden_count = gate.shape
    n_local, row_count, count = picked.shape
    tenants, rank = adapters.shape[0], pool.shape[2]
    span = down.shape[2] // n_ad
    hbm = pl.BlockSpec(memory_space=pltpu.HBM)
    ring = ring_size(gate, down, resident)
    outs = [pltpu.VMEM((count // 2, span * len(order) + 256), BF16)] * 2
    outs.append(pltpu.VMEM((count, span), F32))
    return pl.pallas_call(
        functools.partial(expert_kernel, len(blocks), len(resident), n_ad, order),
        out_shape=tuple(outs),
        in_specs=[vmem()] * (len(blocks) + 1) + [smem()] * 3 + [vmem()] * 5 + [hbm] * 4 + [vmem()] * len(resident),
        out_specs=(vmem(),) * len(outs),
        scratch_shapes=[
            pltpu.VMEM((n_local, row_count, width), BF16),
            pltpu.VMEM((local_halves, row_count, hidden_count), BF16),
            pltpu.VMEM((local_halves, tenants * rank, hidden_count), BF16),
            pltpu.SemaphoreType.DMA((tenants,)),
            pltpu.VMEM((ring, *resident[0].shape[1:]), BF16),
            semaphores(gate, ring),
        ],
        cost_estimate=SMALL,
        compiler_params=params(min(38, LIMIT_EARLY * count // 512)),
        name="experts",
    )(
        *blocks, mark, ids, adapters, pool_slots, picked, pt, cols, tslot, table_rows, gate, up, down, pool,
        *[pltpu.with_memory_space_constraint(x, pltpu.VMEM) for x in resident],
    )


def write_pairs(total, outs, at=0):
    keep, send = outs
    for b in range(total.shape[0] // 128):
        block = total[b * 128 : b * 128 + 128].astype(BF16)
        (send if b % 2 else keep)[b // 2 * 128 : b // 2 * 128 + 128, pl.ds(at, total.shape[1])] = block


def adapter_kernel(slot_column, ids_ref, base_ref, cols_ref, factor_ref, low_ref, keep, send):
    low = low_ref[0].astype(F32)
    for a in range(1, low_ref.shape[0]):
        low = low + low_ref[a].astype(F32)
    low = low.T.astype(BF16)
    zero = jnp.zeros_like(low)
    slot = cols_ref[:, slot_column : slot_column + 1]
    depth = EXPERT_COUNT * RANK
    slot_count = factor_ref.shape[0] // depth
    total = base_ref[...]
    for j in range(0, slot_count, 2):
        spread = jnp.concatenate(
            [jnp.where(slot == (ids_ref[0] * slot_count + j + i).astype(F32), low, zero) for i in range(2)], axis=1
        )
        total = total + mm(spread, factor_ref[j * depth : (j + 2) * depth])
    write_pairs(total, (keep, send))


def adapter_part(ids, base, cols, slot_column, factors, lows):
    count, span = base.shape
    return pl.pallas_call(
        functools.partial(adapter_kernel, slot_column),
        out_shape=(jax.ShapeDtypeStruct((count // 2, span), BF16),) * 2,
        in_specs=[smem()] + [vmem()] * 4,
        out_specs=(vmem(),) * 2,
        cost_estimate=SMALL,
        compiler_params=params(max(LIMIT, 24 * count * span // MIB)),
        name="adapters",
    )(ids, base, cols, factors, lows)


def per_device(
    n_ep,
    n_ad,
    tokens,
    chosen_experts,
    router_gate_logits,
    token_tenant,
    adapter_of_tenant,
    adapter_pool_slot,
    gate_weight,
    up_weight,
    down_weight,
    adapter_input_factors,
    adapter_output_factors,
):
    gate_weight, up_weight, down_weight, adapter_input_factors = [
        pltpu.with_memory_space_constraint(x, pltpu.HBM)
        for x in (gate_weight, up_weight, down_weight, adapter_input_factors)
    ]
    width = tokens.shape[1]
    span = width // n_ad
    local_halves = gate_weight.shape[0]
    n_local = max(1, local_halves // 2)
    row_count = n_ep * CAP
    bits = n_ep.bit_length() - 1
    ids = jnp.stack([lax.axis_index("ep"), lax.axis_index("ad")]).astype(jnp.int32)

    def swap(x, mask):
        return lax.ppermute(x, "ep", [(i, i ^ mask) for i in range(n_ep)])

    def tie(x, y):
        return lax.optimization_barrier((x, y))

    def shift(x, step):
        return lax.ppermute(x, "ad", [(i, (i + step) % n_ad) for i in range(n_ad)])

    order = sorted(range(1, n_ad), key=lambda step: (step != n_ad // 2, step))
    own = with_facts(tokens, chosen_experts, router_gate_logits, token_tenant)
    *resident, mark = prefetch(ids, gate_weight, up_weight, down_weight, n_ep * tokens.shape[0])
    blocks = {0: own}
    for bit in reversed(range(bits)):
        for mask in list(blocks):
            blocks[mask | 1 << bit] = swap(blocks[mask], 1 << bit)
        if bit == bits - 1:
            blocks[1 << bit], mark = tie(blocks[1 << bit], mark)
    blocks = [blocks[mask] for mask in range(n_ep)]
    picked, pt, cols, table_rows, tslot = build_meta(
        blocks, ids, adapter_of_tenant, adapter_pool_slot, n_local, local_halves, row_count
    )
    keep, send, base = expert_part(
        blocks, mark, ids, adapter_of_tenant, adapter_pool_slot, picked, pt, cols, tslot, table_rows, gate_weight,
        up_weight, down_weight, adapter_input_factors, resident, n_ad, order,
    )

    def added(x, y):
        return (x.astype(F32) + y.astype(F32)).astype(BF16)

    def halves(x, fold):
        grouped = x.reshape(x.shape[0] // 256, 2, 128, x.shape[1])
        low, high = (grouped[:, i].reshape(-1, x.shape[1]) for i in range(2))
        if fold:
            return jnp.concatenate([low, high], axis=1), jnp.concatenate([high, low], axis=1)
        return low, high

    def across(mine, low=None):
        for bit in range(1, bits):
            keep, send = halves(mine, False)
            if low is not None:
                parts = halves(low, True)
                keep, send = (jnp.concatenate([x, part], axis=1) for x, part in zip((keep, send), parts))
            mine = added(keep, swap(send, 1 << bit))
            if low is not None:
                mine, low = mine[:, : keep.shape[1] - parts[0].shape[1]], mine[:, keep.shape[1] - parts[0].shape[1] :]
        return mine, low

    mine = added(keep, swap(send, 1))
    at = span * len(order)
    sums, low = across(mine[:, :span], mine[:, at:])
    results = [shift(sums, order[0])]
    rest, _ = across(mine[:, span:at])
    lows = lax.all_to_all(jnp.broadcast_to(low, (n_ad, *low.shape)), "ad", 0, 0, tiled=True)
    slot_count = adapter_output_factors.shape[0]
    flat_factors = adapter_output_factors.reshape(slot_count * EXPERT_COUNT * RANK, span)
    keep, send = adapter_part(ids, base, cols, 2 * n_local, flat_factors, lows)
    results += [shift(rest[:, i * span : (i + 1) * span], step) for i, step in enumerate(order[1:])]
    results.append(across(added(keep, swap(send, 1)))[0])
    return sum(x.astype(F32) for x in results).astype(BF16)


def solution(mesh):
    placed = (
        P(("rep", "ep"), None),
        P(("rep", "ep"), None),
        P(("rep", "ep"), None),
        P(("rep", "ep")),
        P("rep"),
        P(),
        P("ep", None, "ad"),
        P("ep", None, "ad"),
        P("ep", "ad", None),
        P(None, "ep", None, "ad"),
        P("ep", None, None, "ad"),
    )
    return jax.shard_map(
        functools.partial(per_device, mesh.shape["ep"], mesh.shape["ad"]),
        mesh=mesh,
        in_specs=placed,
        out_specs=P(("rep", "ep"), "ad"),
        check_vma=False,
    )
```

time: 256 us -> 118 us (0.46)
  blocking collectives: 79 us -> 0 us
  matrix products: 48.1 us -> 0 us
  Pallas kernels: 0 us -> 45.5 us
  local copies, waits for them, and re-layouts: 45.4 us -> 9.7 us
  between operations: 15.5 us -> 0.25 us
  starting transfers between devices: 10.3 us -> 20.1 us
  other arithmetic: 12 us -> 3.43 us
  waiting for transfers between devices: 45.1 us -> 39 us
    all_to_all x1 -> x0, blocking collectives: 57.8 us -> none  [per_device(): lax.all_to_all(doubled, 'ep', split_axis=0, concat_axis=1, tiled=True)]
    dot_general x17 -> x0, matrix products: 48.1 us -> none  [the longest x4 17.3 us: per_device(): jnp.dot(block_rows, up_weight[half_index], preferred_element_type=jnp.flo...]
    pallas_call x0 -> x5, Pallas kernels: none -> 45.5 us  [the longest x1 30.9 us: expert_part(): pl.pallas_call(functools.partial(expert_kernel, len(blocks), len(resident...]
    gather x12 -> x0, local copies, waits for them, and re-layouts: 35.2 us -> none  [the longest x4 19.4 us: per_device(): adapter_factors = adapter_input_factors[slot_of_tenant, half_index]]
    reduce_scatter x1 -> x0, waiting for transfers between devices: 32.7 us -> none  [per_device(): lax.psum_scatter(partials.astype(jnp.bfloat16), 'ad', scatter_dimension=2...]
    ppermute x0 -> x11, waiting for transfers between devices: none -> 27.5 us  [the longest x8 21.4 us: swap(): return lax.ppermute(x, 'ep', [(i, i ^ mask) for i in range(n_ep)])]
    psum x1 -> x0, blocking collectives: 21.2 us -> none  [per_device(): lax.psum(lowrank.astype(jnp.bfloat16), 'ad').astype(jnp.float32)]
    ppermute x0 -> x11, starting transfers between devices: none -> 14.9 us  [the longest x8 8.14 us: swap(): return lax.ppermute(x, 'ep', [(i, i ^ mask) for i in range(n_ep)])]
  transfers between devices with their start and end apart: 5 -> 12, of which waited for: 2 -> 7; matrix products, arithmetic and copies ran while one was open for 14% -> 5% of each run, Pallas kernels for 0% -> 10%
where the time goes in v4:
time: 118 us
  Pallas kernels  45.5 us (39%)
  waiting for transfers between devices  39 us (33%)
  starting transfers between devices  20.1 us (17%)
  local copies, waits for them, and re-layouts  9.7 us (8%)
  other arithmetic  3.43 us (3%)
    pallas_call x1, Pallas kernels, expert_part(): pl.pallas_call(functools.partial(expert_kernel, len(blocks), len(resident...  30.9 us
    ppermute x8, waiting for transfers between devices, swap(): return lax.ppermute(x, 'ep', [(i, i ^ mask) for i in range(n_ep)])  21.4 us
    all_to_all x1, waiting for transfers between devices, per_device(): lax.all_to_all(jnp.broadcast_to(low, (n_ad, *low.shape)), 'ad', 0, 0, til...  11.5 us
    pallas_call x1, Pallas kernels, prefetch(): pl.pallas_call(prefetch_kernel, out_shape=(*[pltpu.VMEM(shape, BF16) for...  8.99 us
    ppermute x8, starting transfers between devices, swap(): return lax.ppermute(x, 'ep', [(i, i ^ mask) for i in range(n_ep)])  8.14 us
    ppermute x3, starting transfers between devices, shift(): return lax.ppermute(x, 'ad', [(i, (i + step) % n_ad) for i in range(n_ad)])  6.79 us
    ppermute x3, waiting for transfers between devices, shift(): return lax.ppermute(x, 'ad', [(i, (i + step) % n_ad) for i in range(n_ad)])  6.06 us
    all_to_all x1, starting transfers between devices, per_device(): lax.all_to_all(jnp.broadcast_to(low, (n_ad, *low.shape)), 'ad', 0, 0, til...  5.13 us
  transfers between devices with their start and end apart: 12, of which 7 were waited for; matrix products, arithmetic and copies ran while one was open for 5% of the time, Pallas kernels for 10%

profile of v4, /device:TPU:0, one launch (start us, length us, event | category | flops | bytes accessed | tf_op | source)
XLA Modules:
  0.0 118.0 jit_solution(9407496886059610419)
XLA Ops:
  0.0 0.8 copy.12.chosen_ref
  0.8 0.8 copy.13.logits_ref
  1.6 0.6 copy-done.9
  2.2 1.1 tokens_with_facts.1.refs_0_
  3.4 3.0 %collective-permute-start.1 = (bf16[128,3200]{1,0:T(8,128)(2,1)S(1)}, bf16[128,3200]{1,0:T(8,128)(2,1)S(1)}, u32[]{:S(2)}, u32[]{:S(2)}) collective-permute-start(bf16[128,3200]{1,0:T(8,128)(2,1)S(1)} %tokens_with_facts.1.refs_0_), channel_id=1, source_target_pairs={{0,8},{4,12},{8,0},{12,4},{1,9},{5,13},{9,1},{13,5},{2,10},{6,14},... | collective-permute-start | bytes 2457608 | tf_op jit(solution)/shard_map/ppermute | solution.py:432
  6.4 0.0 collective-permute-start
  6.4 0.1 pad_add_fusion.ids_ref.refs_5_
  6.5 9.0 %weight_prefetch.1 = (bf16[2,3072,512]{2,1,0:T(8,128)(2,1)S(1)}, bf16[2,3072,512]{2,1,0:T(8,128)(2,1)S(1)}, bf16[2,3072,512]{2,1,0:T(8,128)(2,1)S(1)}, bf16[2,3072,512]{2,1,0:T(8,128)(2,1)S(1)}, f32[8,128]{1,0:T(8,128)S(1)}) custom-call(s32[2]{0:T(128)S(1)} %pad_add_fusion.ids_ref.refs_5_, bf16[4,3072,1024]{2,1,0:T(8,128)(2,1)} %refs_13_.1, ...), custom_call_target="tpu_custom_call" | custom-call | flops 1 | bytes 1 | tf_op jit(solution)/shard_map/weight_prefetch/pallas_call | solution.py:223
  15.5 9.2 %collective-permute-done.1.refs_2_ = bf16[128,3200]{1,0:T(8,128)(2,1)S(1)} collective-permute-done((bf16[128,3200]{1,0:T(8,128)(2,1)S(1)}, bf16[128,3200]{1,0:T(8,128)(2,1)S(1)}, u32[]{:S(2)}, u32[]{:S(2)}) %collective-permute-start.1) | collective-permute-done | bytes 819232 | tf_op jit(solution)/shard_map/ppermute | solution.py:432
  24.6 0.0 collective-permute-start.2
  24.6 0.0 collective-permute-done.refs_1_
  24.7 2.3 %collective-permute-done.2.refs_3_ = bf16[128,3200]{1,0:T(8,128)(2,1)S(1)} collective-permute-done((bf16[128,3200]{1,0:T(8,128)(2,1)S(1)}, bf16[128,3200]{1,0:T(8,128)(2,1)S(1)}, u32[]{:S(2)}, u32[]{:S(2)}) %collective-permute-start.2) | collective-permute-done | bytes 819232 | tf_op jit(solution)/shard_map/ppermute | solution.py:432
  27.0 0.0 copy-done.8
  27.0 0.0 copy-start.3
  27.0 1.1 routing_tables.1
  28.1 30.9 %experts.1 = (bf16[256,2560]{1,0:T(8,128)(2,1)S(1)}, bf16[256,2560]{1,0:T(8,128)(2,1)S(1)}, f32[512,768]{1,0:T(8,128)S(1)}) custom-call(bf16[128,3200]{1,0:T(8,128)(2,1)} %copy-done, bf16[128,3200]{1,0:T(8,128)(2,1)} %copy-done.2, bf16[128,3200]{1,0:T(8,128)(2,1)} %copy-done.1, bf16[128,3200]{1,0:T(8,128)(2,1)} %copy-done.3, ...), custom_call_target="tpu_custom_call" | custom-call | flops 1 | bytes 1 | tf_op jit(solution)/shard_map/experts/pallas_call | solution.py:344
  59.1 0.0 copy-start.5
  59.1 0.2 collective-permute-start.3
  59.3 2.9 %collective-permute-done.3 = bf16[256,2560]{1,0:T(8,128)(2,1)S(1)} collective-permute-done((bf16[256,2560]{1,0:T(8,128)(2,1)S(1)}, bf16[256,2560]{1,0:T(8,128)(2,1)S(1)}, u32[]{:S(2)}, u32[]{:S(2)}) %collective-permute-start.3) | collective-permute-done | bytes 1310752 | tf_op jit(solution)/shard_map/ppermute | solution.py:432
  62.2 0.3 add_convert_fusion
  62.7 0.0 copy-start.4
  62.7 1.8 %collective-permute-start.4 = (bf16[128,1280]{1,0:T(8,128)(2,1)S(1)}, bf16[128,1280]{1,0:T(8,128)(2,1)S(1)}, u32[]{:S(2)}, u32[]{:S(2)}) collective-permute-start(bf16[128,1280]{1,0:T(8,128)(2,1)S(1)} %pad_maximum_fusion), channel_id=1, source_target_pairs={{0,8},{4,12},{8,0},{12,4},{1,9},{5,13},{9,1},{13,5},{2,10},{6,14},... | collective-permute-start | bytes 983048 | tf_op jit(solution)/shard_map/ppermute | solution.py:432
  64.5 1.0 slice.67
  65.4 7.0 %collective-permute-done.4 = bf16[128,1280]{1,0:T(8,128)(2,1)S(1)} collective-permute-done((bf16[128,1280]{1,0:T(8,128)(2,1)S(1)}, bf16[128,1280]{1,0:T(8,128)(2,1)S(1)}, u32[]{:S(2)}, u32[]{:S(2)}) %collective-permute-start.4) | collective-permute-done | bytes 327712 | tf_op jit(solution)/shard_map/ppermute | solution.py:432
  72.5 0.1 add_convert_fusion.2
  72.6 0.7 copy-done.11
  73.3 0.8 broadcast_in_dim.3
  74.2 5.1 %all-to-all-start = ((bf16[4,128,512]{2,1,0:T(8,128)(2,1)}), bf16[4,128,512]{2,1,0:T(8,128)(2,1)}, u32[]{:S(2)}, u32[]{:S(2)}) async-start(bf16[4,128,512]{2,1,0:T(8,128)(2,1)} %broadcast_in_dim.3), calls=%async_computation | async-start | bytes 1048576 | tf_op jit(solution)/shard_map/all_to_all | solution.py:484
  79.3 1.8 %slice_bitcast_fusion = bf16[128,1536]{1,0:T(8,128)(2,1)} fusion(bf16[1,2,128,1536]{3,2,1,0:T(8,128)(2,1)} %bitcast.32), kind=kLoop, calls=%fused_computation.5 | loop fusion | bytes 786432 | tf_op jit(solution)/shard_map/reshape;squeeze | solution.py:463
  81.1 1.5 %collective-permute-start.6 = (bf16[128,1536]{1,0:T(8,128)(2,1)}, bf16[128,1536]{1,0:T(8,128)(2,1)}, u32[]{:S(2)}, u32[]{:S(2)}) collective-permute-start(bf16[128,1536]{1,0:T(8,128)(2,1)} %slice_bitcast_fusion), channel_id=1, source_target_pairs={{0,8},{4,12},{8,0},{12,4},{1,9},{5,13},{9,1},{13,5},{2,10},{6,14},... | collective-permute-start | bytes 1179656 | tf_op jit(solution)/shard_map/ppermute | solution.py:432
  82.5 1.6 %slice.66 = bf16[128,768]{1,0:T(8,128)(2,1)} slice(bf16[128,1280]{1,0:T(8,128)(2,1)} %copy-done.11), slice={[0:128], [0:768]} | slice | bytes 393216 | tf_op jit(solution)/shard_map/slice | solution.py:476
  84.2 2.9 %collective-permute-start.5 = (bf16[128,768]{1,0:T(8,128)(2,1)}, bf16[128,768]{1,0:T(8,128)(2,1)}, u32[]{:S(2)}, u32[]{:S(2)}) collective-permute-start(bf16[128,768]{1,0:T(8,128)(2,1)} %slice.66), channel_id=1, source_target_pairs={{0,2},{1,3},{2,0},{3,1},{4,6},{5,7},{6,4},{7,5},{8,10},{9,11},{10,... | collective-permute-start | bytes 589832 | tf_op jit(solution)/shard_map/ppermute | solution.py:438
  87.1 11.5 %all-to-all-done.low_ref = bf16[4,128,512]{2,1,0:T(8,128)(2,1)} async-done(((bf16[4,128,512]{2,1,0:T(8,128)(2,1)}), bf16[4,128,512]{2,1,0:T(8,128)(2,1)}, u32[]{:S(2)}, u32[]{:S(2)}) %all-to-all-start) | async-done | bytes 524320 | tf_op jit(solution)/shard_map/all_to_all | solution.py:484
  98.6 1.4 %copy-done.6 = f32[512,768]{1,0:T(8,128)S(1)} copy-done((f32[512,768]{1,0:T(8,128)S(1)}, f32[512,768]{1,0:T(8,128)}, u32[]{:S(2)}) %copy-start.6) | copy-done | bytes 1572888
  100.0 3.3 %adapters.1 = (bf16[256,768]{1,0:T(8,128)(2,1)S(1)}, bf16[256,768]{1,0:T(8,128)(2,1)S(1)}) custom-call(s32[2]{0:T(128)S(1)} %pad_add_fusion.ids_ref.refs_5_, f32[512,768]{1,0:T(8,128)S(1)} %copy-done.6, f32[512,128]{1,0:T(8,128)S(1)} %get-tuple-element.27.refs_10_.cols_ref, bf16[2048,768]{1,0:T(8,128)(2,1)S(1)} %bitcast.30, ...), custom_call_target="tpu_custom_call" | custom-call | flops 1 | bytes 1 | tf_op jit(solution)/shard_map/adapters/pallas_call | solution.py:393
  103.4 0.1 collective-permute-start.9
  103.5 0.0 collective-permute-done.6
  103.5 1.1 fusion
  104.6 0.1 collective-permute-start.7
  104.7 3.8 %collective-permute-start.8 = (bf16[128,768]{1,0:T(8,128)(2,1)S(1)}, bf16[128,768]{1,0:T(8,128)(2,1)S(1)}, u32[]{:S(2)}, u32[]{:S(2)}) collective-permute-start(bf16[128,768]{1,0:T(8,128)(2,1)S(1)} %get-tuple-element.42), channel_id=1, source_target_pairs={{0,3},{1,0},{2,1},{3,2},{4,7},{5,4},{6,5},{7,6},{8,11},{9,8},{10,9... | collective-permute-start | bytes 589832 | tf_op jit(solution)/shard_map/ppermute | solution.py:438
  108.5 0.0 collective-permute-done.9
  108.5 0.1 add_convert_fusion.1
  108.6 1.6 %collective-permute-start.10 = (bf16[128,768]{1,0:T(8,128)(2,1)S(1)}, bf16[128,768]{1,0:T(8,128)(2,1)S(1)}, u32[]{:S(2)}, u32[]{:S(2)}) collective-permute-start(bf16[128,768]{1,0:T(8,128)(2,1)S(1)} %slice_bitcast_fusion.2), channel_id=1, source_target_pairs={{0,8},{4,12},{8,0},{12,4},{1,9},{5,13},{9,1},{13,5},{2,10},{6,14},... | collective-permute-start | bytes 589832 | tf_op jit(solution)/shard_map/ppermute | solution.py:432
  110.2 0.0 collective-permute-done.5
  110.2 4.0 %collective-permute-done.7 = bf16[128,768]{1,0:T(8,128)(2,1)S(1)} collective-permute-done((bf16[128,768]{1,0:T(8,128)(2,1)S(1)}, bf16[128,768]{1,0:T(8,128)(2,1)S(1)}, u32[]{:S(2)}, u32[]{:S(2)}) %collective-permute-start.7) | collective-permute-done | bytes 196640 | tf_op jit(solution)/shard_map/ppermute | solution.py:438
  114.2 2.0 %collective-permute-done.8 = bf16[128,768]{1,0:T(8,128)(2,1)S(1)} collective-permute-done((bf16[128,768]{1,0:T(8,128)(2,1)S(1)}, bf16[128,768]{1,0:T(8,128)(2,1)S(1)}, u32[]{:S(2)}, u32[]{:S(2)}) %collective-permute-start.8) | collective-permute-done | bytes 196640 | tf_op jit(solution)/shard_map/ppermute | solution.py:438
  116.3 0.0 collective-permute-done.10
  116.3 1.7 %add_convert_fusion.3 = bf16[128,768]{1,0:T(8,128)(2,1)} fusion(bf16[128,768]{1,0:T(8,128)(2,1)S(1)} %collective-permute-done.8, bf16[128,768]{1,0:T(8,128)(2,1)S(1)} %collective-permute-done.7, bf16[128,768]{1,0:T(8,128)(2,1)} %collective-permute-done.5, bf16[128,768]{1,0:T(8,128)(2,1)S(1)} %collective-permute-done.10, bf16[1,2,128,768]{3,2,1,0:T(8,128)(2,1)S(1)} %bitcast.35), kind=kLoop, calls=%fused_computation.9 | loop fusion | flops 1179648 | bytes 1179648 | tf_op jit(solution)/shard_map/convert_element_type | solution.py:490
  (25 shorter events, 0.2 us)
Async XLA Ops:
  1.6 0.7 copy-start.9
  3.4 23.6 %copy-start = (bf16[128,3200]{1,0:T(8,128)(2,1)}, bf16[128,3200]{1,0:T(8,128)(2,1)S(1)}, u32[]{:S(2)}) copy-start(bf16[128,3200]{1,0:T(8,128)(2,1)S(1)} %tokens_with_facts.1.refs_0_) | copy-start | bytes 2457604
  3.4 21.2 %collective-permute-start.1 = (bf16[128,3200]{1,0:T(8,128)(2,1)S(1)}, bf16[128,3200]{1,0:T(8,128)(2,1)S(1)}, u32[]{:S(2)}, u32[]{:S(2)}) collective-permute-start(bf16[128,3200]{1,0:T(8,128)(2,1)S(1)} %tokens_with_facts.1.refs_0_), channel_id=1, source_target_pairs={{0,8},{4,12},{8,0},{12,4},{1,9},{5,13},{9,1},{13,5},{2,10},{6,14},... | collective-permute-start | bytes 2457608 | tf_op jit(solution)/shard_map/ppermute | solution.py:432
  6.4 18.3 %collective-permute-start = (bf16[128,3200]{1,0:T(8,128)(2,1)S(1)}, bf16[128,3200]{1,0:T(8,128)(2,1)S(1)}, u32[]{:S(2)}, u32[]{:S(2)}) collective-permute-start(bf16[128,3200]{1,0:T(8,128)(2,1)S(1)} %tokens_with_facts.1.refs_0_), channel_id=1, source_target_pairs={{0,4},{4,0},{8,12},{12,8},{1,5},{5,1},{9,13},{13,9},{2,6},{6,2},{1... | collective-permute-start | bytes 2457608 | tf_op jit(solution)/shard_map/ppermute | solution.py:432
  6.5 20.5 %copy-start.7 = (s32[16]{0:T(128)S(1)}, s32[16]{0:T(128)}, u32[]{:S(2)}) copy-start(s32[16]{0:T(128)} %refs_6_.1) | copy-start | bytes 196
  6.5 20.5 %copy-start.8 = (s32[64]{0:T(128)S(1)}, s32[64]{0:T(128)}, u32[]{:S(2)}) copy-start(s32[64]{0:T(128)} %refs_7_.1) | copy-start | bytes 772
  24.6 3.5 %copy-start.1 = (bf16[128,3200]{1,0:T(8,128)(2,1)}, bf16[128,3200]{1,0:T(8,128)(2,1)S(1)}, u32[]{:S(2)}) copy-start(bf16[128,3200]{1,0:T(8,128)(2,1)S(1)} %collective-permute-done.1.refs_2_) | copy-start | bytes 2457604
  24.6 2.3 %collective-permute-start.2 = (bf16[128,3200]{1,0:T(8,128)(2,1)S(1)}, bf16[128,3200]{1,0:T(8,128)(2,1)S(1)}, u32[]{:S(2)}, u32[]{:S(2)}) collective-permute-start(bf16[128,3200]{1,0:T(8,128)(2,1)S(1)} %collective-permute-done.1.refs_2_), channel_id=1, source_target_pairs={{0,4},{4,0},{8,12},{12,8},{1,5},{5,1},{9,13},{13,9},{2,6},{6,2},{1... | collective-permute-start | bytes 2457608 | tf_op jit(solution)/shard_map/ppermute | solution.py:432
  24.6 3.5 %copy-start.2 = (bf16[128,3200]{1,0:T(8,128)(2,1)}, bf16[128,3200]{1,0:T(8,128)(2,1)S(1)}, u32[]{:S(2)}) copy-start(bf16[128,3200]{1,0:T(8,128)(2,1)S(1)} %collective-permute-done.refs_1_) | copy-start | bytes 2457604
  27.0 1.1 copy-start.3
  59.1 3.5 %copy-start.5 = (f32[512,768]{1,0:T(8,128)}, f32[512,768]{1,0:T(8,128)S(1)}, u32[]{:S(2)}) copy-start(f32[512,768]{1,0:T(8,128)S(1)} %get-tuple-element.36.base_ref) | copy-start | bytes 4718596
  59.1 3.1 %collective-permute-start.3 = (bf16[256,2560]{1,0:T(8,128)(2,1)S(1)}, bf16[256,2560]{1,0:T(8,128)(2,1)S(1)}, u32[]{:S(2)}, u32[]{:S(2)}) collective-permute-start(bf16[256,2560]{1,0:T(8,128)(2,1)S(1)} %get-tuple-element.35), channel_id=1, source_target_pairs={{0,4},{4,0},{8,12},{12,8},{1,5},{5,1},{9,13},{13,9},{2,6},{6,2},{1... | collective-permute-start | bytes 3932168 | tf_op jit(solution)/shard_map/ppermute | solution.py:432
  62.7 36.0 %copy-start.4 = (bf16[16,8,16,768]{3,2,1,0:T(8,128)(2,1)S(1)}, bf16[16,8,16,768]{3,2,1,0:T(8,128)(2,1)}, u32[]{:S(2)}) copy-start(bf16[16,8,16,768]{3,2,1,0:T(8,128)(2,1)} %param.21) | copy-start | bytes 9437188
  62.7 9.8 %collective-permute-start.4 = (bf16[128,1280]{1,0:T(8,128)(2,1)S(1)}, bf16[128,1280]{1,0:T(8,128)(2,1)S(1)}, u32[]{:S(2)}, u32[]{:S(2)}) collective-permute-start(bf16[128,1280]{1,0:T(8,128)(2,1)S(1)} %pad_maximum_fusion), channel_id=1, source_target_pairs={{0,8},{4,12},{8,0},{12,4},{1,9},{5,13},{9,1},{13,5},{2,10},{6,14},... | collective-permute-start | bytes 983048 | tf_op jit(solution)/shard_map/ppermute | solution.py:432
  72.6 0.7 copy-start.11
  74.2 24.5 %all-to-all-start = ((bf16[4,128,512]{2,1,0:T(8,128)(2,1)}), bf16[4,128,512]{2,1,0:T(8,128)(2,1)}, u32[]{:S(2)}, u32[]{:S(2)}) async-start(bf16[4,128,512]{2,1,0:T(8,128)(2,1)} %broadcast_in_dim.3), calls=%async_computation | async-start | bytes 1048576 | tf_op jit(solution)/shard_map/all_to_all | solution.py:484
  81.1 22.4 %collective-permute-start.6 = (bf16[128,1536]{1,0:T(8,128)(2,1)}, bf16[128,1536]{1,0:T(8,128)(2,1)}, u32[]{:S(2)}, u32[]{:S(2)}) collective-permute-start(bf16[128,1536]{1,0:T(8,128)(2,1)} %slice_bitcast_fusion), channel_id=1, source_target_pairs={{0,8},{4,12},{8,0},{12,4},{1,9},{5,13},{9,1},{13,5},{2,10},{6,14},... | collective-permute-start | bytes 1179656 | tf_op jit(solution)/shard_map/ppermute | solution.py:432
  84.2 26.0 %collective-permute-start.5 = (bf16[128,768]{1,0:T(8,128)(2,1)}, bf16[128,768]{1,0:T(8,128)(2,1)}, u32[]{:S(2)}, u32[]{:S(2)}) collective-permute-start(bf16[128,768]{1,0:T(8,128)(2,1)} %slice.66), channel_id=1, source_target_pairs={{0,2},{1,3},{2,0},{3,1},{4,6},{5,7},{6,4},{7,5},{8,10},{9,11},{10,... | collective-permute-start | bytes 589832 | tf_op jit(solution)/shard_map/ppermute | solution.py:438
  98.6 1.4 %copy-start.6 = (f32[512,768]{1,0:T(8,128)S(1)}, f32[512,768]{1,0:T(8,128)}, u32[]{:S(2)}) copy-start(f32[512,768]{1,0:T(8,128)} %copy-done.5) | copy-start | bytes 4718596
  100.0 3.4 %copy-start.10 = (bf16[256,1536]{1,0:T(8,128)(2,1)S(1)}, bf16[256,1536]{1,0:T(8,128)(2,1)}, u32[]{:S(2)}) copy-start(bf16[256,1536]{1,0:T(8,128)(2,1)} %slice.67) | copy-start | bytes 2359300
  103.4 5.1 %collective-permute-start.9 = (bf16[256,768]{1,0:T(8,128)(2,1)S(1)}, bf16[256,768]{1,0:T(8,128)(2,1)S(1)}, u32[]{:S(2)}, u32[]{:S(2)}) collective-permute-start(bf16[256,768]{1,0:T(8,128)(2,1)S(1)} %get-tuple-element.38), channel_id=1, source_target_pairs={{0,4},{4,0},{8,12},{12,8},{1,5},{5,1},{9,13},{13,9},{2,6},{6,2},{1... | collective-permute-start | bytes 1179656 | tf_op jit(solution)/shard_map/ppermute | solution.py:432
  104.6 9.6 %collective-permute-start.7 = (bf16[128,768]{1,0:T(8,128)(2,1)S(1)}, bf16[128,768]{1,0:T(8,128)(2,1)S(1)}, u32[]{:S(2)}, u32[]{:S(2)}) collective-permute-start(bf16[128,768]{1,0:T(8,128)(2,1)S(1)} %get-tuple-element.41), channel_id=1, source_target_pairs={{0,1},{1,2},{2,3},{3,0},{4,5},{5,6},{6,7},{7,4},{8,9},{9,10},{10,1... | collective-permute-start | bytes 589832 | tf_op jit(solution)/shard_map/ppermute | solution.py:438
  104.7 11.6 %collective-permute-start.8 = (bf16[128,768]{1,0:T(8,128)(2,1)S(1)}, bf16[128,768]{1,0:T(8,128)(2,1)S(1)}, u32[]{:S(2)}, u32[]{:S(2)}) collective-permute-start(bf16[128,768]{1,0:T(8,128)(2,1)S(1)} %get-tuple-element.42), channel_id=1, source_target_pairs={{0,3},{1,0},{2,1},{3,2},{4,7},{5,4},{6,5},{7,6},{8,11},{9,8},{10,9... | collective-permute-start | bytes 589832 | tf_op jit(solution)/shard_map/ppermute | solution.py:438
  108.6 7.6 %collective-permute-start.10 = (bf16[128,768]{1,0:T(8,128)(2,1)S(1)}, bf16[128,768]{1,0:T(8,128)(2,1)S(1)}, u32[]{:S(2)}, u32[]{:S(2)}) collective-permute-start(bf16[128,768]{1,0:T(8,128)(2,1)S(1)} %slice_bitcast_fusion.2), channel_id=1, source_target_pairs={{0,8},{4,12},{8,0},{12,4},{1,9},{5,13},{9,1},{13,5},{2,10},{6,14},... | collective-permute-start | bytes 589832 | tf_op jit(solution)/shard_map/ppermute | solution.py:432

commit v5 on v4

--- a/solution.py
+++ b/solution.py
@@ -13,7 +13,7 @@
 RANK = 16
 CAP = 48
 LIMIT = 16
-LIMIT_EARLY = 24
+LIMIT_EARLY = 21
 N_TILE = 512
 HELD_EACH = 2
 HELD_ARRAYS = 4
@@ -165,8 +165,15 @@
         slot = number if number < self.first else (number - self.first) % self.capacity
         if number < self.early:
             half, tile, which = number // (2 * self.tiles), number // 2 % self.tiles, number % 2
-            source = self.sources[which].at[half, :, pl.ds(tile * self.width, self.width)]
-            return [pltpu.make_async_copy(source, place, self.sems.at[slot, 0])]
+            rows = self.depth // 2
+            return [
+                pltpu.make_async_copy(
+                    self.sources[which].at[half, pl.ds(i * rows, rows), pl.ds(tile * self.width, self.width)],
+                    place.at[pl.ds(i * rows, rows)],
+                    self.sems.at[slot, i],
+                )
+                for i in range(2)
+            ]
         made = []
         for i in range(self.held):
             piece = (number - self.early) * self.held + i
@@ -205,7 +212,7 @@
 
 
 def semaphores(gate, slots):
-    return pltpu.SemaphoreType.DMA((slots, max(1, gate.shape[1] // gate.shape[2])))
+    return pltpu.SemaphoreType.DMA((slots, max(2, gate.shape[1] // gate.shape[2])))
 
 
 def prefetch_kernel(ids_ref, gate_ref, up_ref, down_ref, *refs):
@@ -237,7 +244,7 @@
     ids_ref, adapter_ref, pool_slot_ref, p_ref, pt_ref, cols_ref, tslot_ref, rows_ref = refs[1:9]
     gate_ref, up_ref, down_ref, pool_ref = refs[9:13]
     resident, refs = refs[13 : 13 + n_resident], refs[13 + n_resident :]
-    keep, send, base, packed, hidden, factors, factor_sems, ring, sems = refs
+    keep, send, keep_rest, send_rest, base, packed, hidden, factors, factor_sems, ring, sems = refs
     slabs = Slabs(gate_ref, up_ref, down_ref, resident, ring, sems)
     n_local = p_ref.shape[0]
     local_halves, depth, _ = gate_ref.shape
@@ -279,7 +286,7 @@
             span = slice(tile * slabs.width, (tile + 1) * slabs.width)
             hidden[half, :, span] = (jax.nn.silu(values[0]) * values[1]).astype(BF16)
     span = base.shape[1]
-    at = span * len(order)
+    at = span
     for copy in factor_copies:
         copy.wait()
     for out in (keep, send):
@@ -325,9 +332,13 @@
             def _():
                 base[:, inside : inside + part] = value
 
-            @pl.when(step != 0)
+            @pl.when(step == order[0])
             def _():
-                write_pairs(value, (keep, send), pl.multiple_of(position * span + inside, 128))
+                write_pairs(value, (keep, send), inside)
+
+            @pl.when((step != 0) & (step != order[0]))
+            def _():
+                write_pairs(value, (keep_rest, send_rest), pl.multiple_of((position - 1) * span + inside, 128))
 
 
 def expert_part(
@@ -339,7 +350,8 @@
     span = down.shape[2] // n_ad
     hbm = pl.BlockSpec(memory_space=pltpu.HBM)
     ring = ring_size(gate, down, resident)
-    outs = [pltpu.VMEM((count // 2, span * len(order) + 256), BF16)] * 2
+    outs = [pltpu.VMEM((count // 2, span + 256), BF16)] * 2
+    outs += [pltpu.VMEM((count // 2, span * (len(order) - 1)), BF16)] * 2
     outs.append(pltpu.VMEM((count, span), F32))
     return pl.pallas_call(
         functools.partial(expert_kernel, len(blocks), len(resident), n_ad, order),
@@ -370,11 +382,8 @@
         (send if b % 2 else keep)[b // 2 * 128 : b // 2 * 128 + 128, pl.ds(at, total.shape[1])] = block
 
 
-def adapter_kernel(slot_column, ids_ref, base_ref, cols_ref, factor_ref, low_ref, keep, send):
-    low = low_ref[0].astype(F32)
-    for a in range(1, low_ref.shape[0]):
-        low = low + low_ref[a].astype(F32)
-    low = low.T.astype(BF16)
+def adapter_kernel(slot_column, ids_ref, base_ref, cols_ref, factor_ref, low_ref, other_ref, keep, send):
+    low = (low_ref[...].astype(F32) + other_ref[...].astype(F32)).T.astype(BF16)
     zero = jnp.zeros_like(low)
     slot = cols_ref[:, slot_column : slot_column + 1]
     depth = EXPERT_COUNT * RANK
@@ -388,17 +397,64 @@
     write_pairs(total, (keep, send))
 
 
-def adapter_part(ids, base, cols, slot_column, factors, lows):
+def adapter_part(ids, base, cols, slot_column, factors, low, other):
     count, span = base.shape
     return pl.pallas_call(
         functools.partial(adapter_kernel, slot_column),
         out_shape=(jax.ShapeDtypeStruct((count // 2, span), BF16),) * 2,
-        in_specs=[smem()] + [vmem()] * 4,
+        in_specs=[smem()] + [vmem()] * 5,
         out_specs=(vmem(),) * 2,
         cost_estimate=SMALL,
         compiler_params=params(max(LIMIT, 24 * count * span // MIB)),
         name="adapters",
-    )(ids, base, cols, factors, lows)
+    )(ids, base, cols, factors, low, other)
+
+
+def split_kernel(wide, keep_ref, came_ref, keep, send):
+    blocks = keep_ref.shape[0] // 128
+    low = keep_ref.shape[1] - wide
+    for b in range(blocks):
+        total = keep_ref[b * 128 : b * 128 + 128].astype(F32) + came_ref[b * 128 : b * 128 + 128].astype(F32)
+        total = total.astype(BF16)
+        rows = slice(b // 2 * 128, b // 2 * 128 + 128)
+        (send if b % 2 else keep)[rows, 0:wide] = total[:, 0:wide]
+        if low:
+            for place, out in enumerate((keep, send)):
+                lane = wide + (b % 2 ^ place) * low
+                out[rows, lane : lane + low] = total[:, wide:]
+
+
+def split_sum(keep, came, wide):
+    rows, columns = keep.shape
+    shape = jax.ShapeDtypeStruct((rows // 2, wide + 2 * (columns - wide)), BF16)
+    return pl.pallas_call(
+        functools.partial(split_kernel, wide),
+        out_shape=(shape, shape),
+        in_specs=[vmem()] * 2,
+        out_specs=(vmem(),) * 2,
+        cost_estimate=SMALL,
+        compiler_params=params(LIMIT),
+        name="sum_and_split",
+    )(keep, came)
+
+
+def cut_kernel(edges, keep_ref, came_ref, *outs):
+    for first, last, out in zip(edges, edges[1:], outs):
+        out[...] = (keep_ref[:, first:last].astype(F32) + came_ref[:, first:last].astype(F32)).astype(BF16)
+
+
+def cut_sum(keep, came, edges):
+    return pl.pallas_call(
+        functools.partial(cut_kernel, edges),
+        out_shape=tuple(
+            jax.ShapeDtypeStruct((keep.shape[0], last - first), BF16) for first, last in zip(edges, edges[1:])
+        ),
+        in_specs=[vmem()] * 2,
+        out_specs=(vmem(),) * (len(edges) - 1),
+        cost_estimate=SMALL,
+        compiler_params=params(LIMIT),
+        name="sum_and_cut",
+    )(keep, came)
 
 
 def per_device(
@@ -450,44 +506,43 @@
     picked, pt, cols, table_rows, tslot = build_meta(
         blocks, ids, adapter_of_tenant, adapter_pool_slot, n_local, local_halves, row_count
     )
-    keep, send, base = expert_part(
+    keep, send, keep_rest, send_rest, base = expert_part(
         blocks, mark, ids, adapter_of_tenant, adapter_pool_slot, picked, pt, cols, tslot, table_rows, gate_weight,
         up_weight, down_weight, adapter_input_factors, resident, n_ad, order,
     )
 
-    def added(x, y):
-        return (x.astype(F32) + y.astype(F32)).astype(BF16)
-
-    def halves(x, fold):
-        grouped = x.reshape(x.shape[0] // 256, 2, 128, x.shape[1])
-        low, high = (grouped[:, i].reshape(-1, x.shape[1]) for i in range(2))
-        if fold:
-            return jnp.concatenate([low, high], axis=1), jnp.concatenate([high, low], axis=1)
-        return low, high
-
-    def across(mine, low=None):
-        for bit in range(1, bits):
-            keep, send = halves(mine, False)
-            if low is not None:
-                parts = halves(low, True)
-                keep, send = (jnp.concatenate([x, part], axis=1) for x, part in zip((keep, send), parts))
-            mine = added(keep, swap(send, 1 << bit))
-            if low is not None:
-                mine, low = mine[:, : keep.shape[1] - parts[0].shape[1]], mine[:, keep.shape[1] - parts[0].shape[1] :]
-        return mine, low
-
-    mine = added(keep, swap(send, 1))
-    at = span * len(order)
-    sums, low = across(mine[:, :span], mine[:, at:])
+    def across(keep, came, wide, edges):
+        for bit in range(2, bits):
+            keep, send = split_sum(keep, came, wide)
+            came = swap(send, 1 << bit)
+        return cut_sum(keep, came, edges)
+
+    came, came_rest = swap(send, 1), swap(send_rest, 1)
+    wide = span * (n_ad - 2)
+    if bits > 1:
+        keep, send = split_sum(keep, came, span)
+        keep_rest, send_rest = split_sum(keep_rest, came_rest, wide)
+        came = swap(send, 2)
+        came, keep_rest = tie(came, keep_rest)
+        came_rest = swap(send_rest, 2)
+    sums, low = across(keep, came, span, (0, span, span + n_ep * 128))
+    low_steps = n_ad.bit_length() - 1
+    for bit in range(low_steps):
+        other = lax.ppermute(low, "ad", [(i, i ^ 1 << bit) for i in range(n_ad)])
+        if bit < low_steps - 1:
+            low = (low.astype(F32) + other.astype(F32)).astype(BF16)
+    came_rest, other = tie(came_rest, other)
+    rest = across(keep_rest, came_rest, wide, [span * i for i in range(n_ad - 1)])
     results = [shift(sums, order[0])]
-    rest, _ = across(mine[:, span:at])
-    lows = lax.all_to_all(jnp.broadcast_to(low, (n_ad, *low.shape)), "ad", 0, 0, tiled=True)
     slot_count = adapter_output_factors.shape[0]
     flat_factors = adapter_output_factors.reshape(slot_count * EXPERT_COUNT * RANK, span)
-    keep, send = adapter_part(ids, base, cols, 2 * n_local, flat_factors, lows)
-    results += [shift(rest[:, i * span : (i + 1) * span], step) for i, step in enumerate(order[1:])]
-    results.append(across(added(keep, swap(send, 1)))[0])
-    return sum(x.astype(F32) for x in results).astype(BF16)
+    keep, send = adapter_part(ids, base, cols, 2 * n_local, flat_factors, low, other)
+    results += [shift(x, step) for x, step in zip(rest, order[1:])]
+    came = swap(send, 1)
+    for bit in range(1, bits):
+        keep, send = split_sum(keep, came, span)
+        came = swap(send, 1 << bit)
+    return sum(x.astype(F32) for x in [keep, came] + results).astype(BF16)
 
 
 def solution(mesh):

time: 118 us -> 105 us (0.89)
  local copies, waits for them, and re-layouts: 9.7 us -> 2.23 us
  other arithmetic: 3.43 us -> 0.91 us
  Pallas kernels: 45.5 us -> 44.1 us
  waiting for transfers between devices: 39 us -> 37.8 us
    all_to_all x1 -> x0, waiting for transfers between devices: 11.5 us -> none  [per_device(): lax.all_to_all(jnp.broadcast_to(low, (n_ad, *low.shape)), 'ad', 0, 0, til...]
    ppermute x0 -> x2, waiting for transfers between devices: none -> 6.25 us  [per_device(): other = lax.ppermute(low, 'ad', [(i, i ^ 1 << bit) for i in range(n_ad)])]
    all_to_all x1 -> x0, starting transfers between devices: 5.13 us -> none  [per_device(): lax.all_to_all(jnp.broadcast_to(low, (n_ad, *low.shape)), 'ad', 0, 0, til...]
    ppermute x0 -> x2, starting transfers between devices: none -> 4.82 us  [per_device(): other = lax.ppermute(low, 'ad', [(i, i ^ 1 << bit) for i in range(n_ad)])]
    ppermute x3, waiting for transfers between devices: 6.06 us -> 10.8 us  [shift(): return lax.ppermute(x, 'ad', [(i, (i + step) % n_ad) for i in range(n_ad)])]
    slice x6 -> x0, local copies, waits for them, and re-layouts: 2.65 us -> none  [the longest x1 1.62 us: across(): mine[:, :keep.shape[1] - parts[0].shape[1]]]
    convert_element_type x5 -> x2, other arithmetic: 3.33 us -> 0.84 us  [the longest x1 0.8 us: per_device(): return sum((x.astype(F32) for x in [keep, came] + results)).astype(BF16)]
    unnamed x26 -> x10, local copies, waits for them, and re-layouts: 4.38 us -> 2.23 us
  transfers between devices with their start and end apart: 12 -> 14, of which waited for: 7 -> 8; matrix products, arithmetic and copies ran while one was open for 5% -> 0% of each run, Pallas kernels for 10% -> 9%
where the time goes in v5:
time: 105 us; the launch traced here: 104 us
  Pallas kernels  44.1 us (42%)
  waiting for transfers between devices  37.8 us (36%)
  starting transfers between devices  19.2 us (18%)
  local copies, waits for them, and re-layouts  2.23 us (2%)
    pallas_call x1, Pallas kernels, expert_part(): pl.pallas_call(functools.partial(expert_kernel, len(blocks), len(resident...  29.6 us
    ppermute x9, waiting for transfers between devices, swap(): return lax.ppermute(x, 'ep', [(i, i ^ mask) for i in range(n_ep)])  20.8 us
    ppermute x3, waiting for transfers between devices, shift(): return lax.ppermute(x, 'ad', [(i, (i + step) % n_ad) for i in range(n_ad)])  10.8 us
    pallas_call x1, Pallas kernels, prefetch(): pl.pallas_call(prefetch_kernel, out_shape=(*[pltpu.VMEM(shape, BF16) for...  8.97 us
    ppermute x9, starting transfers between devices, swap(): return lax.ppermute(x, 'ep', [(i, i ^ mask) for i in range(n_ep)])  8.5 us
    ppermute x2, waiting for transfers between devices, per_device(): other = lax.ppermute(low, 'ad', [(i, i ^ 1 << bit) for i in range(n_ad)])  6.25 us
    ppermute x3, starting transfers between devices, shift(): return lax.ppermute(x, 'ad', [(i, (i + step) % n_ad) for i in range(n_ad)])  5.89 us
    ppermute x2, starting transfers between devices, per_device(): other = lax.ppermute(low, 'ad', [(i, i ^ 1 << bit) for i in range(n_ad)])  4.82 us
  transfers between devices with their start and end apart: 14, of which 8 were waited for; matrix products, arithmetic and copies ran while one was open for 0% of the time, Pallas kernels for 9%

profile of v5, /device:TPU:0, one launch (start us, length us, event | category | flops | bytes accessed | tf_op | source)
XLA Modules:
  0.0 104.3 jit_solution(2052365522565256733)
XLA Ops:
  0.0 0.8 copy.12.chosen_ref
  0.8 0.8 copy.13.logits_ref
  1.6 0.0 copy-start.3
  1.6 0.6 copy-done.3
  2.2 1.1 %tokens_with_facts.1.refs_0_ = bf16[128,3200]{1,0:T(8,128)(2,1)S(1)} custom-call(bf16[128,3072]{1,0:T(8,128)(2,1)} %tokens_ref.1, s32[128,2]{1,0:T(8,128)S(1)} %copy.12.chosen_ref, f32[128,2]{1,0:T(8,128)S(1)} %copy.13.logits_ref, s32[1,128]{1,0:T(1,128)S(1)} %bitcast.5), custom_call_target="tpu_custom_call" | custom-call | flops 1 | bytes 1 | tf_op jit(solution)/shard_map/tokens_with_facts/pallas_call | solution.py:72
  3.4 3.0 %collective-permute-start.1 = (bf16[128,3200]{1,0:T(8,128)(2,1)S(1)}, bf16[128,3200]{1,0:T(8,128)(2,1)S(1)}, u32[]{:S(2)}, u32[]{:S(2)}) collective-permute-start(bf16[128,3200]{1,0:T(8,128)(2,1)S(1)} %tokens_with_facts.1.refs_0_), channel_id=1, source_target_pairs={{0,8},{4,12},{8,0},{12,4},{1,9},{5,13},{9,1},{13,5},{2,10},{6,14},... | collective-permute-start | bytes 2457608 | tf_op jit(solution)/shard_map/ppermute | solution.py:488
  6.4 0.0 collective-permute-start
  6.4 0.1 pad_add_fusion.ids_ref.refs_5_
  6.5 9.0 %weight_prefetch.1 = (bf16[2,3072,512]{2,1,0:T(8,128)(2,1)S(1)}, bf16[2,3072,512]{2,1,0:T(8,128)(2,1)S(1)}, bf16[2,3072,512]{2,1,0:T(8,128)(2,1)S(1)}, bf16[2,3072,512]{2,1,0:T(8,128)(2,1)S(1)}, f32[8,128]{1,0:T(8,128)S(1)}) custom-call(s32[2]{0:T(128)S(1)} %pad_add_fusion.ids_ref.refs_5_, bf16[4,3072,1024]{2,1,0:T(8,128)(2,1)} %refs_13_.1, ...), custom_call_target="tpu_custom_call" | custom-call | flops 1 | bytes 1 | tf_op jit(solution)/shard_map/weight_prefetch/pallas_call | solution.py:230
  15.4 9.2 %collective-permute-done.1.refs_2_ = bf16[128,3200]{1,0:T(8,128)(2,1)S(1)} collective-permute-done((bf16[128,3200]{1,0:T(8,128)(2,1)S(1)}, bf16[128,3200]{1,0:T(8,128)(2,1)S(1)}, u32[]{:S(2)}, u32[]{:S(2)}) %collective-permute-start.1) | collective-permute-done | bytes 819232 | tf_op jit(solution)/shard_map/ppermute | solution.py:488
  24.6 0.0 collective-permute-start.2
  24.6 0.0 collective-permute-done.refs_1_
  24.6 2.3 %collective-permute-done.2.refs_3_ = bf16[128,3200]{1,0:T(8,128)(2,1)S(1)} collective-permute-done((bf16[128,3200]{1,0:T(8,128)(2,1)S(1)}, bf16[128,3200]{1,0:T(8,128)(2,1)S(1)}, u32[]{:S(2)}, u32[]{:S(2)}) %collective-permute-start.2) | collective-permute-done | bytes 819232 | tf_op jit(solution)/shard_map/ppermute | solution.py:488
  27.0 0.0 copy-done.1
  27.0 0.0 copy-done.2
  27.0 1.1 %routing_tables.1 = (bf16[2,192,512]{2,1,0:T(8,128)(2,1)S(1)}, bf16[2,512,192]{2,1,0:T(8,128)(2,1)S(1)}, f32[512,128]{1,0:T(8,128)S(1)}, f32[8,512]{1,0:T(8,128)S(1)}, f32[2,8,192]{2,1,0:T(8,128)S(1)}) custom-call(s32[2]{0:T(128)S(1)} %pad_add_fusion.ids_ref.refs_5_, s32[16]{0:T(128)S(1)} %copy-done.1, s32[64]{0:T(128)S(1)} %copy-done.2, ...), custom_call_target="tpu_custom_call" | custom-call | flops 1 | bytes 1 | tf_op jit(solution)/shard_map/routing_tables/pallas_call | solution.py:127
  28.1 0.0 copy-start
  28.1 29.6 %experts.1 = (bf16[256,1024]{1,0:T(8,128)(2,1)S(1)}, bf16[256,1024]{1,0:T(8,128)(2,1)S(1)}, bf16[256,1536]{1,0:T(8,128)(2,1)S(1)}, bf16[256,1536]{1,0:T(8,128)(2,1)S(1)}, f32[512,768]{1,0:T(8,128)S(1)}) custom-call(bf16[128,3200]{1,0:T(8,128)(2,1)S(1)} %tokens_with_facts.1.refs_0_, bf16[128,3200]{1,0:T(8,128)(2,1)S(1)} %collective-permute-done.refs_1_, ...), custom_call_target="tpu_custom_call" | custom-call | flops 1 | bytes 1 | tf_op jit(solution)/shard_map/experts/pallas_call | solution.py:356
  57.7 0.2 collective-permute-start.3
  57.9 0.4 collective-permute-start.5
  58.2 1.4 %collective-permute-done.3.came_ref = bf16[256,1024]{1,0:T(8,128)(2,1)S(1)} collective-permute-done((bf16[256,1024]{1,0:T(8,128)(2,1)S(1)}, bf16[256,1024]{1,0:T(8,128)(2,1)S(1)}, u32[]{:S(2)}, u32[]{:S(2)}) %collective-permute-start.3) | collective-permute-done | bytes 524320 | tf_op jit(solution)/shard_map/ppermute | solution.py:488
  59.6 0.1 sum_and_split.3
  59.8 1.8 %collective-permute-start.4 = (bf16[128,1280]{1,0:T(8,128)(2,1)S(1)}, bf16[128,1280]{1,0:T(8,128)(2,1)S(1)}, u32[]{:S(2)}, u32[]{:S(2)}) collective-permute-start(bf16[128,1280]{1,0:T(8,128)(2,1)S(1)} %get-tuple-element.54), channel_id=1, source_target_pairs={{0,8},{4,12},{8,0},{12,4},{1,9},{5,13},{9,1},{13,5},{2,10},{6,14},... | collective-permute-start | bytes 983048 | tf_op jit(solution)/shard_map/ppermute | solution.py:488
  61.6 0.0 collective-permute-done.5.came_ref
  61.6 0.2 sum_and_split.4
  61.8 7.8 %collective-permute-done.4.came_ref = bf16[128,1280]{1,0:T(8,128)(2,1)S(1)} collective-permute-done((bf16[128,1280]{1,0:T(8,128)(2,1)S(1)}, bf16[128,1280]{1,0:T(8,128)(2,1)S(1)}, u32[]{:S(2)}, u32[]{:S(2)}) %collective-permute-start.4) | collective-permute-done | bytes 327712 | tf_op jit(solution)/shard_map/ppermute | solution.py:488
  69.6 0.1 sum_and_cut.2
  69.7 1.9 %collective-permute-start.6 = (bf16[128,512]{1,0:T(8,128)(2,1)S(1)}, bf16[128,512]{1,0:T(8,128)(2,1)S(1)}, u32[]{:S(2)}, u32[]{:S(2)}) collective-permute-start(bf16[128,512]{1,0:T(8,128)(2,1)S(1)} %get-tuple-element.59), channel_id=1, source_target_pairs={{0,1},{1,0},{2,3},{3,2},{4,5},{5,4},{6,7},{7,6},{8,9},{9,8},{10,11... | collective-permute-start | bytes 393224 | tf_op jit(solution)/shard_map/ppermute | solution.py:531
  71.6 1.5 %collective-permute-start.7 = (bf16[128,1536]{1,0:T(8,128)(2,1)S(1)}, bf16[128,1536]{1,0:T(8,128)(2,1)S(1)}, u32[]{:S(2)}, u32[]{:S(2)}) collective-permute-start(bf16[128,1536]{1,0:T(8,128)(2,1)S(1)} %get-tuple-element.60), channel_id=1, source_target_pairs={{0,8},{4,12},{8,0},{12,4},{1,9},{5,13},{9,1},{13,5},{2,10},{6,14},... | collective-permute-start | bytes 1179656 | tf_op jit(solution)/shard_map/ppermute | solution.py:488
  73.1 1.6 %collective-permute-done.6 = bf16[128,512]{1,0:T(8,128)(2,1)S(1)} collective-permute-done((bf16[128,512]{1,0:T(8,128)(2,1)S(1)}, bf16[128,512]{1,0:T(8,128)(2,1)S(1)}, u32[]{:S(2)}, u32[]{:S(2)}) %collective-permute-start.6) | collective-permute-done | bytes 131104 | tf_op jit(solution)/shard_map/ppermute | solution.py:531
  74.7 2.9 %collective-permute-start.8 = (bf16[128,512]{1,0:T(8,128)(2,1)S(1)}, bf16[128,512]{1,0:T(8,128)(2,1)S(1)}, u32[]{:S(2)}, u32[]{:S(2)}) collective-permute-start(bf16[128,512]{1,0:T(8,128)(2,1)S(1)} %add_convert_fusion.1.low_ref), channel_id=1, source_target_pairs={{0,2},{1,3},{2,0},{3,1},{4,6},{5,7},{6,4},{7,5},{8,10},{9,11},{10,... | collective-permute-start | bytes 393224 | tf_op jit(solution)/shard_map/ppermute | solution.py:531
  77.6 4.6 %collective-permute-done.8.other_ref = bf16[128,512]{1,0:T(8,128)(2,1)S(1)} collective-permute-done((bf16[128,512]{1,0:T(8,128)(2,1)S(1)}, bf16[128,512]{1,0:T(8,128)(2,1)S(1)}, u32[]{:S(2)}, u32[]{:S(2)}) %collective-permute-start.8) | collective-permute-done | bytes 131104 | tf_op jit(solution)/shard_map/ppermute | solution.py:531
  82.3 0.0 collective-permute-done.7.came_ref
  82.3 0.0 copy-done
  82.3 2.7 %adapters.1 = (bf16[256,768]{1,0:T(8,128)(2,1)S(1)}, bf16[256,768]{1,0:T(8,128)(2,1)S(1)}) custom-call(s32[2]{0:T(128)S(1)} %pad_add_fusion.ids_ref.refs_5_, f32[512,768]{1,0:T(8,128)S(1)} %get-tuple-element.50.base_ref, f32[512,128]{1,0:T(8,128)S(1)} %get-tuple-element.43.refs_10_.cols_ref, bf16[2048,768]{1,0:T(8,128)(2,1)S(1)} %bitcast.4, ...), custom_call_target="tpu_custom_call" | custom-call | flops 1 | bytes 1 | tf_op jit(solution)/shard_map/adapters/pallas_call | solution.py:402
  85.0 0.1 collective-permute-start.9
  85.1 2.0 %collective-permute-start.11 = (bf16[128,768]{1,0:T(8,128)(2,1)S(1)}, bf16[128,768]{1,0:T(8,128)(2,1)S(1)}, u32[]{:S(2)}, u32[]{:S(2)}) collective-permute-start(bf16[128,768]{1,0:T(8,128)(2,1)S(1)} %get-tuple-element.66), channel_id=1, source_target_pairs={{0,2},{1,3},{2,0},{3,1},{4,6},{5,7},{6,4},{7,5},{8,10},{9,11},{10,... | collective-permute-start | bytes 589832 | tf_op jit(solution)/shard_map/ppermute | solution.py:494
  87.1 0.1 sum_and_cut.3
  87.2 2.2 %collective-permute-start.12 = (bf16[128,768]{1,0:T(8,128)(2,1)S(1)}, bf16[128,768]{1,0:T(8,128)(2,1)S(1)}, u32[]{:S(2)}, u32[]{:S(2)}) collective-permute-start(bf16[128,768]{1,0:T(8,128)(2,1)S(1)} %get-tuple-element.69), channel_id=1, source_target_pairs={{0,1},{1,2},{2,3},{3,0},{4,5},{5,6},{6,7},{7,4},{8,9},{9,10},{10,1... | collective-permute-start | bytes 589832 | tf_op jit(solution)/shard_map/ppermute | solution.py:494
  89.4 1.7 %collective-permute-start.13 = (bf16[128,768]{1,0:T(8,128)(2,1)S(1)}, bf16[128,768]{1,0:T(8,128)(2,1)S(1)}, u32[]{:S(2)}, u32[]{:S(2)}) collective-permute-start(bf16[128,768]{1,0:T(8,128)(2,1)S(1)} %get-tuple-element.70), channel_id=1, source_target_pairs={{0,3},{1,0},{2,1},{3,2},{4,7},{5,4},{6,5},{7,6},{8,11},{9,8},{10,9... | collective-permute-start | bytes 589832 | tf_op jit(solution)/shard_map/ppermute | solution.py:494
  91.1 0.0 collective-permute-done.9.came_ref
  91.1 0.1 sum_and_split.5
  91.2 1.5 %collective-permute-start.10 = (bf16[128,768]{1,0:T(8,128)(2,1)S(1)}, bf16[128,768]{1,0:T(8,128)(2,1)S(1)}, u32[]{:S(2)}, u32[]{:S(2)}) collective-permute-start(bf16[128,768]{1,0:T(8,128)(2,1)S(1)} %get-tuple-element.65), channel_id=1, source_target_pairs={{0,8},{4,12},{8,0},{12,4},{1,9},{5,13},{9,1},{13,5},{2,10},{6,14},... | collective-permute-start | bytes 589832 | tf_op jit(solution)/shard_map/ppermute | solution.py:488
  92.7 9.5 %collective-permute-done.11 = bf16[128,768]{1,0:T(8,128)(2,1)S(1)} collective-permute-done((bf16[128,768]{1,0:T(8,128)(2,1)S(1)}, bf16[128,768]{1,0:T(8,128)(2,1)S(1)}, u32[]{:S(2)}, u32[]{:S(2)}) %collective-permute-start.11) | collective-permute-done | bytes 196640 | tf_op jit(solution)/shard_map/ppermute | solution.py:494
  102.2 0.0 collective-permute-done.12
  102.2 1.3 %collective-permute-done.13 = bf16[128,768]{1,0:T(8,128)(2,1)S(1)} collective-permute-done((bf16[128,768]{1,0:T(8,128)(2,1)S(1)}, bf16[128,768]{1,0:T(8,128)(2,1)S(1)}, u32[]{:S(2)}, u32[]{:S(2)}) %collective-permute-start.13) | collective-permute-done | bytes 196640 | tf_op jit(solution)/shard_map/ppermute | solution.py:494
  103.5 0.0 collective-permute-done.10
  103.5 0.8 add_convert_fusion
  (3 shorter events, 0.0 us)
Async XLA Ops:
  1.6 0.7 copy-start.3
  3.4 21.2 %collective-permute-start.1 = (bf16[128,3200]{1,0:T(8,128)(2,1)S(1)}, bf16[128,3200]{1,0:T(8,128)(2,1)S(1)}, u32[]{:S(2)}, u32[]{:S(2)}) collective-permute-start(bf16[128,3200]{1,0:T(8,128)(2,1)S(1)} %tokens_with_facts.1.refs_0_), channel_id=1, source_target_pairs={{0,8},{4,12},{8,0},{12,4},{1,9},{5,13},{9,1},{13,5},{2,10},{6,14},... | collective-permute-start | bytes 2457608 | tf_op jit(solution)/shard_map/ppermute | solution.py:488
  6.4 18.2 %collective-permute-start = (bf16[128,3200]{1,0:T(8,128)(2,1)S(1)}, bf16[128,3200]{1,0:T(8,128)(2,1)S(1)}, u32[]{:S(2)}, u32[]{:S(2)}) collective-permute-start(bf16[128,3200]{1,0:T(8,128)(2,1)S(1)} %tokens_with_facts.1.refs_0_), channel_id=1, source_target_pairs={{0,4},{4,0},{8,12},{12,8},{1,5},{5,1},{9,13},{13,9},{2,6},{6,2},{1... | collective-permute-start | bytes 2457608 | tf_op jit(solution)/shard_map/ppermute | solution.py:488
  6.5 20.5 %copy-start.1 = (s32[16]{0:T(128)S(1)}, s32[16]{0:T(128)}, u32[]{:S(2)}) copy-start(s32[16]{0:T(128)} %refs_6_.1) | copy-start | bytes 196
  6.5 20.5 %copy-start.2 = (s32[64]{0:T(128)S(1)}, s32[64]{0:T(128)}, u32[]{:S(2)}) copy-start(s32[64]{0:T(128)} %refs_7_.1) | copy-start | bytes 772
  24.6 2.3 %collective-permute-start.2 = (bf16[128,3200]{1,0:T(8,128)(2,1)S(1)}, bf16[128,3200]{1,0:T(8,128)(2,1)S(1)}, u32[]{:S(2)}, u32[]{:S(2)}) collective-permute-start(bf16[128,3200]{1,0:T(8,128)(2,1)S(1)} %collective-permute-done.1.refs_2_), channel_id=1, source_target_pairs={{0,4},{4,0},{8,12},{12,8},{1,5},{5,1},{9,13},{13,9},{2,6},{6,2},{1... | collective-permute-start | bytes 2457608 | tf_op jit(solution)/shard_map/ppermute | solution.py:488
  28.1 54.2 %copy-start = (bf16[16,8,16,768]{3,2,1,0:T(8,128)(2,1)S(1)}, bf16[16,8,16,768]{3,2,1,0:T(8,128)(2,1)}, u32[]{:S(2)}) copy-start(bf16[16,8,16,768]{3,2,1,0:T(8,128)(2,1)} %param.21) | copy-start | bytes 9437188
  57.7 2.0 %collective-permute-start.3 = (bf16[256,1024]{1,0:T(8,128)(2,1)S(1)}, bf16[256,1024]{1,0:T(8,128)(2,1)S(1)}, u32[]{:S(2)}, u32[]{:S(2)}) collective-permute-start(bf16[256,1024]{1,0:T(8,128)(2,1)S(1)} %get-tuple-element.52), channel_id=1, source_target_pairs={{0,4},{4,0},{8,12},{12,8},{1,5},{5,1},{9,13},{13,9},{2,6},{6,2},{1... | collective-permute-start | bytes 1572872 | tf_op jit(solution)/shard_map/ppermute | solution.py:488
  57.9 3.7 %collective-permute-start.5 = (bf16[256,1536]{1,0:T(8,128)(2,1)S(1)}, bf16[256,1536]{1,0:T(8,128)(2,1)S(1)}, u32[]{:S(2)}, u32[]{:S(2)}) collective-permute-start(bf16[256,1536]{1,0:T(8,128)(2,1)S(1)} %get-tuple-element.56), channel_id=1, source_target_pairs={{0,4},{4,0},{8,12},{12,8},{1,5},{5,1},{9,13},{13,9},{2,6},{6,2},{1... | collective-permute-start | bytes 2359304 | tf_op jit(solution)/shard_map/ppermute | solution.py:488
  59.8 9.8 %collective-permute-start.4 = (bf16[128,1280]{1,0:T(8,128)(2,1)S(1)}, bf16[128,1280]{1,0:T(8,128)(2,1)S(1)}, u32[]{:S(2)}, u32[]{:S(2)}) collective-permute-start(bf16[128,1280]{1,0:T(8,128)(2,1)S(1)} %get-tuple-element.54), channel_id=1, source_target_pairs={{0,8},{4,12},{8,0},{12,4},{1,9},{5,13},{9,1},{13,5},{2,10},{6,14},... | collective-permute-start | bytes 983048 | tf_op jit(solution)/shard_map/ppermute | solution.py:488
  69.7 5.0 %collective-permute-start.6 = (bf16[128,512]{1,0:T(8,128)(2,1)S(1)}, bf16[128,512]{1,0:T(8,128)(2,1)S(1)}, u32[]{:S(2)}, u32[]{:S(2)}) collective-permute-start(bf16[128,512]{1,0:T(8,128)(2,1)S(1)} %get-tuple-element.59), channel_id=1, source_target_pairs={{0,1},{1,0},{2,3},{3,2},{4,5},{5,4},{6,7},{7,6},{8,9},{9,8},{10,11... | collective-permute-start | bytes 393224 | tf_op jit(solution)/shard_map/ppermute | solution.py:531
  71.6 10.7 %collective-permute-start.7 = (bf16[128,1536]{1,0:T(8,128)(2,1)S(1)}, bf16[128,1536]{1,0:T(8,128)(2,1)S(1)}, u32[]{:S(2)}, u32[]{:S(2)}) collective-permute-start(bf16[128,1536]{1,0:T(8,128)(2,1)S(1)} %get-tuple-element.60), channel_id=1, source_target_pairs={{0,8},{4,12},{8,0},{12,4},{1,9},{5,13},{9,1},{13,5},{2,10},{6,14},... | collective-permute-start | bytes 1179656 | tf_op jit(solution)/shard_map/ppermute | solution.py:488
  74.7 7.5 %collective-permute-start.8 = (bf16[128,512]{1,0:T(8,128)(2,1)S(1)}, bf16[128,512]{1,0:T(8,128)(2,1)S(1)}, u32[]{:S(2)}, u32[]{:S(2)}) collective-permute-start(bf16[128,512]{1,0:T(8,128)(2,1)S(1)} %add_convert_fusion.1.low_ref), channel_id=1, source_target_pairs={{0,2},{1,3},{2,0},{3,1},{4,6},{5,7},{6,4},{7,5},{8,10},{9,11},{10,... | collective-permute-start | bytes 393224 | tf_op jit(solution)/shard_map/ppermute | solution.py:531
  85.0 6.1 %collective-permute-start.9 = (bf16[256,768]{1,0:T(8,128)(2,1)S(1)}, bf16[256,768]{1,0:T(8,128)(2,1)S(1)}, u32[]{:S(2)}, u32[]{:S(2)}) collective-permute-start(bf16[256,768]{1,0:T(8,128)(2,1)S(1)} %get-tuple-element.63), channel_id=1, source_target_pairs={{0,4},{4,0},{8,12},{12,8},{1,5},{5,1},{9,13},{13,9},{2,6},{6,2},{1... | collective-permute-start | bytes 1179656 | tf_op jit(solution)/shard_map/ppermute | solution.py:488
  85.1 17.1 %collective-permute-start.11 = (bf16[128,768]{1,0:T(8,128)(2,1)S(1)}, bf16[128,768]{1,0:T(8,128)(2,1)S(1)}, u32[]{:S(2)}, u32[]{:S(2)}) collective-permute-start(bf16[128,768]{1,0:T(8,128)(2,1)S(1)} %get-tuple-element.66), channel_id=1, source_target_pairs={{0,2},{1,3},{2,0},{3,1},{4,6},{5,7},{6,4},{7,5},{8,10},{9,11},{10,... | collective-permute-start | bytes 589832 | tf_op jit(solution)/shard_map/ppermute | solution.py:494
  87.2 15.0 %collective-permute-start.12 = (bf16[128,768]{1,0:T(8,128)(2,1)S(1)}, bf16[128,768]{1,0:T(8,128)(2,1)S(1)}, u32[]{:S(2)}, u32[]{:S(2)}) collective-permute-start(bf16[128,768]{1,0:T(8,128)(2,1)S(1)} %get-tuple-element.69), channel_id=1, source_target_pairs={{0,1},{1,2},{2,3},{3,0},{4,5},{5,6},{6,7},{7,4},{8,9},{9,10},{10,1... | collective-permute-start | bytes 589832 | tf_op jit(solution)/shard_map/ppermute | solution.py:494
  89.4 14.1 %collective-permute-start.13 = (bf16[128,768]{1,0:T(8,128)(2,1)S(1)}, bf16[128,768]{1,0:T(8,128)(2,1)S(1)}, u32[]{:S(2)}, u32[]{:S(2)}) collective-permute-start(bf16[128,768]{1,0:T(8,128)(2,1)S(1)} %get-tuple-element.70), channel_id=1, source_target_pairs={{0,3},{1,0},{2,1},{3,2},{4,7},{5,4},{6,5},{7,6},{8,11},{9,8},{10,9... | collective-permute-start | bytes 589832 | tf_op jit(solution)/shard_map/ppermute | solution.py:494
  91.2 12.4 %collective-permute-start.10 = (bf16[128,768]{1,0:T(8,128)(2,1)S(1)}, bf16[128,768]{1,0:T(8,128)(2,1)S(1)}, u32[]{:S(2)}, u32[]{:S(2)}) collective-permute-start(bf16[128,768]{1,0:T(8,128)(2,1)S(1)} %get-tuple-element.65), channel_id=1, source_target_pairs={{0,8},{4,12},{8,0},{12,4},{1,9},{5,13},{9,1},{13,5},{2,10},{6,14},... | collective-permute-start | bytes 589832 | tf_op jit(solution)/shard_map/ppermute | solution.py:488

commit v6 on v5

v6 whole, which is shorter than its diff:
```python
import functools
import math

import jax
import jax.numpy as jnp
from jax import lax
from jax.experimental import pallas as pl
from jax.experimental.pallas import tpu as pltpu
from jax.sharding import PartitionSpec as P

EXPERT_COUNT = 8
TOP = 2
RANK = 16
CAP = 48
LIMIT = 16
LIMIT_EARLY = 21
N_TILE = 512
HELD_EACH = 2
HELD_ARRAYS = 4
RING = 4
MIB = 1 << 20

F32 = jnp.float32
BF16 = jnp.bfloat16


def mm(a, b):
    return jnp.dot(a, b, preferred_element_type=F32)


def mm_nt(a, b):
    return lax.dot_general(a, b, (((1,), (1,)), ((), ())), preferred_element_type=F32)


SMALL = pl.CostEstimate(flops=1, bytes_accessed=1, transcendentals=0)


def params(mib):
    return pltpu.CompilerParams(vmem_limit_bytes=mib * MIB)


def vmem():
    return pl.BlockSpec(memory_space=pltpu.VMEM)


def smem():
    return pl.BlockSpec(memory_space=pltpu.SMEM)


def facts_kernel(tokens_ref, chosen_ref, logits_ref, tenant_ref, out_ref, sem):
    rows, width = tokens_ref.shape
    copy = pltpu.make_async_copy(tokens_ref, out_ref.at[:, pl.ds(0, width)], sem)
    copy.start()
    diagonal = lax.broadcasted_iota(jnp.int32, (rows, rows), 0) == lax.broadcasted_iota(jnp.int32, (rows, rows), 1)

    def column(row):
        return jnp.sum(jnp.where(diagonal, row, 0.0), axis=1, keepdims=True)

    chosen, logits = chosen_ref[...].astype(F32), logits_ref[...]
    columns = [column(chosen[0:1]), column(chosen[1:2]), column(tenant_ref[...].astype(F32))]
    rests = [column(logits[0:1]), column(logits[1:2])]
    for _ in range(3):
        pieces = [rest.astype(BF16).astype(F32) for rest in rests]
        columns += pieces
        rests = [rest - piece for rest, piece in zip(rests, pieces)]
    lane = lax.broadcasted_iota(jnp.int32, (rows, 128), 1)
    facts = jnp.zeros((rows, 128), F32)
    for number, value in enumerate(columns):
        facts = jnp.where(lane == number, value, facts)
    out_ref[:, width:] = facts.astype(BF16)
    copy.wait()


def with_facts(tokens, chosen_experts, logits, tenant):
    rows, width = tokens.shape
    return pl.pallas_call(
        facts_kernel,
        out_shape=jax.ShapeDtypeStruct((rows, width + 128), BF16),
        in_specs=[pl.BlockSpec(memory_space=pltpu.HBM)] + [vmem()] * 3,
        out_specs=vmem(),
        scratch_shapes=[pltpu.SemaphoreType.DMA],
        cost_estimate=SMALL,
        compiler_params=params(LIMIT_EARLY),
        name="tokens_with_facts",
    )(pltpu.with_memory_space_constraint(tokens, pltpu.HBM), chosen_experts.T, logits.T, tenant.reshape(1, rows))


def meta_kernel(n_local, local_halves, ids_ref, adapter_ref, pool_slot_ref, *refs):
    blocks, (p_ref, pt_ref, cols_ref, rows_ref, tslot_ref) = refs[:-5], refs[-5:]
    at = blocks[0].shape[1] - 128
    facts = jnp.concatenate([block[:, at:] for block in blocks], axis=0).astype(F32).T
    count = facts.shape[1]
    first, second, tenant = facts[0:1], facts[1:2], facts[2:3]
    logit_first = (facts[3:4] + facts[5:6]) + facts[7:8]
    logit_second = (facts[4:5] + facts[6:7]) + facts[8:9]
    weight_first = jax.nn.sigmoid(logit_first - logit_second)
    weight_second = jax.nn.sigmoid(logit_second - logit_first)
    slot = jnp.zeros_like(tenant)
    for number in range(adapter_ref.shape[0]):
        slot = jnp.where(tenant == number, pool_slot_ref[adapter_ref[number]].astype(F32), slot)
    members, weights = [], []
    for i in range(n_local):
        expert = (ids_ref[0] * local_halves // 2 + i).astype(F32)
        hit_first, hit_second = first == expert, second == expert
        members.append(jnp.where(hit_first | hit_second, 1.0, 0.0))
        weights.append(jnp.where(hit_first, weight_first, 0.0) + jnp.where(hit_second, weight_second, 0.0))
    member = jnp.concatenate(members + [jnp.zeros((8 - n_local, count), F32)], axis=0)
    before = (
        lax.broadcasted_iota(jnp.int32, (count, count), 0) < lax.broadcasted_iota(jnp.int32, (count, count), 1)
    ).astype(BF16)
    place = jnp.where(member > 0, mm(member.astype(BF16), before), -1.0)
    table = jnp.concatenate(
        [place[0:n_local]] + weights + [slot] + [jnp.zeros((127 - 2 * n_local, count), F32)], axis=0
    )
    columns = table.T
    cols_ref[...] = columns
    rows_ref[...] = table[0:8]
    row_count = p_ref.shape[1]
    tenant_rows = jnp.broadcast_to(tenant, (8, count)).astype(BF16)
    down = lax.broadcasted_iota(jnp.int32, (row_count, count), 0).astype(F32)
    across = lax.broadcasted_iota(jnp.int32, (count, row_count), 1).astype(F32)
    for i in range(n_local):
        picked = (down == place[i : i + 1]).astype(BF16)
        p_ref[i] = picked
        pt_ref[i] = (across == columns[:, i : i + 1]).astype(BF16)
        tslot_ref[i] = mm_nt(tenant_rows, picked)


def build_meta(blocks, ids, adapters, pool_slots, n_local, local_halves, row_count):
    count = sum(block.shape[0] for block in blocks)
    return pl.pallas_call(
        functools.partial(meta_kernel, n_local, local_halves),
        out_shape=(
            jax.ShapeDtypeStruct((n_local, row_count, count), BF16),
            jax.ShapeDtypeStruct((n_local, count, row_count), BF16),
            jax.ShapeDtypeStruct((count, 128), F32),
            jax.ShapeDtypeStruct((8, count), F32),
            jax.ShapeDtypeStruct((n_local, 8, row_count), F32),
        ),
        in_specs=[smem()] * 3 + [vmem()] * len(blocks),
        out_specs=(vmem(),) * 5,
        cost_estimate=SMALL,
        compiler_params=params(min(38, LIMIT_EARLY * count // 512)),
        name="routing_tables",
    )(ids, adapters, pool_slots, *blocks)


class Slabs:
    def __init__(self, gate_ref, up_ref, resident, ring, sems):
        self.sources, self.resident, self.ring, self.sems = (gate_ref, up_ref), resident, ring, sems
        self.halves, self.depth, hidden = gate_ref.shape
        self.width = resident[0].shape[2]
        self.each = resident[0].shape[0]
        self.first = len(resident) * self.each
        self.capacity = 1 if ring is None else ring.shape[0]
        self.tiles = hidden // self.width
        self.count = 2 * self.halves * self.tiles

    def place(self, number):
        if number < self.first:
            return self.resident[number // self.each].at[number % self.each]
        return self.ring.at[(number - self.first) % self.capacity]

    def copies(self, number):
        place, rows = self.place(number), self.depth // 2
        slot = number if number < self.first else (number - self.first) % self.capacity
        half, tile, which = number // (2 * self.tiles), number // 2 % self.tiles, number % 2
        return [
            pltpu.make_async_copy(
                self.sources[which].at[half, pl.ds(i * rows, rows), pl.ds(tile * self.width, self.width)],
                place.at[pl.ds(i * rows, rows)],
                self.sems.at[slot, i],
            )
            for i in range(2)
        ]

    def start(self, number):
        for copy in self.copies(number):
            copy.start()

    def wait(self, number):
        for copy in self.copies(number):
            copy.wait()


def resident_shapes(gate):
    local_halves, width, hidden_count = gate.shape
    tile = min(N_TILE, hidden_count)
    count = 2 * local_halves * hidden_count // tile
    each = min(HELD_EACH, count)
    return [(each, width, tile)] * min(HELD_ARRAYS, count // each)


def down_slabs(down, n_ad):
    return pltpu.VMEM((down.shape[0], down.shape[1], down.shape[2] // n_ad), BF16)


def down_fetch(n_ad, step, ids_ref, down_ref, into_ref, sems):
    _, rows, span = into_ref.shape
    rows = rows // 2
    start = pl.multiple_of(lax.rem(ids_ref[1] + step, n_ad) * span, span)
    return [
        pltpu.make_async_copy(
            down_ref.at[half, pl.ds(i * rows, rows), pl.ds(start, span)],
            into_ref.at[half, pl.ds(i * rows, rows)],
            sems.at[half, i],
        )
        for half in range(down_ref.shape[0])
        for i in range(2)
    ]


def prefetch_kernel(ids_ref, gate_ref, up_ref, *refs):
    resident, mark_ref, sems = refs[:-2], refs[-2], refs[-1]
    slabs = Slabs(gate_ref, up_ref, resident, None, sems)
    for number in range(slabs.first):
        slabs.start(number)
    mark_ref[...] = jnp.zeros_like(mark_ref)
    for number in range(slabs.first):
        slabs.wait(number)


def prefetch(ids, gate, up, count):
    shapes = resident_shapes(gate)
    return pl.pallas_call(
        prefetch_kernel,
        out_shape=(*[pltpu.VMEM(shape, BF16) for shape in shapes], jax.ShapeDtypeStruct((8, 128), F32)),
        in_specs=[smem()] + [pl.BlockSpec(memory_space=pltpu.HBM)] * 2,
        out_specs=(vmem(),) * (len(shapes) + 1),
        scratch_shapes=[pltpu.SemaphoreType.DMA((len(shapes) * shapes[0][0], 2))],
        cost_estimate=SMALL,
        compiler_params=params(min(38, LIMIT_EARLY * count // 512)),
        name="weight_prefetch",
    )(ids, gate, up)


def expert_kernel(n_blocks, n_resident, n_ad, step, *refs):
    blocks, refs = refs[:n_blocks], refs[n_blocks:]
    ids_ref, adapter_ref, pool_slot_ref, p_ref, tslot_ref, rows_ref = refs[1:7]
    gate_ref, up_ref, down_ref, pool_ref = refs[7:11]
    resident, refs = refs[11 : 11 + n_resident], refs[11 + n_resident :]
    hidden, low_ref, next_ref, packed, factors, factor_sems, down_sems, ring, sems = refs
    slabs = Slabs(gate_ref, up_ref, resident, ring, sems)
    n_local = p_ref.shape[0]
    local_halves, depth, _ = gate_ref.shape
    halves_each = local_halves // n_local
    tenants, rank = adapter_ref.shape[0], pool_ref.shape[2]
    factor_copies = [
        pltpu.make_async_copy(
            pool_ref.at[pool_slot_ref[adapter_ref[number]]],
            factors.at[:, number * rank : (number + 1) * rank],
            factor_sems.at[number],
        )
        for number in range(tenants)
    ]
    for copy in factor_copies:
        copy.start()
    for number in range(slabs.first, min(slabs.count, slabs.first + slabs.capacity)):
        slabs.start(number)

    def ready(number):
        if number >= slabs.first:
            slabs.wait(number)

    def used(number):
        if slabs.first <= number < slabs.count - slabs.capacity:
            slabs.start(number + slabs.capacity)

    whole = jnp.concatenate([block[:, :depth] for block in blocks], axis=0)
    for i in range(n_local):
        packed[i] = mm(p_ref[i], whole).astype(BF16)
    for half in range(local_halves):
        rows = packed[half // halves_each]
        for tile in range(slabs.tiles):
            values = []
            for which in range(2):
                number = (half * slabs.tiles + tile) * 2 + which
                ready(number)
                values.append(mm(rows, slabs.place(number)[...]))
                used(number)
            span = slice(tile * slabs.width, (tile + 1) * slabs.width)
            hidden[half, :, span] = (jax.nn.silu(values[0]) * values[1]).astype(BF16)
    down_copies = down_fetch(n_ad, step, ids_ref, down_ref, next_ref, down_sems)
    for copy in down_copies:
        copy.start()
    for copy in factor_copies:
        copy.wait()
    for i in range(n_local):
        low = mm_nt(factors[i * halves_each], hidden[i * halves_each])
        for half in range(i * halves_each + 1, (i + 1) * halves_each):
            low = low + mm_nt(factors[half], hidden[half])
        owner = tslot_ref[i][0:1]
        total = jnp.zeros((rank, low.shape[1]), F32)
        for number in range(tenants):
            total = total + jnp.where(owner == number, low[number * rank : (number + 1) * rank], 0.0)
        weight = rows_ref[n_local + i : n_local + i + 1]
        low_ref[i * rank : (i + 1) * rank] = (mm(total.astype(BF16), p_ref[i]) * weight).astype(BF16)
    for copy in down_copies:
        copy.wait()


def expert_part(
    blocks, mark, ids, adapters, pool_slots, picked, tslot, table_rows, gate, up, down, pool, resident, n_ad, step
):
    local_halves, width, hidden_count = gate.shape
    n_local, row_count, count = picked.shape
    tenants, rank = adapters.shape[0], pool.shape[2]
    hbm = pl.BlockSpec(memory_space=pltpu.HBM)
    each, _, tile = resident[0].shape
    ring = max(1, min(RING, 2 * local_halves * hidden_count // tile - len(resident) * each))
    return pl.pallas_call(
        functools.partial(expert_kernel, len(blocks), len(resident), n_ad, step),
        out_shape=(
            pltpu.VMEM((local_halves, row_count, hidden_count), BF16),
            jax.ShapeDtypeStruct((n_local * rank, count), BF16),
            down_slabs(down, n_ad),
        ),
        in_specs=[vmem()] * (len(blocks) + 1) + [smem()] * 3 + [vmem()] * 3 + [hbm] * 4 + [vmem()] * len(resident),
        out_specs=(vmem(),) * 3,
        scratch_shapes=[
            pltpu.VMEM((n_local, row_count, width), BF16),
            pltpu.VMEM((local_halves, tenants * rank, hidden_count), BF16),
            pltpu.SemaphoreType.DMA((tenants,)),
            pltpu.SemaphoreType.DMA((local_halves, 2)),
            pltpu.VMEM((ring, width, tile), BF16),
            pltpu.SemaphoreType.DMA((ring, 2)),
        ],
        cost_estimate=SMALL,
        compiler_params=params(min(38, LIMIT_EARLY * count // 512)),
        name="experts",
    )(
        *blocks, mark, ids, adapters, pool_slots, picked, tslot, table_rows, gate, up, down, pool,
        *[pltpu.with_memory_space_constraint(x, pltpu.VMEM) for x in resident],
    )


def weighted_down(hidden_ref, weight_ref, pt_ref, cols_ref):
    n_local = pt_ref.shape[0]
    halves_each = hidden_ref.shape[0] // n_local
    total = None
    for i in range(n_local):
        part_sum = mm(hidden_ref[i * halves_each], weight_ref[i * halves_each])
        for half in range(i * halves_each + 1, (i + 1) * halves_each):
            part_sum = part_sum + mm(hidden_ref[half], weight_ref[half])
        laid = mm(pt_ref[i], part_sum.astype(BF16)) * cols_ref[:, n_local + i : n_local + i + 1]
        total = laid if total is None else total + laid
    return total


def down_first_kernel(n_ad, step, ids_ref, hidden_ref, weight_ref, pt_ref, cols_ref, down_ref, keep, send, next_ref, sems):
    copies = down_fetch(n_ad, step, ids_ref, down_ref, next_ref, sems)
    for copy in copies:
        copy.start()
    write_pairs(weighted_down(hidden_ref, weight_ref, pt_ref, cols_ref), (keep, send))
    for copy in copies:
        copy.wait()


def down_first(ids, hidden, weights, pt, cols, down, n_ad, step):
    count, span = pt.shape[1], weights.shape[2]
    return pl.pallas_call(
        functools.partial(down_first_kernel, n_ad, step),
        out_shape=(jax.ShapeDtypeStruct((count // 2, span), BF16),) * 2 + (down_slabs(down, n_ad),),
        in_specs=[smem()] + [vmem()] * 4 + [pl.BlockSpec(memory_space=pltpu.HBM)],
        out_specs=(vmem(),) * 3,
        scratch_shapes=[pltpu.SemaphoreType.DMA((down.shape[0], 2))],
        cost_estimate=SMALL,
        compiler_params=params(max(LIMIT, 12 * count * span // MIB)),
        name="down_first",
    )(ids, hidden, pltpu.with_memory_space_constraint(weights, pltpu.VMEM), pt, cols, down)


def down_rest_kernel(n_ad, steps, ids_ref, hidden_ref, weight_ref, pt_ref, cols_ref, down_ref, keep, send, base, *refs):
    held, sems = refs[:-1], refs[-1]
    copies = [
        down_fetch(n_ad, step, ids_ref, down_ref, into, sems.at[number])
        for number, (step, into) in enumerate(zip(steps[1:], held))
    ]
    for copy in [copy for group in copies for copy in group]:
        copy.start()
    span = weight_ref.shape[2]
    for number in range(len(steps)):
        if number:
            for copy in copies[number - 1]:
                copy.wait()
        total = weighted_down(hidden_ref, held[number - 1] if number else weight_ref, pt_ref, cols_ref)
        if number < len(steps) - 1:
            write_pairs(total, (keep, send), number * span)
        else:
            base[...] = total


def down_rest(ids, hidden, weights, pt, cols, down, n_ad, steps):
    count, span = pt.shape[1], weights.shape[2]
    return pl.pallas_call(
        functools.partial(down_rest_kernel, n_ad, steps),
        out_shape=(jax.ShapeDtypeStruct((count // 2, span * (len(steps) - 1)), BF16),) * 2
        + (jax.ShapeDtypeStruct((count, span), F32),),
        in_specs=[smem()] + [vmem()] * 4 + [pl.BlockSpec(memory_space=pltpu.HBM)],
        out_specs=(vmem(),) * 3,
        scratch_shapes=[pltpu.VMEM(weights.shape, BF16)] * (len(steps) - 1)
        + [pltpu.SemaphoreType.DMA((len(steps) - 1, down.shape[0], 2))],
        cost_estimate=SMALL,
        compiler_params=params(max(LIMIT, 12 * count * span // MIB) + (len(steps) - 1) * weights.size * 2 // MIB),
        name="down_rest",
    )(ids, hidden, pltpu.with_memory_space_constraint(weights, pltpu.VMEM), pt, cols, down)


def write_pairs(total, outs, at=0):
    keep, send = outs
    for b in range(total.shape[0] // 128):
        block = total[b * 128 : b * 128 + 128].astype(BF16)
        (send if b % 2 else keep)[b // 2 * 128 : b // 2 * 128 + 128, pl.ds(at, total.shape[1])] = block


def adapter_kernel(slot_column, local_halves, ids_ref, base_ref, cols_ref, factor_ref, low_ref, keep, send, wide):
    blocks = base_ref.shape[0] // 128
    height = low_ref.shape[0] // blocks
    wide[...] = jnp.zeros_like(wide)
    for m in range(blocks):
        row = pl.multiple_of(((ids_ref[0] ^ m) * local_halves // 2) * RANK, RANK)
        value = low_ref[m * height : (m + 1) * height].astype(F32)
        value = jnp.concatenate([value[:, (m ^ b) * 128 : (m ^ b) * 128 + 128] for b in range(blocks)], axis=1)
        wide[pl.ds(row, height)] += value
    low = wide[...].T.astype(BF16)
    zero = jnp.zeros_like(low)
    slot = cols_ref[:, slot_column : slot_column + 1]
    depth = EXPERT_COUNT * RANK
    slot_count = factor_ref.shape[0] // depth
    total = base_ref[...]
    for j in range(0, slot_count, 2):
        spread = jnp.concatenate(
            [jnp.where(slot == (ids_ref[0] * slot_count + j + i).astype(F32), low, zero) for i in range(2)], axis=1
        )
        total = total + mm(spread, factor_ref[j * depth : (j + 2) * depth])
    write_pairs(total, (keep, send))


def adapter_part(ids, base, cols, slot_column, local_halves, factors, low):
    count, span = base.shape
    return pl.pallas_call(
        functools.partial(adapter_kernel, slot_column, local_halves),
        out_shape=(jax.ShapeDtypeStruct((count // 2, span), BF16),) * 2,
        in_specs=[smem()] + [vmem()] * 4,
        out_specs=(vmem(),) * 2,
        scratch_shapes=[pltpu.VMEM((EXPERT_COUNT * RANK, count), F32)],
        cost_estimate=SMALL,
        compiler_params=params(max(LIMIT, 24 * count * span // MIB)),
        name="adapters",
    )(ids, base, cols, factors, low)


def split_kernel(keep_ref, came_ref, keep, send):
    for b in range(keep_ref.shape[0] // 128):
        total = keep_ref[b * 128 : b * 128 + 128].astype(F32) + came_ref[b * 128 : b * 128 + 128].astype(F32)
        (send if b % 2 else keep)[b // 2 * 128 : b // 2 * 128 + 128] = total.astype(BF16)


def split_sum(keep, came):
    return pl.pallas_call(
        split_kernel,
        out_shape=(jax.ShapeDtypeStruct((keep.shape[0] // 2, keep.shape[1]), BF16),) * 2,
        in_specs=[vmem()] * 2,
        out_specs=(vmem(),) * 2,
        cost_estimate=SMALL,
        compiler_params=params(LIMIT),
        name="sum_and_split",
    )(keep, came)


def cut_kernel(edges, keep_ref, came_ref, *outs):
    for first, last, out in zip(edges, edges[1:], outs):
        out[...] = (keep_ref[:, first:last].astype(F32) + came_ref[:, first:last].astype(F32)).astype(BF16)


def cut_sum(keep, came, edges):
    return pl.pallas_call(
        functools.partial(cut_kernel, edges),
        out_shape=tuple(
            jax.ShapeDtypeStruct((keep.shape[0], last - first), BF16) for first, last in zip(edges, edges[1:])
        ),
        in_specs=[vmem()] * 2,
        out_specs=(vmem(),) * (len(edges) - 1),
        cost_estimate=SMALL,
        compiler_params=params(LIMIT),
        name="sum_and_cut",
    )(keep, came)


def per_device(
    n_ep,
    n_ad,
    tokens,
    chosen_experts,
    router_gate_logits,
    token_tenant,
    adapter_of_tenant,
    adapter_pool_slot,
    gate_weight,
    up_weight,
    down_weight,
    adapter_input_factors,
    adapter_output_factors,
):
    gate_weight, up_weight, down_weight, adapter_input_factors = [
        pltpu.with_memory_space_constraint(x, pltpu.HBM)
        for x in (gate_weight, up_weight, down_weight, adapter_input_factors)
    ]
    width = tokens.shape[1]
    span = width // n_ad
    local_halves = gate_weight.shape[0]
    n_local = max(1, local_halves // 2)
    row_count = n_ep * CAP
    bits = n_ep.bit_length() - 1
    ids = jnp.stack([lax.axis_index("ep"), lax.axis_index("ad")]).astype(jnp.int32)

    def swap(x, mask):
        return lax.ppermute(x, "ep", [(i, i ^ mask) for i in range(n_ep)])

    def tie(x, y):
        return lax.optimization_barrier((x, y))

    def shift(x, step):
        return lax.ppermute(x, "ad", [(i, (i + step) % n_ad) for i in range(n_ad)])

    order = sorted(range(1, n_ad), key=lambda step: (step != n_ad // 2, step))
    own = with_facts(tokens, chosen_experts, router_gate_logits, token_tenant)
    *resident, mark = prefetch(ids, gate_weight, up_weight, n_ep * tokens.shape[0])
    blocks = {0: own}
    for bit in reversed(range(bits)):
        for mask in list(blocks):
            blocks[mask | 1 << bit] = swap(blocks[mask], 1 << bit)
        if bit == bits - 1:
            blocks[1 << bit], mark = tie(blocks[1 << bit], mark)
    blocks = [blocks[mask] for mask in range(n_ep)]
    picked, pt, cols, table_rows, tslot = build_meta(
        blocks, ids, adapter_of_tenant, adapter_pool_slot, n_local, local_halves, row_count
    )
    hidden, low, weights = expert_part(
        blocks, mark, ids, adapter_of_tenant, adapter_pool_slot, picked, tslot, table_rows, gate_weight, up_weight,
        down_weight, adapter_input_factors, resident, n_ad, order[0],
    )

    def onward(keep, came, first=1):
        for bit in range(first, bits):
            keep, send = split_sum(keep, came)
            came = swap(send, 1 << bit)
        return keep, came

    def other_of(low, bit):
        return lax.ppermute(low, "ad", [(i, i ^ 1 << bit) for i in range(n_ad)])

    def added(x, y):
        return (x.astype(F32) + y.astype(F32)).astype(BF16)

    far_steps = range(1, n_ad.bit_length() - 1)
    others = [other_of(low, bit) for bit in far_steps[:1]]
    keep, send, weights = down_first(ids, hidden, weights, pt, cols, down_weight, n_ad, order[1])
    others, keep, send, weights = lax.optimization_barrier((others, keep, send, weights))
    for bit in far_steps:
        low = added(low, others[0] if bit == 1 else other_of(low, bit))
    for bit in range(bits - 1):
        low = jnp.concatenate([low, swap(low, 1 << bit)], axis=0)
    crossed = swap(low, 1 << (bits - 1))
    keep, came = onward(keep, swap(send, 1), 1)
    keep, hidden = tie(keep, hidden)
    keep_rest, send_rest, base = down_rest(ids, hidden, weights, pt, cols, down_weight, n_ad, (*order[1:], 0))
    came, crossed, keep_rest, send_rest, base = lax.optimization_barrier((came, crossed, keep_rest, send_rest, base))
    low = jnp.concatenate([low, crossed], axis=0)
    low = added(low, other_of(low, 0))
    (sums,) = cut_sum(keep, came, (0, span))
    results = [shift(sums, order[0])]
    keep_rest, came_rest = onward(keep_rest, swap(send_rest, 1))
    slot_count = adapter_output_factors.shape[0]
    flat_factors = adapter_output_factors.reshape(slot_count * EXPERT_COUNT * RANK, span)
    keep, send = adapter_part(ids, base, cols, 2 * n_local, local_halves, flat_factors, low)
    came = swap(send, 1)
    if bits > 1:
        keep, send = split_sum(keep, came)
        came_rest, keep, send = lax.optimization_barrier((came_rest, keep, send))
        came = swap(send, 2)
    keep, came = onward(keep, came, 2)
    parts = cut_sum(keep_rest, came_rest, [span * i for i in range(n_ad - 1)])
    results += [shift(x, step) for x, step in zip(parts, order[1:])]
    return sum(x.astype(F32) for x in [keep, came] + results).astype(BF16)


def solution(mesh):
    placed = (
        P(("rep", "ep"), None),
        P(("rep", "ep"), None),
        P(("rep", "ep"), None),
        P(("rep", "ep")),
        P("rep"),
        P(),
        P("ep", None, "ad"),
        P("ep", None, "ad"),
        P("ep", "ad", None),
        P(None, "ep", None, "ad"),
        P("ep", None, None, "ad"),
    )
    return jax.shard_map(
        functools.partial(per_device, mesh.shape["ep"], mesh.shape["ad"]),
        mesh=mesh,
        in_specs=placed,
        out_specs=P(("rep", "ep"), "ad"),
        check_vma=False,
    )
```

time: 105 us -> 102 us (0.971)
  waiting for transfers between devices: 37.8 us -> 33.2 us
  Pallas kernels: 44.1 us -> 47.9 us
  starting transfers between devices: 19.2 us -> 17.8 us
    pallas_call x4 -> x6, Pallas kernels: 3.11 us -> 16.4 us  [the longest x1 8.08 us: down_rest(): pl.pallas_call(functools.partial(down_rest_kernel, n_ad, steps), out_shap...]
    pallas_call x1, Pallas kernels: 29.6 us -> 20.2 us  [expert_part(): pl.pallas_call(functools.partial(expert_kernel, len(blocks), len(resident...]
    ppermute x3, waiting for transfers between devices: 10.8 us -> 6.71 us  [shift(): return lax.ppermute(x, 'ad', [(i, (i + step) % n_ad) for i in range(n_ad)])]
    ppermute x2, waiting for transfers between devices: 6.25 us -> 4.32 us  [other_of(): return lax.ppermute(low, 'ad', [(i, i ^ 1 << bit) for i in range(n_ad)])]
    ppermute x3, starting transfers between devices: 5.89 us -> 4.28 us  [shift(): return lax.ppermute(x, 'ad', [(i, (i + step) % n_ad) for i in range(n_ad)])]
    ppermute x9 -> x11, waiting for transfers between devices: 20.8 us -> 22.2 us  [swap(): return lax.ppermute(x, 'ep', [(i, i ^ mask) for i in range(n_ep)])]
    ppermute x9 -> x11, starting transfers between devices: 8.5 us -> 8.98 us  [swap(): return lax.ppermute(x, 'ep', [(i, i ^ mask) for i in range(n_ep)])]
    unnamed x10 -> x18, local copies, waits for them, and re-layouts: 2.23 us -> 2.03 us
  transfers between devices with their start and end apart: 14 -> 16, of which waited for: 8 -> 7; matrix products, arithmetic and copies ran while one was open for 0% -> 0% of each run, Pallas kernels for 9% -> 25%
where the time goes in v6:
time: 102 us
  Pallas kernels  47.9 us (47%)
  waiting for transfers between devices  33.2 us (33%)
  starting transfers between devices  17.8 us (17%)
  local copies, waits for them, and re-layouts  2.03 us (2%)
    ppermute x11, waiting for transfers between devices, swap(): return lax.ppermute(x, 'ep', [(i, i ^ mask) for i in range(n_ep)])  22.2 us
    pallas_call x1, Pallas kernels, expert_part(): pl.pallas_call(functools.partial(expert_kernel, len(blocks), len(resident...  20.2 us
    ppermute x11, starting transfers between devices, swap(): return lax.ppermute(x, 'ep', [(i, i ^ mask) for i in range(n_ep)])  8.98 us
    pallas_call x1, Pallas kernels, prefetch(): pl.pallas_call(prefetch_kernel, out_shape=(*[pltpu.VMEM(shape, BF16) for...  8.89 us
    pallas_call x1, Pallas kernels, down_rest(): pl.pallas_call(functools.partial(down_rest_kernel, n_ad, steps), out_shap...  8.08 us
    ppermute x3, waiting for transfers between devices, shift(): return lax.ppermute(x, 'ad', [(i, (i + step) % n_ad) for i in range(n_ad)])  6.71 us
    pallas_call x1, Pallas kernels, down_first(): pl.pallas_call(functools.partial(down_first_kernel, n_ad, step), out_shap...  5.21 us
    ppermute x2, starting transfers between devices, other_of(): return lax.ppermute(low, 'ad', [(i, i ^ 1 << bit) for i in range(n_ad)])  4.53 us
  transfers between devices with their start and end apart: 16, of which 7 were waited for; matrix products, arithmetic and copies ran while one was open for 0% of the time, Pallas kernels for 25%

profile of v6, /device:TPU:0, one launch (start us, length us, event | category | flops | bytes accessed | tf_op | source)
XLA Modules:
  0.0 102.1 jit_solution(2877263628183417609)
XLA Ops:
  0.0 0.7 copy-done.6
  0.7 0.7 copy-done.7
  1.4 0.7 copy-done.8
  2.0 1.1 %tokens_with_facts.1.refs_0_ = bf16[128,3200]{1,0:T(8,128)(2,1)S(1)} custom-call(bf16[128,3072]{1,0:T(8,128)(2,1)} %tokens_ref.1, s32[2,128]{1,0:T(2,128)S(1)} %bitcast.7, f32[2,128]{1,0:T(2,128)S(1)} %bitcast.8, s32[1,128]{1,0:T(1,128)S(1)} %bitcast.9), custom_call_target="tpu_custom_call" | custom-call | flops 1 | bytes 1 | tf_op jit(solution)/shard_map/tokens_with_facts/pallas_call | solution.py:76
  3.2 3.0 %collective-permute-start.1 = (bf16[128,3200]{1,0:T(8,128)(2,1)S(1)}, bf16[128,3200]{1,0:T(8,128)(2,1)S(1)}, u32[]{:S(2)}, u32[]{:S(2)}) collective-permute-start(bf16[128,3200]{1,0:T(8,128)(2,1)S(1)} %tokens_with_facts.1.refs_0_), channel_id=1, source_target_pairs={{0,8},{4,12},{8,0},{12,4},{1,9},{5,13},{9,1},{13,5},{2,10},{6,14},... | collective-permute-start | bytes 2457608 | tf_op jit(solution)/shard_map/ppermute | solution.py:518
  6.2 0.0 collective-permute-start
  6.2 0.1 pad_add_fusion.ids_ref.refs_5_
  6.3 8.9 %weight_prefetch.1 = (bf16[2,3072,512]{2,1,0:T(8,128)(2,1)S(1)}, bf16[2,3072,512]{2,1,0:T(8,128)(2,1)S(1)}, bf16[2,3072,512]{2,1,0:T(8,128)(2,1)S(1)}, bf16[2,3072,512]{2,1,0:T(8,128)(2,1)S(1)}, f32[8,128]{1,0:T(8,128)S(1)}) custom-call(s32[2]{0:T(128)S(1)} %pad_add_fusion.ids_ref.refs_5_, bf16[4,3072,1024]{2,1,0:T(8,128)(2,1)} %refs_11_.1, ...), custom_call_target="tpu_custom_call" | custom-call | flops 1 | bytes 1 | tf_op jit(solution)/shard_map/weight_prefetch/pallas_call | solution.py:225
  15.2 9.3 %collective-permute-done.1.refs_2_ = bf16[128,3200]{1,0:T(8,128)(2,1)S(1)} collective-permute-done((bf16[128,3200]{1,0:T(8,128)(2,1)S(1)}, bf16[128,3200]{1,0:T(8,128)(2,1)S(1)}, u32[]{:S(2)}, u32[]{:S(2)}) %collective-permute-start.1) | collective-permute-done | bytes 819232 | tf_op jit(solution)/shard_map/ppermute | solution.py:518
  24.4 0.0 collective-permute-start.2
  24.4 0.0 collective-permute-done.refs_1_
  24.4 2.3 %collective-permute-done.2.refs_3_ = bf16[128,3200]{1,0:T(8,128)(2,1)S(1)} collective-permute-done((bf16[128,3200]{1,0:T(8,128)(2,1)S(1)}, bf16[128,3200]{1,0:T(8,128)(2,1)S(1)}, u32[]{:S(2)}, u32[]{:S(2)}) %collective-permute-start.2) | collective-permute-done | bytes 819232 | tf_op jit(solution)/shard_map/ppermute | solution.py:518
  26.8 1.1 %routing_tables.1 = (bf16[2,192,512]{2,1,0:T(8,128)(2,1)S(1)}, bf16[2,512,192]{2,1,0:T(8,128)(2,1)S(1)}, f32[512,128]{1,0:T(8,128)S(1)}, f32[8,512]{1,0:T(8,128)S(1)}, f32[2,8,192]{2,1,0:T(8,128)S(1)}) custom-call(s32[2]{0:T(128)S(1)} %pad_add_fusion.ids_ref.refs_5_, s32[16]{0:T(128)S(1)} %copy-done.4, s32[64]{0:T(128)S(1)} %copy-done.5, ...), custom_call_target="tpu_custom_call" | custom-call | flops 1 | bytes 1 | tf_op jit(solution)/shard_map/routing_tables/pallas_call | solution.py:131
  27.9 20.2 %experts.1 = (bf16[4,192,1024]{2,1,0:T(8,128)(2,1)S(1)}, bf16[32,512]{1,0:T(8,128)(2,1)S(1)}, bf16[4,1024,768]{2,1,0:T(8,128)(2,1)S(1)}) custom-call(bf16[128,3200]{1,0:T(8,128)(2,1)S(1)} %tokens_with_facts.1.refs_0_, bf16[128,3200]{1,0:T(8,128)(2,1)} %copy-done.1, bf16[128,3200]{1,0:T(8,128)(2,1)} %copy-done, bf16[128,3200]{1,0:T(8,128)(2,1)} %copy-done.2, ...), custom_call_target="tpu_custom_call" | custom-call | flops 1 | bytes 1 | tf_op jit(solution)/shard_map/experts/pallas_call | solution.py:311
  48.1 2.9 %collective-permute-start.3 = (bf16[32,512]{1,0:T(8,128)(2,1)S(1)}, bf16[32,512]{1,0:T(8,128)(2,1)S(1)}, u32[]{:S(2)}, u32[]{:S(2)}) collective-permute-start(bf16[32,512]{1,0:T(8,128)(2,1)S(1)} %get-tuple-element.60), channel_id=1, source_target_pairs={{0,2},{1,3},{2,0},{3,1},{4,6},{5,7},{6,4},{7,5},{8,10},{9,11},{10,... | collective-permute-start | bytes 98312 | tf_op jit(solution)/shard_map/ppermute | solution.py:551
  51.0 5.2 %down_first.1 = (bf16[256,768]{1,0:T(8,128)(2,1)S(1)}, bf16[256,768]{1,0:T(8,128)(2,1)S(1)}, bf16[4,1024,768]{2,1,0:T(8,128)(2,1)S(1)}) custom-call(s32[2]{0:T(128)S(1)} %pad_add_fusion.ids_ref.refs_5_, bf16[4,192,1024]{2,1,0:T(8,128)(2,1)S(1)} %get-tuple-element.73.hidden_ref, bf16[4,1024,768]{2,1,0:T(8,128)(2,1)S(1)} %get-tuple-element.62.weight_ref, ...), custom_call_target="tpu_custom_call" | custom-call | flops 1 | bytes 1 | tf_op jit(solution)/shard_map/down_first/pallas_call | solution.py:361
  56.2 0.0 collective-permute-done.3
  56.2 0.1 collective-permute-start.4
  56.3 0.6 collective-permute-start.6
  56.9 1.1 %collective-permute-done.4.came_ref = bf16[256,768]{1,0:T(8,128)(2,1)S(1)} collective-permute-done((bf16[256,768]{1,0:T(8,128)(2,1)S(1)}, bf16[256,768]{1,0:T(8,128)(2,1)S(1)}, u32[]{:S(2)}, u32[]{:S(2)}) %collective-permute-start.4) | collective-permute-done | bytes 393248 | tf_op jit(solution)/shard_map/ppermute | solution.py:518
  58.0 0.1 sum_and_split.3
  58.1 1.6 %collective-permute-start.5 = (bf16[128,768]{1,0:T(8,128)(2,1)S(1)}, bf16[128,768]{1,0:T(8,128)(2,1)S(1)}, u32[]{:S(2)}, u32[]{:S(2)}) collective-permute-start(bf16[128,768]{1,0:T(8,128)(2,1)S(1)} %get-tuple-element.70), channel_id=1, source_target_pairs={{0,8},{4,12},{8,0},{12,4},{1,9},{5,13},{9,1},{13,5},{2,10},{6,14},... | collective-permute-start | bytes 589832 | tf_op jit(solution)/shard_map/ppermute | solution.py:518
  59.6 0.0 collective-permute-done.6
  59.6 0.6 collective-permute-start.7
  60.2 8.1 %down_rest.1 = (bf16[256,1536]{1,0:T(8,128)(2,1)S(1)}, bf16[256,1536]{1,0:T(8,128)(2,1)S(1)}, f32[512,768]{1,0:T(8,128)S(1)}) custom-call(s32[2]{0:T(128)S(1)} %pad_add_fusion.ids_ref.refs_5_, bf16[4,192,1024]{2,1,0:T(8,128)(2,1)S(1)} %get-tuple-element.73.hidden_ref, bf16[4,1024,768]{2,1,0:T(8,128)(2,1)S(1)} %get-tuple-element.74.weight_ref, ...), custom_call_target="tpu_custom_call" | custom-call | flops 1 | bytes 1 | tf_op jit(solution)/shard_map/down_rest/pallas_call | solution.py:395
  68.3 0.0 collective-permute-done.7
  68.3 0.0 collective-permute-done.5.came_ref
  68.4 0.1 collective-permute-start.8
  68.5 1.6 %collective-permute-start.10 = (bf16[128,512]{1,0:T(8,128)(2,1)S(1)}, bf16[128,512]{1,0:T(8,128)(2,1)S(1)}, u32[]{:S(2)}, u32[]{:S(2)}) collective-permute-start(bf16[128,512]{1,0:T(8,128)(2,1)S(1)} %pad_maximum_fusion), channel_id=1, source_target_pairs={{0,1},{1,0},{2,3},{3,2},{4,5},{5,4},{6,7},{7,6},{8,9},{9,8},{10,11... | collective-permute-start | bytes 393224 | tf_op jit(solution)/shard_map/ppermute | solution.py:551
  70.1 4.3 %collective-permute-done.10 = bf16[128,512]{1,0:T(8,128)(2,1)S(1)} collective-permute-done((bf16[128,512]{1,0:T(8,128)(2,1)S(1)}, bf16[128,512]{1,0:T(8,128)(2,1)S(1)}, u32[]{:S(2)}, u32[]{:S(2)}) %collective-permute-start.10) | collective-permute-done | bytes 131104 | tf_op jit(solution)/shard_map/ppermute | solution.py:551
  74.5 2.8 %adapters.1 = (bf16[256,768]{1,0:T(8,128)(2,1)S(1)}, bf16[256,768]{1,0:T(8,128)(2,1)S(1)}) custom-call(s32[2]{0:T(128)S(1)} %pad_add_fusion.ids_ref.refs_5_, f32[512,768]{1,0:T(8,128)S(1)} %get-tuple-element.81.base_ref, f32[512,128]{1,0:T(8,128)S(1)} %get-tuple-element.64.cols_ref, bf16[2048,768]{1,0:T(8,128)(2,1)S(1)} %bitcast.6, ...), custom_call_target="tpu_custom_call" | custom-call | flops 1 | bytes 1 | tf_op jit(solution)/shard_map/adapters/pallas_call | solution.py:441
  77.2 0.1 collective-permute-start.11
  77.3 0.0 collective-permute-done.8.came_ref
  77.3 0.2 sum_and_split.4
  77.5 1.6 %collective-permute-start.9 = (bf16[128,1536]{1,0:T(8,128)(2,1)S(1)}, bf16[128,1536]{1,0:T(8,128)(2,1)S(1)}, u32[]{:S(2)}, u32[]{:S(2)}) collective-permute-start(bf16[128,1536]{1,0:T(8,128)(2,1)S(1)} %get-tuple-element.80), channel_id=1, source_target_pairs={{0,8},{4,12},{8,0},{12,4},{1,9},{5,13},{9,1},{13,5},{2,10},{6,14},... | collective-permute-start | bytes 1179656 | tf_op jit(solution)/shard_map/ppermute | solution.py:518
  79.1 0.4 collective-permute-start.13
  79.5 0.0 collective-permute-done.11.came_ref
  79.5 0.1 sum_and_split.5
  79.6 9.5 %collective-permute-done.9.came_ref = bf16[128,1536]{1,0:T(8,128)(2,1)S(1)} collective-permute-done((bf16[128,1536]{1,0:T(8,128)(2,1)S(1)}, bf16[128,1536]{1,0:T(8,128)(2,1)S(1)}, u32[]{:S(2)}, u32[]{:S(2)}) %collective-permute-start.9) | collective-permute-done | bytes 393248 | tf_op jit(solution)/shard_map/ppermute | solution.py:518
  89.1 0.1 sum_and_cut.3
  89.2 1.6 %collective-permute-start.14 = (bf16[128,768]{1,0:T(8,128)(2,1)S(1)}, bf16[128,768]{1,0:T(8,128)(2,1)S(1)}, u32[]{:S(2)}, u32[]{:S(2)}) collective-permute-start(bf16[128,768]{1,0:T(8,128)(2,1)S(1)} %get-tuple-element.93), channel_id=1, source_target_pairs={{0,1},{1,2},{2,3},{3,0},{4,5},{5,6},{6,7},{7,4},{8,9},{9,10},{10,1... | collective-permute-start | bytes 589832 | tf_op jit(solution)/shard_map/ppermute | solution.py:524
  90.8 2.2 %collective-permute-start.15 = (bf16[128,768]{1,0:T(8,128)(2,1)S(1)}, bf16[128,768]{1,0:T(8,128)(2,1)S(1)}, u32[]{:S(2)}, u32[]{:S(2)}) collective-permute-start(bf16[128,768]{1,0:T(8,128)(2,1)S(1)} %get-tuple-element.94), channel_id=1, source_target_pairs={{0,3},{1,0},{2,1},{3,2},{4,7},{5,4},{6,5},{7,6},{8,11},{9,8},{10,9... | collective-permute-start | bytes 589832 | tf_op jit(solution)/shard_map/ppermute | solution.py:524
  93.1 1.5 %collective-permute-start.12 = (bf16[128,768]{1,0:T(8,128)(2,1)S(1)}, bf16[128,768]{1,0:T(8,128)(2,1)S(1)}, u32[]{:S(2)}, u32[]{:S(2)}) collective-permute-start(bf16[128,768]{1,0:T(8,128)(2,1)S(1)} %get-tuple-element.88), channel_id=1, source_target_pairs={{0,8},{4,12},{8,0},{12,4},{1,9},{5,13},{9,1},{13,5},{2,10},{6,14},... | collective-permute-start | bytes 589832 | tf_op jit(solution)/shard_map/ppermute | solution.py:518
  94.6 0.0 collective-permute-done.13
  94.6 4.3 %collective-permute-done.14 = bf16[128,768]{1,0:T(8,128)(2,1)S(1)} collective-permute-done((bf16[128,768]{1,0:T(8,128)(2,1)S(1)}, bf16[128,768]{1,0:T(8,128)(2,1)S(1)}, u32[]{:S(2)}, u32[]{:S(2)}) %collective-permute-start.14) | collective-permute-done | bytes 196640 | tf_op jit(solution)/shard_map/ppermute | solution.py:524
  98.9 2.4 %collective-permute-done.15 = bf16[128,768]{1,0:T(8,128)(2,1)S(1)} collective-permute-done((bf16[128,768]{1,0:T(8,128)(2,1)S(1)}, bf16[128,768]{1,0:T(8,128)(2,1)S(1)}, u32[]{:S(2)}, u32[]{:S(2)}) %collective-permute-start.15) | collective-permute-done | bytes 196640 | tf_op jit(solution)/shard_map/ppermute | solution.py:524
  101.3 0.0 collective-permute-done.12
  101.3 0.8 add_convert_fusion
  (20 shorter events, 0.1 us)
Async XLA Ops:
  0.0 0.7 copy-start.6
  0.7 0.7 copy-start.7
  1.4 0.7 copy-start.8
  3.2 21.2 %collective-permute-start.1 = (bf16[128,3200]{1,0:T(8,128)(2,1)S(1)}, bf16[128,3200]{1,0:T(8,128)(2,1)S(1)}, u32[]{:S(2)}, u32[]{:S(2)}) collective-permute-start(bf16[128,3200]{1,0:T(8,128)(2,1)S(1)} %tokens_with_facts.1.refs_0_), channel_id=1, source_target_pairs={{0,8},{4,12},{8,0},{12,4},{1,9},{5,13},{9,1},{13,5},{2,10},{6,14},... | collective-permute-start | bytes 2457608 | tf_op jit(solution)/shard_map/ppermute | solution.py:518
  6.2 18.3 %collective-permute-start = (bf16[128,3200]{1,0:T(8,128)(2,1)S(1)}, bf16[128,3200]{1,0:T(8,128)(2,1)S(1)}, u32[]{:S(2)}, u32[]{:S(2)}) collective-permute-start(bf16[128,3200]{1,0:T(8,128)(2,1)S(1)} %tokens_with_facts.1.refs_0_), channel_id=1, source_target_pairs={{0,4},{4,0},{8,12},{12,8},{1,5},{5,1},{9,13},{13,9},{2,6},{6,2},{1... | collective-permute-start | bytes 2457608 | tf_op jit(solution)/shard_map/ppermute | solution.py:518
  6.2 20.5 %copy-start.4 = (s32[16]{0:T(128)S(1)}, s32[16]{0:T(128)}, u32[]{:S(2)}) copy-start(s32[16]{0:T(128)} %refs_6_.1) | copy-start | bytes 196
  6.3 20.5 %copy-start.5 = (s32[64]{0:T(128)S(1)}, s32[64]{0:T(128)}, u32[]{:S(2)}) copy-start(s32[64]{0:T(128)} %refs_7_.1) | copy-start | bytes 772
  24.4 3.4 %copy-start = (bf16[128,3200]{1,0:T(8,128)(2,1)}, bf16[128,3200]{1,0:T(8,128)(2,1)S(1)}, u32[]{:S(2)}) copy-start(bf16[128,3200]{1,0:T(8,128)(2,1)S(1)} %collective-permute-done.1.refs_2_) | copy-start | bytes 2457604
  24.4 2.3 %collective-permute-start.2 = (bf16[128,3200]{1,0:T(8,128)(2,1)S(1)}, bf16[128,3200]{1,0:T(8,128)(2,1)S(1)}, u32[]{:S(2)}, u32[]{:S(2)}) collective-permute-start(bf16[128,3200]{1,0:T(8,128)(2,1)S(1)} %collective-permute-done.1.refs_2_), channel_id=1, source_target_pairs={{0,4},{4,0},{8,12},{12,8},{1,5},{5,1},{9,13},{13,9},{2,6},{6,2},{1... | collective-permute-start | bytes 2457608 | tf_op jit(solution)/shard_map/ppermute | solution.py:518
  24.4 3.4 %copy-start.1 = (bf16[128,3200]{1,0:T(8,128)(2,1)}, bf16[128,3200]{1,0:T(8,128)(2,1)S(1)}, u32[]{:S(2)}) copy-start(bf16[128,3200]{1,0:T(8,128)(2,1)S(1)} %collective-permute-done.refs_1_) | copy-start | bytes 2457604
  26.8 1.1 %copy-start.2 = (bf16[128,3200]{1,0:T(8,128)(2,1)}, bf16[128,3200]{1,0:T(8,128)(2,1)S(1)}, u32[]{:S(2)}) copy-start(bf16[128,3200]{1,0:T(8,128)(2,1)S(1)} %collective-permute-done.2.refs_3_) | copy-start | bytes 2457604
  48.1 8.1 %collective-permute-start.3 = (bf16[32,512]{1,0:T(8,128)(2,1)S(1)}, bf16[32,512]{1,0:T(8,128)(2,1)S(1)}, u32[]{:S(2)}, u32[]{:S(2)}) collective-permute-start(bf16[32,512]{1,0:T(8,128)(2,1)S(1)} %get-tuple-element.60), channel_id=1, source_target_pairs={{0,2},{1,3},{2,0},{3,1},{4,6},{5,7},{6,4},{7,5},{8,10},{9,11},{10,... | collective-permute-start | bytes 98312 | tf_op jit(solution)/shard_map/ppermute | solution.py:551
  56.2 1.8 %collective-permute-start.4 = (bf16[256,768]{1,0:T(8,128)(2,1)S(1)}, bf16[256,768]{1,0:T(8,128)(2,1)S(1)}, u32[]{:S(2)}, u32[]{:S(2)}) collective-permute-start(bf16[256,768]{1,0:T(8,128)(2,1)S(1)} %get-tuple-element.69), channel_id=1, source_target_pairs={{0,4},{4,0},{8,12},{12,8},{1,5},{5,1},{9,13},{13,9},{2,6},{6,2},{1... | collective-permute-start | bytes 1179656 | tf_op jit(solution)/shard_map/ppermute | solution.py:518
  56.3 3.3 %collective-permute-start.6 = (bf16[32,512]{1,0:T(8,128)(2,1)S(1)}, bf16[32,512]{1,0:T(8,128)(2,1)S(1)}, u32[]{:S(2)}, u32[]{:S(2)}) collective-permute-start(bf16[32,512]{1,0:T(8,128)(2,1)S(1)} %add_convert_fusion.2), channel_id=1, source_target_pairs={{0,4},{4,0},{8,12},{12,8},{1,5},{5,1},{9,13},{13,9},{2,6},{6,2},{1... | collective-permute-start | bytes 98312 | tf_op jit(solution)/shard_map/ppermute | solution.py:518
  58.1 10.3 %collective-permute-start.5 = (bf16[128,768]{1,0:T(8,128)(2,1)S(1)}, bf16[128,768]{1,0:T(8,128)(2,1)S(1)}, u32[]{:S(2)}, u32[]{:S(2)}) collective-permute-start(bf16[128,768]{1,0:T(8,128)(2,1)S(1)} %get-tuple-element.70), channel_id=1, source_target_pairs={{0,8},{4,12},{8,0},{12,4},{1,9},{5,13},{9,1},{13,5},{2,10},{6,14},... | collective-permute-start | bytes 589832 | tf_op jit(solution)/shard_map/ppermute | solution.py:518
  59.6 8.7 %collective-permute-start.7 = (bf16[64,512]{1,0:T(8,128)(2,1)S(1)}, bf16[64,512]{1,0:T(8,128)(2,1)S(1)}, u32[]{:S(2)}, u32[]{:S(2)}) collective-permute-start(bf16[64,512]{1,0:T(8,128)(2,1)S(1)} %pad_maximum_fusion.1), channel_id=1, source_target_pairs={{0,8},{4,12},{8,0},{12,4},{1,9},{5,13},{9,1},{13,5},{2,10},{6,14},... | collective-permute-start | bytes 196616 | tf_op jit(solution)/shard_map/ppermute | solution.py:518
  60.2 14.2 %copy-start.3 = (bf16[16,8,16,768]{3,2,1,0:T(8,128)(2,1)S(1)}, bf16[16,8,16,768]{3,2,1,0:T(8,128)(2,1)}, u32[]{:S(2)}) copy-start(bf16[16,8,16,768]{3,2,1,0:T(8,128)(2,1)} %param.21) | copy-start | bytes 9437188
  68.4 9.0 %collective-permute-start.8 = (bf16[256,1536]{1,0:T(8,128)(2,1)S(1)}, bf16[256,1536]{1,0:T(8,128)(2,1)S(1)}, u32[]{:S(2)}, u32[]{:S(2)}) collective-permute-start(bf16[256,1536]{1,0:T(8,128)(2,1)S(1)} %get-tuple-element.79), channel_id=1, source_target_pairs={{0,4},{4,0},{8,12},{12,8},{1,5},{5,1},{9,13},{13,9},{2,6},{6,2},{1... | collective-permute-start | bytes 2359304 | tf_op jit(solution)/shard_map/ppermute | solution.py:518
  68.5 6.0 %collective-permute-start.10 = (bf16[128,512]{1,0:T(8,128)(2,1)S(1)}, bf16[128,512]{1,0:T(8,128)(2,1)S(1)}, u32[]{:S(2)}, u32[]{:S(2)}) collective-permute-start(bf16[128,512]{1,0:T(8,128)(2,1)S(1)} %pad_maximum_fusion), channel_id=1, source_target_pairs={{0,1},{1,0},{2,3},{3,2},{4,5},{5,4},{6,7},{7,6},{8,9},{9,8},{10,11... | collective-permute-start | bytes 393224 | tf_op jit(solution)/shard_map/ppermute | solution.py:551
  77.2 2.3 %collective-permute-start.11 = (bf16[256,768]{1,0:T(8,128)(2,1)S(1)}, bf16[256,768]{1,0:T(8,128)(2,1)S(1)}, u32[]{:S(2)}, u32[]{:S(2)}) collective-permute-start(bf16[256,768]{1,0:T(8,128)(2,1)S(1)} %get-tuple-element.84), channel_id=1, source_target_pairs={{0,4},{4,0},{8,12},{12,8},{1,5},{5,1},{9,13},{13,9},{2,6},{6,2},{1... | collective-permute-start | bytes 1179656 | tf_op jit(solution)/shard_map/ppermute | solution.py:518
  77.5 11.6 %collective-permute-start.9 = (bf16[128,1536]{1,0:T(8,128)(2,1)S(1)}, bf16[128,1536]{1,0:T(8,128)(2,1)S(1)}, u32[]{:S(2)}, u32[]{:S(2)}) collective-permute-start(bf16[128,1536]{1,0:T(8,128)(2,1)S(1)} %get-tuple-element.80), channel_id=1, source_target_pairs={{0,8},{4,12},{8,0},{12,4},{1,9},{5,13},{9,1},{13,5},{2,10},{6,14},... | collective-permute-start | bytes 1179656 | tf_op jit(solution)/shard_map/ppermute | solution.py:518
  79.1 15.4 %collective-permute-start.13 = (bf16[128,768]{1,0:T(8,128)(2,1)S(1)}, bf16[128,768]{1,0:T(8,128)(2,1)S(1)}, u32[]{:S(2)}, u32[]{:S(2)}) collective-permute-start(bf16[128,768]{1,0:T(8,128)(2,1)S(1)} %sum_and_cut.2), channel_id=1, source_target_pairs={{0,2},{1,3},{2,0},{3,1},{4,6},{5,7},{6,4},{7,5},{8,10},{9,11},{10,... | collective-permute-start | bytes 589832 | tf_op jit(solution)/shard_map/ppermute | solution.py:524
  89.2 9.7 %collective-permute-start.14 = (bf16[128,768]{1,0:T(8,128)(2,1)S(1)}, bf16[128,768]{1,0:T(8,128)(2,1)S(1)}, u32[]{:S(2)}, u32[]{:S(2)}) collective-permute-start(bf16[128,768]{1,0:T(8,128)(2,1)S(1)} %get-tuple-element.93), channel_id=1, source_target_pairs={{0,1},{1,2},{2,3},{3,0},{4,5},{5,6},{6,7},{7,4},{8,9},{9,10},{10,1... | collective-permute-start | bytes 589832 | tf_op jit(solution)/shard_map/ppermute | solution.py:524
  90.8 10.4 %collective-permute-start.15 = (bf16[128,768]{1,0:T(8,128)(2,1)S(1)}, bf16[128,768]{1,0:T(8,128)(2,1)S(1)}, u32[]{:S(2)}, u32[]{:S(2)}) collective-permute-start(bf16[128,768]{1,0:T(8,128)(2,1)S(1)} %get-tuple-element.94), channel_id=1, source_target_pairs={{0,3},{1,0},{2,1},{3,2},{4,7},{5,4},{6,5},{7,6},{8,11},{9,8},{10,9... | collective-permute-start | bytes 589832 | tf_op jit(solution)/shard_map/ppermute | solution.py:524
  93.1 8.2 %collective-permute-start.12 = (bf16[128,768]{1,0:T(8,128)(2,1)S(1)}, bf16[128,768]{1,0:T(8,128)(2,1)S(1)}, u32[]{:S(2)}, u32[]{:S(2)}) collective-permute-start(bf16[128,768]{1,0:T(8,128)(2,1)S(1)} %get-tuple-element.88), channel_id=1, source_target_pairs={{0,8},{4,12},{8,0},{12,4},{1,9},{5,13},{9,1},{13,5},{2,10},{6,14},... | collective-permute-start | bytes 589832 | tf_op jit(solution)/shard_map/ppermute | solution.py:518

commit v7 on v6

--- a/solution.py
+++ b/solution.py
@@ -574,6 +574,7 @@
     slot_count = adapter_output_factors.shape[0]
     flat_factors = adapter_output_factors.reshape(slot_count * EXPERT_COUNT * RANK, span)
     keep, send = adapter_part(ids, base, cols, 2 * n_local, local_halves, flat_factors, low)
+    came_rest, keep, send = lax.optimization_barrier((came_rest, keep, send))
     came = swap(send, 1)
     if bits > 1:
         keep, send = split_sum(keep, came)

time: 102 us -> 102 us (level); the launches traced: 102 us -> 100 us
  waiting for transfers between devices: 33.2 us -> 31.9 us
    ppermute x11, waiting for transfers between devices: 22.2 us -> 18 us  [swap(): return lax.ppermute(x, 'ep', [(i, i ^ mask) for i in range(n_ep)])]
    ppermute x3, waiting for transfers between devices: 6.71 us -> 10.2 us  [shift(): return lax.ppermute(x, 'ad', [(i, (i + step) % n_ad) for i in range(n_ad)])]
  transfers between devices with their start and end apart: 16 -> 16, of which waited for: 7 -> 9; matrix products, arithmetic and copies ran while one was open for 0% -> 0% of each run, Pallas kernels for 25% -> 25%
where the time goes in v7:
time: 102 us; the launch traced here: 100 us
  Pallas kernels  47.9 us (47%)
  waiting for transfers between devices  31.9 us (31%)
  starting transfers between devices  17.5 us (17%)
  local copies, waits for them, and re-layouts  2.03 us (2%)
    pallas_call x1, Pallas kernels, expert_part(): pl.pallas_call(functools.partial(expert_kernel, len(blocks), len(resident...  20.2 us
    ppermute x11, waiting for transfers between devices, swap(): return lax.ppermute(x, 'ep', [(i, i ^ mask) for i in range(n_ep)])  18 us
    ppermute x3, waiting for transfers between devices, shift(): return lax.ppermute(x, 'ad', [(i, (i + step) % n_ad) for i in range(n_ad)])  10.2 us
    ppermute x11, starting transfers between devices, swap(): return lax.ppermute(x, 'ep', [(i, i ^ mask) for i in range(n_ep)])  8.91 us
    pallas_call x1, Pallas kernels, prefetch(): pl.pallas_call(prefetch_kernel, out_shape=(*[pltpu.VMEM(shape, BF16) for...  8.89 us
    pallas_call x1, Pallas kernels, down_rest(): pl.pallas_call(functools.partial(down_rest_kernel, n_ad, steps), out_shap...  8.08 us
    pallas_call x1, Pallas kernels, down_first(): pl.pallas_call(functools.partial(down_first_kernel, n_ad, step), out_shap...  5.21 us
    ppermute x2, starting transfers between devices, other_of(): return lax.ppermute(low, 'ad', [(i, i ^ 1 << bit) for i in range(n_ad)])  4.52 us
  transfers between devices with their start and end apart: 16, of which 9 were waited for; matrix products, arithmetic and copies ran while one was open for 0% of the time, Pallas kernels for 25%

profile of v7, /device:TPU:0, one launch (start us, length us, event | category | flops | bytes accessed | tf_op | source)
XLA Modules:
  0.0 100.4 jit_solution(15200197126590739032)
XLA Ops:
  0.0 0.7 copy-done.6
  0.7 0.7 copy-done.7
  1.4 0.7 copy-done.8
  2.0 1.1 %tokens_with_facts.1.refs_0_ = bf16[128,3200]{1,0:T(8,128)(2,1)S(1)} custom-call(bf16[128,3072]{1,0:T(8,128)(2,1)} %tokens_ref.1, s32[2,128]{1,0:T(2,128)S(1)} %bitcast.7, f32[2,128]{1,0:T(2,128)S(1)} %bitcast.8, s32[1,128]{1,0:T(1,128)S(1)} %bitcast.9), custom_call_target="tpu_custom_call" | custom-call | flops 1 | bytes 1 | tf_op jit(solution)/shard_map/tokens_with_facts/pallas_call | solution.py:76
  3.2 3.0 %collective-permute-start.1 = (bf16[128,3200]{1,0:T(8,128)(2,1)S(1)}, bf16[128,3200]{1,0:T(8,128)(2,1)S(1)}, u32[]{:S(2)}, u32[]{:S(2)}) collective-permute-start(bf16[128,3200]{1,0:T(8,128)(2,1)S(1)} %tokens_with_facts.1.refs_0_), channel_id=1, source_target_pairs={{0,8},{4,12},{8,0},{12,4},{1,9},{5,13},{9,1},{13,5},{2,10},{6,14},... | collective-permute-start | bytes 2457608 | tf_op jit(solution)/shard_map/ppermute | solution.py:518
  6.2 0.0 collective-permute-start
  6.2 0.1 pad_add_fusion.ids_ref.refs_5_
  6.3 8.9 %weight_prefetch.1 = (bf16[2,3072,512]{2,1,0:T(8,128)(2,1)S(1)}, bf16[2,3072,512]{2,1,0:T(8,128)(2,1)S(1)}, bf16[2,3072,512]{2,1,0:T(8,128)(2,1)S(1)}, bf16[2,3072,512]{2,1,0:T(8,128)(2,1)S(1)}, f32[8,128]{1,0:T(8,128)S(1)}) custom-call(s32[2]{0:T(128)S(1)} %pad_add_fusion.ids_ref.refs_5_, bf16[4,3072,1024]{2,1,0:T(8,128)(2,1)} %refs_11_.1, ...), custom_call_target="tpu_custom_call" | custom-call | flops 1 | bytes 1 | tf_op jit(solution)/shard_map/weight_prefetch/pallas_call | solution.py:225
  15.2 9.3 %collective-permute-done.1.refs_2_ = bf16[128,3200]{1,0:T(8,128)(2,1)S(1)} collective-permute-done((bf16[128,3200]{1,0:T(8,128)(2,1)S(1)}, bf16[128,3200]{1,0:T(8,128)(2,1)S(1)}, u32[]{:S(2)}, u32[]{:S(2)}) %collective-permute-start.1) | collective-permute-done | bytes 819232 | tf_op jit(solution)/shard_map/ppermute | solution.py:518
  24.4 0.0 collective-permute-start.2
  24.4 0.0 collective-permute-done.refs_1_
  24.4 2.3 %collective-permute-done.2.refs_3_ = bf16[128,3200]{1,0:T(8,128)(2,1)S(1)} collective-permute-done((bf16[128,3200]{1,0:T(8,128)(2,1)S(1)}, bf16[128,3200]{1,0:T(8,128)(2,1)S(1)}, u32[]{:S(2)}, u32[]{:S(2)}) %collective-permute-start.2) | collective-permute-done | bytes 819232 | tf_op jit(solution)/shard_map/ppermute | solution.py:518
  26.8 1.1 %routing_tables.1 = (bf16[2,192,512]{2,1,0:T(8,128)(2,1)S(1)}, bf16[2,512,192]{2,1,0:T(8,128)(2,1)S(1)}, f32[512,128]{1,0:T(8,128)S(1)}, f32[8,512]{1,0:T(8,128)S(1)}, f32[2,8,192]{2,1,0:T(8,128)S(1)}) custom-call(s32[2]{0:T(128)S(1)} %pad_add_fusion.ids_ref.refs_5_, s32[16]{0:T(128)S(1)} %copy-done.4, s32[64]{0:T(128)S(1)} %copy-done.5, ...), custom_call_target="tpu_custom_call" | custom-call | flops 1 | bytes 1 | tf_op jit(solution)/shard_map/routing_tables/pallas_call | solution.py:131
  27.9 20.2 %experts.1 = (bf16[4,192,1024]{2,1,0:T(8,128)(2,1)S(1)}, bf16[32,512]{1,0:T(8,128)(2,1)S(1)}, bf16[4,1024,768]{2,1,0:T(8,128)(2,1)S(1)}) custom-call(bf16[128,3200]{1,0:T(8,128)(2,1)S(1)} %tokens_with_facts.1.refs_0_, bf16[128,3200]{1,0:T(8,128)(2,1)} %copy-done.1, bf16[128,3200]{1,0:T(8,128)(2,1)} %copy-done, bf16[128,3200]{1,0:T(8,128)(2,1)} %copy-done.2, ...), custom_call_target="tpu_custom_call" | custom-call | flops 1 | bytes 1 | tf_op jit(solution)/shard_map/experts/pallas_call | solution.py:311
  48.1 2.9 %collective-permute-start.3 = (bf16[32,512]{1,0:T(8,128)(2,1)S(1)}, bf16[32,512]{1,0:T(8,128)(2,1)S(1)}, u32[]{:S(2)}, u32[]{:S(2)}) collective-permute-start(bf16[32,512]{1,0:T(8,128)(2,1)S(1)} %get-tuple-element.63), channel_id=1, source_target_pairs={{0,2},{1,3},{2,0},{3,1},{4,6},{5,7},{6,4},{7,5},{8,10},{9,11},{10,... | collective-permute-start | bytes 98312 | tf_op jit(solution)/shard_map/ppermute | solution.py:551
  51.0 5.2 %down_first.1 = (bf16[256,768]{1,0:T(8,128)(2,1)S(1)}, bf16[256,768]{1,0:T(8,128)(2,1)S(1)}, bf16[4,1024,768]{2,1,0:T(8,128)(2,1)S(1)}) custom-call(s32[2]{0:T(128)S(1)} %pad_add_fusion.ids_ref.refs_5_, bf16[4,192,1024]{2,1,0:T(8,128)(2,1)S(1)} %get-tuple-element.76.hidden_ref, bf16[4,1024,768]{2,1,0:T(8,128)(2,1)S(1)} %get-tuple-element.65.weight_ref, ...), custom_call_target="tpu_custom_call" | custom-call | flops 1 | bytes 1 | tf_op jit(solution)/shard_map/down_first/pallas_call | solution.py:361
  56.2 0.0 collective-permute-done.3
  56.2 0.1 collective-permute-start.4
  56.3 0.6 collective-permute-start.6
  56.8 1.1 %collective-permute-done.4.came_ref = bf16[256,768]{1,0:T(8,128)(2,1)S(1)} collective-permute-done((bf16[256,768]{1,0:T(8,128)(2,1)S(1)}, bf16[256,768]{1,0:T(8,128)(2,1)S(1)}, u32[]{:S(2)}, u32[]{:S(2)}) %collective-permute-start.4) | collective-permute-done | bytes 393248 | tf_op jit(solution)/shard_map/ppermute | solution.py:518
  58.0 0.1 sum_and_split.3
  58.1 1.6 %collective-permute-start.5 = (bf16[128,768]{1,0:T(8,128)(2,1)S(1)}, bf16[128,768]{1,0:T(8,128)(2,1)S(1)}, u32[]{:S(2)}, u32[]{:S(2)}) collective-permute-start(bf16[128,768]{1,0:T(8,128)(2,1)S(1)} %get-tuple-element.73), channel_id=1, source_target_pairs={{0,8},{4,12},{8,0},{12,4},{1,9},{5,13},{9,1},{13,5},{2,10},{6,14},... | collective-permute-start | bytes 589832 | tf_op jit(solution)/shard_map/ppermute | solution.py:518
  59.6 0.0 collective-permute-done.6
  59.6 0.6 collective-permute-start.7
  60.2 8.1 %down_rest.1 = (bf16[256,1536]{1,0:T(8,128)(2,1)S(1)}, bf16[256,1536]{1,0:T(8,128)(2,1)S(1)}, f32[512,768]{1,0:T(8,128)S(1)}) custom-call(s32[2]{0:T(128)S(1)} %pad_add_fusion.ids_ref.refs_5_, bf16[4,192,1024]{2,1,0:T(8,128)(2,1)S(1)} %get-tuple-element.76.hidden_ref, bf16[4,1024,768]{2,1,0:T(8,128)(2,1)S(1)} %get-tuple-element.77.weight_ref, ...), custom_call_target="tpu_custom_call" | custom-call | flops 1 | bytes 1 | tf_op jit(solution)/shard_map/down_rest/pallas_call | solution.py:395
  68.3 0.0 collective-permute-done.7
  68.3 0.0 collective-permute-done.5.came_ref
  68.3 0.1 collective-permute-start.8
  68.4 2.3 %collective-permute-done.8.came_ref = bf16[256,1536]{1,0:T(8,128)(2,1)S(1)} collective-permute-done((bf16[256,1536]{1,0:T(8,128)(2,1)S(1)}, bf16[256,1536]{1,0:T(8,128)(2,1)S(1)}, u32[]{:S(2)}, u32[]{:S(2)}) %collective-permute-start.8) | collective-permute-done | bytes 786464 | tf_op jit(solution)/shard_map/ppermute | solution.py:518
  70.7 0.2 sum_and_split.4
  70.9 1.6 %collective-permute-start.9 = (bf16[128,1536]{1,0:T(8,128)(2,1)S(1)}, bf16[128,1536]{1,0:T(8,128)(2,1)S(1)}, u32[]{:S(2)}, u32[]{:S(2)}) collective-permute-start(bf16[128,1536]{1,0:T(8,128)(2,1)S(1)} %get-tuple-element.83), channel_id=1, source_target_pairs={{0,8},{4,12},{8,0},{12,4},{1,9},{5,13},{9,1},{13,5},{2,10},{6,14},... | collective-permute-start | bytes 1179656 | tf_op jit(solution)/shard_map/ppermute | solution.py:518
  72.4 1.6 %collective-permute-start.10 = (bf16[128,512]{1,0:T(8,128)(2,1)S(1)}, bf16[128,512]{1,0:T(8,128)(2,1)S(1)}, u32[]{:S(2)}, u32[]{:S(2)}) collective-permute-start(bf16[128,512]{1,0:T(8,128)(2,1)S(1)} %pad_maximum_fusion), channel_id=1, source_target_pairs={{0,1},{1,0},{2,3},{3,2},{4,5},{5,4},{6,7},{7,6},{8,9},{9,8},{10,11... | collective-permute-start | bytes 393224 | tf_op jit(solution)/shard_map/ppermute | solution.py:551
  74.1 3.7 %collective-permute-done.10 = bf16[128,512]{1,0:T(8,128)(2,1)S(1)} collective-permute-done((bf16[128,512]{1,0:T(8,128)(2,1)S(1)}, bf16[128,512]{1,0:T(8,128)(2,1)S(1)}, u32[]{:S(2)}, u32[]{:S(2)}) %collective-permute-start.10) | collective-permute-done | bytes 131104 | tf_op jit(solution)/shard_map/ppermute | solution.py:551
  77.8 2.8 %adapters.1 = (bf16[256,768]{1,0:T(8,128)(2,1)S(1)}, bf16[256,768]{1,0:T(8,128)(2,1)S(1)}) custom-call(s32[2]{0:T(128)S(1)} %pad_add_fusion.ids_ref.refs_5_, f32[512,768]{1,0:T(8,128)S(1)} %get-tuple-element.84.base_ref, f32[512,128]{1,0:T(8,128)S(1)} %get-tuple-element.67.cols_ref, bf16[2048,768]{1,0:T(8,128)(2,1)S(1)} %bitcast.6, ...), custom_call_target="tpu_custom_call" | custom-call | flops 1 | bytes 1 | tf_op jit(solution)/shard_map/adapters/pallas_call | solution.py:441
  80.6 1.5 %collective-permute-done.9.came_ref = bf16[128,1536]{1,0:T(8,128)(2,1)S(1)} collective-permute-done((bf16[128,1536]{1,0:T(8,128)(2,1)S(1)}, bf16[128,1536]{1,0:T(8,128)(2,1)S(1)}, u32[]{:S(2)}, u32[]{:S(2)}) %collective-permute-start.9) | collective-permute-done | bytes 393248 | tf_op jit(solution)/shard_map/ppermute | solution.py:518
  82.1 0.0 collective-permute-start.11
  82.2 0.2 collective-permute-start.13
  82.3 1.5 %collective-permute-done.11.came_ref = bf16[256,768]{1,0:T(8,128)(2,1)S(1)} collective-permute-done((bf16[256,768]{1,0:T(8,128)(2,1)S(1)}, bf16[256,768]{1,0:T(8,128)(2,1)S(1)}, u32[]{:S(2)}, u32[]{:S(2)}) %collective-permute-start.11) | collective-permute-done | bytes 393248 | tf_op jit(solution)/shard_map/ppermute | solution.py:518
  83.8 0.1 sum_and_split.5
  83.9 0.1 sum_and_cut.3
  84.0 1.6 %collective-permute-start.14 = (bf16[128,768]{1,0:T(8,128)(2,1)S(1)}, bf16[128,768]{1,0:T(8,128)(2,1)S(1)}, u32[]{:S(2)}, u32[]{:S(2)}) collective-permute-start(bf16[128,768]{1,0:T(8,128)(2,1)S(1)} %get-tuple-element.99), channel_id=1, source_target_pairs={{0,1},{1,2},{2,3},{3,0},{4,5},{5,6},{6,7},{7,4},{8,9},{9,10},{10,1... | collective-permute-start | bytes 589832 | tf_op jit(solution)/shard_map/ppermute | solution.py:524
  85.7 2.2 %collective-permute-start.15 = (bf16[128,768]{1,0:T(8,128)(2,1)S(1)}, bf16[128,768]{1,0:T(8,128)(2,1)S(1)}, u32[]{:S(2)}, u32[]{:S(2)}) collective-permute-start(bf16[128,768]{1,0:T(8,128)(2,1)S(1)} %get-tuple-element.100), channel_id=1, source_target_pairs={{0,3},{1,0},{2,1},{3,2},{4,7},{5,4},{6,5},{7,6},{8,11},{9,8},{10,9... | collective-permute-start | bytes 589832 | tf_op jit(solution)/shard_map/ppermute | solution.py:524
  87.9 1.5 %collective-permute-start.12 = (bf16[128,768]{1,0:T(8,128)(2,1)S(1)}, bf16[128,768]{1,0:T(8,128)(2,1)S(1)}, u32[]{:S(2)}, u32[]{:S(2)}) collective-permute-start(bf16[128,768]{1,0:T(8,128)(2,1)S(1)} %get-tuple-element.94), channel_id=1, source_target_pairs={{0,8},{4,12},{8,0},{12,4},{1,9},{5,13},{9,1},{13,5},{2,10},{6,14},... | collective-permute-start | bytes 589832 | tf_op jit(solution)/shard_map/ppermute | solution.py:518
  89.4 9.9 %collective-permute-done.13 = bf16[128,768]{1,0:T(8,128)(2,1)S(1)} collective-permute-done((bf16[128,768]{1,0:T(8,128)(2,1)S(1)}, bf16[128,768]{1,0:T(8,128)(2,1)S(1)}, u32[]{:S(2)}, u32[]{:S(2)}) %collective-permute-start.13) | collective-permute-done | bytes 196640 | tf_op jit(solution)/shard_map/ppermute | solution.py:524
  99.3 0.0 collective-permute-done.14
  99.3 0.3 collective-permute-done.15
  99.6 0.0 collective-permute-done.12
  99.6 0.8 add_convert_fusion
  (20 shorter events, 0.1 us)
Async XLA Ops:
  0.0 0.7 copy-start.6
  0.7 0.7 copy-start.7
  1.4 0.7 copy-start.8
  3.2 21.2 %collective-permute-start.1 = (bf16[128,3200]{1,0:T(8,128)(2,1)S(1)}, bf16[128,3200]{1,0:T(8,128)(2,1)S(1)}, u32[]{:S(2)}, u32[]{:S(2)}) collective-permute-start(bf16[128,3200]{1,0:T(8,128)(2,1)S(1)} %tokens_with_facts.1.refs_0_), channel_id=1, source_target_pairs={{0,8},{4,12},{8,0},{12,4},{1,9},{5,13},{9,1},{13,5},{2,10},{6,14},... | collective-permute-start | bytes 2457608 | tf_op jit(solution)/shard_map/ppermute | solution.py:518
  6.2 18.3 %collective-permute-start = (bf16[128,3200]{1,0:T(8,128)(2,1)S(1)}, bf16[128,3200]{1,0:T(8,128)(2,1)S(1)}, u32[]{:S(2)}, u32[]{:S(2)}) collective-permute-start(bf16[128,3200]{1,0:T(8,128)(2,1)S(1)} %tokens_with_facts.1.refs_0_), channel_id=1, source_target_pairs={{0,4},{4,0},{8,12},{12,8},{1,5},{5,1},{9,13},{13,9},{2,6},{6,2},{1... | collective-permute-start | bytes 2457608 | tf_op jit(solution)/shard_map/ppermute | solution.py:518
  6.2 20.5 %copy-start.4 = (s32[16]{0:T(128)S(1)}, s32[16]{0:T(128)}, u32[]{:S(2)}) copy-start(s32[16]{0:T(128)} %refs_6_.1) | copy-start | bytes 196
  6.3 20.5 %copy-start.5 = (s32[64]{0:T(128)S(1)}, s32[64]{0:T(128)}, u32[]{:S(2)}) copy-start(s32[64]{0:T(128)} %refs_7_.1) | copy-start | bytes 772
  24.4 3.4 %copy-start = (bf16[128,3200]{1,0:T(8,128)(2,1)}, bf16[128,3200]{1,0:T(8,128)(2,1)S(1)}, u32[]{:S(2)}) copy-start(bf16[128,3200]{1,0:T(8,128)(2,1)S(1)} %collective-permute-done.1.refs_2_) | copy-start | bytes 2457604
  24.4 2.3 %collective-permute-start.2 = (bf16[128,3200]{1,0:T(8,128)(2,1)S(1)}, bf16[128,3200]{1,0:T(8,128)(2,1)S(1)}, u32[]{:S(2)}, u32[]{:S(2)}) collective-permute-start(bf16[128,3200]{1,0:T(8,128)(2,1)S(1)} %collective-permute-done.1.refs_2_), channel_id=1, source_target_pairs={{0,4},{4,0},{8,12},{12,8},{1,5},{5,1},{9,13},{13,9},{2,6},{6,2},{1... | collective-permute-start | bytes 2457608 | tf_op jit(solution)/shard_map/ppermute | solution.py:518
  24.4 3.4 %copy-start.1 = (bf16[128,3200]{1,0:T(8,128)(2,1)}, bf16[128,3200]{1,0:T(8,128)(2,1)S(1)}, u32[]{:S(2)}) copy-start(bf16[128,3200]{1,0:T(8,128)(2,1)S(1)} %collective-permute-done.refs_1_) | copy-start | bytes 2457604
  26.8 1.1 %copy-start.2 = (bf16[128,3200]{1,0:T(8,128)(2,1)}, bf16[128,3200]{1,0:T(8,128)(2,1)S(1)}, u32[]{:S(2)}) copy-start(bf16[128,3200]{1,0:T(8,128)(2,1)S(1)} %collective-permute-done.2.refs_3_) | copy-start | bytes 2457604
  48.1 8.1 %collective-permute-start.3 = (bf16[32,512]{1,0:T(8,128)(2,1)S(1)}, bf16[32,512]{1,0:T(8,128)(2,1)S(1)}, u32[]{:S(2)}, u32[]{:S(2)}) collective-permute-start(bf16[32,512]{1,0:T(8,128)(2,1)S(1)} %get-tuple-element.63), channel_id=1, source_target_pairs={{0,2},{1,3},{2,0},{3,1},{4,6},{5,7},{6,4},{7,5},{8,10},{9,11},{10,... | collective-permute-start | bytes 98312 | tf_op jit(solution)/shard_map/ppermute | solution.py:551
  56.2 1.8 %collective-permute-start.4 = (bf16[256,768]{1,0:T(8,128)(2,1)S(1)}, bf16[256,768]{1,0:T(8,128)(2,1)S(1)}, u32[]{:S(2)}, u32[]{:S(2)}) collective-permute-start(bf16[256,768]{1,0:T(8,128)(2,1)S(1)} %get-tuple-element.72), channel_id=1, source_target_pairs={{0,4},{4,0},{8,12},{12,8},{1,5},{5,1},{9,13},{13,9},{2,6},{6,2},{1... | collective-permute-start | bytes 1179656 | tf_op jit(solution)/shard_map/ppermute | solution.py:518
  56.3 3.3 %collective-permute-start.6 = (bf16[32,512]{1,0:T(8,128)(2,1)S(1)}, bf16[32,512]{1,0:T(8,128)(2,1)S(1)}, u32[]{:S(2)}, u32[]{:S(2)}) collective-permute-start(bf16[32,512]{1,0:T(8,128)(2,1)S(1)} %add_convert_fusion.2), channel_id=1, source_target_pairs={{0,4},{4,0},{8,12},{12,8},{1,5},{5,1},{9,13},{13,9},{2,6},{6,2},{1... | collective-permute-start | bytes 98312 | tf_op jit(solution)/shard_map/ppermute | solution.py:518
  58.1 10.3 %collective-permute-start.5 = (bf16[128,768]{1,0:T(8,128)(2,1)S(1)}, bf16[128,768]{1,0:T(8,128)(2,1)S(1)}, u32[]{:S(2)}, u32[]{:S(2)}) collective-permute-start(bf16[128,768]{1,0:T(8,128)(2,1)S(1)} %get-tuple-element.73), channel_id=1, source_target_pairs={{0,8},{4,12},{8,0},{12,4},{1,9},{5,13},{9,1},{13,5},{2,10},{6,14},... | collective-permute-start | bytes 589832 | tf_op jit(solution)/shard_map/ppermute | solution.py:518
  59.6 8.7 %collective-permute-start.7 = (bf16[64,512]{1,0:T(8,128)(2,1)S(1)}, bf16[64,512]{1,0:T(8,128)(2,1)S(1)}, u32[]{:S(2)}, u32[]{:S(2)}) collective-permute-start(bf16[64,512]{1,0:T(8,128)(2,1)S(1)} %pad_maximum_fusion.1), channel_id=1, source_target_pairs={{0,8},{4,12},{8,0},{12,4},{1,9},{5,13},{9,1},{13,5},{2,10},{6,14},... | collective-permute-start | bytes 196616 | tf_op jit(solution)/shard_map/ppermute | solution.py:518
  60.2 17.6 %copy-start.3 = (bf16[16,8,16,768]{3,2,1,0:T(8,128)(2,1)S(1)}, bf16[16,8,16,768]{3,2,1,0:T(8,128)(2,1)}, u32[]{:S(2)}) copy-start(bf16[16,8,16,768]{3,2,1,0:T(8,128)(2,1)} %param.21) | copy-start | bytes 9437188
  68.3 2.4 %collective-permute-start.8 = (bf16[256,1536]{1,0:T(8,128)(2,1)S(1)}, bf16[256,1536]{1,0:T(8,128)(2,1)S(1)}, u32[]{:S(2)}, u32[]{:S(2)}) collective-permute-start(bf16[256,1536]{1,0:T(8,128)(2,1)S(1)} %get-tuple-element.82), channel_id=1, source_target_pairs={{0,4},{4,0},{8,12},{12,8},{1,5},{5,1},{9,13},{13,9},{2,6},{6,2},{1... | collective-permute-start | bytes 2359304 | tf_op jit(solution)/shard_map/ppermute | solution.py:518
  70.9 11.2 %collective-permute-start.9 = (bf16[128,1536]{1,0:T(8,128)(2,1)S(1)}, bf16[128,1536]{1,0:T(8,128)(2,1)S(1)}, u32[]{:S(2)}, u32[]{:S(2)}) collective-permute-start(bf16[128,1536]{1,0:T(8,128)(2,1)S(1)} %get-tuple-element.83), channel_id=1, source_target_pairs={{0,8},{4,12},{8,0},{12,4},{1,9},{5,13},{9,1},{13,5},{2,10},{6,14},... | collective-permute-start | bytes 1179656 | tf_op jit(solution)/shard_map/ppermute | solution.py:518
  72.4 5.3 %collective-permute-start.10 = (bf16[128,512]{1,0:T(8,128)(2,1)S(1)}, bf16[128,512]{1,0:T(8,128)(2,1)S(1)}, u32[]{:S(2)}, u32[]{:S(2)}) collective-permute-start(bf16[128,512]{1,0:T(8,128)(2,1)S(1)} %pad_maximum_fusion), channel_id=1, source_target_pairs={{0,1},{1,0},{2,3},{3,2},{4,5},{5,4},{6,7},{7,6},{8,9},{9,8},{10,11... | collective-permute-start | bytes 393224 | tf_op jit(solution)/shard_map/ppermute | solution.py:551
  82.1 1.7 %collective-permute-start.11 = (bf16[256,768]{1,0:T(8,128)(2,1)S(1)}, bf16[256,768]{1,0:T(8,128)(2,1)S(1)}, u32[]{:S(2)}, u32[]{:S(2)}) collective-permute-start(bf16[256,768]{1,0:T(8,128)(2,1)S(1)} %get-tuple-element.90), channel_id=1, source_target_pairs={{0,4},{4,0},{8,12},{12,8},{1,5},{5,1},{9,13},{13,9},{2,6},{6,2},{1... | collective-permute-start | bytes 1179656 | tf_op jit(solution)/shard_map/ppermute | solution.py:518
  82.2 17.1 %collective-permute-start.13 = (bf16[128,768]{1,0:T(8,128)(2,1)S(1)}, bf16[128,768]{1,0:T(8,128)(2,1)S(1)}, u32[]{:S(2)}, u32[]{:S(2)}) collective-permute-start(bf16[128,768]{1,0:T(8,128)(2,1)S(1)} %sum_and_cut.2), channel_id=1, source_target_pairs={{0,2},{1,3},{2,0},{3,1},{4,6},{5,7},{6,4},{7,5},{8,10},{9,11},{10,... | collective-permute-start | bytes 589832 | tf_op jit(solution)/shard_map/ppermute | solution.py:524
  84.0 15.3 %collective-permute-start.14 = (bf16[128,768]{1,0:T(8,128)(2,1)S(1)}, bf16[128,768]{1,0:T(8,128)(2,1)S(1)}, u32[]{:S(2)}, u32[]{:S(2)}) collective-permute-start(bf16[128,768]{1,0:T(8,128)(2,1)S(1)} %get-tuple-element.99), channel_id=1, source_target_pairs={{0,1},{1,2},{2,3},{3,0},{4,5},{5,6},{6,7},{7,4},{8,9},{9,10},{10,1... | collective-permute-start | bytes 589832 | tf_op jit(solution)/shard_map/ppermute | solution.py:524
  85.7 14.0 %collective-permute-start.15 = (bf16[128,768]{1,0:T(8,128)(2,1)S(1)}, bf16[128,768]{1,0:T(8,128)(2,1)S(1)}, u32[]{:S(2)}, u32[]{:S(2)}) collective-permute-start(bf16[128,768]{1,0:T(8,128)(2,1)S(1)} %get-tuple-element.100), channel_id=1, source_target_pairs={{0,3},{1,0},{2,1},{3,2},{4,7},{5,4},{6,5},{7,6},{8,11},{9,8},{10,9... | collective-permute-start | bytes 589832 | tf_op jit(solution)/shard_map/ppermute | solution.py:524
  87.9 11.7 %collective-permute-start.12 = (bf16[128,768]{1,0:T(8,128)(2,1)S(1)}, bf16[128,768]{1,0:T(8,128)(2,1)S(1)}, u32[]{:S(2)}, u32[]{:S(2)}) collective-permute-start(bf16[128,768]{1,0:T(8,128)(2,1)S(1)} %get-tuple-element.94), channel_id=1, source_target_pairs={{0,8},{4,12},{8,0},{12,4},{1,9},{5,13},{9,1},{13,5},{2,10},{6,14},... | collective-permute-start | bytes 589832 | tf_op jit(solution)/shard_map/ppermute | solution.py:518

commit v8 on v6

--- a/solution.py
+++ b/solution.py
@@ -13,11 +13,8 @@
 RANK = 16
 CAP = 48
 LIMIT = 16
-LIMIT_EARLY = 21
+LIMIT_EARLY = 8
 N_TILE = 512
-HELD_EACH = 2
-HELD_ARRAYS = 4
-RING = 4
 MIB = 1 << 20
 
 F32 = jnp.float32
@@ -47,10 +44,14 @@
     return pl.BlockSpec(memory_space=pltpu.SMEM)
 
 
-def facts_kernel(tokens_ref, chosen_ref, logits_ref, tenant_ref, out_ref, sem):
-    rows, width = tokens_ref.shape
-    copy = pltpu.make_async_copy(tokens_ref, out_ref.at[:, pl.ds(0, width)], sem)
-    copy.start()
+def parts_kernel(tokens_ref, chosen_ref, logits_ref, tenant_ref, first_ref, second_ref, sems):
+    rows, width = second_ref.shape
+    copies = [
+        pltpu.make_async_copy(tokens_ref.at[:, pl.ds(0, width)], first_ref.at[:, pl.ds(0, width)], sems.at[0]),
+        pltpu.make_async_copy(tokens_ref.at[:, pl.ds(width, width)], second_ref, sems.at[1]),
+    ]
+    for copy in copies:
+        copy.start()
     diagonal = lax.broadcasted_iota(jnp.int32, (rows, rows), 0) == lax.broadcasted_iota(jnp.int32, (rows, rows), 1)
 
     def column(row):
@@ -67,21 +68,25 @@
     facts = jnp.zeros((rows, 128), F32)
     for number, value in enumerate(columns):
         facts = jnp.where(lane == number, value, facts)
-    out_ref[:, width:] = facts.astype(BF16)
-    copy.wait()
-
-
-def with_facts(tokens, chosen_experts, logits, tenant):
-    rows, width = tokens.shape
-    return pl.pallas_call(
-        facts_kernel,
-        out_shape=jax.ShapeDtypeStruct((rows, width + 128), BF16),
+    first_ref[:, width:] = facts.astype(BF16)
+    for copy in copies:
+        copy.wait()
+
+
+def token_parts_of(tokens, chosen_experts, logits, tenant):
+    rows, width = tokens.shape[0], tokens.shape[1] // 2
+    return pl.pallas_call(
+        parts_kernel,
+        out_shape=(
+            jax.ShapeDtypeStruct((rows, width + 128), BF16),
+            jax.ShapeDtypeStruct((rows, width), BF16),
+        ),
         in_specs=[pl.BlockSpec(memory_space=pltpu.HBM)] + [vmem()] * 3,
-        out_specs=vmem(),
-        scratch_shapes=[pltpu.SemaphoreType.DMA],
+        out_specs=(vmem(),) * 2,
+        scratch_shapes=[pltpu.SemaphoreType.DMA((2,))],
         cost_estimate=SMALL,
         compiler_params=params(LIMIT_EARLY),
-        name="tokens_with_facts",
+        name="token_parts",
     )(pltpu.with_memory_space_constraint(tokens, pltpu.HBM), chosen_experts.T, logits.T, tenant.reshape(1, rows))
 
 
@@ -140,55 +145,51 @@
         in_specs=[smem()] * 3 + [vmem()] * len(blocks),
         out_specs=(vmem(),) * 5,
         cost_estimate=SMALL,
-        compiler_params=params(min(38, LIMIT_EARLY * count // 512)),
+        compiler_params=params(max(LIMIT_EARLY, 12 * count * count // MIB)),
         name="routing_tables",
     )(ids, adapters, pool_slots, *blocks)
 
 
-class Slabs:
-    def __init__(self, gate_ref, up_ref, resident, ring, sems):
-        self.sources, self.resident, self.ring, self.sems = (gate_ref, up_ref), resident, ring, sems
-        self.halves, self.depth, hidden = gate_ref.shape
-        self.width = resident[0].shape[2]
-        self.each = resident[0].shape[0]
-        self.first = len(resident) * self.each
-        self.capacity = 1 if ring is None else ring.shape[0]
-        self.tiles = hidden // self.width
-        self.count = 2 * self.halves * self.tiles
-
-    def place(self, number):
-        if number < self.first:
-            return self.resident[number // self.each].at[number % self.each]
-        return self.ring.at[(number - self.first) % self.capacity]
-
-    def copies(self, number):
-        place, rows = self.place(number), self.depth // 2
-        slot = number if number < self.first else (number - self.first) % self.capacity
-        half, tile, which = number // (2 * self.tiles), number // 2 % self.tiles, number % 2
-        return [
-            pltpu.make_async_copy(
-                self.sources[which].at[half, pl.ds(i * rows, rows), pl.ds(tile * self.width, self.width)],
-                place.at[pl.ds(i * rows, rows)],
-                self.sems.at[slot, i],
-            )
-            for i in range(2)
-        ]
-
-    def start(self, number):
-        for copy in self.copies(number):
-            copy.start()
-
-    def wait(self, number):
-        for copy in self.copies(number):
-            copy.wait()
-
-
-def resident_shapes(gate):
-    local_halves, width, hidden_count = gate.shape
+def slab_copies(gate_ref, up_ref, into_ref, sems, part, half):
+    depth, width = into_ref.shape[1], into_ref.shape[2]
+    copies = []
+    for number in range(into_ref.shape[0]):
+        source = (gate_ref, up_ref)[number % 2].at[half, pl.ds(part * depth, depth), pl.ds(number // 2 * width, width)]
+        copies.append(pltpu.make_async_copy(source, into_ref.at[number], sems.at[half, number]))
+    return copies
+
+
+def prefetch_kernel(ids_ref, gate_ref, up_ref, *refs):
+    slabs, mark_ref, sems = refs[:-2], refs[-2], refs[-1]
+    copies = [copy for half, slab in enumerate(slabs) for copy in slab_copies(gate_ref, up_ref, slab, sems, 0, half)]
+    for copy in copies:
+        copy.start()
+    mark_ref[...] = jnp.zeros_like(mark_ref)
+    for copy in copies:
+        copy.wait()
+
+
+def prefetch(ids, gate, up, part_width):
+    local_halves, _, hidden_count = gate.shape
     tile = min(N_TILE, hidden_count)
-    count = 2 * local_halves * hidden_count // tile
-    each = min(HELD_EACH, count)
-    return [(each, width, tile)] * min(HELD_ARRAYS, count // each)
+    each = 2 * hidden_count // tile
+    return pl.pallas_call(
+        prefetch_kernel,
+        out_shape=(pltpu.VMEM((each, part_width, tile), BF16),) * local_halves + (jax.ShapeDtypeStruct((8, 128), F32),),
+        in_specs=[smem()] + [pl.BlockSpec(memory_space=pltpu.HBM)] * 2,
+        out_specs=(vmem(),) * (local_halves + 1),
+        scratch_shapes=[pltpu.SemaphoreType.DMA((local_halves, each))],
+        cost_estimate=SMALL,
+        compiler_params=params(LIMIT_EARLY),
+        name="weight_prefetch",
+    )(ids, gate, up)
+
+
+def pack(blocks, p_ref, packed):
+    depth = packed.shape[2]
+    whole = jnp.concatenate([block[:, :depth] for block in blocks], axis=0)
+    for i in range(p_ref.shape[0]):
+        packed[i] = mm(p_ref[i], whole).astype(BF16)
 
 
 def down_slabs(down, n_ad):
@@ -210,40 +211,67 @@
     ]
 
 
-def prefetch_kernel(ids_ref, gate_ref, up_ref, *refs):
-    resident, mark_ref, sems = refs[:-2], refs[-2], refs[-1]
-    slabs = Slabs(gate_ref, up_ref, resident, None, sems)
-    for number in range(slabs.first):
-        slabs.start(number)
-    mark_ref[...] = jnp.zeros_like(mark_ref)
-    for number in range(slabs.first):
-        slabs.wait(number)
-
-
-def prefetch(ids, gate, up, count):
-    shapes = resident_shapes(gate)
-    return pl.pallas_call(
-        prefetch_kernel,
-        out_shape=(*[pltpu.VMEM(shape, BF16) for shape in shapes], jax.ShapeDtypeStruct((8, 128), F32)),
-        in_specs=[smem()] + [pl.BlockSpec(memory_space=pltpu.HBM)] * 2,
-        out_specs=(vmem(),) * (len(shapes) + 1),
-        scratch_shapes=[pltpu.SemaphoreType.DMA((len(shapes) * shapes[0][0], 2))],
-        cost_estimate=SMALL,
-        compiler_params=params(min(38, LIMIT_EARLY * count // 512)),
-        name="weight_prefetch",
-    )(ids, gate, up)
-
-
-def expert_kernel(n_blocks, n_resident, n_ad, step, *refs):
+def first_kernel(n_blocks, local_halves, *refs):
     blocks, refs = refs[:n_blocks], refs[n_blocks:]
-    ids_ref, adapter_ref, pool_slot_ref, p_ref, tslot_ref, rows_ref = refs[1:7]
-    gate_ref, up_ref, down_ref, pool_ref = refs[7:11]
-    resident, refs = refs[11 : 11 + n_resident], refs[11 + n_resident :]
-    hidden, low_ref, next_ref, packed, factors, factor_sems, down_sems, ring, sems = refs
-    slabs = Slabs(gate_ref, up_ref, resident, ring, sems)
+    _, p_ref, gate_ref, up_ref, refs = *refs[:4], refs[4:]
+    slabs, refs = refs[:local_halves], refs[local_halves:]
+    ahead, (gate_out, up_out, mark_out, packed, sems) = refs[:-5], refs[-5:]
+    mark_out[...] = jnp.zeros_like(mark_out)
+    pack(blocks, p_ref, packed)
+    slabs = list(ahead) + list(slabs[len(ahead) :])
+    copies = [slab_copies(gate_ref, up_ref, slab, sems, 1, half) for half, slab in enumerate(ahead)]
+    halves_each = local_halves // p_ref.shape[0]
+    for half in range(local_halves):
+        rows = packed[half // halves_each]
+        tiles, _, width = slabs[half].shape
+        for tile in range(tiles // 2):
+            span = slice(tile * width, (tile + 1) * width)
+            gate_out[half, :, span] = mm(rows, slabs[half][2 * tile])
+            up_out[half, :, span] = mm(rows, slabs[half][2 * tile + 1])
+            if half < len(ahead):
+                copies[half][2 * tile].start()
+                copies[half][2 * tile + 1].start()
+    for copy in [copy for half in copies for copy in half]:
+        copy.wait()
+
+
+def first_part(blocks, mark, picked, gate, up, slabs):
+    local_halves, _, hidden_count = gate.shape
+    n_local, row_count, _ = picked.shape
+    each, part_width, _ = slabs[0].shape
+    hbm = pl.BlockSpec(memory_space=pltpu.HBM)
+    sums = pltpu.VMEM((local_halves, row_count, hidden_count), F32)
+    n_ahead = max(1, local_halves - 1)
+    return pl.pallas_call(
+        functools.partial(first_kernel, len(blocks), local_halves),
+        out_shape=(pltpu.VMEM(slabs[0].shape, BF16),) * n_ahead
+        + (sums, sums, jax.ShapeDtypeStruct((8, 128), F32)),
+        in_specs=[vmem()] * (len(blocks) + 2) + [hbm, hbm] + [vmem()] * local_halves,
+        out_specs=(vmem(),) * (n_ahead + 3),
+        scratch_shapes=[
+            pltpu.VMEM((n_local, row_count, part_width), BF16),
+            pltpu.SemaphoreType.DMA((n_ahead, each)),
+        ],
+        input_output_aliases={len(blocks) + 4 + half: half for half in range(n_ahead)},
+        cost_estimate=SMALL,
+        compiler_params=params(max(LIMIT_EARLY, 10 * n_local * row_count * part_width // MIB)),
+        name="gate_up_first",
+    )(*blocks, mark, picked, gate, up, *[pltpu.with_memory_space_constraint(x, pltpu.VMEM) for x in slabs])
+
+
+def second_kernel(n_blocks, n_ahead, n_ad, step, *refs):
+    blocks, refs = refs[:n_blocks], refs[n_blocks:]
+    p_ref, gate_ref, up_ref, refs = *refs[1:4], refs[4:]
+    ahead, gate_in, up_in, refs = refs[:n_ahead], refs[n_ahead], refs[n_ahead + 1], refs[n_ahead + 2 :]
+    ids_ref, adapter_ref, pool_slot_ref, pool_ref, tslot_ref, rows_ref, down_ref, refs = *refs[:7], refs[7:]
+    hidden_ref, low_ref, next_ref, packed, factors, factor_sems, down_sems, late, sems = refs
     n_local = p_ref.shape[0]
-    local_halves, depth, _ = gate_ref.shape
+    local_halves, _, hidden_count = gate_ref.shape
     halves_each = local_halves // n_local
+    slabs = list(ahead) + [late] * (local_halves - n_ahead)
+    copies = {
+        half: slab_copies(gate_ref, up_ref, slabs[half], sems, 1, half) for half in range(n_ahead, local_halves)
+    }
     tenants, rank = adapter_ref.shape[0], pool_ref.shape[2]
     factor_copies = [
         pltpu.make_async_copy(
@@ -253,42 +281,31 @@
         )
         for number in range(tenants)
     ]
-    for copy in factor_copies:
+    down_copies = down_fetch(n_ad, step, ids_ref, down_ref, next_ref, down_sems)
+    for copy in copies.get(n_ahead, []) + factor_copies + down_copies:
         copy.start()
-    for number in range(slabs.first, min(slabs.count, slabs.first + slabs.capacity)):
-        slabs.start(number)
-
-    def ready(number):
-        if number >= slabs.first:
-            slabs.wait(number)
-
-    def used(number):
-        if slabs.first <= number < slabs.count - slabs.capacity:
-            slabs.start(number + slabs.capacity)
-
-    whole = jnp.concatenate([block[:, :depth] for block in blocks], axis=0)
-    for i in range(n_local):
-        packed[i] = mm(p_ref[i], whole).astype(BF16)
+    pack(blocks, p_ref, packed)
     for half in range(local_halves):
         rows = packed[half // halves_each]
-        for tile in range(slabs.tiles):
+        tiles, _, width = slabs[half].shape
+        for tile in range(tiles // 2):
+            span = slice(tile * width, (tile + 1) * width)
             values = []
-            for which in range(2):
-                number = (half * slabs.tiles + tile) * 2 + which
-                ready(number)
-                values.append(mm(rows, slabs.place(number)[...]))
-                used(number)
-            span = slice(tile * slabs.width, (tile + 1) * slabs.width)
-            hidden[half, :, span] = (jax.nn.silu(values[0]) * values[1]).astype(BF16)
-    down_copies = down_fetch(n_ad, step, ids_ref, down_ref, next_ref, down_sems)
-    for copy in down_copies:
-        copy.start()
+            for number in (2 * tile, 2 * tile + 1):
+                if half in copies:
+                    copies[half][number].wait()
+                values.append(mm(rows, slabs[half][number]))
+                if half in copies and half + 1 in copies:
+                    copies[half + 1][number].start()
+            gate = values[0] + gate_in[half, :, span]
+            up = values[1] + up_in[half, :, span]
+            hidden_ref[half, :, span] = (jax.nn.silu(gate) * up).astype(BF16)
     for copy in factor_copies:
         copy.wait()
     for i in range(n_local):
-        low = mm_nt(factors[i * halves_each], hidden[i * halves_each])
+        low = mm_nt(factors[i * halves_each], hidden_ref[i * halves_each])
         for half in range(i * halves_each + 1, (i + 1) * halves_each):
-            low = low + mm_nt(factors[half], hidden[half])
+            low = low + mm_nt(factors[half], hidden_ref[half])
         owner = tslot_ref[i][0:1]
         total = jnp.zeros((rank, low.shape[1]), F32)
         for number in range(tenants):
@@ -299,39 +316,39 @@
         copy.wait()
 
 
-def expert_part(
-    blocks, mark, ids, adapters, pool_slots, picked, tslot, table_rows, gate, up, down, pool, resident, n_ad, step
+def second_part(
+    blocks, mark, picked, gate, up, ahead, sums, ids, adapters, pool_slots, pool, tslot, table_rows, down, n_ad, step
 ):
-    local_halves, width, hidden_count = gate.shape
+    local_halves, _, hidden_count = gate.shape
     n_local, row_count, count = picked.shape
+    each, part_width, tile = ahead[0].shape
     tenants, rank = adapters.shape[0], pool.shape[2]
     hbm = pl.BlockSpec(memory_space=pltpu.HBM)
-    each, _, tile = resident[0].shape
-    ring = max(1, min(RING, 2 * local_halves * hidden_count // tile - len(resident) * each))
-    return pl.pallas_call(
-        functools.partial(expert_kernel, len(blocks), len(resident), n_ad, step),
+    held = [pltpu.with_memory_space_constraint(x, pltpu.VMEM) for x in (*ahead, *sums)]
+    late_bytes = 2 * each * part_width * tile
+    return pl.pallas_call(
+        functools.partial(second_kernel, len(blocks), len(ahead), n_ad, step),
         out_shape=(
             pltpu.VMEM((local_halves, row_count, hidden_count), BF16),
             jax.ShapeDtypeStruct((n_local * rank, count), BF16),
             down_slabs(down, n_ad),
         ),
-        in_specs=[vmem()] * (len(blocks) + 1) + [smem()] * 3 + [vmem()] * 3 + [hbm] * 4 + [vmem()] * len(resident),
+        in_specs=[vmem()] * (len(blocks) + 2) + [hbm, hbm] + [vmem()] * len(held) + [smem()] * 3 + [hbm, vmem(), vmem(), hbm],
         out_specs=(vmem(),) * 3,
         scratch_shapes=[
-            pltpu.VMEM((n_local, row_count, width), BF16),
+            pltpu.VMEM((n_local, row_count, part_width), BF16),
             pltpu.VMEM((local_halves, tenants * rank, hidden_count), BF16),
             pltpu.SemaphoreType.DMA((tenants,)),
             pltpu.SemaphoreType.DMA((local_halves, 2)),
-            pltpu.VMEM((ring, width, tile), BF16),
-            pltpu.SemaphoreType.DMA((ring, 2)),
+            pltpu.VMEM((each, part_width, tile), BF16),
+            pltpu.SemaphoreType.DMA((local_halves, each)),
         ],
         cost_estimate=SMALL,
-        compiler_params=params(min(38, LIMIT_EARLY * count // 512)),
-        name="experts",
-    )(
-        *blocks, mark, ids, adapters, pool_slots, picked, tslot, table_rows, gate, up, down, pool,
-        *[pltpu.with_memory_space_constraint(x, pltpu.VMEM) for x in resident],
-    )
+        compiler_params=params(
+            max(LIMIT_EARLY, 10 * n_local * row_count * part_width // MIB) + late_bytes // MIB + 1
+        ),
+        name="gate_up_second",
+    )(*blocks, mark, picked, gate, up, *held, ids, adapters, pool_slots, pool, tslot, table_rows, down)
 
 
 def weighted_down(hidden_ref, weight_ref, pt_ref, cols_ref):
@@ -524,21 +541,28 @@
         return lax.ppermute(x, "ad", [(i, (i + step) % n_ad) for i in range(n_ad)])
 
     order = sorted(range(1, n_ad), key=lambda step: (step != n_ad // 2, step))
-    own = with_facts(tokens, chosen_experts, router_gate_logits, token_tenant)
-    *resident, mark = prefetch(ids, gate_weight, up_weight, n_ep * tokens.shape[0])
-    blocks = {0: own}
-    for bit in reversed(range(bits)):
-        for mask in list(blocks):
-            blocks[mask | 1 << bit] = swap(blocks[mask], 1 << bit)
-        if bit == bits - 1:
-            blocks[1 << bit], mark = tie(blocks[1 << bit], mark)
-    blocks = [blocks[mask] for mask in range(n_ep)]
+    token_part = token_parts_of(tokens, chosen_experts, router_gate_logits, token_tenant)
+    *slabs, mark = prefetch(ids, gate_weight, up_weight, width // 2)
+    high = 1 << (bits - 1)
+    crossing = [swap(own, high) for own in token_part]
+
+    def spread(part, crossed):
+        blocks = {0: token_part[part], high: crossed}
+        for bit in reversed(range(bits - 1)):
+            for mask in list(blocks):
+                blocks[mask | 1 << bit] = swap(blocks[mask], 1 << bit)
+        return [blocks[mask] for mask in range(n_ep)]
+
+    crossing[0], mark = tie(crossing[0], mark)
+    blocks = spread(0, crossing[0])
     picked, pt, cols, table_rows, tslot = build_meta(
         blocks, ids, adapter_of_tenant, adapter_pool_slot, n_local, local_halves, row_count
     )
-    hidden, low, weights = expert_part(
-        blocks, mark, ids, adapter_of_tenant, adapter_pool_slot, picked, tslot, table_rows, gate_weight, up_weight,
-        down_weight, adapter_input_factors, resident, n_ad, order[0],
+    *ahead, gate_sum, up_sum, mark = first_part(blocks, mark, picked, gate_weight, up_weight, slabs)
+    crossing[1], mark = tie(crossing[1], mark)
+    hidden, low, weights = second_part(
+        spread(1, crossing[1]), mark, picked, gate_weight, up_weight, ahead, (gate_sum, up_sum), ids,
+        adapter_of_tenant, adapter_pool_slot, adapter_input_factors, tslot, table_rows, down_weight, n_ad, order[0],
     )
 
     def onward(keep, came, first=1):
@@ -574,6 +598,7 @@
     slot_count = adapter_output_factors.shape[0]
     flat_factors = adapter_output_factors.reshape(slot_count * EXPERT_COUNT * RANK, span)
     keep, send = adapter_part(ids, base, cols, 2 * n_local, local_halves, flat_factors, low)
+    came_rest, results, keep, send = lax.optimization_barrier((came_rest, results, keep, send))
     came = swap(send, 1)
     if bits > 1:
         keep, send = split_sum(keep, came)

time: 102 us -> 93.9 us (0.921)
  waiting for transfers between devices: 33.2 us -> 23.4 us
    ppermute x11 -> x14, waiting for transfers between devices: 22.2 us -> 8.2 us  [swap(): return lax.ppermute(x, 'ep', [(i, i ^ mask) for i in range(n_ep)])]
    ppermute x3, waiting for transfers between devices: 6.71 us -> 11.5 us  [shift(): return lax.ppermute(x, 'ad', [(i, (i + step) % n_ad) for i in range(n_ad)])]
    ppermute x11 -> x14, starting transfers between devices: 8.98 us -> 9.94 us  [swap(): return lax.ppermute(x, 'ep', [(i, i ^ mask) for i in range(n_ep)])]
    pallas_call x3 -> x4, Pallas kernels: 30.2 us -> 30.7 us  [the longest x1 12.8 us: second_part(): pl.pallas_call(functools.partial(second_kernel, len(blocks), len(ahead),...]
  transfers between devices with their start and end apart: 16 -> 19, of which waited for: 7 -> 10; matrix products, arithmetic and copies ran while one was open for 0% -> 0% of each run, Pallas kernels for 25% -> 37%
where the time goes in v8:
time: 93.9 us; the launch traced here: 93.8 us
  Pallas kernels  48.5 us (52%)
  waiting for transfers between devices  23.4 us (25%)
  starting transfers between devices  18.8 us (20%)
  local copies, waits for them, and re-layouts  2.02 us (2%)
  other arithmetic  0.94 us (1%)
    pallas_call x1, Pallas kernels, second_part(): pl.pallas_call(functools.partial(second_kernel, len(blocks), len(ahead),...  12.8 us
    ppermute x3, waiting for transfers between devices, shift(): return lax.ppermute(x, 'ad', [(i, (i + step) % n_ad) for i in range(n_ad)])  11.5 us
    ppermute x14, starting transfers between devices, swap(): return lax.ppermute(x, 'ep', [(i, i ^ mask) for i in range(n_ep)])  9.94 us
    pallas_call x1, Pallas kernels, prefetch(): pl.pallas_call(prefetch_kernel, out_shape=(pltpu.VMEM((each, part_width,...  8.89 us
    ppermute x14, waiting for transfers between devices, swap(): return lax.ppermute(x, 'ep', [(i, i ^ mask) for i in range(n_ep)])  8.2 us
    pallas_call x1, Pallas kernels, down_rest(): pl.pallas_call(functools.partial(down_rest_kernel, n_ad, steps), out_shap...  8.07 us
    pallas_call x1, Pallas kernels, first_part(): pl.pallas_call(functools.partial(first_kernel, len(blocks), local_halves)...  7.93 us
    pallas_call x1, Pallas kernels, down_first(): pl.pallas_call(functools.partial(down_first_kernel, n_ad, step), out_shap...  5.37 us
  transfers between devices with their start and end apart: 19, of which 10 were waited for; matrix products, arithmetic and copies ran while one was open for 0% of the time, Pallas kernels for 37%

profile of v8, /device:TPU:0, one launch (start us, length us, event | category | flops | bytes accessed | tf_op | source)
XLA Modules:
  0.0 93.8 jit_solution(11253045468770011072)
XLA Ops:
  0.0 0.7 copy-done.3
  0.7 0.7 copy-done.4
  1.4 0.7 copy-done.5
  2.0 1.1 %token_parts.1 = (bf16[128,1664]{1,0:T(8,128)(2,1)S(1)}, bf16[128,1536]{1,0:T(8,128)(2,1)S(1)}) custom-call(bf16[128,3072]{1,0:T(8,128)(2,1)} %tokens_ref.1, s32[2,128]{1,0:T(2,128)S(1)} %bitcast.7, f32[2,128]{1,0:T(2,128)S(1)} %bitcast.8, s32[1,128]{1,0:T(1,128)S(1)} %bitcast.9), custom_call_target="tpu_custom_call" | custom-call | flops 1 | bytes 1 | tf_op jit(solution)/shard_map/token_parts/pallas_call | solution.py:78
  3.2 3.0 %collective-permute-start.3 = (bf16[128,1664]{1,0:T(8,128)(2,1)S(1)}, bf16[128,1664]{1,0:T(8,128)(2,1)S(1)}, u32[]{:S(2)}, u32[]{:S(2)}) collective-permute-start(bf16[128,1664]{1,0:T(8,128)(2,1)S(1)} %get-tuple-element.65.refs_0_), channel_id=1, source_target_pairs={{0,8},{4,12},{8,0},{12,4},{1,9},{5,13},{9,1},{13,5},{2,10},{6,14},... | collective-permute-start | bytes 1277960 | tf_op jit(solution)/shard_map/ppermute | solution.py:535
  6.2 0.0 collective-permute-start.2
  6.2 0.1 pad_add_fusion.ids_ref.refs_13_
  6.2 8.9 %weight_prefetch.1 = (bf16[4,1536,512]{2,1,0:T(8,128)(2,1)S(1)}, bf16[4,1536,512]{2,1,0:T(8,128)(2,1)S(1)}, bf16[4,1536,512]{2,1,0:T(8,128)(2,1)S(1)}, bf16[4,1536,512]{2,1,0:T(8,128)(2,1)S(1)}, f32[8,128]{1,0:T(8,128)S(1)}) custom-call(s32[2]{0:T(128)S(1)} %pad_add_fusion.ids_ref.refs_13_, bf16[4,3072,1024]{2,1,0:T(8,128)(2,1)} %refs_6_.3, ...), custom_call_target="tpu_custom_call" | custom-call | flops 1 | bytes 1 | tf_op jit(solution)/shard_map/weight_prefetch/pallas_call | solution.py:176
  15.1 0.8 collective-permute-done.3.refs_2_
  16.0 0.0 collective-permute-start.4
  16.0 1.7 %collective-permute-start.1 = (bf16[128,1536]{1,0:T(8,128)(2,1)S(1)}, bf16[128,1536]{1,0:T(8,128)(2,1)S(1)}, u32[]{:S(2)}, u32[]{:S(2)}) collective-permute-start(bf16[128,1536]{1,0:T(8,128)(2,1)S(1)} %get-tuple-element.64.refs_0_), channel_id=1, source_target_pairs={{0,8},{4,12},{8,0},{12,4},{1,9},{5,13},{9,1},{13,5},{2,10},{6,14},... | collective-permute-start | bytes 1179656 | tf_op jit(solution)/shard_map/ppermute | solution.py:535
  17.7 0.2 collective-permute-start
  17.9 0.0 collective-permute-done.2.refs_1_
  18.0 0.0 collective-permute-done.4.refs_3_
  18.0 1.1 %routing_tables.1 = (bf16[2,192,512]{2,1,0:T(8,128)(2,1)S(1)}, bf16[2,512,192]{2,1,0:T(8,128)(2,1)S(1)}, f32[512,128]{1,0:T(8,128)S(1)}, f32[8,512]{1,0:T(8,128)S(1)}, f32[2,8,192]{2,1,0:T(8,128)S(1)}) custom-call(s32[2]{0:T(128)S(1)} %pad_add_fusion.ids_ref.refs_13_, s32[16]{0:T(128)S(1)} %copy-done.1, s32[64]{0:T(128)S(1)} %copy-done.2, ...), custom_call_target="tpu_custom_call" | custom-call | flops 1 | bytes 1 | tf_op jit(solution)/shard_map/routing_tables/pallas_call | solution.py:136
  19.1 7.9 %gate_up_first.1 = (bf16[4,1536,512]{2,1,0:T(8,128)(2,1)S(1)}, bf16[4,1536,512]{2,1,0:T(8,128)(2,1)S(1)}, bf16[4,1536,512]{2,1,0:T(8,128)(2,1)S(1)}, f32[4,192,1...) custom-call(bf16[128,1664]{1,0:T(8,128)(2,1)S(1)} %get-tuple-element, ...), custom_call_target="tpu_custom_call", output_to_operand_aliasing={{0}: (8, {}), {1}: (9, {}), {2}: (10, {})} | custom-call | flops 1 | bytes 1 | tf_op jit(solution)/shard_map/gate_up_first/pallas_call | solution.py:245
  27.0 0.5 collective-permute-done.1.refs_2_
  27.5 0.0 collective-permute-start.5
  27.5 0.0 collective-permute-done.refs_1_
  27.5 1.7 %collective-permute-done.5.refs_3_ = bf16[128,1536]{1,0:T(8,128)(2,1)S(1)} collective-permute-done((bf16[128,1536]{1,0:T(8,128)(2,1)S(1)}, bf16[128,1536]{1,0:T(8,128)(2,1)S(1)}, u32[]{:S(2)}, u32[]{:S(2)}) %collective-permute-start.5) | collective-permute-done | bytes 393248 | tf_op jit(solution)/shard_map/ppermute | solution.py:535
  29.2 12.8 %gate_up_second.1 = (bf16[4,192,1024]{2,1,0:T(8,128)(2,1)S(1)}, bf16[32,512]{1,0:T(8,128)(2,1)S(1)}, bf16[4,1024,768]{2,1,0:T(8,128)(2,1)S(1)}) custom-call(bf16[128,1536]{1,0:T(8,128)(2,1)S(1)} %get-tuple-element.64.refs_0_, bf16[128,1536]{1,0:T(8,128)(2,1)S(1)} %collective-permute-done.refs_1_, bf16[128,1536]{1,0:T(8,128)(2,1)S(1)} %collective-permute-done.1.refs_2_, ...), custom_call_target="tpu_custom_call" | custom-call | flops 1 | bytes 1 | tf_op jit(solution)/shard_map/gate_up_second/pallas_call | solution.py:329
  42.0 2.9 %collective-permute-start.6 = (bf16[32,512]{1,0:T(8,128)(2,1)S(1)}, bf16[32,512]{1,0:T(8,128)(2,1)S(1)}, u32[]{:S(2)}, u32[]{:S(2)}) collective-permute-start(bf16[32,512]{1,0:T(8,128)(2,1)S(1)} %get-tuple-element.84), channel_id=1, source_target_pairs={{0,2},{1,3},{2,0},{3,1},{4,6},{5,7},{6,4},{7,5},{8,10},{9,11},{10,... | collective-permute-start | bytes 98312 | tf_op jit(solution)/shard_map/ppermute | solution.py:575
  44.9 5.4 %down_first.1 = (bf16[256,768]{1,0:T(8,128)(2,1)S(1)}, bf16[256,768]{1,0:T(8,128)(2,1)S(1)}, bf16[4,1024,768]{2,1,0:T(8,128)(2,1)S(1)}) custom-call(s32[2]{0:T(128)S(1)} %pad_add_fusion.ids_ref.refs_13_, bf16[4,192,1024]{2,1,0:T(8,128)(2,1)S(1)} %get-tuple-element.97.hidden_ref, bf16[4,1024,768]{2,1,0:T(8,128)(2,1)S(1)} %get-tuple-element.86.weight_ref, ...), custom_call_target="tpu_custom_call" | custom-call | flops 1 | bytes 1 | tf_op jit(solution)/shard_map/down_first/pallas_call | solution.py:378
  50.3 0.1 collective-permute-start.7
  50.4 0.6 collective-permute-start.9
  50.9 1.1 %collective-permute-done.7.came_ref = bf16[256,768]{1,0:T(8,128)(2,1)S(1)} collective-permute-done((bf16[256,768]{1,0:T(8,128)(2,1)S(1)}, bf16[256,768]{1,0:T(8,128)(2,1)S(1)}, u32[]{:S(2)}, u32[]{:S(2)}) %collective-permute-start.7) | collective-permute-done | bytes 393248 | tf_op jit(solution)/shard_map/ppermute | solution.py:535
  52.1 0.1 sum_and_split.3
  52.2 1.6 %collective-permute-start.8 = (bf16[128,768]{1,0:T(8,128)(2,1)S(1)}, bf16[128,768]{1,0:T(8,128)(2,1)S(1)}, u32[]{:S(2)}, u32[]{:S(2)}) collective-permute-start(bf16[128,768]{1,0:T(8,128)(2,1)S(1)} %get-tuple-element.94), channel_id=1, source_target_pairs={{0,8},{4,12},{8,0},{12,4},{1,9},{5,13},{9,1},{13,5},{2,10},{6,14},... | collective-permute-start | bytes 589832 | tf_op jit(solution)/shard_map/ppermute | solution.py:535
  53.7 0.6 collective-permute-start.10
  54.3 8.1 %down_rest.1 = (bf16[256,1536]{1,0:T(8,128)(2,1)S(1)}, bf16[256,1536]{1,0:T(8,128)(2,1)S(1)}, f32[512,768]{1,0:T(8,128)S(1)}) custom-call(s32[2]{0:T(128)S(1)} %pad_add_fusion.ids_ref.refs_13_, bf16[4,192,1024]{2,1,0:T(8,128)(2,1)S(1)} %get-tuple-element.97.hidden_ref, bf16[4,1024,768]{2,1,0:T(8,128)(2,1)S(1)} %get-tuple-element.98.weight_ref, ...), custom_call_target="tpu_custom_call" | custom-call | flops 1 | bytes 1 | tf_op jit(solution)/shard_map/down_rest/pallas_call | solution.py:412
  62.4 0.1 collective-permute-start.11
  62.5 2.3 %collective-permute-done.11.came_ref = bf16[256,1536]{1,0:T(8,128)(2,1)S(1)} collective-permute-done((bf16[256,1536]{1,0:T(8,128)(2,1)S(1)}, bf16[256,1536]{1,0:T(8,128)(2,1)S(1)}, u32[]{:S(2)}, u32[]{:S(2)}) %collective-permute-start.11) | collective-permute-done | bytes 786464 | tf_op jit(solution)/shard_map/ppermute | solution.py:535
  64.8 0.2 sum_and_split.4
  65.0 1.6 %collective-permute-start.12 = (bf16[128,1536]{1,0:T(8,128)(2,1)S(1)}, bf16[128,1536]{1,0:T(8,128)(2,1)S(1)}, u32[]{:S(2)}, u32[]{:S(2)}) collective-permute-start(bf16[128,1536]{1,0:T(8,128)(2,1)S(1)} %get-tuple-element.104), channel_id=1, source_target_pairs={{0,8},{4,12},{8,0},{12,4},{1,9},{5,13},{9,1},{13,5},{2,10},{6,14},... | collective-permute-start | bytes 1179656 | tf_op jit(solution)/shard_map/ppermute | solution.py:535
  66.5 1.6 %collective-permute-start.14 = (bf16[128,512]{1,0:T(8,128)(2,1)S(1)}, bf16[128,512]{1,0:T(8,128)(2,1)S(1)}, u32[]{:S(2)}, u32[]{:S(2)}) collective-permute-start(bf16[128,512]{1,0:T(8,128)(2,1)S(1)} %pad_maximum_fusion), channel_id=1, source_target_pairs={{0,1},{1,0},{2,3},{3,2},{4,5},{5,4},{6,7},{7,6},{8,9},{9,8},{10,11... | collective-permute-start | bytes 393224 | tf_op jit(solution)/shard_map/ppermute | solution.py:575
  68.2 0.4 collective-permute-start.13
  68.6 3.6 %collective-permute-done.14 = bf16[128,512]{1,0:T(8,128)(2,1)S(1)} collective-permute-done((bf16[128,512]{1,0:T(8,128)(2,1)S(1)}, bf16[128,512]{1,0:T(8,128)(2,1)S(1)}, u32[]{:S(2)}, u32[]{:S(2)}) %collective-permute-start.14) | collective-permute-done | bytes 131104 | tf_op jit(solution)/shard_map/ppermute | solution.py:575
  72.3 2.8 %adapters.1 = (bf16[256,768]{1,0:T(8,128)(2,1)S(1)}, bf16[256,768]{1,0:T(8,128)(2,1)S(1)}) custom-call(s32[2]{0:T(128)S(1)} %pad_add_fusion.ids_ref.refs_13_, f32[512,768]{1,0:T(8,128)S(1)} %get-tuple-element.107.base_ref, f32[512,128]{1,0:T(8,128)S(1)} %get-tuple-element.88.cols_ref, bf16[2048,768]{1,0:T(8,128)(2,1)S(1)} %bitcast.6, ...), custom_call_target="tpu_custom_call" | custom-call | flops 1 | bytes 1 | tf_op jit(solution)/shard_map/adapters/pallas_call | solution.py:458
  75.1 4.7 %collective-permute-done.13 = bf16[128,768]{1,0:T(8,128)(2,1)S(1)} collective-permute-done((bf16[128,768]{1,0:T(8,128)(2,1)S(1)}, bf16[128,768]{1,0:T(8,128)(2,1)S(1)}, u32[]{:S(2)}, u32[]{:S(2)}) %collective-permute-start.13) | collective-permute-done | bytes 196640 | tf_op jit(solution)/shard_map/ppermute | solution.py:541
  79.8 1.7 %collective-permute-done.15.came_ref = bf16[256,768]{1,0:T(8,128)(2,1)S(1)} collective-permute-done((bf16[256,768]{1,0:T(8,128)(2,1)S(1)}, bf16[256,768]{1,0:T(8,128)(2,1)S(1)}, u32[]{:S(2)}, u32[]{:S(2)}) %collective-permute-start.15) | collective-permute-done | bytes 393248 | tf_op jit(solution)/shard_map/ppermute | solution.py:535
  81.5 0.1 sum_and_split.5
  81.6 0.1 sum_and_cut.3
  81.7 0.1 collective-permute-start.17
  81.8 3.8 %collective-permute-start.18 = (bf16[128,768]{1,0:T(8,128)(2,1)S(1)}, bf16[128,768]{1,0:T(8,128)(2,1)S(1)}, u32[]{:S(2)}, u32[]{:S(2)}) collective-permute-start(bf16[128,768]{1,0:T(8,128)(2,1)S(1)} %get-tuple-element.122), channel_id=1, source_target_pairs={{0,3},{1,0},{2,1},{3,2},{4,7},{5,4},{6,5},{7,6},{8,11},{9,8},{10,9... | collective-permute-start | bytes 589832 | tf_op jit(solution)/shard_map/ppermute | solution.py:541
  85.6 0.6 collective-permute-start.16
  86.1 5.2 %collective-permute-done.17 = bf16[128,768]{1,0:T(8,128)(2,1)S(1)} collective-permute-done((bf16[128,768]{1,0:T(8,128)(2,1)S(1)}, bf16[128,768]{1,0:T(8,128)(2,1)S(1)}, u32[]{:S(2)}, u32[]{:S(2)}) %collective-permute-start.17) | collective-permute-done | bytes 196640 | tf_op jit(solution)/shard_map/ppermute | solution.py:541
  91.3 1.6 %collective-permute-done.18 = bf16[128,768]{1,0:T(8,128)(2,1)S(1)} collective-permute-done((bf16[128,768]{1,0:T(8,128)(2,1)S(1)}, bf16[128,768]{1,0:T(8,128)(2,1)S(1)}, u32[]{:S(2)}, u32[]{:S(2)}) %collective-permute-start.18) | collective-permute-done | bytes 196640 | tf_op jit(solution)/shard_map/ppermute | solution.py:541
  93.0 0.8 add_convert_fusion
  (21 shorter events, 0.1 us)
Async XLA Ops:
  0.0 0.7 copy-start.3
  0.7 0.7 copy-start.4
  1.4 0.7 copy-start.5
  3.2 12.8 %collective-permute-start.3 = (bf16[128,1664]{1,0:T(8,128)(2,1)S(1)}, bf16[128,1664]{1,0:T(8,128)(2,1)S(1)}, u32[]{:S(2)}, u32[]{:S(2)}) collective-permute-start(bf16[128,1664]{1,0:T(8,128)(2,1)S(1)} %get-tuple-element.65.refs_0_), channel_id=1, source_target_pairs={{0,8},{4,12},{8,0},{12,4},{1,9},{5,13},{9,1},{13,5},{2,10},{6,14},... | collective-permute-start | bytes 1277960 | tf_op jit(solution)/shard_map/ppermute | solution.py:535
  6.2 11.8 %collective-permute-start.2 = (bf16[128,1664]{1,0:T(8,128)(2,1)S(1)}, bf16[128,1664]{1,0:T(8,128)(2,1)S(1)}, u32[]{:S(2)}, u32[]{:S(2)}) collective-permute-start(bf16[128,1664]{1,0:T(8,128)(2,1)S(1)} %get-tuple-element.65.refs_0_), channel_id=1, source_target_pairs={{0,4},{4,0},{8,12},{12,8},{1,5},{5,1},{9,13},{13,9},{2,6},{6,2},{1... | collective-permute-start | bytes 1277960 | tf_op jit(solution)/shard_map/ppermute | solution.py:535
  6.2 11.7 %copy-start.1 = (s32[16]{0:T(128)S(1)}, s32[16]{0:T(128)}, u32[]{:S(2)}) copy-start(s32[16]{0:T(128)} %refs_14_.1) | copy-start | bytes 196
  6.2 11.7 %copy-start.2 = (s32[64]{0:T(128)S(1)}, s32[64]{0:T(128)}, u32[]{:S(2)}) copy-start(s32[64]{0:T(128)} %refs_15_.1) | copy-start | bytes 772
  16.0 2.0 %collective-permute-start.4 = (bf16[128,1664]{1,0:T(8,128)(2,1)S(1)}, bf16[128,1664]{1,0:T(8,128)(2,1)S(1)}, u32[]{:S(2)}, u32[]{:S(2)}) collective-permute-start(bf16[128,1664]{1,0:T(8,128)(2,1)S(1)} %collective-permute-done.3.refs_2_), channel_id=1, source_target_pairs={{0,4},{4,0},{8,12},{12,8},{1,5},{5,1},{9,13},{13,9},{2,6},{6,2},{1... | collective-permute-start | bytes 1277960 | tf_op jit(solution)/shard_map/ppermute | solution.py:535
  16.0 11.5 %collective-permute-start.1 = (bf16[128,1536]{1,0:T(8,128)(2,1)S(1)}, bf16[128,1536]{1,0:T(8,128)(2,1)S(1)}, u32[]{:S(2)}, u32[]{:S(2)}) collective-permute-start(bf16[128,1536]{1,0:T(8,128)(2,1)S(1)} %get-tuple-element.64.refs_0_), channel_id=1, source_target_pairs={{0,8},{4,12},{8,0},{12,4},{1,9},{5,13},{9,1},{13,5},{2,10},{6,14},... | collective-permute-start | bytes 1179656 | tf_op jit(solution)/shard_map/ppermute | solution.py:535
  17.7 9.8 %collective-permute-start = (bf16[128,1536]{1,0:T(8,128)(2,1)S(1)}, bf16[128,1536]{1,0:T(8,128)(2,1)S(1)}, u32[]{:S(2)}, u32[]{:S(2)}) collective-permute-start(bf16[128,1536]{1,0:T(8,128)(2,1)S(1)} %get-tuple-element.64.refs_0_), channel_id=1, source_target_pairs={{0,4},{4,0},{8,12},{12,8},{1,5},{5,1},{9,13},{13,9},{2,6},{6,2},{1... | collective-permute-start | bytes 1179656 | tf_op jit(solution)/shard_map/ppermute | solution.py:535
  27.5 1.7 %collective-permute-start.5 = (bf16[128,1536]{1,0:T(8,128)(2,1)S(1)}, bf16[128,1536]{1,0:T(8,128)(2,1)S(1)}, u32[]{:S(2)}, u32[]{:S(2)}) collective-permute-start(bf16[128,1536]{1,0:T(8,128)(2,1)S(1)} %collective-permute-done.1.refs_2_), channel_id=1, source_target_pairs={{0,4},{4,0},{8,12},{12,8},{1,5},{5,1},{9,13},{13,9},{2,6},{6,2},{1... | collective-permute-start | bytes 1179656 | tf_op jit(solution)/shard_map/ppermute | solution.py:535
  42.0 8.3 %collective-permute-start.6 = (bf16[32,512]{1,0:T(8,128)(2,1)S(1)}, bf16[32,512]{1,0:T(8,128)(2,1)S(1)}, u32[]{:S(2)}, u32[]{:S(2)}) collective-permute-start(bf16[32,512]{1,0:T(8,128)(2,1)S(1)} %get-tuple-element.84), channel_id=1, source_target_pairs={{0,2},{1,3},{2,0},{3,1},{4,6},{5,7},{6,4},{7,5},{8,10},{9,11},{10,... | collective-permute-start | bytes 98312 | tf_op jit(solution)/shard_map/ppermute | solution.py:575
  50.3 1.8 %collective-permute-start.7 = (bf16[256,768]{1,0:T(8,128)(2,1)S(1)}, bf16[256,768]{1,0:T(8,128)(2,1)S(1)}, u32[]{:S(2)}, u32[]{:S(2)}) collective-permute-start(bf16[256,768]{1,0:T(8,128)(2,1)S(1)} %get-tuple-element.93), channel_id=1, source_target_pairs={{0,4},{4,0},{8,12},{12,8},{1,5},{5,1},{9,13},{13,9},{2,6},{6,2},{1... | collective-permute-start | bytes 1179656 | tf_op jit(solution)/shard_map/ppermute | solution.py:535
  50.4 3.3 %collective-permute-start.9 = (bf16[32,512]{1,0:T(8,128)(2,1)S(1)}, bf16[32,512]{1,0:T(8,128)(2,1)S(1)}, u32[]{:S(2)}, u32[]{:S(2)}) collective-permute-start(bf16[32,512]{1,0:T(8,128)(2,1)S(1)} %add_convert_fusion.2), channel_id=1, source_target_pairs={{0,4},{4,0},{8,12},{12,8},{1,5},{5,1},{9,13},{13,9},{2,6},{6,2},{1... | collective-permute-start | bytes 98312 | tf_op jit(solution)/shard_map/ppermute | solution.py:535
  52.2 10.3 %collective-permute-start.8 = (bf16[128,768]{1,0:T(8,128)(2,1)S(1)}, bf16[128,768]{1,0:T(8,128)(2,1)S(1)}, u32[]{:S(2)}, u32[]{:S(2)}) collective-permute-start(bf16[128,768]{1,0:T(8,128)(2,1)S(1)} %get-tuple-element.94), channel_id=1, source_target_pairs={{0,8},{4,12},{8,0},{12,4},{1,9},{5,13},{9,1},{13,5},{2,10},{6,14},... | collective-permute-start | bytes 589832 | tf_op jit(solution)/shard_map/ppermute | solution.py:535
  53.7 8.7 %collective-permute-start.10 = (bf16[64,512]{1,0:T(8,128)(2,1)S(1)}, bf16[64,512]{1,0:T(8,128)(2,1)S(1)}, u32[]{:S(2)}, u32[]{:S(2)}) collective-permute-start(bf16[64,512]{1,0:T(8,128)(2,1)S(1)} %pad_maximum_fusion.1), channel_id=1, source_target_pairs={{0,8},{4,12},{8,0},{12,4},{1,9},{5,13},{9,1},{13,5},{2,10},{6,14},... | collective-permute-start | bytes 196616 | tf_op jit(solution)/shard_map/ppermute | solution.py:535
  54.3 18.0 %copy-start = (bf16[16,8,16,768]{3,2,1,0:T(8,128)(2,1)S(1)}, bf16[16,8,16,768]{3,2,1,0:T(8,128)(2,1)}, u32[]{:S(2)}) copy-start(bf16[16,8,16,768]{3,2,1,0:T(8,128)(2,1)} %param.21) | copy-start | bytes 9437188
  62.4 2.4 %collective-permute-start.11 = (bf16[256,1536]{1,0:T(8,128)(2,1)S(1)}, bf16[256,1536]{1,0:T(8,128)(2,1)S(1)}, u32[]{:S(2)}, u32[]{:S(2)}) collective-permute-start(bf16[256,1536]{1,0:T(8,128)(2,1)S(1)} %get-tuple-element.103), channel_id=1, source_target_pairs={{0,4},{4,0},{8,12},{12,8},{1,5},{5,1},{9,13},{13,9},{2,6},{6,2},{1... | collective-permute-start | bytes 2359304 | tf_op jit(solution)/shard_map/ppermute | solution.py:535
  65.0 14.8 %collective-permute-start.12 = (bf16[128,1536]{1,0:T(8,128)(2,1)S(1)}, bf16[128,1536]{1,0:T(8,128)(2,1)S(1)}, u32[]{:S(2)}, u32[]{:S(2)}) collective-permute-start(bf16[128,1536]{1,0:T(8,128)(2,1)S(1)} %get-tuple-element.104), channel_id=1, source_target_pairs={{0,8},{4,12},{8,0},{12,4},{1,9},{5,13},{9,1},{13,5},{2,10},{6,14},... | collective-permute-start | bytes 1179656 | tf_op jit(solution)/shard_map/ppermute | solution.py:535
  66.5 5.7 %collective-permute-start.14 = (bf16[128,512]{1,0:T(8,128)(2,1)S(1)}, bf16[128,512]{1,0:T(8,128)(2,1)S(1)}, u32[]{:S(2)}, u32[]{:S(2)}) collective-permute-start(bf16[128,512]{1,0:T(8,128)(2,1)S(1)} %pad_maximum_fusion), channel_id=1, source_target_pairs={{0,1},{1,0},{2,3},{3,2},{4,5},{5,4},{6,7},{7,6},{8,9},{9,8},{10,11... | collective-permute-start | bytes 393224 | tf_op jit(solution)/shard_map/ppermute | solution.py:575
  68.2 11.5 %collective-permute-start.13 = (bf16[128,768]{1,0:T(8,128)(2,1)S(1)}, bf16[128,768]{1,0:T(8,128)(2,1)S(1)}, u32[]{:S(2)}, u32[]{:S(2)}) collective-permute-start(bf16[128,768]{1,0:T(8,128)(2,1)S(1)} %sum_and_cut.2), channel_id=1, source_target_pairs={{0,2},{1,3},{2,0},{3,1},{4,6},{5,7},{6,4},{7,5},{8,10},{9,11},{10,... | collective-permute-start | bytes 589832 | tf_op jit(solution)/shard_map/ppermute | solution.py:541
  79.8 1.7 %collective-permute-start.15 = (bf16[256,768]{1,0:T(8,128)(2,1)S(1)}, bf16[256,768]{1,0:T(8,128)(2,1)S(1)}, u32[]{:S(2)}, u32[]{:S(2)}) collective-permute-start(bf16[256,768]{1,0:T(8,128)(2,1)S(1)} %get-tuple-element.113), channel_id=1, source_target_pairs={{0,4},{4,0},{8,12},{12,8},{1,5},{5,1},{9,13},{13,9},{2,6},{6,2},{1... | collective-permute-start | bytes 1179656 | tf_op jit(solution)/shard_map/ppermute | solution.py:535
  81.7 9.6 %collective-permute-start.17 = (bf16[128,768]{1,0:T(8,128)(2,1)S(1)}, bf16[128,768]{1,0:T(8,128)(2,1)S(1)}, u32[]{:S(2)}, u32[]{:S(2)}) collective-permute-start(bf16[128,768]{1,0:T(8,128)(2,1)S(1)} %get-tuple-element.121), channel_id=1, source_target_pairs={{0,1},{1,2},{2,3},{3,0},{4,5},{5,6},{6,7},{7,4},{8,9},{9,10},{10,1... | collective-permute-start | bytes 589832 | tf_op jit(solution)/shard_map/ppermute | solution.py:541
  81.8 11.2 %collective-permute-start.18 = (bf16[128,768]{1,0:T(8,128)(2,1)S(1)}, bf16[128,768]{1,0:T(8,128)(2,1)S(1)}, u32[]{:S(2)}, u32[]{:S(2)}) collective-permute-start(bf16[128,768]{1,0:T(8,128)(2,1)S(1)} %get-tuple-element.122), channel_id=1, source_target_pairs={{0,3},{1,0},{2,1},{3,2},{4,7},{5,4},{6,5},{7,6},{8,11},{9,8},{10,9... | collective-permute-start | bytes 589832 | tf_op jit(solution)/shard_map/ppermute | solution.py:541
  85.6 7.4 %collective-permute-start.16 = (bf16[128,768]{1,0:T(8,128)(2,1)S(1)}, bf16[128,768]{1,0:T(8,128)(2,1)S(1)}, u32[]{:S(2)}, u32[]{:S(2)}) collective-permute-start(bf16[128,768]{1,0:T(8,128)(2,1)S(1)} %get-tuple-element.117), channel_id=1, source_target_pairs={{0,8},{4,12},{8,0},{12,4},{1,9},{5,13},{9,1},{13,5},{2,10},{6,14},... | collective-permute-start | bytes 589832 | tf_op jit(solution)/shard_map/ppermute | solution.py:535

commit v9 on v8

--- a/solution.py
+++ b/solution.py
@@ -32,6 +32,11 @@
 SMALL = pl.CostEstimate(flops=1, bytes_accessed=1, transcendentals=0)
 
 
+def silu(x):
+    half = 0.5 * x
+    return half + half * jnp.tanh(half)
+
+
 def params(mib):
     return pltpu.CompilerParams(vmem_limit_bytes=mib * MIB)
 
@@ -44,14 +49,22 @@
     return pl.BlockSpec(memory_space=pltpu.SMEM)
 
 
-def parts_kernel(tokens_ref, chosen_ref, logits_ref, tenant_ref, first_ref, second_ref, sems):
+def parts_kernel(tokens_ref, chosen_in, logits_in, tenant_in, first_ref, second_ref, chosen_ref, logits_ref, tenant_ref, sems):
     rows, width = second_ref.shape
     copies = [
         pltpu.make_async_copy(tokens_ref.at[:, pl.ds(0, width)], first_ref.at[:, pl.ds(0, width)], sems.at[0]),
         pltpu.make_async_copy(tokens_ref.at[:, pl.ds(width, width)], second_ref, sems.at[1]),
     ]
-    for copy in copies:
+    small = [
+        pltpu.make_async_copy(source, into, sems.at[2 + number])
+        for number, (source, into) in enumerate(
+            [(chosen_in, chosen_ref), (logits_in, logits_ref), (tenant_in, tenant_ref)]
+        )
+    ]
+    for copy in small + copies:
         copy.start()
+    for copy in small:
+        copy.wait()
     diagonal = lax.broadcasted_iota(jnp.int32, (rows, rows), 0) == lax.broadcasted_iota(jnp.int32, (rows, rows), 1)
 
     def column(row):
@@ -81,13 +94,23 @@
             jax.ShapeDtypeStruct((rows, width + 128), BF16),
             jax.ShapeDtypeStruct((rows, width), BF16),
         ),
-        in_specs=[pl.BlockSpec(memory_space=pltpu.HBM)] + [vmem()] * 3,
+        in_specs=[pl.BlockSpec(memory_space=pltpu.HBM)] * 4,
         out_specs=(vmem(),) * 2,
-        scratch_shapes=[pltpu.SemaphoreType.DMA((2,))],
+        scratch_shapes=[
+            pltpu.VMEM((2, rows), jnp.int32),
+            pltpu.VMEM((2, rows), F32),
+            pltpu.VMEM((1, rows), jnp.int32),
+            pltpu.SemaphoreType.DMA((5,)),
+        ],
         cost_estimate=SMALL,
         compiler_params=params(LIMIT_EARLY),
         name="token_parts",
-    )(pltpu.with_memory_space_constraint(tokens, pltpu.HBM), chosen_experts.T, logits.T, tenant.reshape(1, rows))
+    )(
+        *[
+            pltpu.with_memory_space_constraint(x, pltpu.HBM)
+            for x in (tokens, chosen_experts.T, logits.T, tenant.reshape(1, rows))
+        ]
+    )
 
 
 def meta_kernel(n_local, local_halves, ids_ref, adapter_ref, pool_slot_ref, *refs):
@@ -159,9 +182,14 @@
     return copies
 
 
-def prefetch_kernel(ids_ref, gate_ref, up_ref, *refs):
-    slabs, mark_ref, sems = refs[:-2], refs[-2], refs[-1]
+def prefetch_kernel(ids_ref, adapter_ref, pool_slot_ref, gate_ref, up_ref, pool_ref, *refs):
+    slabs, (factors, mark_ref, sems, factor_sems) = refs[:-4], refs[-4:]
     copies = [copy for half, slab in enumerate(slabs) for copy in slab_copies(gate_ref, up_ref, slab, sems, 0, half)]
+    rank = pool_ref.shape[2]
+    for number in range(adapter_ref.shape[0]):
+        source = pool_ref.at[pool_slot_ref[adapter_ref[number]]]
+        into = factors.at[:, number * rank : (number + 1) * rank]
+        copies.append(pltpu.make_async_copy(source, into, factor_sems.at[number]))
     for copy in copies:
         copy.start()
     mark_ref[...] = jnp.zeros_like(mark_ref)
@@ -169,20 +197,22 @@
         copy.wait()
 
 
-def prefetch(ids, gate, up, part_width):
+def prefetch(ids, adapters, pool_slots, gate, up, pool, part_width):
     local_halves, _, hidden_count = gate.shape
     tile = min(N_TILE, hidden_count)
     each = 2 * hidden_count // tile
+    tenants, rank = adapters.shape[0], pool.shape[2]
     return pl.pallas_call(
         prefetch_kernel,
-        out_shape=(pltpu.VMEM((each, part_width, tile), BF16),) * local_halves + (jax.ShapeDtypeStruct((8, 128), F32),),
-        in_specs=[smem()] + [pl.BlockSpec(memory_space=pltpu.HBM)] * 2,
-        out_specs=(vmem(),) * (local_halves + 1),
-        scratch_shapes=[pltpu.SemaphoreType.DMA((local_halves, each))],
+        out_shape=(pltpu.VMEM((each, part_width, tile), BF16),) * local_halves
+        + (pltpu.VMEM((local_halves, tenants * rank, hidden_count), BF16), jax.ShapeDtypeStruct((8, 128), F32)),
+        in_specs=[smem()] * 3 + [pl.BlockSpec(memory_space=pltpu.HBM)] * 3,
+        out_specs=(vmem(),) * (local_halves + 2),
+        scratch_shapes=[pltpu.SemaphoreType.DMA((local_halves, each)), pltpu.SemaphoreType.DMA((tenants,))],
         cost_estimate=SMALL,
         compiler_params=params(LIMIT_EARLY),
         name="weight_prefetch",
-    )(ids, gate, up)
+    )(ids, adapters, pool_slots, gate, up, pool)
 
 
 def pack(blocks, p_ref, packed):
@@ -192,22 +222,22 @@
         packed[i] = mm(p_ref[i], whole).astype(BF16)
 
 
-def down_slabs(down, n_ad):
-    return pltpu.VMEM((down.shape[0], down.shape[1], down.shape[2] // n_ad), BF16)
-
-
-def down_fetch(n_ad, step, ids_ref, down_ref, into_ref, sems):
-    _, rows, span = into_ref.shape
-    rows = rows // 2
+def down_slabs(down, n_ad, halves=None):
+    return pltpu.VMEM((halves or down.shape[0], down.shape[1], down.shape[2] // n_ad), BF16)
+
+
+def down_fetch(n_ad, step, ids_ref, down_ref, into_ref, sems, pieces=2, first=0):
+    halves, rows, span = into_ref.shape
+    rows = rows // pieces
     start = pl.multiple_of(lax.rem(ids_ref[1] + step, n_ad) * span, span)
     return [
         pltpu.make_async_copy(
-            down_ref.at[half, pl.ds(i * rows, rows), pl.ds(start, span)],
+            down_ref.at[first + half, pl.ds(i * rows, rows), pl.ds(start, span)],
             into_ref.at[half, pl.ds(i * rows, rows)],
             sems.at[half, i],
         )
-        for half in range(down_ref.shape[0])
-        for i in range(2)
+        for half in range(halves)
+        for i in range(pieces)
     ]
 
 
@@ -241,7 +271,7 @@
     each, part_width, _ = slabs[0].shape
     hbm = pl.BlockSpec(memory_space=pltpu.HBM)
     sums = pltpu.VMEM((local_halves, row_count, hidden_count), F32)
-    n_ahead = max(1, local_halves - 1)
+    n_ahead = max(1, local_halves - 2)
     return pl.pallas_call(
         functools.partial(first_kernel, len(blocks), local_halves),
         out_shape=(pltpu.VMEM(slabs[0].shape, BF16),) * n_ahead
@@ -259,12 +289,13 @@
     )(*blocks, mark, picked, gate, up, *[pltpu.with_memory_space_constraint(x, pltpu.VMEM) for x in slabs])
 
 
-def second_kernel(n_blocks, n_ahead, n_ad, step, *refs):
+def second_kernel(n_blocks, n_ahead, n_ad, steps, *refs):
     blocks, refs = refs[:n_blocks], refs[n_blocks:]
     p_ref, gate_ref, up_ref, refs = *refs[1:4], refs[4:]
     ahead, gate_in, up_in, refs = refs[:n_ahead], refs[n_ahead], refs[n_ahead + 1], refs[n_ahead + 2 :]
-    ids_ref, adapter_ref, pool_slot_ref, pool_ref, tslot_ref, rows_ref, down_ref, refs = *refs[:7], refs[7:]
-    hidden_ref, low_ref, next_ref, packed, factors, factor_sems, down_sems, late, sems = refs
+    ids_ref, factors, tslot_ref, rows_ref, down_ref, refs = *refs[:5], refs[5:]
+    hidden_ref, low_ref, refs = refs[0], refs[1], refs[2:]
+    nexts, (packed, down_sems, late, sems) = refs[:-4], refs[-4:]
     n_local = p_ref.shape[0]
     local_halves, _, hidden_count = gate_ref.shape
     halves_each = local_halves // n_local
@@ -272,17 +303,12 @@
     copies = {
         half: slab_copies(gate_ref, up_ref, slabs[half], sems, 1, half) for half in range(n_ahead, local_halves)
     }
-    tenants, rank = adapter_ref.shape[0], pool_ref.shape[2]
-    factor_copies = [
-        pltpu.make_async_copy(
-            pool_ref.at[pool_slot_ref[adapter_ref[number]]],
-            factors.at[:, number * rank : (number + 1) * rank],
-            factor_sems.at[number],
-        )
-        for number in range(tenants)
-    ]
-    down_copies = down_fetch(n_ad, step, ids_ref, down_ref, next_ref, down_sems)
-    for copy in copies.get(n_ahead, []) + factor_copies + down_copies:
+    rank = RANK
+    tenants = factors.shape[1] // rank
+    down_copies = []
+    for number, step in enumerate(steps):
+        down_copies += down_fetch(n_ad, step, ids_ref, down_ref, nexts[number], down_sems.at[number], 1)
+    for copy in copies.get(n_ahead, []) + down_copies:
         copy.start()
     pack(blocks, p_ref, packed)
     for half in range(local_halves):
@@ -299,9 +325,7 @@
                     copies[half + 1][number].start()
             gate = values[0] + gate_in[half, :, span]
             up = values[1] + up_in[half, :, span]
-            hidden_ref[half, :, span] = (jax.nn.silu(gate) * up).astype(BF16)
-    for copy in factor_copies:
-        copy.wait()
+            hidden_ref[half, :, span] = (silu(gate) * up).astype(BF16)
     for i in range(n_local):
         low = mm_nt(factors[i * halves_each], hidden_ref[i * halves_each])
         for half in range(i * halves_each + 1, (i + 1) * halves_each):
@@ -317,29 +341,28 @@
 
 
 def second_part(
-    blocks, mark, picked, gate, up, ahead, sums, ids, adapters, pool_slots, pool, tslot, table_rows, down, n_ad, step
+    blocks, mark, picked, gate, up, ahead, sums, ids, factors, tslot, table_rows, down, n_ad, steps
 ):
     local_halves, _, hidden_count = gate.shape
     n_local, row_count, count = picked.shape
     each, part_width, tile = ahead[0].shape
-    tenants, rank = adapters.shape[0], pool.shape[2]
+    rank = RANK
     hbm = pl.BlockSpec(memory_space=pltpu.HBM)
     held = [pltpu.with_memory_space_constraint(x, pltpu.VMEM) for x in (*ahead, *sums)]
+    factors = pltpu.with_memory_space_constraint(factors, pltpu.VMEM)
     late_bytes = 2 * each * part_width * tile
     return pl.pallas_call(
-        functools.partial(second_kernel, len(blocks), len(ahead), n_ad, step),
+        functools.partial(second_kernel, len(blocks), len(ahead), n_ad, steps),
         out_shape=(
             pltpu.VMEM((local_halves, row_count, hidden_count), BF16),
             jax.ShapeDtypeStruct((n_local * rank, count), BF16),
-            down_slabs(down, n_ad),
+            *[down_slabs(down, n_ad, None if i == 0 else max(1, local_halves // 2)) for i in range(len(steps))],
         ),
-        in_specs=[vmem()] * (len(blocks) + 2) + [hbm, hbm] + [vmem()] * len(held) + [smem()] * 3 + [hbm, vmem(), vmem(), hbm],
-        out_specs=(vmem(),) * 3,
+        in_specs=[vmem()] * (len(blocks) + 2) + [hbm, hbm] + [vmem()] * len(held) + [smem()] + [vmem()] * 3 + [hbm],
+        out_specs=(vmem(),) * (2 + len(steps)),
         scratch_shapes=[
             pltpu.VMEM((n_local, row_count, part_width), BF16),
-            pltpu.VMEM((local_halves, tenants * rank, hidden_count), BF16),
-            pltpu.SemaphoreType.DMA((tenants,)),
-            pltpu.SemaphoreType.DMA((local_halves, 2)),
+            pltpu.SemaphoreType.DMA((len(steps), local_halves, 2)),
             pltpu.VMEM((each, part_width, tile), BF16),
             pltpu.SemaphoreType.DMA((local_halves, each)),
         ],
@@ -348,46 +371,52 @@
             max(LIMIT_EARLY, 10 * n_local * row_count * part_width // MIB) + late_bytes // MIB + 1
         ),
         name="gate_up_second",
-    )(*blocks, mark, picked, gate, up, *held, ids, adapters, pool_slots, pool, tslot, table_rows, down)
-
-
-def weighted_down(hidden_ref, weight_ref, pt_ref, cols_ref):
+    )(*blocks, mark, picked, gate, up, *held, ids, factors, tslot, table_rows, down)
+
+
+def weighted_down(hidden_ref, weights, pt_ref, cols_ref):
+    slabs = [ref.at[half] for ref in weights for half in range(ref.shape[0])]
     n_local = pt_ref.shape[0]
     halves_each = hidden_ref.shape[0] // n_local
     total = None
     for i in range(n_local):
-        part_sum = mm(hidden_ref[i * halves_each], weight_ref[i * halves_each])
+        part_sum = mm(hidden_ref[i * halves_each], slabs[i * halves_each][...])
         for half in range(i * halves_each + 1, (i + 1) * halves_each):
-            part_sum = part_sum + mm(hidden_ref[half], weight_ref[half])
+            part_sum = part_sum + mm(hidden_ref[half], slabs[half][...])
         laid = mm(pt_ref[i], part_sum.astype(BF16)) * cols_ref[:, n_local + i : n_local + i + 1]
         total = laid if total is None else total + laid
     return total
 
 
-def down_first_kernel(n_ad, step, ids_ref, hidden_ref, weight_ref, pt_ref, cols_ref, down_ref, keep, send, next_ref, sems):
-    copies = down_fetch(n_ad, step, ids_ref, down_ref, next_ref, sems)
+def down_first_kernel(n_ad, step, ids_ref, hidden_ref, weight_ref, pt_ref, cols_ref, down_ref, keep, send, *refs):
+    copies = []
+    if refs:
+        into, sems = refs
+        copies = down_fetch(n_ad, step, ids_ref, down_ref, into, sems, 2, down_ref.shape[0] - into.shape[0])
     for copy in copies:
         copy.start()
-    write_pairs(weighted_down(hidden_ref, weight_ref, pt_ref, cols_ref), (keep, send))
+    write_pairs(weighted_down(hidden_ref, [weight_ref], pt_ref, cols_ref), (keep, send))
     for copy in copies:
         copy.wait()
 
 
-def down_first(ids, hidden, weights, pt, cols, down, n_ad, step):
+def down_first(ids, hidden, weights, pt, cols, down, n_ad, step, left):
     count, span = pt.shape[1], weights.shape[2]
     return pl.pallas_call(
         functools.partial(down_first_kernel, n_ad, step),
-        out_shape=(jax.ShapeDtypeStruct((count // 2, span), BF16),) * 2 + (down_slabs(down, n_ad),),
+        out_shape=(jax.ShapeDtypeStruct((count // 2, span), BF16),) * 2
+        + ((down_slabs(down, n_ad, left),) if left else ()),
         in_specs=[smem()] + [vmem()] * 4 + [pl.BlockSpec(memory_space=pltpu.HBM)],
-        out_specs=(vmem(),) * 3,
-        scratch_shapes=[pltpu.SemaphoreType.DMA((down.shape[0], 2))],
+        out_specs=(vmem(),) * (3 if left else 2),
+        scratch_shapes=[pltpu.SemaphoreType.DMA((left, 2))] if left else [],
         cost_estimate=SMALL,
         compiler_params=params(max(LIMIT, 12 * count * span // MIB)),
         name="down_first",
     )(ids, hidden, pltpu.with_memory_space_constraint(weights, pltpu.VMEM), pt, cols, down)
 
 
-def down_rest_kernel(n_ad, steps, ids_ref, hidden_ref, weight_ref, pt_ref, cols_ref, down_ref, keep, send, base, *refs):
+def down_rest_kernel(n_weights, n_ad, steps, ids_ref, hidden_ref, pt_ref, cols_ref, down_ref, *refs):
+    weights, (keep, send, base), refs = refs[:n_weights], refs[n_weights : n_weights + 3], refs[n_weights + 3 :]
     held, sems = refs[:-1], refs[-1]
     copies = [
         down_fetch(n_ad, step, ids_ref, down_ref, into, sems.at[number])
@@ -395,12 +424,12 @@
     ]
     for copy in [copy for group in copies for copy in group]:
         copy.start()
-    span = weight_ref.shape[2]
+    span = base.shape[1]
     for number in range(len(steps)):
         if number:
             for copy in copies[number - 1]:
                 copy.wait()
-        total = weighted_down(hidden_ref, held[number - 1] if number else weight_ref, pt_ref, cols_ref)
+        total = weighted_down(hidden_ref, [held[number - 1]] if number else weights, pt_ref, cols_ref)
         if number < len(steps) - 1:
             write_pairs(total, (keep, send), number * span)
         else:
@@ -408,19 +437,20 @@
 
 
 def down_rest(ids, hidden, weights, pt, cols, down, n_ad, steps):
-    count, span = pt.shape[1], weights.shape[2]
-    return pl.pallas_call(
-        functools.partial(down_rest_kernel, n_ad, steps),
+    count, span = pt.shape[1], down.shape[2] // n_ad
+    chunk = (*down.shape[:2], span)
+    return pl.pallas_call(
+        functools.partial(down_rest_kernel, len(weights), n_ad, steps),
         out_shape=(jax.ShapeDtypeStruct((count // 2, span * (len(steps) - 1)), BF16),) * 2
         + (jax.ShapeDtypeStruct((count, span), F32),),
-        in_specs=[smem()] + [vmem()] * 4 + [pl.BlockSpec(memory_space=pltpu.HBM)],
+        in_specs=[smem()] + [vmem()] * 3 + [pl.BlockSpec(memory_space=pltpu.HBM)] + [vmem()] * len(weights),
         out_specs=(vmem(),) * 3,
-        scratch_shapes=[pltpu.VMEM(weights.shape, BF16)] * (len(steps) - 1)
+        scratch_shapes=[pltpu.VMEM(chunk, BF16)] * (len(steps) - 1)
         + [pltpu.SemaphoreType.DMA((len(steps) - 1, down.shape[0], 2))],
         cost_estimate=SMALL,
-        compiler_params=params(max(LIMIT, 12 * count * span // MIB) + (len(steps) - 1) * weights.size * 2 // MIB),
+        compiler_params=params(max(LIMIT, 12 * count * span // MIB) + (len(steps) - 1) * math.prod(chunk) * 2 // MIB),
         name="down_rest",
-    )(ids, hidden, pltpu.with_memory_space_constraint(weights, pltpu.VMEM), pt, cols, down)
+    )(ids, hidden, pt, cols, down, *[pltpu.with_memory_space_constraint(x, pltpu.VMEM) for x in weights])
 
 
 def write_pairs(total, outs, at=0):
@@ -542,7 +572,9 @@
 
     order = sorted(range(1, n_ad), key=lambda step: (step != n_ad // 2, step))
     token_part = token_parts_of(tokens, chosen_experts, router_gate_logits, token_tenant)
-    *slabs, mark = prefetch(ids, gate_weight, up_weight, width // 2)
+    *slabs, factors, mark = prefetch(
+        ids, adapter_of_tenant, adapter_pool_slot, gate_weight, up_weight, adapter_input_factors, width // 2
+    )
     high = 1 << (bits - 1)
     crossing = [swap(own, high) for own in token_part]
 
@@ -560,9 +592,9 @@
     )
     *ahead, gate_sum, up_sum, mark = first_part(blocks, mark, picked, gate_weight, up_weight, slabs)
     crossing[1], mark = tie(crossing[1], mark)
-    hidden, low, weights = second_part(
-        spread(1, crossing[1]), mark, picked, gate_weight, up_weight, ahead, (gate_sum, up_sum), ids,
-        adapter_of_tenant, adapter_pool_slot, adapter_input_factors, tslot, table_rows, down_weight, n_ad, order[0],
+    hidden, low, weights, *following = second_part(
+        spread(1, crossing[1]), mark, picked, gate_weight, up_weight, ahead, (gate_sum, up_sum), ids, factors,
+        tslot, table_rows, down_weight, n_ad, order[:2],
     )
 
     def onward(keep, came, first=1):
@@ -579,8 +611,9 @@
 
     far_steps = range(1, n_ad.bit_length() - 1)
     others = [other_of(low, bit) for bit in far_steps[:1]]
-    keep, send, weights = down_first(ids, hidden, weights, pt, cols, down_weight, n_ad, order[1])
-    others, keep, send, weights = lax.optimization_barrier((others, keep, send, weights))
+    left = local_halves - following[0].shape[0]
+    keep, send, *later = down_first(ids, hidden, weights, pt, cols, down_weight, n_ad, order[1], left)
+    others, keep, send, later = lax.optimization_barrier((others, keep, send, later))
     for bit in far_steps:
         low = added(low, others[0] if bit == 1 else other_of(low, bit))
     for bit in range(bits - 1):
@@ -588,7 +621,7 @@
     crossed = swap(low, 1 << (bits - 1))
     keep, came = onward(keep, swap(send, 1), 1)
     keep, hidden = tie(keep, hidden)
-    keep_rest, send_rest, base = down_rest(ids, hidden, weights, pt, cols, down_weight, n_ad, (*order[1:], 0))
+    keep_rest, send_rest, base = down_rest(ids, hidden, following + later, pt, cols, down_weight, n_ad, (*order[1:], 0))
     came, crossed, keep_rest, send_rest, base = lax.optimization_barrier((came, crossed, keep_rest, send_rest, base))
     low = jnp.concatenate([low, crossed], axis=0)
     low = added(low, other_of(low, 0))

time: 93.9 us -> 92 us (0.980)
  starting transfers between devices: 18.8 us -> 17.7 us
    ppermute x14, starting transfers between devices: 9.94 us -> 8.69 us  [swap(): return lax.ppermute(x, 'ep', [(i, i ^ mask) for i in range(n_ep)])]
    pallas_call x1, Pallas kernels: 5.37 us -> 4.25 us  [down_first(): pl.pallas_call(functools.partial(down_first_kernel, n_ad, step), out_shap...]
    ppermute x3, waiting for transfers between devices: 11.5 us -> 10.5 us  [shift(): return lax.ppermute(x, 'ad', [(i, (i + step) % n_ad) for i in range(n_ad)])]
    ppermute x14, waiting for transfers between devices: 8.2 us -> 9.26 us  [swap(): return lax.ppermute(x, 'ep', [(i, i ^ mask) for i in range(n_ep)])]
    unnamed x12 -> x10, local copies, waits for them, and re-layouts: 2.02 us -> 1.32 us
where the time goes in v9:
time: 92 us; the launch traced here: 91.8 us
  Pallas kernels  48.7 us (53%)
  waiting for transfers between devices  23 us (25%)
  starting transfers between devices  17.7 us (19%)
  local copies, waits for them, and re-layouts  1.32 us (1%)
  other arithmetic  0.94 us (1%)
    pallas_call x1, Pallas kernels, second_part(): pl.pallas_call(functools.partial(second_kernel, len(blocks), len(ahead),...  13.1 us
    ppermute x3, waiting for transfers between devices, shift(): return lax.ppermute(x, 'ad', [(i, (i + step) % n_ad) for i in range(n_ad)])  10.5 us
    pallas_call x1, Pallas kernels, prefetch(): pl.pallas_call(prefetch_kernel, out_shape=(pltpu.VMEM((each, part_width,...  9.64 us
    ppermute x14, waiting for transfers between devices, swap(): return lax.ppermute(x, 'ep', [(i, i ^ mask) for i in range(n_ep)])  9.26 us
    pallas_call x1, Pallas kernels, down_rest(): pl.pallas_call(functools.partial(down_rest_kernel, len(weights), n_ad, st...  8.69 us
    ppermute x14, starting transfers between devices, swap(): return lax.ppermute(x, 'ep', [(i, i ^ mask) for i in range(n_ep)])  8.69 us
    pallas_call x1, Pallas kernels, first_part(): pl.pallas_call(functools.partial(first_kernel, len(blocks), local_halves)...  7.43 us
    ppermute x3, starting transfers between devices, shift(): return lax.ppermute(x, 'ad', [(i, (i + step) % n_ad) for i in range(n_ad)])  4.66 us
  transfers between devices with their start and end apart: 19, of which 10 were waited for; matrix products, arithmetic and copies ran while one was open for 0% of the time, Pallas kernels for 37%

profile of v9, /device:TPU:0, one launch (start us, length us, event | category | flops | bytes accessed | tf_op | source)
XLA Modules:
  0.0 91.8 jit_solution(6216436123412159744)
XLA Ops:
  0.0 1.2 %token_parts.1 = (bf16[128,1664]{1,0:T(8,128)(2,1)S(1)}, bf16[128,1536]{1,0:T(8,128)(2,1)S(1)}) custom-call(bf16[128,3072]{1,0:T(8,128)(2,1)} %tokens_ref.1, s32[2,128]{1,0:T(2,128)} %bitcast.7, f32[2,128]{1,0:T(2,128)} %bitcast.8, s32[1,128]{1,0:T(1,128)} %bitcast.9), custom_call_target="tpu_custom_call" | custom-call | flops 1 | bytes 1 | tf_op jit(solution)/shard_map/token_parts/pallas_call | solution.py:91
  1.2 3.0 %collective-permute-start.3 = (bf16[128,1664]{1,0:T(8,128)(2,1)S(1)}, bf16[128,1664]{1,0:T(8,128)(2,1)S(1)}, u32[]{:S(2)}, u32[]{:S(2)}) collective-permute-start(bf16[128,1664]{1,0:T(8,128)(2,1)S(1)} %get-tuple-element.66.refs_0_), channel_id=1, source_target_pairs={{0,8},{4,12},{8,0},{12,4},{1,9},{5,13},{9,1},{13,5},{2,10},{6,14},... | collective-permute-start | bytes 1277960 | tf_op jit(solution)/shard_map/ppermute | solution.py:565
  4.2 0.0 collective-permute-start.2
  4.2 0.1 pad_add_fusion.ids_ref.refs_12_
  4.3 0.7 copy-done.1
  5.0 0.7 copy-done.3
  5.6 9.6 %weight_prefetch.1 = (bf16[4,1536,512]{2,1,0:T(8,128)(2,1)S(1)}, bf16[4,1536,512]{2,1,0:T(8,128)(2,1)S(1)}, bf16[4,1536,512]{2,1,0:T(8,128)(2,1)S(1)}, bf16[4,15...) custom-call(s32[2]{0:T(128)S(1)} %pad_add_fusion.ids_ref.refs_12_, ...), custom_call_target="tpu_custom_call" | custom-call | flops 1 | bytes 1 | tf_op jit(solution)/shard_map/weight_prefetch/pallas_call | solution.py:205
  15.3 0.6 collective-permute-start.4
  15.8 0.1 collective-permute-start.1
  15.9 0.1 collective-permute-start
  16.0 0.0 collective-permute-done.2.refs_1_
  16.0 1.2 %collective-permute-done.4.refs_3_ = bf16[128,1664]{1,0:T(8,128)(2,1)S(1)} collective-permute-done((bf16[128,1664]{1,0:T(8,128)(2,1)S(1)}, bf16[128,1664]{1,0:T(8,128)(2,1)S(1)}, u32[]{:S(2)}, u32[]{:S(2)}) %collective-permute-start.4) | collective-permute-done | bytes 426016 | tf_op jit(solution)/shard_map/ppermute | solution.py:565
  17.2 1.1 %routing_tables.1 = (bf16[2,192,512]{2,1,0:T(8,128)(2,1)S(1)}, bf16[2,512,192]{2,1,0:T(8,128)(2,1)S(1)}, f32[512,128]{1,0:T(8,128)S(1)}, f32[8,512]{1,0:T(8,128)S(1)}, f32[2,8,192]{2,1,0:T(8,128)S(1)}) custom-call(s32[2]{0:T(128)S(1)} %pad_add_fusion.ids_ref.refs_12_, s32[16]{0:T(128)S(1)} %copy-done.2, s32[64]{0:T(128)S(1)} %copy-done.4, ...), custom_call_target="tpu_custom_call" | custom-call | flops 1 | bytes 1 | tf_op jit(solution)/shard_map/routing_tables/pallas_call | solution.py:159
  18.3 7.4 %gate_up_first.1 = (bf16[4,1536,512]{2,1,0:T(8,128)(2,1)S(1)}, bf16[4,1536,512]{2,1,0:T(8,128)(2,1)S(1)}, f32[4,192,1024]{2,1,0:T(8,128)S(1)}, f32[4,192,1024]{2,1,0:T(8,128)S(1)}, f32[8,128]{1,0:T(8,128)S(1)}) custom-call(bf16[128,1664]{1,0:T(8,128)(2,1)S(1)} %get-tuple-element.66.refs_0_, ...), custom_call_target="tpu_custom_call", output_to_operand_aliasing={{0}: (8, {}), {1}: (9, {})} | custom-call | flops 1 | bytes 1 | tf_op jit(solution)/shard_map/gate_up_first/pallas_call | solution.py:275
  25.8 1.2 %collective-permute-done.1.refs_2_ = bf16[128,1536]{1,0:T(8,128)(2,1)S(1)} collective-permute-done((bf16[128,1536]{1,0:T(8,128)(2,1)S(1)}, bf16[128,1536]{1,0:T(8,128)(2,1)S(1)}, u32[]{:S(2)}, u32[]{:S(2)}) %collective-permute-start.1) | collective-permute-done | bytes 393248 | tf_op jit(solution)/shard_map/ppermute | solution.py:565
  26.9 1.7 %collective-permute-done.5.refs_3_ = bf16[128,1536]{1,0:T(8,128)(2,1)S(1)} collective-permute-done((bf16[128,1536]{1,0:T(8,128)(2,1)S(1)}, bf16[128,1536]{1,0:T(8,128)(2,1)S(1)}, u32[]{:S(2)}, u32[]{:S(2)}) %collective-permute-start.5) | collective-permute-done | bytes 393248 | tf_op jit(solution)/shard_map/ppermute | solution.py:565
  28.7 13.1 %gate_up_second.1 = (bf16[4,192,1024]{2,1,0:T(8,128)(2,1)S(1)}, bf16[32,512]{1,0:T(8,128)(2,1)S(1)}, bf16[4,1024,768]{2,1,0:T(8,128)(2,1)S(1)}, bf16[2,1024,768]{2,1,0:T(8,128)(2,1)S(1)}) custom-call(bf16[128,1536]{1,0:T(8,128)(2,1)S(1)} %get-tuple-element.65.refs_0_, bf16[128,1536]{1,0:T(8,128)(2,1)S(1)} %collective-permute-done.refs_1_, ...), custom_call_target="tpu_custom_call" | custom-call | flops 1 | bytes 1 | tf_op jit(solution)/shard_map/gate_up_second/pallas_call | solution.py:354
  41.8 2.7 %collective-permute-start.6 = (bf16[32,512]{1,0:T(8,128)(2,1)S(1)}, bf16[32,512]{1,0:T(8,128)(2,1)S(1)}, u32[]{:S(2)}, u32[]{:S(2)}) collective-permute-start(bf16[32,512]{1,0:T(8,128)(2,1)S(1)} %get-tuple-element.85), channel_id=1, source_target_pairs={{0,2},{1,3},{2,0},{3,1},{4,6},{5,7},{6,4},{7,5},{8,10},{9,11},{10,... | collective-permute-start | bytes 98312 | tf_op jit(solution)/shard_map/ppermute | solution.py:607
  44.4 4.2 %down_first.1 = (bf16[256,768]{1,0:T(8,128)(2,1)S(1)}, bf16[256,768]{1,0:T(8,128)(2,1)S(1)}, bf16[2,1024,768]{2,1,0:T(8,128)(2,1)S(1)}) custom-call(s32[2]{0:T(128)S(1)} %pad_add_fusion.ids_ref.refs_12_, bf16[4,192,1024]{2,1,0:T(8,128)(2,1)S(1)} %get-tuple-element.98.hidden_ref, bf16[4,1024,768]{2,1,0:T(8,128)(2,1)S(1)} %get-tuple-element.87.weight_ref, ...), custom_call_target="tpu_custom_call" | custom-call | flops 1 | bytes 1 | tf_op jit(solution)/shard_map/down_first/pallas_call | solution.py:405
  48.7 0.0 collective-permute-done.6
  48.7 0.1 collective-permute-start.7
  48.8 0.6 collective-permute-start.9
  49.4 1.1 %collective-permute-done.7.came_ref = bf16[256,768]{1,0:T(8,128)(2,1)S(1)} collective-permute-done((bf16[256,768]{1,0:T(8,128)(2,1)S(1)}, bf16[256,768]{1,0:T(8,128)(2,1)S(1)}, u32[]{:S(2)}, u32[]{:S(2)}) %collective-permute-start.7) | collective-permute-done | bytes 393248 | tf_op jit(solution)/shard_map/ppermute | solution.py:565
  50.5 0.1 sum_and_split.3
  50.6 0.6 collective-permute-start.8
  51.2 0.0 collective-permute-done.9
  51.2 1.6 %collective-permute-start.10 = (bf16[64,512]{1,0:T(8,128)(2,1)S(1)}, bf16[64,512]{1,0:T(8,128)(2,1)S(1)}, u32[]{:S(2)}, u32[]{:S(2)}) collective-permute-start(bf16[64,512]{1,0:T(8,128)(2,1)S(1)} %pad_maximum_fusion.1), channel_id=1, source_target_pairs={{0,8},{4,12},{8,0},{12,4},{1,9},{5,13},{9,1},{13,5},{2,10},{6,14},... | collective-permute-start | bytes 196616 | tf_op jit(solution)/shard_map/ppermute | solution.py:565
  52.8 8.7 %down_rest.1 = (bf16[256,1536]{1,0:T(8,128)(2,1)S(1)}, bf16[256,1536]{1,0:T(8,128)(2,1)S(1)}, f32[512,768]{1,0:T(8,128)S(1)}) custom-call(s32[2]{0:T(128)S(1)} %pad_add_fusion.ids_ref.refs_12_, bf16[4,192,1024]{2,1,0:T(8,128)(2,1)S(1)} %get-tuple-element.98.hidden_ref, bf16[2,512,192]{2,1,0:T(8,128)(2,1)S(1)} %get-tuple-element.88.pt_ref, ...), custom_call_target="tpu_custom_call" | custom-call | flops 1 | bytes 1 | tf_op jit(solution)/shard_map/down_rest/pallas_call | solution.py:442
  61.5 0.0 collective-permute-done.10
  61.5 0.1 collective-permute-start.11
  61.6 2.3 %collective-permute-done.11.came_ref = bf16[256,1536]{1,0:T(8,128)(2,1)S(1)} collective-permute-done((bf16[256,1536]{1,0:T(8,128)(2,1)S(1)}, bf16[256,1536]{1,0:T(8,128)(2,1)S(1)}, u32[]{:S(2)}, u32[]{:S(2)}) %collective-permute-start.11) | collective-permute-done | bytes 786464 | tf_op jit(solution)/shard_map/ppermute | solution.py:565
  63.8 0.2 sum_and_split.4
  64.0 0.6 collective-permute-start.12
  64.6 1.7 %collective-permute-start.14 = (bf16[128,512]{1,0:T(8,128)(2,1)S(1)}, bf16[128,512]{1,0:T(8,128)(2,1)S(1)}, u32[]{:S(2)}, u32[]{:S(2)}) collective-permute-start(bf16[128,512]{1,0:T(8,128)(2,1)S(1)} %pad_maximum_fusion), channel_id=1, source_target_pairs={{0,1},{1,0},{2,3},{3,2},{4,5},{5,4},{6,7},{7,6},{8,9},{9,8},{10,11... | collective-permute-start | bytes 393224 | tf_op jit(solution)/shard_map/ppermute | solution.py:607
  66.3 0.8 collective-permute-start.13
  67.1 3.3 %collective-permute-done.14 = bf16[128,512]{1,0:T(8,128)(2,1)S(1)} collective-permute-done((bf16[128,512]{1,0:T(8,128)(2,1)S(1)}, bf16[128,512]{1,0:T(8,128)(2,1)S(1)}, u32[]{:S(2)}, u32[]{:S(2)}) %collective-permute-start.14) | collective-permute-done | bytes 131104 | tf_op jit(solution)/shard_map/ppermute | solution.py:607
  70.5 2.8 %adapters.1 = (bf16[256,768]{1,0:T(8,128)(2,1)S(1)}, bf16[256,768]{1,0:T(8,128)(2,1)S(1)}) custom-call(s32[2]{0:T(128)S(1)} %pad_add_fusion.ids_ref.refs_12_, f32[512,768]{1,0:T(8,128)S(1)} %get-tuple-element.109.base_ref, f32[512,128]{1,0:T(8,128)S(1)} %get-tuple-element.89.cols_ref, bf16[2048,768]{1,0:T(8,128)(2,1)S(1)} %bitcast.6, ...), custom_call_target="tpu_custom_call" | custom-call | flops 1 | bytes 1 | tf_op jit(solution)/shard_map/adapters/pallas_call | solution.py:488
  73.3 4.6 %collective-permute-done.13 = bf16[128,768]{1,0:T(8,128)(2,1)S(1)} collective-permute-done((bf16[128,768]{1,0:T(8,128)(2,1)S(1)}, bf16[128,768]{1,0:T(8,128)(2,1)S(1)}, u32[]{:S(2)}, u32[]{:S(2)}) %collective-permute-start.13) | collective-permute-done | bytes 196640 | tf_op jit(solution)/shard_map/ppermute | solution.py:571
  77.8 0.0 collective-permute-done.12.came_ref
  77.8 1.7 %collective-permute-done.15.came_ref = bf16[256,768]{1,0:T(8,128)(2,1)S(1)} collective-permute-done((bf16[256,768]{1,0:T(8,128)(2,1)S(1)}, bf16[256,768]{1,0:T(8,128)(2,1)S(1)}, u32[]{:S(2)}, u32[]{:S(2)}) %collective-permute-start.15) | collective-permute-done | bytes 393248 | tf_op jit(solution)/shard_map/ppermute | solution.py:565
  79.6 0.1 sum_and_split.5
  79.6 0.1 sum_and_cut.3
  79.8 0.1 collective-permute-start.17
  79.8 3.8 %collective-permute-start.18 = (bf16[128,768]{1,0:T(8,128)(2,1)S(1)}, bf16[128,768]{1,0:T(8,128)(2,1)S(1)}, u32[]{:S(2)}, u32[]{:S(2)}) collective-permute-start(bf16[128,768]{1,0:T(8,128)(2,1)S(1)} %get-tuple-element.124), channel_id=1, source_target_pairs={{0,3},{1,0},{2,1},{3,2},{4,7},{5,4},{6,5},{7,6},{8,11},{9,8},{10,9... | collective-permute-start | bytes 589832 | tf_op jit(solution)/shard_map/ppermute | solution.py:571
  83.6 1.5 %collective-permute-start.16 = (bf16[128,768]{1,0:T(8,128)(2,1)S(1)}, bf16[128,768]{1,0:T(8,128)(2,1)S(1)}, u32[]{:S(2)}, u32[]{:S(2)}) collective-permute-start(bf16[128,768]{1,0:T(8,128)(2,1)S(1)} %get-tuple-element.119), channel_id=1, source_target_pairs={{0,8},{4,12},{8,0},{12,4},{1,9},{5,13},{9,1},{13,5},{2,10},{6,14},... | collective-permute-start | bytes 589832 | tf_op jit(solution)/shard_map/ppermute | solution.py:565
  85.1 4.3 %collective-permute-done.17 = bf16[128,768]{1,0:T(8,128)(2,1)S(1)} collective-permute-done((bf16[128,768]{1,0:T(8,128)(2,1)S(1)}, bf16[128,768]{1,0:T(8,128)(2,1)S(1)}, u32[]{:S(2)}, u32[]{:S(2)}) %collective-permute-start.17) | collective-permute-done | bytes 196640 | tf_op jit(solution)/shard_map/ppermute | solution.py:571
  89.4 1.6 %collective-permute-done.18 = bf16[128,768]{1,0:T(8,128)(2,1)S(1)} collective-permute-done((bf16[128,768]{1,0:T(8,128)(2,1)S(1)}, bf16[128,768]{1,0:T(8,128)(2,1)S(1)}, u32[]{:S(2)}, u32[]{:S(2)}) %collective-permute-start.18) | collective-permute-done | bytes 196640 | tf_op jit(solution)/shard_map/ppermute | solution.py:571
  91.0 0.8 add_convert_fusion
  (19 shorter events, 0.1 us)
Async XLA Ops:
  1.2 14.1 %collective-permute-start.3 = (bf16[128,1664]{1,0:T(8,128)(2,1)S(1)}, bf16[128,1664]{1,0:T(8,128)(2,1)S(1)}, u32[]{:S(2)}, u32[]{:S(2)}) collective-permute-start(bf16[128,1664]{1,0:T(8,128)(2,1)S(1)} %get-tuple-element.66.refs_0_), channel_id=1, source_target_pairs={{0,8},{4,12},{8,0},{12,4},{1,9},{5,13},{9,1},{13,5},{2,10},{6,14},... | collective-permute-start | bytes 1277960 | tf_op jit(solution)/shard_map/ppermute | solution.py:565
  4.2 11.8 %collective-permute-start.2 = (bf16[128,1664]{1,0:T(8,128)(2,1)S(1)}, bf16[128,1664]{1,0:T(8,128)(2,1)S(1)}, u32[]{:S(2)}, u32[]{:S(2)}) collective-permute-start(bf16[128,1664]{1,0:T(8,128)(2,1)S(1)} %get-tuple-element.66.refs_0_), channel_id=1, source_target_pairs={{0,4},{4,0},{8,12},{12,8},{1,5},{5,1},{9,13},{13,9},{2,6},{6,2},{1... | collective-permute-start | bytes 1277960 | tf_op jit(solution)/shard_map/ppermute | solution.py:565
  4.3 0.7 copy-start.1
  5.0 0.7 copy-start.3
  5.6 11.6 %copy-start.2 = (s32[16]{0:T(128)S(1)}, s32[16]{0:T(128)}, u32[]{:S(2)}) copy-start(s32[16]{0:T(128)} %adapter_ref.3) | copy-start | bytes 196
  5.6 11.6 %copy-start.4 = (s32[64]{0:T(128)S(1)}, s32[64]{0:T(128)}, u32[]{:S(2)}) copy-start(s32[64]{0:T(128)} %pool_slot_ref.3) | copy-start | bytes 772
  15.3 2.0 %collective-permute-start.4 = (bf16[128,1664]{1,0:T(8,128)(2,1)S(1)}, bf16[128,1664]{1,0:T(8,128)(2,1)S(1)}, u32[]{:S(2)}, u32[]{:S(2)}) collective-permute-start(bf16[128,1664]{1,0:T(8,128)(2,1)S(1)} %collective-permute-done.3.refs_2_), channel_id=1, source_target_pairs={{0,4},{4,0},{8,12},{12,8},{1,5},{5,1},{9,13},{13,9},{2,6},{6,2},{1... | collective-permute-start | bytes 1277960 | tf_op jit(solution)/shard_map/ppermute | solution.py:565
  15.8 11.1 %collective-permute-start.1 = (bf16[128,1536]{1,0:T(8,128)(2,1)S(1)}, bf16[128,1536]{1,0:T(8,128)(2,1)S(1)}, u32[]{:S(2)}, u32[]{:S(2)}) collective-permute-start(bf16[128,1536]{1,0:T(8,128)(2,1)S(1)} %get-tuple-element.65.refs_0_), channel_id=1, source_target_pairs={{0,8},{4,12},{8,0},{12,4},{1,9},{5,13},{9,1},{13,5},{2,10},{6,14},... | collective-permute-start | bytes 1179656 | tf_op jit(solution)/shard_map/ppermute | solution.py:565
  15.9 11.0 %collective-permute-start = (bf16[128,1536]{1,0:T(8,128)(2,1)S(1)}, bf16[128,1536]{1,0:T(8,128)(2,1)S(1)}, u32[]{:S(2)}, u32[]{:S(2)}) collective-permute-start(bf16[128,1536]{1,0:T(8,128)(2,1)S(1)} %get-tuple-element.65.refs_0_), channel_id=1, source_target_pairs={{0,4},{4,0},{8,12},{12,8},{1,5},{5,1},{9,13},{13,9},{2,6},{6,2},{1... | collective-permute-start | bytes 1179656 | tf_op jit(solution)/shard_map/ppermute | solution.py:565
  26.9 1.7 %collective-permute-start.5 = (bf16[128,1536]{1,0:T(8,128)(2,1)S(1)}, bf16[128,1536]{1,0:T(8,128)(2,1)S(1)}, u32[]{:S(2)}, u32[]{:S(2)}) collective-permute-start(bf16[128,1536]{1,0:T(8,128)(2,1)S(1)} %collective-permute-done.1.refs_2_), channel_id=1, source_target_pairs={{0,4},{4,0},{8,12},{12,8},{1,5},{5,1},{9,13},{13,9},{2,6},{6,2},{1... | collective-permute-start | bytes 1179656 | tf_op jit(solution)/shard_map/ppermute | solution.py:565
  41.8 6.9 %collective-permute-start.6 = (bf16[32,512]{1,0:T(8,128)(2,1)S(1)}, bf16[32,512]{1,0:T(8,128)(2,1)S(1)}, u32[]{:S(2)}, u32[]{:S(2)}) collective-permute-start(bf16[32,512]{1,0:T(8,128)(2,1)S(1)} %get-tuple-element.85), channel_id=1, source_target_pairs={{0,2},{1,3},{2,0},{3,1},{4,6},{5,7},{6,4},{7,5},{8,10},{9,11},{10,... | collective-permute-start | bytes 98312 | tf_op jit(solution)/shard_map/ppermute | solution.py:607
  48.7 1.8 %collective-permute-start.7 = (bf16[256,768]{1,0:T(8,128)(2,1)S(1)}, bf16[256,768]{1,0:T(8,128)(2,1)S(1)}, u32[]{:S(2)}, u32[]{:S(2)}) collective-permute-start(bf16[256,768]{1,0:T(8,128)(2,1)S(1)} %get-tuple-element.94), channel_id=1, source_target_pairs={{0,4},{4,0},{8,12},{12,8},{1,5},{5,1},{9,13},{13,9},{2,6},{6,2},{1... | collective-permute-start | bytes 1179656 | tf_op jit(solution)/shard_map/ppermute | solution.py:565
  48.8 2.4 %collective-permute-start.9 = (bf16[32,512]{1,0:T(8,128)(2,1)S(1)}, bf16[32,512]{1,0:T(8,128)(2,1)S(1)}, u32[]{:S(2)}, u32[]{:S(2)}) collective-permute-start(bf16[32,512]{1,0:T(8,128)(2,1)S(1)} %add_convert_fusion.2), channel_id=1, source_target_pairs={{0,4},{4,0},{8,12},{12,8},{1,5},{5,1},{9,13},{13,9},{2,6},{6,2},{1... | collective-permute-start | bytes 98312 | tf_op jit(solution)/shard_map/ppermute | solution.py:565
  50.6 10.9 %collective-permute-start.8 = (bf16[128,768]{1,0:T(8,128)(2,1)S(1)}, bf16[128,768]{1,0:T(8,128)(2,1)S(1)}, u32[]{:S(2)}, u32[]{:S(2)}) collective-permute-start(bf16[128,768]{1,0:T(8,128)(2,1)S(1)} %get-tuple-element.95), channel_id=1, source_target_pairs={{0,8},{4,12},{8,0},{12,4},{1,9},{5,13},{9,1},{13,5},{2,10},{6,14},... | collective-permute-start | bytes 589832 | tf_op jit(solution)/shard_map/ppermute | solution.py:565
  51.2 10.3 %collective-permute-start.10 = (bf16[64,512]{1,0:T(8,128)(2,1)S(1)}, bf16[64,512]{1,0:T(8,128)(2,1)S(1)}, u32[]{:S(2)}, u32[]{:S(2)}) collective-permute-start(bf16[64,512]{1,0:T(8,128)(2,1)S(1)} %pad_maximum_fusion.1), channel_id=1, source_target_pairs={{0,8},{4,12},{8,0},{12,4},{1,9},{5,13},{9,1},{13,5},{2,10},{6,14},... | collective-permute-start | bytes 196616 | tf_op jit(solution)/shard_map/ppermute | solution.py:565
  52.8 17.7 %copy-start = (bf16[16,8,16,768]{3,2,1,0:T(8,128)(2,1)S(1)}, bf16[16,8,16,768]{3,2,1,0:T(8,128)(2,1)}, u32[]{:S(2)}) copy-start(bf16[16,8,16,768]{3,2,1,0:T(8,128)(2,1)} %param.21) | copy-start | bytes 9437188
  61.5 2.4 %collective-permute-start.11 = (bf16[256,1536]{1,0:T(8,128)(2,1)S(1)}, bf16[256,1536]{1,0:T(8,128)(2,1)S(1)}, u32[]{:S(2)}, u32[]{:S(2)}) collective-permute-start(bf16[256,1536]{1,0:T(8,128)(2,1)S(1)} %get-tuple-element.105), channel_id=1, source_target_pairs={{0,4},{4,0},{8,12},{12,8},{1,5},{5,1},{9,13},{13,9},{2,6},{6,2},{1... | collective-permute-start | bytes 2359304 | tf_op jit(solution)/shard_map/ppermute | solution.py:565
  64.0 13.8 %collective-permute-start.12 = (bf16[128,1536]{1,0:T(8,128)(2,1)S(1)}, bf16[128,1536]{1,0:T(8,128)(2,1)S(1)}, u32[]{:S(2)}, u32[]{:S(2)}) collective-permute-start(bf16[128,1536]{1,0:T(8,128)(2,1)S(1)} %get-tuple-element.106), channel_id=1, source_target_pairs={{0,8},{4,12},{8,0},{12,4},{1,9},{5,13},{9,1},{13,5},{2,10},{6,14},... | collective-permute-start | bytes 1179656 | tf_op jit(solution)/shard_map/ppermute | solution.py:565
  64.6 5.8 %collective-permute-start.14 = (bf16[128,512]{1,0:T(8,128)(2,1)S(1)}, bf16[128,512]{1,0:T(8,128)(2,1)S(1)}, u32[]{:S(2)}, u32[]{:S(2)}) collective-permute-start(bf16[128,512]{1,0:T(8,128)(2,1)S(1)} %pad_maximum_fusion), channel_id=1, source_target_pairs={{0,1},{1,0},{2,3},{3,2},{4,5},{5,4},{6,7},{7,6},{8,9},{9,8},{10,11... | collective-permute-start | bytes 393224 | tf_op jit(solution)/shard_map/ppermute | solution.py:607
  66.3 11.5 %collective-permute-start.13 = (bf16[128,768]{1,0:T(8,128)(2,1)S(1)}, bf16[128,768]{1,0:T(8,128)(2,1)S(1)}, u32[]{:S(2)}, u32[]{:S(2)}) collective-permute-start(bf16[128,768]{1,0:T(8,128)(2,1)S(1)} %sum_and_cut.2), channel_id=1, source_target_pairs={{0,2},{1,3},{2,0},{3,1},{4,6},{5,7},{6,4},{7,5},{8,10},{9,11},{10,... | collective-permute-start | bytes 589832 | tf_op jit(solution)/shard_map/ppermute | solution.py:571
  77.8 1.7 %collective-permute-start.15 = (bf16[256,768]{1,0:T(8,128)(2,1)S(1)}, bf16[256,768]{1,0:T(8,128)(2,1)S(1)}, u32[]{:S(2)}, u32[]{:S(2)}) collective-permute-start(bf16[256,768]{1,0:T(8,128)(2,1)S(1)} %get-tuple-element.115), channel_id=1, source_target_pairs={{0,4},{4,0},{8,12},{12,8},{1,5},{5,1},{9,13},{13,9},{2,6},{6,2},{1... | collective-permute-start | bytes 1179656 | tf_op jit(solution)/shard_map/ppermute | solution.py:565
  79.8 9.6 %collective-permute-start.17 = (bf16[128,768]{1,0:T(8,128)(2,1)S(1)}, bf16[128,768]{1,0:T(8,128)(2,1)S(1)}, u32[]{:S(2)}, u32[]{:S(2)}) collective-permute-start(bf16[128,768]{1,0:T(8,128)(2,1)S(1)} %get-tuple-element.123), channel_id=1, source_target_pairs={{0,1},{1,2},{2,3},{3,0},{4,5},{5,6},{6,7},{7,4},{8,9},{9,10},{10,1... | collective-permute-start | bytes 589832 | tf_op jit(solution)/shard_map/ppermute | solution.py:571
  79.8 11.2 %collective-permute-start.18 = (bf16[128,768]{1,0:T(8,128)(2,1)S(1)}, bf16[128,768]{1,0:T(8,128)(2,1)S(1)}, u32[]{:S(2)}, u32[]{:S(2)}) collective-permute-start(bf16[128,768]{1,0:T(8,128)(2,1)S(1)} %get-tuple-element.124), channel_id=1, source_target_pairs={{0,3},{1,0},{2,1},{3,2},{4,7},{5,4},{6,5},{7,6},{8,11},{9,8},{10,9... | collective-permute-start | bytes 589832 | tf_op jit(solution)/shard_map/ppermute | solution.py:571
  83.6 7.4 %collective-permute-start.16 = (bf16[128,768]{1,0:T(8,128)(2,1)S(1)}, bf16[128,768]{1,0:T(8,128)(2,1)S(1)}, u32[]{:S(2)}, u32[]{:S(2)}) collective-permute-start(bf16[128,768]{1,0:T(8,128)(2,1)S(1)} %get-tuple-element.119), channel_id=1, source_target_pairs={{0,8},{4,12},{8,0},{12,4},{1,9},{5,13},{9,1},{13,5},{2,10},{6,14},... | collective-permute-start | bytes 589832 | tf_op jit(solution)/shard_map/ppermute | solution.py:565

commit v10 on v9

--- a/solution.py
+++ b/solution.py
@@ -305,10 +305,10 @@
     }
     rank = RANK
     tenants = factors.shape[1] // rank
-    down_copies = []
-    for number, step in enumerate(steps):
-        down_copies += down_fetch(n_ad, step, ids_ref, down_ref, nexts[number], down_sems.at[number], 1)
-    for copy in copies.get(n_ahead, []) + down_copies:
+    down_copies = [
+        down_fetch(n_ad, step, ids_ref, down_ref, nexts[number], down_sems.at[number]) for number, step in enumerate(steps)
+    ]
+    for copy in copies.get(n_ahead, []):
         copy.start()
     pack(blocks, p_ref, packed)
     for half in range(local_halves):
@@ -326,6 +326,10 @@
             gate = values[0] + gate_in[half, :, span]
             up = values[1] + up_in[half, :, span]
             hidden_ref[half, :, span] = (silu(gate) * up).astype(BF16)
+        for number, group in enumerate(down_copies):
+            if half == min(local_halves - 1, number * n_ahead):
+                for copy in group:
+                    copy.start()
     for i in range(n_local):
         low = mm_nt(factors[i * halves_each], hidden_ref[i * halves_each])
         for half in range(i * halves_each + 1, (i + 1) * halves_each):
@@ -336,7 +340,7 @@
             total = total + jnp.where(owner == number, low[number * rank : (number + 1) * rank], 0.0)
         weight = rows_ref[n_local + i : n_local + i + 1]
         low_ref[i * rank : (i + 1) * rank] = (mm(total.astype(BF16), p_ref[i]) * weight).astype(BF16)
-    for copy in down_copies:
+    for copy in [copy for group in down_copies for copy in group]:
         copy.wait()
 
 

time: 92 us -> 92.7 us (level)
  no operation moved by 1% of the time
where the time goes in v10:
time: 92.7 us; the launch traced here: 92.6 us
  Pallas kernels  49.5 us (53%)
  waiting for transfers between devices  23.1 us (25%)
  starting transfers between devices  17.6 us (19%)
  local copies, waits for them, and re-layouts  1.32 us (1%)
  other arithmetic  0.94 us (1%)
    pallas_call x1, Pallas kernels, second_part(): pl.pallas_call(functools.partial(second_kernel, len(blocks), len(ahead),...  13.8 us
    ppermute x3, waiting for transfers between devices, shift(): return lax.ppermute(x, 'ad', [(i, (i + step) % n_ad) for i in range(n_ad)])  10.5 us
    pallas_call x1, Pallas kernels, prefetch(): pl.pallas_call(prefetch_kernel, out_shape=(pltpu.VMEM((each, part_width,...  9.73 us
    ppermute x14, waiting for transfers between devices, swap(): return lax.ppermute(x, 'ep', [(i, i ^ mask) for i in range(n_ep)])  9.26 us
    pallas_call x1, Pallas kernels, down_rest(): pl.pallas_call(functools.partial(down_rest_kernel, len(weights), n_ad, st...  8.69 us
    ppermute x14, starting transfers between devices, swap(): return lax.ppermute(x, 'ep', [(i, i ^ mask) for i in range(n_ep)])  8.69 us
    pallas_call x1, Pallas kernels, first_part(): pl.pallas_call(functools.partial(first_kernel, len(blocks), local_halves)...  7.43 us
    ppermute x3, starting transfers between devices, shift(): return lax.ppermute(x, 'ad', [(i, (i + step) % n_ad) for i in range(n_ad)])  4.66 us
  transfers between devices with their start and end apart: 19, of which 10 were waited for; matrix products, arithmetic and copies ran while one was open for 0% of the time, Pallas kernels for 37%

profile of v10, /device:TPU:0, one launch (start us, length us, event | category | flops | bytes accessed | tf_op | source)
XLA Modules:
  0.0 92.6 jit_solution(13297603073446473347)
XLA Ops:
  0.0 1.2 %token_parts.1 = (bf16[128,1664]{1,0:T(8,128)(2,1)S(1)}, bf16[128,1536]{1,0:T(8,128)(2,1)S(1)}) custom-call(bf16[128,3072]{1,0:T(8,128)(2,1)} %tokens_ref.1, s32[2,128]{1,0:T(2,128)} %bitcast.7, f32[2,128]{1,0:T(2,128)} %bitcast.8, s32[1,128]{1,0:T(1,128)} %bitcast.9), custom_call_target="tpu_custom_call" | custom-call | flops 1 | bytes 1 | tf_op jit(solution)/shard_map/token_parts/pallas_call | solution.py:91
  1.2 3.0 %collective-permute-start.3 = (bf16[128,1664]{1,0:T(8,128)(2,1)S(1)}, bf16[128,1664]{1,0:T(8,128)(2,1)S(1)}, u32[]{:S(2)}, u32[]{:S(2)}) collective-permute-start(bf16[128,1664]{1,0:T(8,128)(2,1)S(1)} %get-tuple-element.66.refs_0_), channel_id=1, source_target_pairs={{0,8},{4,12},{8,0},{12,4},{1,9},{5,13},{9,1},{13,5},{2,10},{6,14},... | collective-permute-start | bytes 1277960 | tf_op jit(solution)/shard_map/ppermute | solution.py:569
  4.2 0.0 collective-permute-start.2
  4.2 0.1 pad_add_fusion.ids_ref.refs_12_
  4.3 0.7 copy-done.1
  5.0 0.7 copy-done.3
  5.6 9.7 %weight_prefetch.1 = (bf16[4,1536,512]{2,1,0:T(8,128)(2,1)S(1)}, bf16[4,1536,512]{2,1,0:T(8,128)(2,1)S(1)}, bf16[4,1536,512]{2,1,0:T(8,128)(2,1)S(1)}, bf16[4,15...) custom-call(s32[2]{0:T(128)S(1)} %pad_add_fusion.ids_ref.refs_12_, ...), custom_call_target="tpu_custom_call" | custom-call | flops 1 | bytes 1 | tf_op jit(solution)/shard_map/weight_prefetch/pallas_call | solution.py:205
  15.4 0.0 collective-permute-done.3.refs_2_
  15.4 0.6 collective-permute-start.4
  15.9 0.1 collective-permute-start.1
  16.0 0.1 collective-permute-start
  16.1 1.2 %collective-permute-done.4.refs_3_ = bf16[128,1664]{1,0:T(8,128)(2,1)S(1)} collective-permute-done((bf16[128,1664]{1,0:T(8,128)(2,1)S(1)}, bf16[128,1664]{1,0:T(8,128)(2,1)S(1)}, u32[]{:S(2)}, u32[]{:S(2)}) %collective-permute-start.4) | collective-permute-done | bytes 426016 | tf_op jit(solution)/shard_map/ppermute | solution.py:569
  17.3 1.1 %routing_tables.1 = (bf16[2,192,512]{2,1,0:T(8,128)(2,1)S(1)}, bf16[2,512,192]{2,1,0:T(8,128)(2,1)S(1)}, f32[512,128]{1,0:T(8,128)S(1)}, f32[8,512]{1,0:T(8,128)S(1)}, f32[2,8,192]{2,1,0:T(8,128)S(1)}) custom-call(s32[2]{0:T(128)S(1)} %pad_add_fusion.ids_ref.refs_12_, s32[16]{0:T(128)S(1)} %copy-done.2, s32[64]{0:T(128)S(1)} %copy-done.4, ...), custom_call_target="tpu_custom_call" | custom-call | flops 1 | bytes 1 | tf_op jit(solution)/shard_map/routing_tables/pallas_call | solution.py:159
  18.4 7.4 %gate_up_first.1 = (bf16[4,1536,512]{2,1,0:T(8,128)(2,1)S(1)}, bf16[4,1536,512]{2,1,0:T(8,128)(2,1)S(1)}, f32[4,192,1024]{2,1,0:T(8,128)S(1)}, f32[4,192,1024]{2,1,0:T(8,128)S(1)}, f32[8,128]{1,0:T(8,128)S(1)}) custom-call(bf16[128,1664]{1,0:T(8,128)(2,1)S(1)} %get-tuple-element.66.refs_0_, ...), custom_call_target="tpu_custom_call", output_to_operand_aliasing={{0}: (8, {}), {1}: (9, {})} | custom-call | flops 1 | bytes 1 | tf_op jit(solution)/shard_map/gate_up_first/pallas_call | solution.py:275
  25.9 1.2 %collective-permute-done.1.refs_2_ = bf16[128,1536]{1,0:T(8,128)(2,1)S(1)} collective-permute-done((bf16[128,1536]{1,0:T(8,128)(2,1)S(1)}, bf16[128,1536]{1,0:T(8,128)(2,1)S(1)}, u32[]{:S(2)}, u32[]{:S(2)}) %collective-permute-start.1) | collective-permute-done | bytes 393248 | tf_op jit(solution)/shard_map/ppermute | solution.py:569
  27.0 0.0 collective-permute-start.5
  27.0 0.0 collective-permute-done.refs_1_
  27.0 1.7 %collective-permute-done.5.refs_3_ = bf16[128,1536]{1,0:T(8,128)(2,1)S(1)} collective-permute-done((bf16[128,1536]{1,0:T(8,128)(2,1)S(1)}, bf16[128,1536]{1,0:T(8,128)(2,1)S(1)}, u32[]{:S(2)}, u32[]{:S(2)}) %collective-permute-start.5) | collective-permute-done | bytes 393248 | tf_op jit(solution)/shard_map/ppermute | solution.py:569
  28.8 13.8 %gate_up_second.1 = (bf16[4,192,1024]{2,1,0:T(8,128)(2,1)S(1)}, bf16[32,512]{1,0:T(8,128)(2,1)S(1)}, bf16[4,1024,768]{2,1,0:T(8,128)(2,1)S(1)}, bf16[2,1024,768]{2,1,0:T(8,128)(2,1)S(1)}) custom-call(bf16[128,1536]{1,0:T(8,128)(2,1)S(1)} %get-tuple-element.65.refs_0_, bf16[128,1536]{1,0:T(8,128)(2,1)S(1)} %collective-permute-done.refs_1_, ...), custom_call_target="tpu_custom_call" | custom-call | flops 1 | bytes 1 | tf_op jit(solution)/shard_map/gate_up_second/pallas_call | solution.py:358
  42.5 2.7 %collective-permute-start.6 = (bf16[32,512]{1,0:T(8,128)(2,1)S(1)}, bf16[32,512]{1,0:T(8,128)(2,1)S(1)}, u32[]{:S(2)}, u32[]{:S(2)}) collective-permute-start(bf16[32,512]{1,0:T(8,128)(2,1)S(1)} %get-tuple-element.85), channel_id=1, source_target_pairs={{0,2},{1,3},{2,0},{3,1},{4,6},{5,7},{6,4},{7,5},{8,10},{9,11},{10,... | collective-permute-start | bytes 98312 | tf_op jit(solution)/shard_map/ppermute | solution.py:611
  45.2 4.3 %down_first.1 = (bf16[256,768]{1,0:T(8,128)(2,1)S(1)}, bf16[256,768]{1,0:T(8,128)(2,1)S(1)}, bf16[2,1024,768]{2,1,0:T(8,128)(2,1)S(1)}) custom-call(s32[2]{0:T(128)S(1)} %pad_add_fusion.ids_ref.refs_12_, bf16[4,192,1024]{2,1,0:T(8,128)(2,1)S(1)} %get-tuple-element.98.hidden_ref, bf16[4,1024,768]{2,1,0:T(8,128)(2,1)S(1)} %get-tuple-element.87.weight_ref, ...), custom_call_target="tpu_custom_call" | custom-call | flops 1 | bytes 1 | tf_op jit(solution)/shard_map/down_first/pallas_call | solution.py:409
  49.4 0.1 collective-permute-start.7
  49.5 0.6 collective-permute-start.9
  50.1 1.1 %collective-permute-done.7.came_ref = bf16[256,768]{1,0:T(8,128)(2,1)S(1)} collective-permute-done((bf16[256,768]{1,0:T(8,128)(2,1)S(1)}, bf16[256,768]{1,0:T(8,128)(2,1)S(1)}, u32[]{:S(2)}, u32[]{:S(2)}) %collective-permute-start.7) | collective-permute-done | bytes 393248 | tf_op jit(solution)/shard_map/ppermute | solution.py:569
  51.2 0.1 sum_and_split.3
  51.3 0.6 collective-permute-start.8
  51.9 0.0 collective-permute-done.9
  51.9 1.6 %collective-permute-start.10 = (bf16[64,512]{1,0:T(8,128)(2,1)S(1)}, bf16[64,512]{1,0:T(8,128)(2,1)S(1)}, u32[]{:S(2)}, u32[]{:S(2)}) collective-permute-start(bf16[64,512]{1,0:T(8,128)(2,1)S(1)} %pad_maximum_fusion.1), channel_id=1, source_target_pairs={{0,8},{4,12},{8,0},{12,4},{1,9},{5,13},{9,1},{13,5},{2,10},{6,14},... | collective-permute-start | bytes 196616 | tf_op jit(solution)/shard_map/ppermute | solution.py:569
  53.5 8.7 %down_rest.1 = (bf16[256,1536]{1,0:T(8,128)(2,1)S(1)}, bf16[256,1536]{1,0:T(8,128)(2,1)S(1)}, f32[512,768]{1,0:T(8,128)S(1)}) custom-call(s32[2]{0:T(128)S(1)} %pad_add_fusion.ids_ref.refs_12_, bf16[4,192,1024]{2,1,0:T(8,128)(2,1)S(1)} %get-tuple-element.98.hidden_ref, bf16[2,512,192]{2,1,0:T(8,128)(2,1)S(1)} %get-tuple-element.88.pt_ref, ...), custom_call_target="tpu_custom_call" | custom-call | flops 1 | bytes 1 | tf_op jit(solution)/shard_map/down_rest/pallas_call | solution.py:446
  62.2 0.0 collective-permute-done.10
  62.2 0.1 collective-permute-start.11
  62.3 2.3 %collective-permute-done.11.came_ref = bf16[256,1536]{1,0:T(8,128)(2,1)S(1)} collective-permute-done((bf16[256,1536]{1,0:T(8,128)(2,1)S(1)}, bf16[256,1536]{1,0:T(8,128)(2,1)S(1)}, u32[]{:S(2)}, u32[]{:S(2)}) %collective-permute-start.11) | collective-permute-done | bytes 786464 | tf_op jit(solution)/shard_map/ppermute | solution.py:569
  64.6 0.2 sum_and_split.4
  64.8 0.6 collective-permute-start.12
  65.4 1.6 %collective-permute-start.14 = (bf16[128,512]{1,0:T(8,128)(2,1)S(1)}, bf16[128,512]{1,0:T(8,128)(2,1)S(1)}, u32[]{:S(2)}, u32[]{:S(2)}) collective-permute-start(bf16[128,512]{1,0:T(8,128)(2,1)S(1)} %pad_maximum_fusion), channel_id=1, source_target_pairs={{0,1},{1,0},{2,3},{3,2},{4,5},{5,4},{6,7},{7,6},{8,9},{9,8},{10,11... | collective-permute-start | bytes 393224 | tf_op jit(solution)/shard_map/ppermute | solution.py:611
  67.1 0.8 collective-permute-start.13
  67.8 3.3 %collective-permute-done.14 = bf16[128,512]{1,0:T(8,128)(2,1)S(1)} collective-permute-done((bf16[128,512]{1,0:T(8,128)(2,1)S(1)}, bf16[128,512]{1,0:T(8,128)(2,1)S(1)}, u32[]{:S(2)}, u32[]{:S(2)}) %collective-permute-start.14) | collective-permute-done | bytes 131104 | tf_op jit(solution)/shard_map/ppermute | solution.py:611
  71.2 2.8 %adapters.1 = (bf16[256,768]{1,0:T(8,128)(2,1)S(1)}, bf16[256,768]{1,0:T(8,128)(2,1)S(1)}) custom-call(s32[2]{0:T(128)S(1)} %pad_add_fusion.ids_ref.refs_12_, f32[512,768]{1,0:T(8,128)S(1)} %get-tuple-element.109.base_ref, f32[512,128]{1,0:T(8,128)S(1)} %get-tuple-element.89.cols_ref, bf16[2048,768]{1,0:T(8,128)(2,1)S(1)} %bitcast.6, ...), custom_call_target="tpu_custom_call" | custom-call | flops 1 | bytes 1 | tf_op jit(solution)/shard_map/adapters/pallas_call | solution.py:492
  74.0 4.6 %collective-permute-done.13 = bf16[128,768]{1,0:T(8,128)(2,1)S(1)} collective-permute-done((bf16[128,768]{1,0:T(8,128)(2,1)S(1)}, bf16[128,768]{1,0:T(8,128)(2,1)S(1)}, u32[]{:S(2)}, u32[]{:S(2)}) %collective-permute-start.13) | collective-permute-done | bytes 196640 | tf_op jit(solution)/shard_map/ppermute | solution.py:575
  78.6 1.7 %collective-permute-done.15.came_ref = bf16[256,768]{1,0:T(8,128)(2,1)S(1)} collective-permute-done((bf16[256,768]{1,0:T(8,128)(2,1)S(1)}, bf16[256,768]{1,0:T(8,128)(2,1)S(1)}, u32[]{:S(2)}, u32[]{:S(2)}) %collective-permute-start.15) | collective-permute-done | bytes 393248 | tf_op jit(solution)/shard_map/ppermute | solution.py:569
  80.3 0.1 sum_and_split.5
  80.4 0.1 sum_and_cut.3
  80.5 0.1 collective-permute-start.17
  80.6 3.8 %collective-permute-start.18 = (bf16[128,768]{1,0:T(8,128)(2,1)S(1)}, bf16[128,768]{1,0:T(8,128)(2,1)S(1)}, u32[]{:S(2)}, u32[]{:S(2)}) collective-permute-start(bf16[128,768]{1,0:T(8,128)(2,1)S(1)} %get-tuple-element.124), channel_id=1, source_target_pairs={{0,3},{1,0},{2,1},{3,2},{4,7},{5,4},{6,5},{7,6},{8,11},{9,8},{10,9... | collective-permute-start | bytes 589832 | tf_op jit(solution)/shard_map/ppermute | solution.py:575
  84.4 1.5 %collective-permute-start.16 = (bf16[128,768]{1,0:T(8,128)(2,1)S(1)}, bf16[128,768]{1,0:T(8,128)(2,1)S(1)}, u32[]{:S(2)}, u32[]{:S(2)}) collective-permute-start(bf16[128,768]{1,0:T(8,128)(2,1)S(1)} %get-tuple-element.119), channel_id=1, source_target_pairs={{0,8},{4,12},{8,0},{12,4},{1,9},{5,13},{9,1},{13,5},{2,10},{6,14},... | collective-permute-start | bytes 589832 | tf_op jit(solution)/shard_map/ppermute | solution.py:569
  85.9 4.3 %collective-permute-done.17 = bf16[128,768]{1,0:T(8,128)(2,1)S(1)} collective-permute-done((bf16[128,768]{1,0:T(8,128)(2,1)S(1)}, bf16[128,768]{1,0:T(8,128)(2,1)S(1)}, u32[]{:S(2)}, u32[]{:S(2)}) %collective-permute-start.17) | collective-permute-done | bytes 196640 | tf_op jit(solution)/shard_map/ppermute | solution.py:575
  90.1 1.6 %collective-permute-done.18 = bf16[128,768]{1,0:T(8,128)(2,1)S(1)} collective-permute-done((bf16[128,768]{1,0:T(8,128)(2,1)S(1)}, bf16[128,768]{1,0:T(8,128)(2,1)S(1)}, u32[]{:S(2)}, u32[]{:S(2)}) %collective-permute-start.18) | collective-permute-done | bytes 196640 | tf_op jit(solution)/shard_map/ppermute | solution.py:575
  91.8 0.8 add_convert_fusion
  (19 shorter events, 0.1 us)
Async XLA Ops:
  1.2 14.1 %collective-permute-start.3 = (bf16[128,1664]{1,0:T(8,128)(2,1)S(1)}, bf16[128,1664]{1,0:T(8,128)(2,1)S(1)}, u32[]{:S(2)}, u32[]{:S(2)}) collective-permute-start(bf16[128,1664]{1,0:T(8,128)(2,1)S(1)} %get-tuple-element.66.refs_0_), channel_id=1, source_target_pairs={{0,8},{4,12},{8,0},{12,4},{1,9},{5,13},{9,1},{13,5},{2,10},{6,14},... | collective-permute-start | bytes 1277960 | tf_op jit(solution)/shard_map/ppermute | solution.py:569
  4.2 11.9 %collective-permute-start.2 = (bf16[128,1664]{1,0:T(8,128)(2,1)S(1)}, bf16[128,1664]{1,0:T(8,128)(2,1)S(1)}, u32[]{:S(2)}, u32[]{:S(2)}) collective-permute-start(bf16[128,1664]{1,0:T(8,128)(2,1)S(1)} %get-tuple-element.66.refs_0_), channel_id=1, source_target_pairs={{0,4},{4,0},{8,12},{12,8},{1,5},{5,1},{9,13},{13,9},{2,6},{6,2},{1... | collective-permute-start | bytes 1277960 | tf_op jit(solution)/shard_map/ppermute | solution.py:569
  4.3 0.7 copy-start.1
  5.0 0.7 copy-start.3
  5.6 11.7 %copy-start.2 = (s32[16]{0:T(128)S(1)}, s32[16]{0:T(128)}, u32[]{:S(2)}) copy-start(s32[16]{0:T(128)} %adapter_ref.3) | copy-start | bytes 196
  5.6 11.7 %copy-start.4 = (s32[64]{0:T(128)S(1)}, s32[64]{0:T(128)}, u32[]{:S(2)}) copy-start(s32[64]{0:T(128)} %pool_slot_ref.3) | copy-start | bytes 772
  15.4 2.0 %collective-permute-start.4 = (bf16[128,1664]{1,0:T(8,128)(2,1)S(1)}, bf16[128,1664]{1,0:T(8,128)(2,1)S(1)}, u32[]{:S(2)}, u32[]{:S(2)}) collective-permute-start(bf16[128,1664]{1,0:T(8,128)(2,1)S(1)} %collective-permute-done.3.refs_2_), channel_id=1, source_target_pairs={{0,4},{4,0},{8,12},{12,8},{1,5},{5,1},{9,13},{13,9},{2,6},{6,2},{1... | collective-permute-start | bytes 1277960 | tf_op jit(solution)/shard_map/ppermute | solution.py:569
  15.9 11.1 %collective-permute-start.1 = (bf16[128,1536]{1,0:T(8,128)(2,1)S(1)}, bf16[128,1536]{1,0:T(8,128)(2,1)S(1)}, u32[]{:S(2)}, u32[]{:S(2)}) collective-permute-start(bf16[128,1536]{1,0:T(8,128)(2,1)S(1)} %get-tuple-element.65.refs_0_), channel_id=1, source_target_pairs={{0,8},{4,12},{8,0},{12,4},{1,9},{5,13},{9,1},{13,5},{2,10},{6,14},... | collective-permute-start | bytes 1179656 | tf_op jit(solution)/shard_map/ppermute | solution.py:569
  16.0 11.0 %collective-permute-start = (bf16[128,1536]{1,0:T(8,128)(2,1)S(1)}, bf16[128,1536]{1,0:T(8,128)(2,1)S(1)}, u32[]{:S(2)}, u32[]{:S(2)}) collective-permute-start(bf16[128,1536]{1,0:T(8,128)(2,1)S(1)} %get-tuple-element.65.refs_0_), channel_id=1, source_target_pairs={{0,4},{4,0},{8,12},{12,8},{1,5},{5,1},{9,13},{13,9},{2,6},{6,2},{1... | collective-permute-start | bytes 1179656 | tf_op jit(solution)/shard_map/ppermute | solution.py:569
  27.0 1.7 %collective-permute-start.5 = (bf16[128,1536]{1,0:T(8,128)(2,1)S(1)}, bf16[128,1536]{1,0:T(8,128)(2,1)S(1)}, u32[]{:S(2)}, u32[]{:S(2)}) collective-permute-start(bf16[128,1536]{1,0:T(8,128)(2,1)S(1)} %collective-permute-done.1.refs_2_), channel_id=1, source_target_pairs={{0,4},{4,0},{8,12},{12,8},{1,5},{5,1},{9,13},{13,9},{2,6},{6,2},{1... | collective-permute-start | bytes 1179656 | tf_op jit(solution)/shard_map/ppermute | solution.py:569
  42.5 6.9 %collective-permute-start.6 = (bf16[32,512]{1,0:T(8,128)(2,1)S(1)}, bf16[32,512]{1,0:T(8,128)(2,1)S(1)}, u32[]{:S(2)}, u32[]{:S(2)}) collective-permute-start(bf16[32,512]{1,0:T(8,128)(2,1)S(1)} %get-tuple-element.85), channel_id=1, source_target_pairs={{0,2},{1,3},{2,0},{3,1},{4,6},{5,7},{6,4},{7,5},{8,10},{9,11},{10,... | collective-permute-start | bytes 98312 | tf_op jit(solution)/shard_map/ppermute | solution.py:611
  49.4 1.8 %collective-permute-start.7 = (bf16[256,768]{1,0:T(8,128)(2,1)S(1)}, bf16[256,768]{1,0:T(8,128)(2,1)S(1)}, u32[]{:S(2)}, u32[]{:S(2)}) collective-permute-start(bf16[256,768]{1,0:T(8,128)(2,1)S(1)} %get-tuple-element.94), channel_id=1, source_target_pairs={{0,4},{4,0},{8,12},{12,8},{1,5},{5,1},{9,13},{13,9},{2,6},{6,2},{1... | collective-permute-start | bytes 1179656 | tf_op jit(solution)/shard_map/ppermute | solution.py:569
  49.5 2.4 %collective-permute-start.9 = (bf16[32,512]{1,0:T(8,128)(2,1)S(1)}, bf16[32,512]{1,0:T(8,128)(2,1)S(1)}, u32[]{:S(2)}, u32[]{:S(2)}) collective-permute-start(bf16[32,512]{1,0:T(8,128)(2,1)S(1)} %add_convert_fusion.2), channel_id=1, source_target_pairs={{0,4},{4,0},{8,12},{12,8},{1,5},{5,1},{9,13},{13,9},{2,6},{6,2},{1... | collective-permute-start | bytes 98312 | tf_op jit(solution)/shard_map/ppermute | solution.py:569
  51.3 10.9 %collective-permute-start.8 = (bf16[128,768]{1,0:T(8,128)(2,1)S(1)}, bf16[128,768]{1,0:T(8,128)(2,1)S(1)}, u32[]{:S(2)}, u32[]{:S(2)}) collective-permute-start(bf16[128,768]{1,0:T(8,128)(2,1)S(1)} %get-tuple-element.95), channel_id=1, source_target_pairs={{0,8},{4,12},{8,0},{12,4},{1,9},{5,13},{9,1},{13,5},{2,10},{6,14},... | collective-permute-start | bytes 589832 | tf_op jit(solution)/shard_map/ppermute | solution.py:569
  51.9 10.3 %collective-permute-start.10 = (bf16[64,512]{1,0:T(8,128)(2,1)S(1)}, bf16[64,512]{1,0:T(8,128)(2,1)S(1)}, u32[]{:S(2)}, u32[]{:S(2)}) collective-permute-start(bf16[64,512]{1,0:T(8,128)(2,1)S(1)} %pad_maximum_fusion.1), channel_id=1, source_target_pairs={{0,8},{4,12},{8,0},{12,4},{1,9},{5,13},{9,1},{13,5},{2,10},{6,14},... | collective-permute-start | bytes 196616 | tf_op jit(solution)/shard_map/ppermute | solution.py:569
  53.5 17.7 %copy-start = (bf16[16,8,16,768]{3,2,1,0:T(8,128)(2,1)S(1)}, bf16[16,8,16,768]{3,2,1,0:T(8,128)(2,1)}, u32[]{:S(2)}) copy-start(bf16[16,8,16,768]{3,2,1,0:T(8,128)(2,1)} %param.21) | copy-start | bytes 9437188
  62.2 2.4 %collective-permute-start.11 = (bf16[256,1536]{1,0:T(8,128)(2,1)S(1)}, bf16[256,1536]{1,0:T(8,128)(2,1)S(1)}, u32[]{:S(2)}, u32[]{:S(2)}) collective-permute-start(bf16[256,1536]{1,0:T(8,128)(2,1)S(1)} %get-tuple-element.105), channel_id=1, source_target_pairs={{0,4},{4,0},{8,12},{12,8},{1,5},{5,1},{9,13},{13,9},{2,6},{6,2},{1... | collective-permute-start | bytes 2359304 | tf_op jit(solution)/shard_map/ppermute | solution.py:569
  64.8 13.8 %collective-permute-start.12 = (bf16[128,1536]{1,0:T(8,128)(2,1)S(1)}, bf16[128,1536]{1,0:T(8,128)(2,1)S(1)}, u32[]{:S(2)}, u32[]{:S(2)}) collective-permute-start(bf16[128,1536]{1,0:T(8,128)(2,1)S(1)} %get-tuple-element.106), channel_id=1, source_target_pairs={{0,8},{4,12},{8,0},{12,4},{1,9},{5,13},{9,1},{13,5},{2,10},{6,14},... | collective-permute-start | bytes 1179656 | tf_op jit(solution)/shard_map/ppermute | solution.py:569
  65.4 5.8 %collective-permute-start.14 = (bf16[128,512]{1,0:T(8,128)(2,1)S(1)}, bf16[128,512]{1,0:T(8,128)(2,1)S(1)}, u32[]{:S(2)}, u32[]{:S(2)}) collective-permute-start(bf16[128,512]{1,0:T(8,128)(2,1)S(1)} %pad_maximum_fusion), channel_id=1, source_target_pairs={{0,1},{1,0},{2,3},{3,2},{4,5},{5,4},{6,7},{7,6},{8,9},{9,8},{10,11... | collective-permute-start | bytes 393224 | tf_op jit(solution)/shard_map/ppermute | solution.py:611
  67.1 11.5 %collective-permute-start.13 = (bf16[128,768]{1,0:T(8,128)(2,1)S(1)}, bf16[128,768]{1,0:T(8,128)(2,1)S(1)}, u32[]{:S(2)}, u32[]{:S(2)}) collective-permute-start(bf16[128,768]{1,0:T(8,128)(2,1)S(1)} %sum_and_cut.2), channel_id=1, source_target_pairs={{0,2},{1,3},{2,0},{3,1},{4,6},{5,7},{6,4},{7,5},{8,10},{9,11},{10,... | collective-permute-start | bytes 589832 | tf_op jit(solution)/shard_map/ppermute | solution.py:575
  78.6 1.7 %collective-permute-start.15 = (bf16[256,768]{1,0:T(8,128)(2,1)S(1)}, bf16[256,768]{1,0:T(8,128)(2,1)S(1)}, u32[]{:S(2)}, u32[]{:S(2)}) collective-permute-start(bf16[256,768]{1,0:T(8,128)(2,1)S(1)} %get-tuple-element.115), channel_id=1, source_target_pairs={{0,4},{4,0},{8,12},{12,8},{1,5},{5,1},{9,13},{13,9},{2,6},{6,2},{1... | collective-permute-start | bytes 1179656 | tf_op jit(solution)/shard_map/ppermute | solution.py:569
  80.5 9.6 %collective-permute-start.17 = (bf16[128,768]{1,0:T(8,128)(2,1)S(1)}, bf16[128,768]{1,0:T(8,128)(2,1)S(1)}, u32[]{:S(2)}, u32[]{:S(2)}) collective-permute-start(bf16[128,768]{1,0:T(8,128)(2,1)S(1)} %get-tuple-element.123), channel_id=1, source_target_pairs={{0,1},{1,2},{2,3},{3,0},{4,5},{5,6},{6,7},{7,4},{8,9},{9,10},{10,1... | collective-permute-start | bytes 589832 | tf_op jit(solution)/shard_map/ppermute | solution.py:575
  80.6 11.2 %collective-permute-start.18 = (bf16[128,768]{1,0:T(8,128)(2,1)S(1)}, bf16[128,768]{1,0:T(8,128)(2,1)S(1)}, u32[]{:S(2)}, u32[]{:S(2)}) collective-permute-start(bf16[128,768]{1,0:T(8,128)(2,1)S(1)} %get-tuple-element.124), channel_id=1, source_target_pairs={{0,3},{1,0},{2,1},{3,2},{4,7},{5,4},{6,5},{7,6},{8,11},{9,8},{10,9... | collective-permute-start | bytes 589832 | tf_op jit(solution)/shard_map/ppermute | solution.py:575
  84.4 7.4 %collective-permute-start.16 = (bf16[128,768]{1,0:T(8,128)(2,1)S(1)}, bf16[128,768]{1,0:T(8,128)(2,1)S(1)}, u32[]{:S(2)}, u32[]{:S(2)}) collective-permute-start(bf16[128,768]{1,0:T(8,128)(2,1)S(1)} %get-tuple-element.119), channel_id=1, source_target_pairs={{0,8},{4,12},{8,0},{12,4},{1,9},{5,13},{9,1},{13,5},{2,10},{6,14},... | collective-permute-start | bytes 589832 | tf_op jit(solution)/shard_map/ppermute | solution.py:569

commit v11 on v9

--- a/solution.py
+++ b/solution.py
@@ -570,7 +570,7 @@
     def shift(x, step):
         return lax.ppermute(x, "ad", [(i, (i + step) % n_ad) for i in range(n_ad)])
 
-    order = sorted(range(1, n_ad), key=lambda step: (step != n_ad // 2, step))
+    order = list(range(1, n_ad))
     token_part = token_parts_of(tokens, chosen_experts, router_gate_logits, token_tenant)
     *slabs, factors, mark = prefetch(
         ids, adapter_of_tenant, adapter_pool_slot, gate_weight, up_weight, adapter_input_factors, width // 2

time: 92 us -> 92 us (level); the launches traced: 91.8 us -> 90.9 us
  starting transfers between devices: 17.7 us -> 16.6 us
where the time goes in v11:
time: 92 us; the launch traced here: 90.9 us
  Pallas kernels  48.7 us (53%)
  waiting for transfers between devices  23.2 us (25%)
  starting transfers between devices  16.6 us (18%)
  local copies, waits for them, and re-layouts  1.32 us (1%)
  other arithmetic  0.94 us (1%)
    pallas_call x1, Pallas kernels, second_part(): pl.pallas_call(functools.partial(second_kernel, len(blocks), len(ahead),...  13.1 us
    ppermute x3, waiting for transfers between devices, shift(): return lax.ppermute(x, 'ad', [(i, (i + step) % n_ad) for i in range(n_ad)])  9.97 us
    ppermute x14, waiting for transfers between devices, swap(): return lax.ppermute(x, 'ep', [(i, i ^ mask) for i in range(n_ep)])  9.9 us
    pallas_call x1, Pallas kernels, prefetch(): pl.pallas_call(prefetch_kernel, out_shape=(pltpu.VMEM((each, part_width,...  9.61 us
    pallas_call x1, Pallas kernels, down_rest(): pl.pallas_call(functools.partial(down_rest_kernel, len(weights), n_ad, st...  8.69 us
    ppermute x14, starting transfers between devices, swap(): return lax.ppermute(x, 'ep', [(i, i ^ mask) for i in range(n_ep)])  7.77 us
    pallas_call x1, Pallas kernels, first_part(): pl.pallas_call(functools.partial(first_kernel, len(blocks), local_halves)...  7.43 us
    ppermute x3, starting transfers between devices, shift(): return lax.ppermute(x, 'ad', [(i, (i + step) % n_ad) for i in range(n_ad)])  4.5 us
  transfers between devices with their start and end apart: 19, of which 10 were waited for; matrix products, arithmetic and copies ran while one was open for 0% of the time, Pallas kernels for 37%

profile of v11, /device:TPU:0, one launch (start us, length us, event | category | flops | bytes accessed | tf_op | source)
XLA Modules:
  0.0 90.9 jit_solution(6358571411020187659)
XLA Ops:
  0.0 1.2 %token_parts.1 = (bf16[128,1664]{1,0:T(8,128)(2,1)S(1)}, bf16[128,1536]{1,0:T(8,128)(2,1)S(1)}) custom-call(bf16[128,3072]{1,0:T(8,128)(2,1)} %tokens_ref.1, s32[2,128]{1,0:T(2,128)} %bitcast.7, f32[2,128]{1,0:T(2,128)} %bitcast.8, s32[1,128]{1,0:T(1,128)} %bitcast.9), custom_call_target="tpu_custom_call" | custom-call | flops 1 | bytes 1 | tf_op jit(solution)/shard_map/token_parts/pallas_call | solution.py:91
  1.2 3.0 %collective-permute-start.3 = (bf16[128,1664]{1,0:T(8,128)(2,1)S(1)}, bf16[128,1664]{1,0:T(8,128)(2,1)S(1)}, u32[]{:S(2)}, u32[]{:S(2)}) collective-permute-start(bf16[128,1664]{1,0:T(8,128)(2,1)S(1)} %get-tuple-element.66.refs_0_), channel_id=1, source_target_pairs={{0,8},{4,12},{8,0},{12,4},{1,9},{5,13},{9,1},{13,5},{2,10},{6,14},... | collective-permute-start | bytes 1277960 | tf_op jit(solution)/shard_map/ppermute | solution.py:565
  4.2 0.0 collective-permute-start.2
  4.2 0.1 pad_add_fusion.ids_ref.refs_12_
  4.3 0.7 copy-done.1
  5.0 0.7 copy-done.3
  5.6 9.6 %weight_prefetch.1 = (bf16[4,1536,512]{2,1,0:T(8,128)(2,1)S(1)}, bf16[4,1536,512]{2,1,0:T(8,128)(2,1)S(1)}, bf16[4,1536,512]{2,1,0:T(8,128)(2,1)S(1)}, bf16[4,15...) custom-call(s32[2]{0:T(128)S(1)} %pad_add_fusion.ids_ref.refs_12_, ...), custom_call_target="tpu_custom_call" | custom-call | flops 1 | bytes 1 | tf_op jit(solution)/shard_map/weight_prefetch/pallas_call | solution.py:205
  15.2 0.6 collective-permute-start.4
  15.8 0.1 collective-permute-start.1
  15.9 0.1 collective-permute-start
  16.0 0.0 collective-permute-done.2.refs_1_
  16.0 1.2 %collective-permute-done.4.refs_3_ = bf16[128,1664]{1,0:T(8,128)(2,1)S(1)} collective-permute-done((bf16[128,1664]{1,0:T(8,128)(2,1)S(1)}, bf16[128,1664]{1,0:T(8,128)(2,1)S(1)}, u32[]{:S(2)}, u32[]{:S(2)}) %collective-permute-start.4) | collective-permute-done | bytes 426016 | tf_op jit(solution)/shard_map/ppermute | solution.py:565
  17.2 1.1 %routing_tables.1 = (bf16[2,192,512]{2,1,0:T(8,128)(2,1)S(1)}, bf16[2,512,192]{2,1,0:T(8,128)(2,1)S(1)}, f32[512,128]{1,0:T(8,128)S(1)}, f32[8,512]{1,0:T(8,128)S(1)}, f32[2,8,192]{2,1,0:T(8,128)S(1)}) custom-call(s32[2]{0:T(128)S(1)} %pad_add_fusion.ids_ref.refs_12_, s32[16]{0:T(128)S(1)} %copy-done.2, s32[64]{0:T(128)S(1)} %copy-done.4, ...), custom_call_target="tpu_custom_call" | custom-call | flops 1 | bytes 1 | tf_op jit(solution)/shard_map/routing_tables/pallas_call | solution.py:159
  18.3 7.4 %gate_up_first.1 = (bf16[4,1536,512]{2,1,0:T(8,128)(2,1)S(1)}, bf16[4,1536,512]{2,1,0:T(8,128)(2,1)S(1)}, f32[4,192,1024]{2,1,0:T(8,128)S(1)}, f32[4,192,1024]{2,1,0:T(8,128)S(1)}, f32[8,128]{1,0:T(8,128)S(1)}) custom-call(bf16[128,1664]{1,0:T(8,128)(2,1)S(1)} %get-tuple-element.66.refs_0_, ...), custom_call_target="tpu_custom_call", output_to_operand_aliasing={{0}: (8, {}), {1}: (9, {})} | custom-call | flops 1 | bytes 1 | tf_op jit(solution)/shard_map/gate_up_first/pallas_call | solution.py:275
  25.7 1.2 %collective-permute-done.1.refs_2_ = bf16[128,1536]{1,0:T(8,128)(2,1)S(1)} collective-permute-done((bf16[128,1536]{1,0:T(8,128)(2,1)S(1)}, bf16[128,1536]{1,0:T(8,128)(2,1)S(1)}, u32[]{:S(2)}, u32[]{:S(2)}) %collective-permute-start.1) | collective-permute-done | bytes 393248 | tf_op jit(solution)/shard_map/ppermute | solution.py:565
  26.9 1.7 %collective-permute-done.5.refs_3_ = bf16[128,1536]{1,0:T(8,128)(2,1)S(1)} collective-permute-done((bf16[128,1536]{1,0:T(8,128)(2,1)S(1)}, bf16[128,1536]{1,0:T(8,128)(2,1)S(1)}, u32[]{:S(2)}, u32[]{:S(2)}) %collective-permute-start.5) | collective-permute-done | bytes 393248 | tf_op jit(solution)/shard_map/ppermute | solution.py:565
  28.6 13.1 %gate_up_second.1 = (bf16[4,192,1024]{2,1,0:T(8,128)(2,1)S(1)}, bf16[32,512]{1,0:T(8,128)(2,1)S(1)}, bf16[4,1024,768]{2,1,0:T(8,128)(2,1)S(1)}, bf16[2,1024,768]{2,1,0:T(8,128)(2,1)S(1)}) custom-call(bf16[128,1536]{1,0:T(8,128)(2,1)S(1)} %get-tuple-element.65.refs_0_, bf16[128,1536]{1,0:T(8,128)(2,1)S(1)} %collective-permute-done.refs_1_, ...), custom_call_target="tpu_custom_call" | custom-call | flops 1 | bytes 1 | tf_op jit(solution)/shard_map/gate_up_second/pallas_call | solution.py:354
  41.8 2.6 %collective-permute-start.6 = (bf16[32,512]{1,0:T(8,128)(2,1)S(1)}, bf16[32,512]{1,0:T(8,128)(2,1)S(1)}, u32[]{:S(2)}, u32[]{:S(2)}) collective-permute-start(bf16[32,512]{1,0:T(8,128)(2,1)S(1)} %get-tuple-element.85), channel_id=1, source_target_pairs={{0,2},{1,3},{2,0},{3,1},{4,6},{5,7},{6,4},{7,5},{8,10},{9,11},{10,... | collective-permute-start | bytes 98312 | tf_op jit(solution)/shard_map/ppermute | solution.py:607
  44.4 4.3 %down_first.1 = (bf16[256,768]{1,0:T(8,128)(2,1)S(1)}, bf16[256,768]{1,0:T(8,128)(2,1)S(1)}, bf16[2,1024,768]{2,1,0:T(8,128)(2,1)S(1)}) custom-call(s32[2]{0:T(128)S(1)} %pad_add_fusion.ids_ref.refs_12_, bf16[4,192,1024]{2,1,0:T(8,128)(2,1)S(1)} %get-tuple-element.98.hidden_ref, bf16[4,1024,768]{2,1,0:T(8,128)(2,1)S(1)} %get-tuple-element.87.weight_ref, ...), custom_call_target="tpu_custom_call" | custom-call | flops 1 | bytes 1 | tf_op jit(solution)/shard_map/down_first/pallas_call | solution.py:405
  48.7 0.1 collective-permute-start.7
  48.8 0.6 collective-permute-start.9
  49.3 1.1 %collective-permute-done.7.came_ref = bf16[256,768]{1,0:T(8,128)(2,1)S(1)} collective-permute-done((bf16[256,768]{1,0:T(8,128)(2,1)S(1)}, bf16[256,768]{1,0:T(8,128)(2,1)S(1)}, u32[]{:S(2)}, u32[]{:S(2)}) %collective-permute-start.7) | collective-permute-done | bytes 393248 | tf_op jit(solution)/shard_map/ppermute | solution.py:565
  50.5 0.1 sum_and_split.3
  50.6 0.6 collective-permute-start.8
  51.2 1.6 %collective-permute-start.10 = (bf16[64,512]{1,0:T(8,128)(2,1)S(1)}, bf16[64,512]{1,0:T(8,128)(2,1)S(1)}, u32[]{:S(2)}, u32[]{:S(2)}) collective-permute-start(bf16[64,512]{1,0:T(8,128)(2,1)S(1)} %pad_maximum_fusion.1), channel_id=1, source_target_pairs={{0,8},{4,12},{8,0},{12,4},{1,9},{5,13},{9,1},{13,5},{2,10},{6,14},... | collective-permute-start | bytes 196616 | tf_op jit(solution)/shard_map/ppermute | solution.py:565
  52.7 8.7 %down_rest.1 = (bf16[256,1536]{1,0:T(8,128)(2,1)S(1)}, bf16[256,1536]{1,0:T(8,128)(2,1)S(1)}, f32[512,768]{1,0:T(8,128)S(1)}) custom-call(s32[2]{0:T(128)S(1)} %pad_add_fusion.ids_ref.refs_12_, bf16[4,192,1024]{2,1,0:T(8,128)(2,1)S(1)} %get-tuple-element.98.hidden_ref, bf16[2,512,192]{2,1,0:T(8,128)(2,1)S(1)} %get-tuple-element.88.pt_ref, ...), custom_call_target="tpu_custom_call" | custom-call | flops 1 | bytes 1 | tf_op jit(solution)/shard_map/down_rest/pallas_call | solution.py:442
  61.4 0.0 collective-permute-done.10
  61.5 0.1 collective-permute-start.11
  61.5 2.3 %collective-permute-done.11.came_ref = bf16[256,1536]{1,0:T(8,128)(2,1)S(1)} collective-permute-done((bf16[256,1536]{1,0:T(8,128)(2,1)S(1)}, bf16[256,1536]{1,0:T(8,128)(2,1)S(1)}, u32[]{:S(2)}, u32[]{:S(2)}) %collective-permute-start.11) | collective-permute-done | bytes 786464 | tf_op jit(solution)/shard_map/ppermute | solution.py:565
  63.8 0.2 sum_and_split.4
  64.0 0.6 collective-permute-start.12
  64.6 1.7 %collective-permute-start.14 = (bf16[128,512]{1,0:T(8,128)(2,1)S(1)}, bf16[128,512]{1,0:T(8,128)(2,1)S(1)}, u32[]{:S(2)}, u32[]{:S(2)}) collective-permute-start(bf16[128,512]{1,0:T(8,128)(2,1)S(1)} %pad_maximum_fusion), channel_id=1, source_target_pairs={{0,1},{1,0},{2,3},{3,2},{4,5},{5,4},{6,7},{7,6},{8,9},{9,8},{10,11... | collective-permute-start | bytes 393224 | tf_op jit(solution)/shard_map/ppermute | solution.py:607
  66.3 0.5 collective-permute-start.13
  66.8 3.4 %collective-permute-done.14 = bf16[128,512]{1,0:T(8,128)(2,1)S(1)} collective-permute-done((bf16[128,512]{1,0:T(8,128)(2,1)S(1)}, bf16[128,512]{1,0:T(8,128)(2,1)S(1)}, u32[]{:S(2)}, u32[]{:S(2)}) %collective-permute-start.14) | collective-permute-done | bytes 131104 | tf_op jit(solution)/shard_map/ppermute | solution.py:607
  70.2 2.8 %adapters.1 = (bf16[256,768]{1,0:T(8,128)(2,1)S(1)}, bf16[256,768]{1,0:T(8,128)(2,1)S(1)}) custom-call(s32[2]{0:T(128)S(1)} %pad_add_fusion.ids_ref.refs_12_, f32[512,768]{1,0:T(8,128)S(1)} %get-tuple-element.109.base_ref, f32[512,128]{1,0:T(8,128)S(1)} %get-tuple-element.89.cols_ref, bf16[2048,768]{1,0:T(8,128)(2,1)S(1)} %bitcast.6, ...), custom_call_target="tpu_custom_call" | custom-call | flops 1 | bytes 1 | tf_op jit(solution)/shard_map/adapters/pallas_call | solution.py:488
  73.0 1.5 %collective-permute-done.13 = bf16[128,768]{1,0:T(8,128)(2,1)S(1)} collective-permute-done((bf16[128,768]{1,0:T(8,128)(2,1)S(1)}, bf16[128,768]{1,0:T(8,128)(2,1)S(1)}, u32[]{:S(2)}, u32[]{:S(2)}) %collective-permute-start.13) | collective-permute-done | bytes 196640 | tf_op jit(solution)/shard_map/ppermute | solution.py:571
  74.5 0.7 collective-permute-done.12.came_ref
  75.2 0.0 collective-permute-start.15
  75.2 1.7 %collective-permute-done.15.came_ref = bf16[256,768]{1,0:T(8,128)(2,1)S(1)} collective-permute-done((bf16[256,768]{1,0:T(8,128)(2,1)S(1)}, bf16[256,768]{1,0:T(8,128)(2,1)S(1)}, u32[]{:S(2)}, u32[]{:S(2)}) %collective-permute-start.15) | collective-permute-done | bytes 393248 | tf_op jit(solution)/shard_map/ppermute | solution.py:565
  76.9 0.1 sum_and_split.5
  77.0 0.1 sum_and_cut.3
  77.1 0.6 collective-permute-start.17
  77.7 3.4 %collective-permute-start.18 = (bf16[128,768]{1,0:T(8,128)(2,1)S(1)}, bf16[128,768]{1,0:T(8,128)(2,1)S(1)}, u32[]{:S(2)}, u32[]{:S(2)}) collective-permute-start(bf16[128,768]{1,0:T(8,128)(2,1)S(1)} %get-tuple-element.124), channel_id=1, source_target_pairs={{0,3},{1,0},{2,1},{3,2},{4,7},{5,4},{6,5},{7,6},{8,11},{9,8},{10,9... | collective-permute-start | bytes 589832 | tf_op jit(solution)/shard_map/ppermute | solution.py:571
  81.1 0.5 collective-permute-start.16
  81.7 8.4 %collective-permute-done.17 = bf16[128,768]{1,0:T(8,128)(2,1)S(1)} collective-permute-done((bf16[128,768]{1,0:T(8,128)(2,1)S(1)}, bf16[128,768]{1,0:T(8,128)(2,1)S(1)}, u32[]{:S(2)}, u32[]{:S(2)}) %collective-permute-start.17) | collective-permute-done | bytes 196640 | tf_op jit(solution)/shard_map/ppermute | solution.py:571
  90.1 0.0 collective-permute-done.18
  90.1 0.0 collective-permute-done.16
  90.1 0.8 add_convert_fusion
  (19 shorter events, 0.1 us)
Async XLA Ops:
  1.2 14.0 %collective-permute-start.3 = (bf16[128,1664]{1,0:T(8,128)(2,1)S(1)}, bf16[128,1664]{1,0:T(8,128)(2,1)S(1)}, u32[]{:S(2)}, u32[]{:S(2)}) collective-permute-start(bf16[128,1664]{1,0:T(8,128)(2,1)S(1)} %get-tuple-element.66.refs_0_), channel_id=1, source_target_pairs={{0,8},{4,12},{8,0},{12,4},{1,9},{5,13},{9,1},{13,5},{2,10},{6,14},... | collective-permute-start | bytes 1277960 | tf_op jit(solution)/shard_map/ppermute | solution.py:565
  4.2 11.8 %collective-permute-start.2 = (bf16[128,1664]{1,0:T(8,128)(2,1)S(1)}, bf16[128,1664]{1,0:T(8,128)(2,1)S(1)}, u32[]{:S(2)}, u32[]{:S(2)}) collective-permute-start(bf16[128,1664]{1,0:T(8,128)(2,1)S(1)} %get-tuple-element.66.refs_0_), channel_id=1, source_target_pairs={{0,4},{4,0},{8,12},{12,8},{1,5},{5,1},{9,13},{13,9},{2,6},{6,2},{1... | collective-permute-start | bytes 1277960 | tf_op jit(solution)/shard_map/ppermute | solution.py:565
  4.3 0.7 copy-start.1
  5.0 0.7 copy-start.3
  5.6 11.6 %copy-start.2 = (s32[16]{0:T(128)S(1)}, s32[16]{0:T(128)}, u32[]{:S(2)}) copy-start(s32[16]{0:T(128)} %adapter_ref.3) | copy-start | bytes 196
  5.6 11.6 %copy-start.4 = (s32[64]{0:T(128)S(1)}, s32[64]{0:T(128)}, u32[]{:S(2)}) copy-start(s32[64]{0:T(128)} %pool_slot_ref.3) | copy-start | bytes 772
  15.2 2.0 %collective-permute-start.4 = (bf16[128,1664]{1,0:T(8,128)(2,1)S(1)}, bf16[128,1664]{1,0:T(8,128)(2,1)S(1)}, u32[]{:S(2)}, u32[]{:S(2)}) collective-permute-start(bf16[128,1664]{1,0:T(8,128)(2,1)S(1)} %collective-permute-done.3.refs_2_), channel_id=1, source_target_pairs={{0,4},{4,0},{8,12},{12,8},{1,5},{5,1},{9,13},{13,9},{2,6},{6,2},{1... | collective-permute-start | bytes 1277960 | tf_op jit(solution)/shard_map/ppermute | solution.py:565
  15.8 11.1 %collective-permute-start.1 = (bf16[128,1536]{1,0:T(8,128)(2,1)S(1)}, bf16[128,1536]{1,0:T(8,128)(2,1)S(1)}, u32[]{:S(2)}, u32[]{:S(2)}) collective-permute-start(bf16[128,1536]{1,0:T(8,128)(2,1)S(1)} %get-tuple-element.65.refs_0_), channel_id=1, source_target_pairs={{0,8},{4,12},{8,0},{12,4},{1,9},{5,13},{9,1},{13,5},{2,10},{6,14},... | collective-permute-start | bytes 1179656 | tf_op jit(solution)/shard_map/ppermute | solution.py:565
  15.9 11.0 %collective-permute-start = (bf16[128,1536]{1,0:T(8,128)(2,1)S(1)}, bf16[128,1536]{1,0:T(8,128)(2,1)S(1)}, u32[]{:S(2)}, u32[]{:S(2)}) collective-permute-start(bf16[128,1536]{1,0:T(8,128)(2,1)S(1)} %get-tuple-element.65.refs_0_), channel_id=1, source_target_pairs={{0,4},{4,0},{8,12},{12,8},{1,5},{5,1},{9,13},{13,9},{2,6},{6,2},{1... | collective-permute-start | bytes 1179656 | tf_op jit(solution)/shard_map/ppermute | solution.py:565
  26.9 1.7 %collective-permute-start.5 = (bf16[128,1536]{1,0:T(8,128)(2,1)S(1)}, bf16[128,1536]{1,0:T(8,128)(2,1)S(1)}, u32[]{:S(2)}, u32[]{:S(2)}) collective-permute-start(bf16[128,1536]{1,0:T(8,128)(2,1)S(1)} %collective-permute-done.1.refs_2_), channel_id=1, source_target_pairs={{0,4},{4,0},{8,12},{12,8},{1,5},{5,1},{9,13},{13,9},{2,6},{6,2},{1... | collective-permute-start | bytes 1179656 | tf_op jit(solution)/shard_map/ppermute | solution.py:565
  41.8 6.9 %collective-permute-start.6 = (bf16[32,512]{1,0:T(8,128)(2,1)S(1)}, bf16[32,512]{1,0:T(8,128)(2,1)S(1)}, u32[]{:S(2)}, u32[]{:S(2)}) collective-permute-start(bf16[32,512]{1,0:T(8,128)(2,1)S(1)} %get-tuple-element.85), channel_id=1, source_target_pairs={{0,2},{1,3},{2,0},{3,1},{4,6},{5,7},{6,4},{7,5},{8,10},{9,11},{10,... | collective-permute-start | bytes 98312 | tf_op jit(solution)/shard_map/ppermute | solution.py:607
  48.7 1.8 %collective-permute-start.7 = (bf16[256,768]{1,0:T(8,128)(2,1)S(1)}, bf16[256,768]{1,0:T(8,128)(2,1)S(1)}, u32[]{:S(2)}, u32[]{:S(2)}) collective-permute-start(bf16[256,768]{1,0:T(8,128)(2,1)S(1)} %get-tuple-element.94), channel_id=1, source_target_pairs={{0,4},{4,0},{8,12},{12,8},{1,5},{5,1},{9,13},{13,9},{2,6},{6,2},{1... | collective-permute-start | bytes 1179656 | tf_op jit(solution)/shard_map/ppermute | solution.py:565
  48.8 2.4 %collective-permute-start.9 = (bf16[32,512]{1,0:T(8,128)(2,1)S(1)}, bf16[32,512]{1,0:T(8,128)(2,1)S(1)}, u32[]{:S(2)}, u32[]{:S(2)}) collective-permute-start(bf16[32,512]{1,0:T(8,128)(2,1)S(1)} %add_convert_fusion.2), channel_id=1, source_target_pairs={{0,4},{4,0},{8,12},{12,8},{1,5},{5,1},{9,13},{13,9},{2,6},{6,2},{1... | collective-permute-start | bytes 98312 | tf_op jit(solution)/shard_map/ppermute | solution.py:565
  50.6 10.9 %collective-permute-start.8 = (bf16[128,768]{1,0:T(8,128)(2,1)S(1)}, bf16[128,768]{1,0:T(8,128)(2,1)S(1)}, u32[]{:S(2)}, u32[]{:S(2)}) collective-permute-start(bf16[128,768]{1,0:T(8,128)(2,1)S(1)} %get-tuple-element.95), channel_id=1, source_target_pairs={{0,8},{4,12},{8,0},{12,4},{1,9},{5,13},{9,1},{13,5},{2,10},{6,14},... | collective-permute-start | bytes 589832 | tf_op jit(solution)/shard_map/ppermute | solution.py:565
  51.2 10.3 %collective-permute-start.10 = (bf16[64,512]{1,0:T(8,128)(2,1)S(1)}, bf16[64,512]{1,0:T(8,128)(2,1)S(1)}, u32[]{:S(2)}, u32[]{:S(2)}) collective-permute-start(bf16[64,512]{1,0:T(8,128)(2,1)S(1)} %pad_maximum_fusion.1), channel_id=1, source_target_pairs={{0,8},{4,12},{8,0},{12,4},{1,9},{5,13},{9,1},{13,5},{2,10},{6,14},... | collective-permute-start | bytes 196616 | tf_op jit(solution)/shard_map/ppermute | solution.py:565
  52.7 17.5 %copy-start = (bf16[16,8,16,768]{3,2,1,0:T(8,128)(2,1)S(1)}, bf16[16,8,16,768]{3,2,1,0:T(8,128)(2,1)}, u32[]{:S(2)}) copy-start(bf16[16,8,16,768]{3,2,1,0:T(8,128)(2,1)} %param.21) | copy-start | bytes 9437188
  61.5 2.4 %collective-permute-start.11 = (bf16[256,1536]{1,0:T(8,128)(2,1)S(1)}, bf16[256,1536]{1,0:T(8,128)(2,1)S(1)}, u32[]{:S(2)}, u32[]{:S(2)}) collective-permute-start(bf16[256,1536]{1,0:T(8,128)(2,1)S(1)} %get-tuple-element.105), channel_id=1, source_target_pairs={{0,4},{4,0},{8,12},{12,8},{1,5},{5,1},{9,13},{13,9},{2,6},{6,2},{1... | collective-permute-start | bytes 2359304 | tf_op jit(solution)/shard_map/ppermute | solution.py:565
  64.0 11.2 %collective-permute-start.12 = (bf16[128,1536]{1,0:T(8,128)(2,1)S(1)}, bf16[128,1536]{1,0:T(8,128)(2,1)S(1)}, u32[]{:S(2)}, u32[]{:S(2)}) collective-permute-start(bf16[128,1536]{1,0:T(8,128)(2,1)S(1)} %get-tuple-element.106), channel_id=1, source_target_pairs={{0,8},{4,12},{8,0},{12,4},{1,9},{5,13},{9,1},{13,5},{2,10},{6,14},... | collective-permute-start | bytes 1179656 | tf_op jit(solution)/shard_map/ppermute | solution.py:565
  64.6 5.6 %collective-permute-start.14 = (bf16[128,512]{1,0:T(8,128)(2,1)S(1)}, bf16[128,512]{1,0:T(8,128)(2,1)S(1)}, u32[]{:S(2)}, u32[]{:S(2)}) collective-permute-start(bf16[128,512]{1,0:T(8,128)(2,1)S(1)} %pad_maximum_fusion), channel_id=1, source_target_pairs={{0,1},{1,0},{2,3},{3,2},{4,5},{5,4},{6,7},{7,6},{8,9},{9,8},{10,11... | collective-permute-start | bytes 393224 | tf_op jit(solution)/shard_map/ppermute | solution.py:607
  66.3 8.2 %collective-permute-start.13 = (bf16[128,768]{1,0:T(8,128)(2,1)S(1)}, bf16[128,768]{1,0:T(8,128)(2,1)S(1)}, u32[]{:S(2)}, u32[]{:S(2)}) collective-permute-start(bf16[128,768]{1,0:T(8,128)(2,1)S(1)} %sum_and_cut.2), channel_id=1, source_target_pairs={{0,1},{1,2},{2,3},{3,0},{4,5},{5,6},{6,7},{7,4},{8,9},{9,10},{10,1... | collective-permute-start | bytes 589832 | tf_op jit(solution)/shard_map/ppermute | solution.py:571
  75.2 1.7 %collective-permute-start.15 = (bf16[256,768]{1,0:T(8,128)(2,1)S(1)}, bf16[256,768]{1,0:T(8,128)(2,1)S(1)}, u32[]{:S(2)}, u32[]{:S(2)}) collective-permute-start(bf16[256,768]{1,0:T(8,128)(2,1)S(1)} %get-tuple-element.115), channel_id=1, source_target_pairs={{0,4},{4,0},{8,12},{12,8},{1,5},{5,1},{9,13},{13,9},{2,6},{6,2},{1... | collective-permute-start | bytes 1179656 | tf_op jit(solution)/shard_map/ppermute | solution.py:565
  77.1 13.0 %collective-permute-start.17 = (bf16[128,768]{1,0:T(8,128)(2,1)S(1)}, bf16[128,768]{1,0:T(8,128)(2,1)S(1)}, u32[]{:S(2)}, u32[]{:S(2)}) collective-permute-start(bf16[128,768]{1,0:T(8,128)(2,1)S(1)} %get-tuple-element.123), channel_id=1, source_target_pairs={{0,2},{1,3},{2,0},{3,1},{4,6},{5,7},{6,4},{7,5},{8,10},{9,11},{10,... | collective-permute-start | bytes 589832 | tf_op jit(solution)/shard_map/ppermute | solution.py:571
  77.7 12.4 %collective-permute-start.18 = (bf16[128,768]{1,0:T(8,128)(2,1)S(1)}, bf16[128,768]{1,0:T(8,128)(2,1)S(1)}, u32[]{:S(2)}, u32[]{:S(2)}) collective-permute-start(bf16[128,768]{1,0:T(8,128)(2,1)S(1)} %get-tuple-element.124), channel_id=1, source_target_pairs={{0,3},{1,0},{2,1},{3,2},{4,7},{5,4},{6,5},{7,6},{8,11},{9,8},{10,9... | collective-permute-start | bytes 589832 | tf_op jit(solution)/shard_map/ppermute | solution.py:571
  81.1 9.0 %collective-permute-start.16 = (bf16[128,768]{1,0:T(8,128)(2,1)S(1)}, bf16[128,768]{1,0:T(8,128)(2,1)S(1)}, u32[]{:S(2)}, u32[]{:S(2)}) collective-permute-start(bf16[128,768]{1,0:T(8,128)(2,1)S(1)} %get-tuple-element.119), channel_id=1, source_target_pairs={{0,8},{4,12},{8,0},{12,4},{1,9},{5,13},{9,1},{13,5},{2,10},{6,14},... | collective-permute-start | bytes 589832 | tf_op jit(solution)/shard_map/ppermute | solution.py:565

commit v12 on v9

--- a/solution.py
+++ b/solution.py
@@ -182,14 +182,9 @@
     return copies
 
 
-def prefetch_kernel(ids_ref, adapter_ref, pool_slot_ref, gate_ref, up_ref, pool_ref, *refs):
-    slabs, (factors, mark_ref, sems, factor_sems) = refs[:-4], refs[-4:]
+def prefetch_kernel(ids_ref, gate_ref, up_ref, *refs):
+    slabs, (mark_ref, sems) = refs[:-2], refs[-2:]
     copies = [copy for half, slab in enumerate(slabs) for copy in slab_copies(gate_ref, up_ref, slab, sems, 0, half)]
-    rank = pool_ref.shape[2]
-    for number in range(adapter_ref.shape[0]):
-        source = pool_ref.at[pool_slot_ref[adapter_ref[number]]]
-        into = factors.at[:, number * rank : (number + 1) * rank]
-        copies.append(pltpu.make_async_copy(source, into, factor_sems.at[number]))
     for copy in copies:
         copy.start()
     mark_ref[...] = jnp.zeros_like(mark_ref)
@@ -197,22 +192,20 @@
         copy.wait()
 
 
-def prefetch(ids, adapters, pool_slots, gate, up, pool, part_width):
+def prefetch(ids, gate, up, part_width):
     local_halves, _, hidden_count = gate.shape
     tile = min(N_TILE, hidden_count)
     each = 2 * hidden_count // tile
-    tenants, rank = adapters.shape[0], pool.shape[2]
     return pl.pallas_call(
         prefetch_kernel,
-        out_shape=(pltpu.VMEM((each, part_width, tile), BF16),) * local_halves
-        + (pltpu.VMEM((local_halves, tenants * rank, hidden_count), BF16), jax.ShapeDtypeStruct((8, 128), F32)),
-        in_specs=[smem()] * 3 + [pl.BlockSpec(memory_space=pltpu.HBM)] * 3,
-        out_specs=(vmem(),) * (local_halves + 2),
-        scratch_shapes=[pltpu.SemaphoreType.DMA((local_halves, each)), pltpu.SemaphoreType.DMA((tenants,))],
+        out_shape=(pltpu.VMEM((each, part_width, tile), BF16),) * local_halves + (jax.ShapeDtypeStruct((8, 128), F32),),
+        in_specs=[smem()] + [pl.BlockSpec(memory_space=pltpu.HBM)] * 2,
+        out_specs=(vmem(),) * (local_halves + 1),
+        scratch_shapes=[pltpu.SemaphoreType.DMA((local_halves, each))],
         cost_estimate=SMALL,
         compiler_params=params(LIMIT_EARLY),
         name="weight_prefetch",
-    )(ids, adapters, pool_slots, gate, up, pool)
+    )(ids, gate, up)
 
 
 def pack(blocks, p_ref, packed):
@@ -243,10 +236,18 @@
 
 def first_kernel(n_blocks, local_halves, *refs):
     blocks, refs = refs[:n_blocks], refs[n_blocks:]
-    _, p_ref, gate_ref, up_ref, refs = *refs[:4], refs[4:]
+    _, p_ref, gate_ref, up_ref, adapter_ref, pool_slot_ref, pool_ref, refs = *refs[:7], refs[7:]
     slabs, refs = refs[:local_halves], refs[local_halves:]
-    ahead, (gate_out, up_out, mark_out, packed, sems) = refs[:-5], refs[-5:]
+    ahead, (gate_out, up_out, factors, mark_out, packed, sems, factor_sems) = refs[:-7], refs[-7:]
     mark_out[...] = jnp.zeros_like(mark_out)
+    factor_copies = []
+    rank = pool_ref.shape[2]
+    for number in range(adapter_ref.shape[0]):
+        source = pool_ref.at[pool_slot_ref[adapter_ref[number]]]
+        into = factors.at[:, number * rank : (number + 1) * rank]
+        factor_copies.append(pltpu.make_async_copy(source, into, factor_sems.at[number]))
+    for copy in factor_copies:
+        copy.start()
     pack(blocks, p_ref, packed)
     slabs = list(ahead) + list(slabs[len(ahead) :])
     copies = [slab_copies(gate_ref, up_ref, slab, sems, 1, half) for half, slab in enumerate(ahead)]
@@ -261,32 +262,34 @@
             if half < len(ahead):
                 copies[half][2 * tile].start()
                 copies[half][2 * tile + 1].start()
-    for copy in [copy for half in copies for copy in half]:
+    for copy in [copy for half in copies for copy in half] + factor_copies:
         copy.wait()
 
 
-def first_part(blocks, mark, picked, gate, up, slabs):
+def first_part(blocks, mark, picked, gate, up, adapters, pool_slots, pool, slabs):
     local_halves, _, hidden_count = gate.shape
     n_local, row_count, _ = picked.shape
     each, part_width, _ = slabs[0].shape
+    tenants, rank = adapters.shape[0], pool.shape[2]
     hbm = pl.BlockSpec(memory_space=pltpu.HBM)
     sums = pltpu.VMEM((local_halves, row_count, hidden_count), F32)
     n_ahead = max(1, local_halves - 2)
     return pl.pallas_call(
         functools.partial(first_kernel, len(blocks), local_halves),
         out_shape=(pltpu.VMEM(slabs[0].shape, BF16),) * n_ahead
-        + (sums, sums, jax.ShapeDtypeStruct((8, 128), F32)),
-        in_specs=[vmem()] * (len(blocks) + 2) + [hbm, hbm] + [vmem()] * local_halves,
-        out_specs=(vmem(),) * (n_ahead + 3),
+        + (sums, sums, pltpu.VMEM((local_halves, tenants * rank, hidden_count), BF16), jax.ShapeDtypeStruct((8, 128), F32)),
+        in_specs=[vmem()] * (len(blocks) + 2) + [hbm, hbm, smem(), smem(), hbm] + [vmem()] * local_halves,
+        out_specs=(vmem(),) * (n_ahead + 4),
         scratch_shapes=[
             pltpu.VMEM((n_local, row_count, part_width), BF16),
             pltpu.SemaphoreType.DMA((n_ahead, each)),
+            pltpu.SemaphoreType.DMA((tenants,)),
         ],
-        input_output_aliases={len(blocks) + 4 + half: half for half in range(n_ahead)},
+        input_output_aliases={len(blocks) + 7 + half: half for half in range(n_ahead)},
         cost_estimate=SMALL,
         compiler_params=params(max(LIMIT_EARLY, 10 * n_local * row_count * part_width // MIB)),
         name="gate_up_first",
-    )(*blocks, mark, picked, gate, up, *[pltpu.with_memory_space_constraint(x, pltpu.VMEM) for x in slabs])
+    )(*blocks, mark, picked, gate, up, adapters, pool_slots, pool, *[pltpu.with_memory_space_constraint(x, pltpu.VMEM) for x in slabs])
 
 
 def second_kernel(n_blocks, n_ahead, n_ad, steps, *refs):
@@ -572,9 +575,7 @@
 
     order = sorted(range(1, n_ad), key=lambda step: (step != n_ad // 2, step))
     token_part = token_parts_of(tokens, chosen_experts, router_gate_logits, token_tenant)
-    *slabs, factors, mark = prefetch(
-        ids, adapter_of_tenant, adapter_pool_slot, gate_weight, up_weight, adapter_input_factors, width // 2
-    )
+    *slabs, mark = prefetch(ids, gate_weight, up_weight, width // 2)
     high = 1 << (bits - 1)
     crossing = [swap(own, high) for own in token_part]
 
@@ -590,7 +591,9 @@
     picked, pt, cols, table_rows, tslot = build_meta(
         blocks, ids, adapter_of_tenant, adapter_pool_slot, n_local, local_halves, row_count
     )
-    *ahead, gate_sum, up_sum, mark = first_part(blocks, mark, picked, gate_weight, up_weight, slabs)
+    *ahead, gate_sum, up_sum, factors, mark = first_part(
+        blocks, mark, picked, gate_weight, up_weight, adapter_of_tenant, adapter_pool_slot, adapter_input_factors, slabs
+    )
     crossing[1], mark = tie(crossing[1], mark)
     hidden, low, weights, *following = second_part(
         spread(1, crossing[1]), mark, picked, gate_weight, up_weight, ahead, (gate_sum, up_sum), ids, factors,

time: 92 us -> 95.2 us (1.035)
  local copies, waits for them, and re-layouts: 1.32 us -> 3.04 us
  starting transfers between devices: 17.7 us -> 19.4 us
  waiting for transfers between devices: 23 us -> 22 us
    ppermute x14, waiting for transfers between devices: 9.26 us -> 7.42 us  [swap(): return lax.ppermute(x, 'ep', [(i, i ^ mask) for i in range(n_ep)])]
    unnamed x10 -> x22, local copies, waits for them, and re-layouts: 1.32 us -> 3.04 us
    ppermute x14, starting transfers between devices: 8.69 us -> 10.3 us  [swap(): return lax.ppermute(x, 'ep', [(i, i ^ mask) for i in range(n_ep)])]
    pallas_call x1, Pallas kernels: 7.43 us -> 8.97 us  [first_part(): pl.pallas_call(functools.partial(first_kernel, len(blocks), local_halves)...]
  transfers between devices with their start and end apart: 19 -> 19, of which waited for: 10 -> 9; matrix products, arithmetic and copies ran while one was open for 0% -> 0% of each run, Pallas kernels for 37% -> 37%
where the time goes in v12:
time: 95.2 us; the launch traced here: 95 us
  Pallas kernels  49.4 us (52%)
  waiting for transfers between devices  22 us (23%)
  starting transfers between devices  19.4 us (20%)
  local copies, waits for them, and re-layouts  3.04 us (3%)
    pallas_call x1, Pallas kernels, second_part(): pl.pallas_call(functools.partial(second_kernel, len(blocks), len(ahead),...  13.1 us
    ppermute x3, waiting for transfers between devices, shift(): return lax.ppermute(x, 'ad', [(i, (i + step) % n_ad) for i in range(n_ad)])  11.4 us
    ppermute x14, starting transfers between devices, swap(): return lax.ppermute(x, 'ep', [(i, i ^ mask) for i in range(n_ep)])  10.3 us
    pallas_call x1, Pallas kernels, first_part(): pl.pallas_call(functools.partial(first_kernel, len(blocks), local_halves)...  8.97 us
    pallas_call x1, Pallas kernels, prefetch(): pl.pallas_call(prefetch_kernel, out_shape=(pltpu.VMEM((each, part_width,...  8.89 us
    pallas_call x1, Pallas kernels, down_rest(): pl.pallas_call(functools.partial(down_rest_kernel, len(weights), n_ad, st...  8.71 us
    ppermute x14, waiting for transfers between devices, swap(): return lax.ppermute(x, 'ep', [(i, i ^ mask) for i in range(n_ep)])  7.42 us
    ppermute x3, starting transfers between devices, shift(): return lax.ppermute(x, 'ad', [(i, (i + step) % n_ad) for i in range(n_ad)])  4.83 us
  transfers between devices with their start and end apart: 19, of which 9 were waited for; matrix products, arithmetic and copies ran while one was open for 0% of the time, Pallas kernels for 37%

profile of v12, /device:TPU:0, one launch (start us, length us, event | category | flops | bytes accessed | tf_op | source)
XLA Modules:
  0.0 95.0 jit_solution(11257799710637023219)
XLA Ops:
  0.0 1.2 %token_parts.1 = (bf16[128,1664]{1,0:T(8,128)(2,1)S(1)}, bf16[128,1536]{1,0:T(8,128)(2,1)S(1)}) custom-call(bf16[128,3072]{1,0:T(8,128)(2,1)} %tokens_ref.1, s32[2,128]{1,0:T(2,128)} %bitcast.7, f32[2,128]{1,0:T(2,128)} %bitcast.8, s32[1,128]{1,0:T(1,128)} %bitcast.9), custom_call_target="tpu_custom_call" | custom-call | flops 1 | bytes 1 | tf_op jit(solution)/shard_map/token_parts/pallas_call | solution.py:91
  1.2 3.0 %collective-permute-start.3 = (bf16[128,1664]{1,0:T(8,128)(2,1)S(1)}, bf16[128,1664]{1,0:T(8,128)(2,1)S(1)}, u32[]{:S(2)}, u32[]{:S(2)}) collective-permute-start(bf16[128,1664]{1,0:T(8,128)(2,1)S(1)} %get-tuple-element.66.refs_0_), channel_id=1, source_target_pairs={{0,8},{4,12},{8,0},{12,4},{1,9},{5,13},{9,1},{13,5},{2,10},{6,14},... | collective-permute-start | bytes 1277960 | tf_op jit(solution)/shard_map/ppermute | solution.py:568
  4.2 0.0 collective-permute-start.2
  4.2 0.1 pad_add_fusion.ids_ref.refs_12_
  4.3 8.9 %weight_prefetch.1 = (bf16[4,1536,512]{2,1,0:T(8,128)(2,1)S(1)}, bf16[4,1536,512]{2,1,0:T(8,128)(2,1)S(1)}, bf16[4,1536,512]{2,1,0:T(8,128)(2,1)S(1)}, bf16[4,1536,512]{2,1,0:T(8,128)(2,1)S(1)}, f32[8,128]{1,0:T(8,128)S(1)}) custom-call(s32[2]{0:T(128)S(1)} %pad_add_fusion.ids_ref.refs_12_, bf16[4,3072,1024]{2,1,0:T(8,128)(2,1)} %refs_6_.3, ...), custom_call_target="tpu_custom_call" | custom-call | flops 1 | bytes 1 | tf_op jit(solution)/shard_map/weight_prefetch/pallas_call | solution.py:199
  13.2 0.8 collective-permute-done.3.refs_2_
  14.1 0.0 collective-permute-start.4
  14.1 1.7 %collective-permute-start.1 = (bf16[128,1536]{1,0:T(8,128)(2,1)S(1)}, bf16[128,1536]{1,0:T(8,128)(2,1)S(1)}, u32[]{:S(2)}, u32[]{:S(2)}) collective-permute-start(bf16[128,1536]{1,0:T(8,128)(2,1)S(1)} %get-tuple-element.65.refs_0_), channel_id=1, source_target_pairs={{0,8},{4,12},{8,0},{12,4},{1,9},{5,13},{9,1},{13,5},{2,10},{6,14},... | collective-permute-start | bytes 1179656 | tf_op jit(solution)/shard_map/ppermute | solution.py:568
  15.8 0.2 collective-permute-start
  16.1 1.1 %routing_tables.1 = (bf16[2,192,512]{2,1,0:T(8,128)(2,1)S(1)}, bf16[2,512,192]{2,1,0:T(8,128)(2,1)S(1)}, f32[512,128]{1,0:T(8,128)S(1)}, f32[8,512]{1,0:T(8,128)S(1)}, f32[2,8,192]{2,1,0:T(8,128)S(1)}) custom-call(s32[2]{0:T(128)S(1)} %pad_add_fusion.ids_ref.refs_12_, s32[16]{0:T(128)S(1)} %copy-done.9, s32[64]{0:T(128)S(1)} %copy-done.10, ...), custom_call_target="tpu_custom_call" | custom-call | flops 1 | bytes 1 | tf_op jit(solution)/shard_map/routing_tables/pallas_call | solution.py:159
  17.2 1.0 %copy-done.2 = bf16[128,1664]{1,0:T(8,128)(2,1)S(1)} copy-done((bf16[128,1664]{1,0:T(8,128)(2,1)S(1)}, bf16[128,1664]{1,0:T(8,128)(2,1)}, u32[]{:S(2)}) %copy-start.2) | copy-done | bytes 426008
  18.2 1.0 %copy-done.4 = bf16[128,1664]{1,0:T(8,128)(2,1)S(1)} copy-done((bf16[128,1664]{1,0:T(8,128)(2,1)S(1)}, bf16[128,1664]{1,0:T(8,128)(2,1)}, u32[]{:S(2)}) %copy-start.4) | copy-done | bytes 426008
  19.2 1.0 %copy-done.6 = bf16[128,1664]{1,0:T(8,128)(2,1)S(1)} copy-done((bf16[128,1664]{1,0:T(8,128)(2,1)S(1)}, bf16[128,1664]{1,0:T(8,128)(2,1)}, u32[]{:S(2)}) %copy-start.6) | copy-done | bytes 426008
  20.2 9.0 %gate_up_first.1 = (bf16[4,1536,512]{2,1,0:T(8,128)(2,1)S(1)}, bf16[4,1536,512]{2,1,0:T(8,128)(2,1)S(1)}, f32[4,192,1024]{2,1,0:T(8,128)S(1)}, f32[4,192,1024]{2...) custom-call(bf16[128,1664]{1,0:T(8,128)(2,1)S(1)} %copy-done.2, ...), custom_call_target="tpu_custom_call", output_to_operand_aliasing={{0}: (11, {}), {1}: (12, {})} | custom-call | flops 1 | bytes 1 | tf_op jit(solution)/shard_map/gate_up_first/pallas_call | solution.py:277
  29.2 0.0 collective-permute-done.1.refs_2_
  29.2 0.3 collective-permute-start.5
  29.5 0.0 collective-permute-done.refs_1_
  29.6 1.4 %collective-permute-done.5.refs_3_ = bf16[128,1536]{1,0:T(8,128)(2,1)S(1)} collective-permute-done((bf16[128,1536]{1,0:T(8,128)(2,1)S(1)}, bf16[128,1536]{1,0:T(8,128)(2,1)S(1)}, u32[]{:S(2)}, u32[]{:S(2)}) %collective-permute-start.5) | collective-permute-done | bytes 393248 | tf_op jit(solution)/shard_map/ppermute | solution.py:568
  31.0 13.1 %gate_up_second.1 = (bf16[4,192,1024]{2,1,0:T(8,128)(2,1)S(1)}, bf16[32,512]{1,0:T(8,128)(2,1)S(1)}, bf16[4,1024,768]{2,1,0:T(8,128)(2,1)S(1)}, bf16[2,1024,768]{2,1,0:T(8,128)(2,1)S(1)}) custom-call(bf16[128,1536]{1,0:T(8,128)(2,1)S(1)} %copy-done.8, bf16[128,1536]{1,0:T(8,128)(2,1)S(1)} %collective-permute-done.refs_1_, ...), custom_call_target="tpu_custom_call" | custom-call | flops 1 | bytes 1 | tf_op jit(solution)/shard_map/gate_up_second/pallas_call | solution.py:357
  44.1 2.7 %collective-permute-start.6 = (bf16[32,512]{1,0:T(8,128)(2,1)S(1)}, bf16[32,512]{1,0:T(8,128)(2,1)S(1)}, u32[]{:S(2)}, u32[]{:S(2)}) collective-permute-start(bf16[32,512]{1,0:T(8,128)(2,1)S(1)} %get-tuple-element.85), channel_id=1, source_target_pairs={{0,2},{1,3},{2,0},{3,1},{4,6},{5,7},{6,4},{7,5},{8,10},{9,11},{10,... | collective-permute-start | bytes 98312 | tf_op jit(solution)/shard_map/ppermute | solution.py:610
  46.8 4.1 %down_first.1 = (bf16[256,768]{1,0:T(8,128)(2,1)S(1)}, bf16[256,768]{1,0:T(8,128)(2,1)S(1)}, bf16[2,1024,768]{2,1,0:T(8,128)(2,1)S(1)}) custom-call(s32[2]{0:T(128)S(1)} %pad_add_fusion.ids_ref.refs_12_, bf16[4,192,1024]{2,1,0:T(8,128)(2,1)S(1)} %get-tuple-element.98.hidden_ref, bf16[4,1024,768]{2,1,0:T(8,128)(2,1)S(1)} %get-tuple-element.87.weight_ref, ...), custom_call_target="tpu_custom_call" | custom-call | flops 1 | bytes 1 | tf_op jit(solution)/shard_map/down_first/pallas_call | solution.py:408
  50.9 0.1 collective-permute-start.7
  51.0 0.6 collective-permute-start.9
  51.5 1.1 %collective-permute-done.7.came_ref = bf16[256,768]{1,0:T(8,128)(2,1)S(1)} collective-permute-done((bf16[256,768]{1,0:T(8,128)(2,1)S(1)}, bf16[256,768]{1,0:T(8,128)(2,1)S(1)}, u32[]{:S(2)}, u32[]{:S(2)}) %collective-permute-start.7) | collective-permute-done | bytes 393248 | tf_op jit(solution)/shard_map/ppermute | solution.py:568
  52.7 0.1 sum_and_split.3
  52.8 1.5 %collective-permute-start.8 = (bf16[128,768]{1,0:T(8,128)(2,1)S(1)}, bf16[128,768]{1,0:T(8,128)(2,1)S(1)}, u32[]{:S(2)}, u32[]{:S(2)}) collective-permute-start(bf16[128,768]{1,0:T(8,128)(2,1)S(1)} %get-tuple-element.95), channel_id=1, source_target_pairs={{0,8},{4,12},{8,0},{12,4},{1,9},{5,13},{9,1},{13,5},{2,10},{6,14},... | collective-permute-start | bytes 589832 | tf_op jit(solution)/shard_map/ppermute | solution.py:568
  54.3 0.0 collective-permute-done.9
  54.3 0.6 collective-permute-start.10
  54.9 8.7 %down_rest.1 = (bf16[256,1536]{1,0:T(8,128)(2,1)S(1)}, bf16[256,1536]{1,0:T(8,128)(2,1)S(1)}, f32[512,768]{1,0:T(8,128)S(1)}) custom-call(s32[2]{0:T(128)S(1)} %pad_add_fusion.ids_ref.refs_12_, bf16[4,192,1024]{2,1,0:T(8,128)(2,1)S(1)} %get-tuple-element.98.hidden_ref, bf16[2,512,192]{2,1,0:T(8,128)(2,1)S(1)} %get-tuple-element.88.pt_ref, ...), custom_call_target="tpu_custom_call" | custom-call | flops 1 | bytes 1 | tf_op jit(solution)/shard_map/down_rest/pallas_call | solution.py:445
  63.7 0.1 collective-permute-start.11
  63.8 2.3 %collective-permute-done.11.came_ref = bf16[256,1536]{1,0:T(8,128)(2,1)S(1)} collective-permute-done((bf16[256,1536]{1,0:T(8,128)(2,1)S(1)}, bf16[256,1536]{1,0:T(8,128)(2,1)S(1)}, u32[]{:S(2)}, u32[]{:S(2)}) %collective-permute-start.11) | collective-permute-done | bytes 786464 | tf_op jit(solution)/shard_map/ppermute | solution.py:568
  66.0 0.2 sum_and_split.4
  66.2 1.5 %collective-permute-start.12 = (bf16[128,1536]{1,0:T(8,128)(2,1)S(1)}, bf16[128,1536]{1,0:T(8,128)(2,1)S(1)}, u32[]{:S(2)}, u32[]{:S(2)}) collective-permute-start(bf16[128,1536]{1,0:T(8,128)(2,1)S(1)} %get-tuple-element.106), channel_id=1, source_target_pairs={{0,8},{4,12},{8,0},{12,4},{1,9},{5,13},{9,1},{13,5},{2,10},{6,14},... | collective-permute-start | bytes 1179656 | tf_op jit(solution)/shard_map/ppermute | solution.py:568
  67.8 1.6 %collective-permute-start.14 = (bf16[128,512]{1,0:T(8,128)(2,1)S(1)}, bf16[128,512]{1,0:T(8,128)(2,1)S(1)}, u32[]{:S(2)}, u32[]{:S(2)}) collective-permute-start(bf16[128,512]{1,0:T(8,128)(2,1)S(1)} %pad_maximum_fusion), channel_id=1, source_target_pairs={{0,1},{1,0},{2,3},{3,2},{4,5},{5,4},{6,7},{7,6},{8,9},{9,8},{10,11... | collective-permute-start | bytes 393224 | tf_op jit(solution)/shard_map/ppermute | solution.py:610
  69.5 1.0 %collective-permute-start.13 = (bf16[128,768]{1,0:T(8,128)(2,1)S(1)}, bf16[128,768]{1,0:T(8,128)(2,1)S(1)}, u32[]{:S(2)}, u32[]{:S(2)}) collective-permute-start(bf16[128,768]{1,0:T(8,128)(2,1)S(1)} %sum_and_cut.2), channel_id=1, source_target_pairs={{0,2},{1,3},{2,0},{3,1},{4,6},{5,7},{6,4},{7,5},{8,10},{9,11},{10,... | collective-permute-start | bytes 589832 | tf_op jit(solution)/shard_map/ppermute | solution.py:574
  70.4 3.2 %collective-permute-done.14 = bf16[128,512]{1,0:T(8,128)(2,1)S(1)} collective-permute-done((bf16[128,512]{1,0:T(8,128)(2,1)S(1)}, bf16[128,512]{1,0:T(8,128)(2,1)S(1)}, u32[]{:S(2)}, u32[]{:S(2)}) %collective-permute-start.14) | collective-permute-done | bytes 131104 | tf_op jit(solution)/shard_map/ppermute | solution.py:610
  73.6 2.8 %adapters.1 = (bf16[256,768]{1,0:T(8,128)(2,1)S(1)}, bf16[256,768]{1,0:T(8,128)(2,1)S(1)}) custom-call(s32[2]{0:T(128)S(1)} %pad_add_fusion.ids_ref.refs_12_, f32[512,768]{1,0:T(8,128)S(1)} %get-tuple-element.109.base_ref, f32[512,128]{1,0:T(8,128)S(1)} %get-tuple-element.89.cols_ref, bf16[2048,768]{1,0:T(8,128)(2,1)S(1)} %bitcast.6, ...), custom_call_target="tpu_custom_call" | custom-call | flops 1 | bytes 1 | tf_op jit(solution)/shard_map/adapters/pallas_call | solution.py:491
  76.4 4.5 %collective-permute-done.13 = bf16[128,768]{1,0:T(8,128)(2,1)S(1)} collective-permute-done((bf16[128,768]{1,0:T(8,128)(2,1)S(1)}, bf16[128,768]{1,0:T(8,128)(2,1)S(1)}, u32[]{:S(2)}, u32[]{:S(2)}) %collective-permute-start.13) | collective-permute-done | bytes 196640 | tf_op jit(solution)/shard_map/ppermute | solution.py:574
  81.0 1.7 %collective-permute-done.15.came_ref = bf16[256,768]{1,0:T(8,128)(2,1)S(1)} collective-permute-done((bf16[256,768]{1,0:T(8,128)(2,1)S(1)}, bf16[256,768]{1,0:T(8,128)(2,1)S(1)}, u32[]{:S(2)}, u32[]{:S(2)}) %collective-permute-start.15) | collective-permute-done | bytes 393248 | tf_op jit(solution)/shard_map/ppermute | solution.py:568
  82.7 0.1 sum_and_split.5
  82.8 0.1 sum_and_cut.3
  82.9 0.1 collective-permute-start.17
  82.9 3.8 %collective-permute-start.18 = (bf16[128,768]{1,0:T(8,128)(2,1)S(1)}, bf16[128,768]{1,0:T(8,128)(2,1)S(1)}, u32[]{:S(2)}, u32[]{:S(2)}) collective-permute-start(bf16[128,768]{1,0:T(8,128)(2,1)S(1)} %get-tuple-element.124), channel_id=1, source_target_pairs={{0,3},{1,0},{2,1},{3,2},{4,7},{5,4},{6,5},{7,6},{8,11},{9,8},{10,9... | collective-permute-start | bytes 589832 | tf_op jit(solution)/shard_map/ppermute | solution.py:574
  86.8 0.5 collective-permute-start.16
  87.3 5.2 %collective-permute-done.17 = bf16[128,768]{1,0:T(8,128)(2,1)S(1)} collective-permute-done((bf16[128,768]{1,0:T(8,128)(2,1)S(1)}, bf16[128,768]{1,0:T(8,128)(2,1)S(1)}, u32[]{:S(2)}, u32[]{:S(2)}) %collective-permute-start.17) | collective-permute-done | bytes 196640 | tf_op jit(solution)/shard_map/ppermute | solution.py:574
  92.5 1.6 %collective-permute-done.18 = bf16[128,768]{1,0:T(8,128)(2,1)S(1)} collective-permute-done((bf16[128,768]{1,0:T(8,128)(2,1)S(1)}, bf16[128,768]{1,0:T(8,128)(2,1)S(1)}, u32[]{:S(2)}, u32[]{:S(2)}) %collective-permute-start.18) | collective-permute-done | bytes 196640 | tf_op jit(solution)/shard_map/ppermute | solution.py:574
  94.2 0.0 collective-permute-done.16
  94.2 0.8 add_convert_fusion
  (31 shorter events, 0.2 us)
Async XLA Ops:
  1.2 14.6 %copy-start.7 = (bf16[128,1536]{1,0:T(8,128)(2,1)}, bf16[128,1536]{1,0:T(8,128)(2,1)S(1)}, u32[]{:S(2)}) copy-start(bf16[128,1536]{1,0:T(8,128)(2,1)S(1)} %get-tuple-element.65.refs_0_) | copy-start | bytes 1179652
  1.2 14.8 %copy-start.1 = (bf16[128,1664]{1,0:T(8,128)(2,1)}, bf16[128,1664]{1,0:T(8,128)(2,1)S(1)}, u32[]{:S(2)}) copy-start(bf16[128,1664]{1,0:T(8,128)(2,1)S(1)} %get-tuple-element.66.refs_0_) | copy-start | bytes 1277956
  1.2 12.8 %collective-permute-start.3 = (bf16[128,1664]{1,0:T(8,128)(2,1)S(1)}, bf16[128,1664]{1,0:T(8,128)(2,1)S(1)}, u32[]{:S(2)}, u32[]{:S(2)}) collective-permute-start(bf16[128,1664]{1,0:T(8,128)(2,1)S(1)} %get-tuple-element.66.refs_0_), channel_id=1, source_target_pairs={{0,8},{4,12},{8,0},{12,4},{1,9},{5,13},{9,1},{13,5},{2,10},{6,14},... | collective-permute-start | bytes 1277960 | tf_op jit(solution)/shard_map/ppermute | solution.py:568
  4.2 11.8 %collective-permute-start.2 = (bf16[128,1664]{1,0:T(8,128)(2,1)S(1)}, bf16[128,1664]{1,0:T(8,128)(2,1)S(1)}, u32[]{:S(2)}, u32[]{:S(2)}) collective-permute-start(bf16[128,1664]{1,0:T(8,128)(2,1)S(1)} %get-tuple-element.66.refs_0_), channel_id=1, source_target_pairs={{0,4},{4,0},{8,12},{12,8},{1,5},{5,1},{9,13},{13,9},{2,6},{6,2},{1... | collective-permute-start | bytes 1277960 | tf_op jit(solution)/shard_map/ppermute | solution.py:568
  4.3 11.7 %copy-start.9 = (s32[16]{0:T(128)S(1)}, s32[16]{0:T(128)}, u32[]{:S(2)}) copy-start(s32[16]{0:T(128)} %refs_8_.1) | copy-start | bytes 196
  4.3 11.7 %copy-start.10 = (s32[64]{0:T(128)S(1)}, s32[64]{0:T(128)}, u32[]{:S(2)}) copy-start(s32[64]{0:T(128)} %refs_9_.1) | copy-start | bytes 772
  14.1 3.1 %copy-start.3 = (bf16[128,1664]{1,0:T(8,128)(2,1)}, bf16[128,1664]{1,0:T(8,128)(2,1)S(1)}, u32[]{:S(2)}) copy-start(bf16[128,1664]{1,0:T(8,128)(2,1)S(1)} %collective-permute-done.3.refs_2_) | copy-start | bytes 1277956
  14.1 2.0 %collective-permute-start.4 = (bf16[128,1664]{1,0:T(8,128)(2,1)S(1)}, bf16[128,1664]{1,0:T(8,128)(2,1)S(1)}, u32[]{:S(2)}, u32[]{:S(2)}) collective-permute-start(bf16[128,1664]{1,0:T(8,128)(2,1)S(1)} %collective-permute-done.3.refs_2_), channel_id=1, source_target_pairs={{0,4},{4,0},{8,12},{12,8},{1,5},{5,1},{9,13},{13,9},{2,6},{6,2},{1... | collective-permute-start | bytes 1277960 | tf_op jit(solution)/shard_map/ppermute | solution.py:568
  14.1 15.1 %collective-permute-start.1 = (bf16[128,1536]{1,0:T(8,128)(2,1)S(1)}, bf16[128,1536]{1,0:T(8,128)(2,1)S(1)}, u32[]{:S(2)}, u32[]{:S(2)}) collective-permute-start(bf16[128,1536]{1,0:T(8,128)(2,1)S(1)} %get-tuple-element.65.refs_0_), channel_id=1, source_target_pairs={{0,8},{4,12},{8,0},{12,4},{1,9},{5,13},{9,1},{13,5},{2,10},{6,14},... | collective-permute-start | bytes 1179656 | tf_op jit(solution)/shard_map/ppermute | solution.py:568
  15.8 13.7 %collective-permute-start = (bf16[128,1536]{1,0:T(8,128)(2,1)S(1)}, bf16[128,1536]{1,0:T(8,128)(2,1)S(1)}, u32[]{:S(2)}, u32[]{:S(2)}) collective-permute-start(bf16[128,1536]{1,0:T(8,128)(2,1)S(1)} %get-tuple-element.65.refs_0_), channel_id=1, source_target_pairs={{0,4},{4,0},{8,12},{12,8},{1,5},{5,1},{9,13},{13,9},{2,6},{6,2},{1... | collective-permute-start | bytes 1179656 | tf_op jit(solution)/shard_map/ppermute | solution.py:568
  16.0 1.1 %copy-start.5 = (bf16[128,1664]{1,0:T(8,128)(2,1)}, bf16[128,1664]{1,0:T(8,128)(2,1)S(1)}, u32[]{:S(2)}) copy-start(bf16[128,1664]{1,0:T(8,128)(2,1)S(1)} %collective-permute-done.2.refs_1_) | copy-start | bytes 1277956
  17.2 1.0 %copy-start.2 = (bf16[128,1664]{1,0:T(8,128)(2,1)S(1)}, bf16[128,1664]{1,0:T(8,128)(2,1)}, u32[]{:S(2)}) copy-start(bf16[128,1664]{1,0:T(8,128)(2,1)} %copy-done.1) | copy-start | bytes 1277956
  18.2 1.0 %copy-start.4 = (bf16[128,1664]{1,0:T(8,128)(2,1)S(1)}, bf16[128,1664]{1,0:T(8,128)(2,1)}, u32[]{:S(2)}) copy-start(bf16[128,1664]{1,0:T(8,128)(2,1)} %copy-done.3) | copy-start | bytes 1277956
  19.2 1.0 %copy-start.6 = (bf16[128,1664]{1,0:T(8,128)(2,1)S(1)}, bf16[128,1664]{1,0:T(8,128)(2,1)}, u32[]{:S(2)}) copy-start(bf16[128,1664]{1,0:T(8,128)(2,1)} %copy-done.5) | copy-start | bytes 1277956
  20.2 10.8 %copy-start.8 = (bf16[128,1536]{1,0:T(8,128)(2,1)S(1)}, bf16[128,1536]{1,0:T(8,128)(2,1)}, u32[]{:S(2)}) copy-start(bf16[128,1536]{1,0:T(8,128)(2,1)} %copy-done.7) | copy-start | bytes 1179652
  29.2 1.8 %collective-permute-start.5 = (bf16[128,1536]{1,0:T(8,128)(2,1)S(1)}, bf16[128,1536]{1,0:T(8,128)(2,1)S(1)}, u32[]{:S(2)}, u32[]{:S(2)}) collective-permute-start(bf16[128,1536]{1,0:T(8,128)(2,1)S(1)} %collective-permute-done.1.refs_2_), channel_id=1, source_target_pairs={{0,4},{4,0},{8,12},{12,8},{1,5},{5,1},{9,13},{13,9},{2,6},{6,2},{1... | collective-permute-start | bytes 1179656 | tf_op jit(solution)/shard_map/ppermute | solution.py:568
  44.1 6.8 %collective-permute-start.6 = (bf16[32,512]{1,0:T(8,128)(2,1)S(1)}, bf16[32,512]{1,0:T(8,128)(2,1)S(1)}, u32[]{:S(2)}, u32[]{:S(2)}) collective-permute-start(bf16[32,512]{1,0:T(8,128)(2,1)S(1)} %get-tuple-element.85), channel_id=1, source_target_pairs={{0,2},{1,3},{2,0},{3,1},{4,6},{5,7},{6,4},{7,5},{8,10},{9,11},{10,... | collective-permute-start | bytes 98312 | tf_op jit(solution)/shard_map/ppermute | solution.py:610
  50.9 1.8 %collective-permute-start.7 = (bf16[256,768]{1,0:T(8,128)(2,1)S(1)}, bf16[256,768]{1,0:T(8,128)(2,1)S(1)}, u32[]{:S(2)}, u32[]{:S(2)}) collective-permute-start(bf16[256,768]{1,0:T(8,128)(2,1)S(1)} %get-tuple-element.94), channel_id=1, source_target_pairs={{0,4},{4,0},{8,12},{12,8},{1,5},{5,1},{9,13},{13,9},{2,6},{6,2},{1... | collective-permute-start | bytes 1179656 | tf_op jit(solution)/shard_map/ppermute | solution.py:568
  51.0 3.3 %collective-permute-start.9 = (bf16[32,512]{1,0:T(8,128)(2,1)S(1)}, bf16[32,512]{1,0:T(8,128)(2,1)S(1)}, u32[]{:S(2)}, u32[]{:S(2)}) collective-permute-start(bf16[32,512]{1,0:T(8,128)(2,1)S(1)} %add_convert_fusion.2), channel_id=1, source_target_pairs={{0,4},{4,0},{8,12},{12,8},{1,5},{5,1},{9,13},{13,9},{2,6},{6,2},{1... | collective-permute-start | bytes 98312 | tf_op jit(solution)/shard_map/ppermute | solution.py:568
  52.8 10.9 %collective-permute-start.8 = (bf16[128,768]{1,0:T(8,128)(2,1)S(1)}, bf16[128,768]{1,0:T(8,128)(2,1)S(1)}, u32[]{:S(2)}, u32[]{:S(2)}) collective-permute-start(bf16[128,768]{1,0:T(8,128)(2,1)S(1)} %get-tuple-element.95), channel_id=1, source_target_pairs={{0,8},{4,12},{8,0},{12,4},{1,9},{5,13},{9,1},{13,5},{2,10},{6,14},... | collective-permute-start | bytes 589832 | tf_op jit(solution)/shard_map/ppermute | solution.py:568
  54.3 9.3 %collective-permute-start.10 = (bf16[64,512]{1,0:T(8,128)(2,1)S(1)}, bf16[64,512]{1,0:T(8,128)(2,1)S(1)}, u32[]{:S(2)}, u32[]{:S(2)}) collective-permute-start(bf16[64,512]{1,0:T(8,128)(2,1)S(1)} %pad_maximum_fusion.1), channel_id=1, source_target_pairs={{0,8},{4,12},{8,0},{12,4},{1,9},{5,13},{9,1},{13,5},{2,10},{6,14},... | collective-permute-start | bytes 196616 | tf_op jit(solution)/shard_map/ppermute | solution.py:568
  54.9 18.7 %copy-start = (bf16[16,8,16,768]{3,2,1,0:T(8,128)(2,1)S(1)}, bf16[16,8,16,768]{3,2,1,0:T(8,128)(2,1)}, u32[]{:S(2)}) copy-start(bf16[16,8,16,768]{3,2,1,0:T(8,128)(2,1)} %param.21) | copy-start | bytes 9437188
  63.7 2.4 %collective-permute-start.11 = (bf16[256,1536]{1,0:T(8,128)(2,1)S(1)}, bf16[256,1536]{1,0:T(8,128)(2,1)S(1)}, u32[]{:S(2)}, u32[]{:S(2)}) collective-permute-start(bf16[256,1536]{1,0:T(8,128)(2,1)S(1)} %get-tuple-element.105), channel_id=1, source_target_pairs={{0,4},{4,0},{8,12},{12,8},{1,5},{5,1},{9,13},{13,9},{2,6},{6,2},{1... | collective-permute-start | bytes 2359304 | tf_op jit(solution)/shard_map/ppermute | solution.py:568
  66.2 14.8 %collective-permute-start.12 = (bf16[128,1536]{1,0:T(8,128)(2,1)S(1)}, bf16[128,1536]{1,0:T(8,128)(2,1)S(1)}, u32[]{:S(2)}, u32[]{:S(2)}) collective-permute-start(bf16[128,1536]{1,0:T(8,128)(2,1)S(1)} %get-tuple-element.106), channel_id=1, source_target_pairs={{0,8},{4,12},{8,0},{12,4},{1,9},{5,13},{9,1},{13,5},{2,10},{6,14},... | collective-permute-start | bytes 1179656 | tf_op jit(solution)/shard_map/ppermute | solution.py:568
  67.8 5.8 %collective-permute-start.14 = (bf16[128,512]{1,0:T(8,128)(2,1)S(1)}, bf16[128,512]{1,0:T(8,128)(2,1)S(1)}, u32[]{:S(2)}, u32[]{:S(2)}) collective-permute-start(bf16[128,512]{1,0:T(8,128)(2,1)S(1)} %pad_maximum_fusion), channel_id=1, source_target_pairs={{0,1},{1,0},{2,3},{3,2},{4,5},{5,4},{6,7},{7,6},{8,9},{9,8},{10,11... | collective-permute-start | bytes 393224 | tf_op jit(solution)/shard_map/ppermute | solution.py:610
  69.5 11.5 %collective-permute-start.13 = (bf16[128,768]{1,0:T(8,128)(2,1)S(1)}, bf16[128,768]{1,0:T(8,128)(2,1)S(1)}, u32[]{:S(2)}, u32[]{:S(2)}) collective-permute-start(bf16[128,768]{1,0:T(8,128)(2,1)S(1)} %sum_and_cut.2), channel_id=1, source_target_pairs={{0,2},{1,3},{2,0},{3,1},{4,6},{5,7},{6,4},{7,5},{8,10},{9,11},{10,... | collective-permute-start | bytes 589832 | tf_op jit(solution)/shard_map/ppermute | solution.py:574
  81.0 1.7 %collective-permute-start.15 = (bf16[256,768]{1,0:T(8,128)(2,1)S(1)}, bf16[256,768]{1,0:T(8,128)(2,1)S(1)}, u32[]{:S(2)}, u32[]{:S(2)}) collective-permute-start(bf16[256,768]{1,0:T(8,128)(2,1)S(1)} %get-tuple-element.115), channel_id=1, source_target_pairs={{0,4},{4,0},{8,12},{12,8},{1,5},{5,1},{9,13},{13,9},{2,6},{6,2},{1... | collective-permute-start | bytes 1179656 | tf_op jit(solution)/shard_map/ppermute | solution.py:568
  82.9 9.6 %collective-permute-start.17 = (bf16[128,768]{1,0:T(8,128)(2,1)S(1)}, bf16[128,768]{1,0:T(8,128)(2,1)S(1)}, u32[]{:S(2)}, u32[]{:S(2)}) collective-permute-start(bf16[128,768]{1,0:T(8,128)(2,1)S(1)} %get-tuple-element.123), channel_id=1, source_target_pairs={{0,1},{1,2},{2,3},{3,0},{4,5},{5,6},{6,7},{7,4},{8,9},{9,10},{10,1... | collective-permute-start | bytes 589832 | tf_op jit(solution)/shard_map/ppermute | solution.py:574
  82.9 11.2 %collective-permute-start.18 = (bf16[128,768]{1,0:T(8,128)(2,1)S(1)}, bf16[128,768]{1,0:T(8,128)(2,1)S(1)}, u32[]{:S(2)}, u32[]{:S(2)}) collective-permute-start(bf16[128,768]{1,0:T(8,128)(2,1)S(1)} %get-tuple-element.124), channel_id=1, source_target_pairs={{0,3},{1,0},{2,1},{3,2},{4,7},{5,4},{6,5},{7,6},{8,11},{9,8},{10,9... | collective-permute-start | bytes 589832 | tf_op jit(solution)/shard_map/ppermute | solution.py:574
  86.8 7.4 %collective-permute-start.16 = (bf16[128,768]{1,0:T(8,128)(2,1)S(1)}, bf16[128,768]{1,0:T(8,128)(2,1)S(1)}, u32[]{:S(2)}, u32[]{:S(2)}) collective-permute-start(bf16[128,768]{1,0:T(8,128)(2,1)S(1)} %get-tuple-element.119), channel_id=1, source_target_pairs={{0,8},{4,12},{8,0},{12,4},{1,9},{5,13},{9,1},{13,5},{2,10},{6,14},... | collective-permute-start | bytes 589832 | tf_op jit(solution)/shard_map/ppermute | solution.py:568
